TPU v7x, 32 devices: a whole 2x2x4 slice. The times are simulated.
32 devices in a mesh: batch: 2 (over core), seq: 16 (over z, y, x).
Axes of the slice: x: 2, y: 2, z: 4, core: 2. Of those that a mesh axis runs over, the one named last changes fastest.
Arguments:
- inputs: bfloat16 [2, 8192, 768], P('batch', 'seq'), may hold values from -8 to 8
- w_qkv: bfloat16 [768, 2304], replicated, may hold values from -0.21875 to 0.21875
- w_out: bfloat16 [768, 768], replicated, may hold values from -0.875 to 0.875
- w_fc: bfloat16 [768, 3072], replicated, may hold values from -0.21875 to 0.21875
- w_proj: bfloat16 [3072, 768], replicated, may hold values from -0.109375 to 0.109375
- map_query: bfloat16 [12, 64, 64], replicated, may hold values from -1.5 to 1.5
- map_key: bfloat16 [12, 64, 64], replicated, may hold values from -1.5 to 1.5
- gain_attn: float32 [768], replicated, may hold values from 0.1 to 1.9
- gain_mlp: float32 [768], replicated, may hold values from 0.1 to 1.9
- starts: int32 [2, 128], P('batch', 'seq'), may hold values from 0 to 1, as said below
- key_mask: int32 [2, 8192], P('batch', 'seq'), may hold values from 0 to 1, as said below
- cotangent: bfloat16 [2, 8192, 768], P('batch', 'seq'), may hold values from -6 to 6
Outputs:
- output: float32 [2, 8192, 768], P('batch', 'seq')
- grad_inputs: float32 [2, 8192, 768], P('batch', 'seq')
- grad_w_qkv: float32 [768, 2304], P(('batch', 'seq'))
- grad_w_out: float32 [768, 768], P(('batch', 'seq'))
- grad_w_fc: float32 [768, 3072], P(('batch', 'seq'))
- grad_w_proj: float32 [3072, 768], P(None, ('batch', 'seq'))
- grad_map_query: float32 [12, 64, 64], replicated
- grad_map_key: float32 [12, 64, 64], replicated
- grad_gain_attn: float32 [768], replicated
- grad_gain_mlp: float32 [768], replicated
Inputs may be any that keep to these rules, and one draw needn't show every extreme that they name: starts[:, 0] = 1; in every stream one sequence begins within the first 512 tokens and ends within the last 512 tokens; every other sequence spans two or more groups of 64 tokens. `key_mask`: padding lies only at the end of the last 64 tokens of a sequence; the first token of every group of 64 tokens is real.
All inputs are finite; a program needn't handle non-finite values.
Results may differ from a plain program's by a relative error of at most 0.012.
Values sent between devices are 32-bit elements; how exact they have to be, the bound alone decides.
No kernel may reach another device: no remote copies, remote signals or barrier semaphores. Data moves between devices by JAX's collectives and lax.ppermute only.
A program may use at most 512 MiB of HBM per device.

v0:
```python
import jax
import jax.numpy as jnp
from jax import lax
from jax.sharding import PartitionSpec as P

EPSILON = 1e-05
EXACT_PRECISION = lax.Precision.HIGHEST


def carried_in(value, axis, join, neutral, backward):
    count, mine = (lax.axis_size(axis), lax.axis_index(axis))
    pieces = jax.tree.map(lambda part: lax.all_gather(part, axis), value)
    if backward:
        pieces = jax.tree.map(lambda part: part[::-1], pieces)
        mine = count - 1 - mine
    so_far = jax.tree.map(
        lambda part, zero: jnp.full_like(part, 0) + jnp.asarray(zero, part.dtype), value, neutral
    )

    def lap(position, so_far):
        longer = join(so_far, jax.tree.map(lambda part: part[position], pieces))
        return jax.tree.map(lambda new, old: jnp.where(position < mine, new, old), longer, so_far)

    return lax.fori_loop(0, count - 1, lap, so_far)


def normalize(states, gain_vec):
    centre = jnp.mean(states, axis=-1, keepdims=True)
    offsets = states - centre
    variance = jnp.mean(offsets * offsets, axis=-1, keepdims=True)
    return offsets * lax.rsqrt(variance + EPSILON) * gain_vec


def feature_map(pre_map):
    return jnp.concatenate(
        [jax.nn.softmax(pre_map, axis=-1), jax.nn.softmax(-pre_map, axis=-1)], axis=-1
    )


def smooth_gate(pre_act):
    return jax.nn.gelu(pre_act, approximate=True)


def merge_states(earlier, latter):
    carried = 1.0 - latter[0]
    return (
        jnp.maximum(earlier[0], latter[0]),
        latter[1] + carried * earlier[1],
        latter[2] + carried * earlier[2],
    )


def allowed_pairs(counts_blk, live_blk):
    position = jnp.arange(counts_blk.shape[0])
    causal = position[None, :] <= position[:, None]
    same_seg = counts_blk[None, :] == counts_blk[:, None]
    return (causal & same_seg).astype(jnp.float32) * live_blk[None, :]


def masked_scores(query_feature_block, key_feature_block, permitted_pairs):
    unmasked_scores = jnp.einsum(
        "oaz,eaz->aoe", query_feature_block, key_feature_block, preferred_element_type=jnp.float32
    )
    return unmasked_scores * permitted_pairs[None]


def column_terms(left_mat, right_mat):
    return lax.dot_general(
        left_mat, right_mat, (((0,), (0,)), ((), ())), preferred_element_type=jnp.float32
    )


def right_product(left_mat, weight_mat):
    return lax.dot_general(
        left_mat, weight_mat, (((1,), (1,)), ((), ())), preferred_element_type=jnp.float32
    )


def local(
    inputs,
    w_qkv,
    w_out,
    w_fc,
    w_proj,
    map_query,
    map_key,
    gain_attn,
    gain_mlp,
    starts,
    key_mask,
    cotangent,
):
    tok_rows = inputs.shape[1]
    model_dim = inputs.shape[2]
    n_heads = map_query.shape[0]
    head_dim = map_query.shape[1]
    ff_width = w_fc.shape[1]
    block_len = min(512, tok_rows)
    n_blocks = tok_rows // block_len
    flag_row = starts[0]
    unit_len = tok_rows // flag_row.shape[0]
    seg_count = jnp.repeat(jnp.cumsum(flag_row), unit_len)
    live_keys = key_mask[0].astype(jnp.float32)
    residual_in = inputs[0].astype(jnp.float32)
    normed_attn, attn_norm_back = jax.vjp(normalize, residual_in, gain_attn)
    attn_in = normed_attn.astype(jnp.bfloat16)
    qkv_low = jnp.dot(attn_in, w_qkv, preferred_element_type=jnp.float32).astype(jnp.bfloat16)
    queries = qkv_low[:, :model_dim].reshape(tok_rows, n_heads, head_dim)
    keys_all = qkv_low[:, model_dim : 2 * model_dim].reshape(tok_rows, n_heads, head_dim)
    every_value = qkv_low[:, 2 * model_dim :].reshape(tok_rows, n_heads, head_dim)
    pre_query = jnp.einsum("thd,hde->the", queries, map_query, preferred_element_type=jnp.float32)
    pre_key = jnp.einsum("thd,hde->the", keys_all, map_key, preferred_element_type=jnp.float32)
    query_feats, query_map_back = jax.vjp(feature_map, pre_query)
    key_feats, key_map_back = jax.vjp(feature_map, pre_key)
    query_feature_map = query_feats.astype(jnp.bfloat16)
    key_feature_map = key_feats.astype(jnp.bfloat16)
    feat_dim = query_feature_map.shape[2]
    empty_state = (
        jnp.zeros((1,), jnp.float32),
        jnp.zeros((n_heads, feat_dim, head_dim), jnp.float32),
        jnp.zeros((n_heads, feat_dim), jnp.float32),
    )
    summary = empty_state
    block_idx = 0
    row_lo = block_idx * block_len
    permitted_pairs = allowed_pairs(seg_count, live_keys)
    score_matrix = masked_scores(query_feature_map, key_feature_map, permitted_pairs)
    numerator_parts = [
        jnp.einsum(
            "hqk,khd->qhd",
            score_matrix.astype(jnp.bfloat16),
            every_value,
            preferred_element_type=jnp.float32,
        )
    ]
    denominator_parts = [jnp.sum(score_matrix, axis=-1).T]
    before = seg_count[0] - flag_row[row_lo // unit_len]
    last_count = seg_count[block_len - 1]
    contin = (seg_count == before).astype(jnp.float32)
    tail_mark = (seg_count == last_count).astype(jnp.float32) * live_keys
    trailing_keys = key_feature_map * tail_mark.astype(jnp.bfloat16)[:, None, None]
    trailing_state = jnp.einsum(
        "wba,wbm->bam", trailing_keys, every_value, preferred_element_type=jnp.float32
    )
    tail_sum = jnp.sum(trailing_keys.astype(jnp.float32), axis=0)
    reset_flag = (last_count > before).astype(jnp.float32).reshape(1)
    element = (reset_flag, trailing_state, tail_sum)
    summary = merge_states(summary, element)
    block_info = [(permitted_pairs, contin, tail_mark, element)]
    incoming = carried_in(summary, "seq", merge_states, empty_state, False)
    block_idx = 0
    permitted_pairs, contin, tail_mark, element = block_info[block_idx]
    fq_wide = query_feature_map.astype(jnp.float32)
    carried_list = [incoming]
    numerator = numerator_parts[block_idx] + contin[:, None, None] * jnp.einsum(
        "qhf,hfd->qhd", fq_wide, incoming[1], precision=EXACT_PRECISION
    )
    denominator = denominator_parts[block_idx] + contin[:, None] * jnp.einsum(
        "qhf,hf->qh", fq_wide, incoming[2], precision=EXACT_PRECISION
    )
    mixed_low = (
        (numerator / denominator[:, :, None]).reshape(tok_rows, model_dim).astype(jnp.bfloat16)
    )
    hidden = residual_in + jnp.dot(mixed_low, w_out, preferred_element_type=jnp.float32)
    normed_mlp, mlp_norm_back = jax.vjp(normalize, hidden, gain_mlp)
    mlp_in = normed_mlp.astype(jnp.bfloat16)
    pre_act = jnp.dot(mlp_in, w_fc, preferred_element_type=jnp.float32)
    act_value, gate_back = jax.vjp(smooth_gate, pre_act)
    act_low = act_value.astype(jnp.bfloat16)
    output = hidden + jnp.dot(act_low, w_proj, preferred_element_type=jnp.float32)
    grad_out_low = cotangent[0]
    grad_act = right_product(grad_out_low, w_proj)
    grad_pre = gate_back(grad_act)[0].astype(jnp.bfloat16)
    grad_norm_mlp = right_product(grad_pre, w_fc)
    grad_hidden_ln, grad_gain_mlp = mlp_norm_back(grad_norm_mlp)
    grad_hidden = grad_out_low.astype(jnp.float32) + grad_hidden_ln
    grad_hidden_low = grad_hidden.astype(jnp.bfloat16)
    grad_mixed = right_product(grad_hidden_low, w_out).reshape(tok_rows, n_heads, head_dim)
    grad_numer_all = (grad_mixed / denominator[:, :, None]).astype(jnp.bfloat16)
    grad_denom_all = -jnp.sum(grad_mixed * numerator, axis=-1) / (denominator * denominator)
    device_sum = jnp.zeros((n_heads, feat_dim), jnp.float32)
    pass_rate = jnp.ones((1,), jnp.float32)
    block_idx = 0
    permitted_pairs, contin, tail_mark, element = block_info[block_idx]
    score_matrix = masked_scores(query_feature_map, key_feature_map, permitted_pairs)
    score_gradient = (
        jnp.einsum("qhd,khd->hqk", grad_numer_all, every_value, preferred_element_type=jnp.float32)
        + grad_denom_all.T[:, :, None]
    )
    score_gradient = (
        score_gradient.astype(jnp.bfloat16) * permitted_pairs.astype(jnp.bfloat16)[None]
    )
    query_feature_gradient = jnp.einsum(
        "gzs,sgd->zgd", score_gradient, key_feature_map, preferred_element_type=jnp.float32
    )
    grad_fk = jnp.einsum(
        "lpo,plt->olt", score_gradient, query_feature_map, preferred_element_type=jnp.float32
    )
    grad_val = jnp.einsum(
        "hqk,qhd->khd",
        score_matrix.astype(jnp.bfloat16),
        grad_numer_all,
        preferred_element_type=jnp.float32,
    )
    carried = carried_list[block_idx]
    inter_term = (
        jnp.einsum(
            "qhd,hfd->qhf",
            grad_numer_all.astype(jnp.float32),
            carried[1],
            precision=EXACT_PRECISION,
        )
        + grad_denom_all[:, :, None] * carried[2][None]
    )
    query_feature_gradient = query_feature_gradient + contin[:, None, None] * inter_term
    local_state = jnp.einsum(
        "qhf,qhd->hfd",
        query_feature_map * contin.astype(jnp.bfloat16)[:, None, None],
        grad_numer_all,
        preferred_element_type=jnp.float32,
    )
    local_sum = jnp.einsum(
        "qhf,qh->hf",
        query_feature_map.astype(jnp.float32),
        grad_denom_all * contin[:, None],
        precision=EXACT_PRECISION,
    )
    device_state = pass_rate * local_state
    device_sum = device_sum + pass_rate * local_sum
    grad_fk_parts = [grad_fk]
    grad_val_parts = [grad_val]
    local_states = [local_state]
    local_sums = [local_sum]
    outgoing = carried_in(
        (summary[0], device_state, device_sum), "seq", merge_states, empty_state, True
    )
    upstream_gradient = (outgoing[1], outgoing[2])
    for block_idx in reversed(range(n_blocks)):
        row_lo = block_idx * block_len
        permitted_pairs, contin, tail_mark, element = block_info[block_idx]
        key_feature_full = key_feature_map.astype(jnp.float32)
        value_full = every_value.astype(jnp.float32)
        key_term = (
            jnp.einsum("jlc,lpc->jlp", value_full, upstream_gradient[0], precision=EXACT_PRECISION)
            + upstream_gradient[1][None]
        )
        grad_fk_parts[block_idx] = grad_fk_parts[block_idx] + tail_mark[:, None, None] * key_term
        value_contribution = jnp.einsum(
            "gjs,jsw->gjw", key_feature_full, upstream_gradient[0], precision=EXACT_PRECISION
        )
        grad_val_parts[block_idx] = (
            grad_val_parts[block_idx] + tail_mark[:, None, None] * value_contribution
        )
        keep_rate = 1.0 - element[0]
        upstream_gradient = (
            local_states[block_idx] + keep_rate * upstream_gradient[0],
            local_sums[block_idx] + keep_rate * upstream_gradient[1],
        )
    grad_pre_query = query_map_back(query_feature_gradient)[0].astype(jnp.bfloat16)
    grad_pre_key = key_map_back(grad_fk_parts[0])[0].astype(jnp.bfloat16)
    grad_values = grad_val_parts[0]
    grad_map_query = jnp.einsum(
        "thd,the->hde", queries, grad_pre_query, preferred_element_type=jnp.float32
    )
    grad_map_key = jnp.einsum(
        "thd,the->hde", keys_all, grad_pre_key, preferred_element_type=jnp.float32
    )
    grad_queries = jnp.einsum(
        "the,hde->thd", grad_pre_query, map_query, preferred_element_type=jnp.float32
    )
    grad_keys = jnp.einsum(
        "the,hde->thd", grad_pre_key, map_key, preferred_element_type=jnp.float32
    )
    grad_qkv = jnp.concatenate(
        [
            grad_queries.reshape(tok_rows, model_dim),
            grad_keys.reshape(tok_rows, model_dim),
            grad_values.reshape(tok_rows, model_dim),
        ],
        axis=1,
    ).astype(jnp.bfloat16)
    grad_norm_attn = right_product(grad_qkv, w_qkv)
    grad_resid_ln, grad_gain_attn = attn_norm_back(grad_norm_attn)
    grad_inputs = grad_hidden + grad_resid_ln
    summed = lax.psum_scatter(
        jnp.concatenate(
            [
                column_terms(attn_in, grad_qkv),
                column_terms(mixed_low, grad_hidden_low),
                column_terms(mlp_in, grad_pre),
                column_terms(grad_out_low, act_low),
            ],
            axis=1,
        ),
        ("batch", "seq"),
        scatter_dimension=0,
        tiled=True,
    )
    grad_w_qkv = summed[:, : 3 * model_dim]
    grad_w_out = summed[:, 3 * model_dim : 4 * model_dim]
    grad_w_fc = summed[:, 4 * model_dim : 4 * model_dim + ff_width]
    grad_proj_rows = summed[:, 4 * model_dim + ff_width :]
    reduced = lax.psum(
        (grad_map_query, grad_map_key, grad_gain_attn, grad_gain_mlp), ("batch", "seq")
    )
    return (
        output[None],
        grad_inputs[None],
        grad_w_qkv,
        grad_w_out,
        grad_w_fc,
        grad_proj_rows.T,
        reduced[0],
        reduced[1],
        reduced[2],
        reduced[3],
    )


def solution(mesh):
    return jax.shard_map(
        local,
        mesh=mesh,
        in_specs=(
            P("batch", "seq", None),
            P(),
            P(),
            P(),
            P(),
            P(),
            P(),
            P(),
            P(),
            P("batch", "seq"),
            P("batch", "seq"),
            P("batch", "seq", None),
        ),
        out_specs=(
            P("batch", "seq", None),
            P("batch", "seq", None),
            P(("batch", "seq"), None),
            P(("batch", "seq"), None),
            P(("batch", "seq"), None),
            P(None, ("batch", "seq")),
            P(),
            P(),
            P(),
            P(),
        ),
        check_vma=False,
    )
```

profile of v0, /device:TPU:0, one launch (start us, length us, event | category | flops | bytes accessed | tf_op | source)
XLA Modules:
  0.0 938.1 jit_solution(15702854728393927870)
XLA Ops:
  16.8 3.6 fusion.103
  20.4 3.5 fusion.104
  40.7 44.8 %all-reduce = f32[16]{0:T(128)} all-reduce(f32[16]{0:T(128)} %dynamic-update-slice), channel_id=1, replica_groups=mesh['batch'=2,'seq'=16] {'seq'}, use_global_device_ids=true, to_apply=%add | all-reduce | flops 16 | bytes 128
  87.3 39.7 %all-gather.4 = f32[16,12,128]{2,1,0:T(8,128)} all-gather(f32[1,12,128]{2,1,0:T(8,128)S(1)} %add_bitcast_fusion.3), channel_id=3, replica_groups=mesh['batch'=2,'seq'=16] {'seq'}, dimensions={0}, use_global_device_ids=true | all-gather | bytes 104448 | tf_op jit(solution)/shard_map/all_gather | solution.py:12
  129.5 3.6 fusion.105
  133.1 3.5 fusion.106
  136.6 2.5 divide_convert_fusion.3
  141.7 4.6 copy-done.1
  146.3 2.6 fusion.25
  148.9 133.3 %while.32 = (s32[]{:T(128)}, f32[12,128,64]{2,1,0:T(8,128)}, f32[12,128]{1,0:T(8,128)S(1)}, s32[]{:T(128)}, f32[16,12,128,64]{2,3,1,0:T(8,128)}, /*index=5*/f32[...) while((s32[]{:T(128)}, f32[12,128,64]{2,1,0:T(8,128)}, ...), condition=%wide.region_13.14_spmd.clone, body=%wide.region_12.13_spmd.clone.sunk | while | flops 399365 | bytes 2771095 | solution.py:24
  155.2 2.8 fusion.163
  163.9 3.0 fusion.163
  172.7 3.0 fusion.163
  181.6 3.0 fusion.163
  190.5 3.0 fusion.163
  199.4 3.0 fusion.163
  208.2 3.0 fusion.163
  217.1 3.0 fusion.163
  226.0 3.0 fusion.163
  234.8 3.0 fusion.163
  243.7 3.0 fusion.163
  252.6 3.0 fusion.163
  261.5 3.0 fusion.163
  270.3 3.0 fusion.163
  279.2 3.0 fusion.163
  285.1 2.9 fusion.36
  289.7 2.7 fusion.92
  292.5 6.2 fusion.14
  298.7 3.4 multiply_reduce_fusion.1
  317.1 2.7 fusion.79
  319.8 41.0 %all-gather.5 = f32[16,12,128]{2,1,0:T(8,128)} all-gather(f32[1,12,128]{2,1,0:T(8,128)S(1)} %bitcast.245), channel_id=5, replica_groups=mesh['batch'=2,'seq'=16] {'seq'}, dimensions={0}, use_global_device_ids=true | all-gather | bytes 104448 | tf_op jit(solution)/shard_map/all_gather | solution.py:12
  363.2 3.7 fusion.15
  377.3 2.6 fusion.95
  380.5 6.2 fusion.91
  388.2 3.2 fusion.24
  391.4 5.6 convolution_bitcast_fusion
  397.0 4.1 all-gather.11.cloned.1.call-done
  401.1 9.5 %copy.89 = f32[16,12,128,64]{3,2,1,0:T(8,128)} copy(f32[16,12,128,64]{2,3,1,0:T(8,128)} %bitcast.230) | data formatting | bytes 12582912 | tf_op jit(solution)/shard_map/all_gather | solution.py:12
  410.7 11.3 %rev.9 = f32[16,12,128,64]{3,2,1,0:T(8,128)} reverse(f32[16,12,128,64]{3,2,1,0:T(8,128)} %copy.89), dimensions={0} | reverse | bytes 12582912 | tf_op jit(solution)/shard_map/rev | solution.py:14
  422.0 74.2 %while.33 = (s32[]{:T(128)}, f32[12,128,64]{2,1,0:T(8,128)}, f32[12,128]{1,0:T(8,128)S(1)}, s32[]{:T(128)}, f32[16,12,128,64]{3,2,1,0:T(8,128)}, /*index=5*/f32[...) while((s32[]{:T(128)}, f32[12,128,64]{2,1,0:T(8,128)}, ...), condition=%wide.region_23.24_spmd.clone, body=%wide.region_22.23_spmd.clone.sunk | while | flops 399365 | bytes 1198231 | solution.py:24
  423.9 2.8 fusion.166
  428.7 3.0 fusion.166
  433.6 3.0 fusion.166
  438.6 3.0 fusion.166
  443.6 3.0 fusion.166
  448.5 3.0 fusion.166
  453.5 3.0 fusion.166
  458.4 3.0 fusion.166
  463.4 3.0 fusion.166
  468.4 3.0 fusion.166
  473.3 3.0 fusion.166
  478.3 3.0 fusion.166
  483.2 3.0 fusion.166
  488.2 3.0 fusion.166
  493.2 3.0 fusion.166
  496.2 3.3 add_convert_fusion.1
  506.0 5.2 fusion.60
  511.3 19.2 %pad_maximum_fusion = f32[768,9216]{1,0:T(8,128)} fusion(f32[768,3072]{1,0:T(8,128)} %convolution_bitcast_fusion, f32[768,3072]{1,0:T(8,128)} %fusion.91, f32[768,768]{1,0:T(8,128)} %fusion.109, f32[768,2304]{1,0:T(8,128)} %fusion.60), kind=kLoop, calls=%fused_computation.15 | loop fusion | flops 21233664 | bytes 56623104 | tf_op jit(solution)/shard_map/concatenate | solution.py:286
  530.7 2.6 fusion.110
  533.4 10.6 %add_bitcast_fusion.2 = f32[1,512,768]{2,1,0:T(8,128)} fusion(f32[512,768]{1,0:T(8,128)S(1)} %copy-done.21, bf16[3072,768]{1,0:T(8,128)(2,1)} %param.20, f32[512,3072]{1,0:T(8,128)} %copy-done.97), kind=kOutput, calls=%fused_computation.86 | convolution fusion | flops 2430468096 | bytes 14155776 | tf_op jit(solution)/shard_map/dot_general | solution.py:170
  547.7 38.5 %all-reduce.1 = (f32[768]{0:T(1024)}, f32[768]{0:T(1024)}) all-reduce(f32[768]{0:T(1024)} %get-tuple-element.339, f32[768]{0:T(1024)} %get-tuple-element.333), channel_id=1, replica_groups=mesh['batch'=2,'seq'=16] {'batch','seq'}, use_global_device_ids=true, to_apply=%region_32.33 | all-reduce | flops 1536 | bytes 12288 | tf_op jit(solution)/shard_map/psum | solution.py:303
  589.9 4.2 add_bitcast_fusion.1
  594.1 198.6 %reduce-scatter.2.cloned.1.call-done = f32[24,9216]{1,0:T(8,128)} async-done(((f32[768,9216]{1,0:T(8,128)}), f32[24,9216]{1,0:T(8,128)}) %reduce-scatter.2.cloned.1.call-update) | async-done | bytes 884752 | tf_op jit(solution)/shard_map/reduce_scatter | solution.py:285
  797.8 129.9 %all-reduce.5.cloned.1.call-done = (f32[12,64,64]{2,1,0:T(8,128)}, f32[12,64,64]{2,1,0:T(8,128)}) async-done(((f32[12,64,64]{2,1,0:T(8,128)}, f32[12,64,64]{2,1,0:T(8,128)}), (f32[12,64,64]{2,1,0:T(8,128)}, f32[12,64,64]{2,1,0:T(8,128)})) %all-reduce.5.cloned.1.call-update) | async-done | bytes 393232 | tf_op jit(solution)/shard_map/psum | solution.py:303
  (391 shorter events, 205.1 us)
Async XLA Ops:
  7.2 3.7 copy-start
  7.2 3.6 copy-start.87
  7.2 141.7 %all-gather.9.cloned.1.call-start = ((), (), s32[]{:S(2)}) async-start(), calls=%async_computation.2 | async-start | bytes 6684672 | tf_op jit(solution)/shard_map/all_gather | solution.py:12
  7.2 3.6 copy-start.22
  8.7 4.3 copy-start.77
  20.4 3.5 copy-start.91
  20.4 3.5 copy-start.94
  23.9 8.2 copy-start.79
  24.2 103.3 %copy-start.69 = (s32[512]{0:T(512)}, s32[512]{0:T(512)S(1)}, u32[]{:S(2)}) copy-start(s32[512]{0:T(512)S(1)} %eq.52) | copy-start | bytes 6148
  27.4 4.8 copy-start.89
  29.7 3.6 copy-start.32
  34.7 50.8 %copy-start.90 = (bf16[512]{0:T(512)(128)(2,1)S(1)}, bf16[512]{0:T(512)(128)(2,1)}, u32[]{:S(2)}) copy-start(bf16[512]{0:T(512)(128)(2,1)} %copy-done.89) | copy-start | bytes 3076
  34.8 366.4 %all-gather.11.cloned.1.call-start = ((), (), s32[]{:S(2)}) async-start(), calls=%async_computation.3 | async-start | bytes 6684672 | tf_op jit(solution)/shard_map/all_gather | solution.py:12
  127.6 157.5 %copy-start.75 = (f32[512]{0:T(512)}, f32[512]{0:T(512)S(1)}, u32[]{:S(2)}) copy-start(f32[512]{0:T(512)S(1)} %get-tuple-element.376) | copy-start | bytes 6148
  136.6 2.7 copy-start.14
  139.1 2.6 copy-start.26
  139.1 2.6 copy-start.29
  139.3 7.0 copy-start.33
  141.7 4.6 copy-start.1
  146.3 2.6 copy-start.95
  282.2 2.9 copy-start.3
  282.2 2.9 copy-start.27
  282.2 7.1 slice-start.3
  285.1 19.8 %copy-start.61 = (f32[512,12]{0,1:T(8,128)}, f32[512,12]{0,1:T(8,128)S(1)}, u32[]{:S(2)}) copy-start(f32[512,12]{0,1:T(8,128)S(1)} %fusion.81) | copy-start | bytes 73732
  285.1 2.9 copy-start.23
  285.1 2.9 copy-start.93
  285.1 4.2 slice-start.4
  288.9 13.2 %copy-start.19 = (f32[512,768]{1,0:T(8,128)}, f32[512,768]{1,0:T(8,128)S(1)}, u32[]{:S(2)}) copy-start(f32[512,768]{1,0:T(8,128)S(1)} %get-tuple-element.403) | copy-start | bytes 4718596
  289.0 13.1 %copy-start.71 = (f32[512]{0:T(512)}, f32[512]{0:T(512)S(1)}, u32[]{:S(2)}) copy-start(f32[512]{0:T(512)S(1)} %broadcast_multiply_fusion) | copy-start | bytes 6148
  289.0 3.5 slice-start.5
  289.7 12.4 %copy-start.73 = (f32[512]{0:T(512)}, f32[512]{0:T(512)S(1)}, u32[]{:S(2)}) copy-start(f32[512]{0:T(512)S(1)} %fusion.85) | copy-start | bytes 6148
  289.7 2.8 copy-start.40
  289.7 2.8 slice-start.6
  292.5 6.2 copy-start.97
  298.7 3.4 copy-start.44
  308.3 484.5 %reduce-scatter.2.cloned.1.call-start = ((), (), s32[]{:S(2)}) async-start(), calls=%async_computation.1 | async-start | bytes 29196288 | tf_op jit(solution)/shard_map/reduce_scatter | solution.py:285
  363.2 3.7 copy-start.10
  363.2 3.7 copy-start.13
  373.0 4.2 copy-start.37
  377.2 2.7 copy-start.20
  377.2 3.2 copy-start.45
  377.2 3.2 copy-start.63
  377.2 3.2 copy-start.72
  377.3 3.2 copy-start.74
  377.3 9.4 %slice-start = ((s8[12582912]{0:T(1024)(128)(4,1)}), s8[4194304]{0:T(1024)(128)(4,1)S(1)}, s32[]{:S(2)}) async-start(s8[12582912]{0:T(1024)(128)(4,1)} %bitcast.218), calls=%async_computation.5 | async-start | bytes 8388608
  377.3 9.4 %slice-start.1 = ((s8[12582912]{0:T(1024)(128)(4,1)}), s8[4194304]{0:T(1024)(128)(4,1)S(1)}, s32[]{:S(2)}) async-start(s8[12582912]{0:T(1024)(128)(4,1)} %bitcast.218), calls=%async_computation.6 | async-start | bytes 8388608
  380.4 7.4 slice-start.2
  380.5 7.7 copy-start.15
  380.5 10.9 %slice-start.7 = ((s8[6291456]{0:T(1024)(128)(4,1)}), s8[4194304]{0:T(1024)(128)(4,1)S(1)}, s32[]{:S(2)}) async-start(s8[6291456]{0:T(1024)(128)(4,1)} %bitcast.256), calls=%async_computation.12 | async-start | bytes 8388608
  388.1 3.3 copy-start.41
  388.1 3.3 slice-start.8
  410.7 11.3 %copy-start.96 = (f32[16]{0:T(128)S(1)}, f32[16]{0:T(128)}, u32[]{:S(2)}) copy-start(f32[16]{0:T(128)} %reverse) | copy-start | bytes 196
  422.0 74.2 %copy-start.84 = (f32[512]{0:T(512)S(1)}, f32[512]{0:T(512)}, u32[]{:S(2)}) copy-start(f32[512]{0:T(512)} %get-tuple-element.380) | copy-start | bytes 6148
  496.2 3.3 copy-start.2
  496.2 3.3 copy-start.5
  496.2 3.5 copy-start.34
  499.5 5.3 copy-start.54
  530.4 397.2 %all-reduce.5.cloned.1.call-start = ((), (), s32[]{:S(2)}) async-start(), calls=%async_computation.4 | async-start | bytes 1572864 | tf_op jit(solution)/shard_map/psum | solution.py:303
  530.7 2.6 copy-start.21
  533.3 10.6 %copy-start.25 = (bf16[1,512,768]{2,1,0:T(8,128)(2,1)S(1)}, bf16[1,512,768]{2,1,0:T(8,128)(2,1)}, u32[]{:S(2)}) copy-start(bf16[1,512,768]{2,1,0:T(8,128)(2,1)} %param.16) | copy-start | bytes 2359300
  533.3 10.6 %copy-start.47 = (bf16[12,512,64]{1,2,0:T(8,128)(2,1)S(1)}, bf16[12,512,64]{1,2,0:T(8,128)(2,1)}, u32[]{:S(2)}) copy-start(bf16[12,512,64]{1,2,0:T(8,128)(2,1)} %convolution_convert_fusion.2) | copy-start | bytes 2359300
  533.3 10.6 %copy-start.49 = (bf16[12,512,64]{1,2,0:T(8,128)(2,1)S(1)}, bf16[12,512,64]{1,2,0:T(8,128)(2,1)}, u32[]{:S(2)}) copy-start(bf16[12,512,64]{1,2,0:T(8,128)(2,1)} %copy-done.48) | copy-start | bytes 2359300
  533.3 10.6 %copy-start.55 = (bf16[12,64,512]{2,1,0:T(8,128)(2,1)S(1)}, bf16[12,64,512]{2,1,0:T(8,128)(2,1)}, u32[]{:S(2)}) copy-start(bf16[12,64,512]{2,1,0:T(8,128)(2,1)} %copy-done.54) | copy-start | bytes 2359300
  547.6 42.2 %copy-start.83 = (f32[512]{0:T(512)S(1)}, f32[512]{0:T(512)}, u32[]{:S(2)}) copy-start(f32[512]{0:T(512)} %copy-done.82) | copy-start | bytes 6148
  (47 other events, 73.9 us)
Sparse Core Ops, SparseCore 0:
  34.9 98.4 all-gather.8
  308.4 92.7 all-gather.10
  530.6 262.1 reduce-scatter.1
  798.5 129.0 all-reduce.4
where the time goes:
time: 951 us; the launch traced here: 938 us
  waiting for transfers between devices  333 us (35%)
  other arithmetic  200 us (21%)
  blocking collectives  164 us (17%)
  local copies, waits for them, and re-layouts  120 us (13%)
  matrix products  103 us (11%)
  between operations  16.6 us (2%)
    reduce_scatter x1, waiting for transfers between devices, local(): lax.psum_scatter(jnp.concatenate([column_terms(attn_in, grad_qkv), column...  199 us
    select_n x60, other arithmetic, lap(): jnp.where(position < mine, new, old)  131 us
    psum x1, waiting for transfers between devices, local(): lax.psum((grad_map_query, grad_map_key, grad_gain_attn, grad_gain_mlp), (...  130 us
    all_gather x2, blocking collectives, carried_in(): pieces = jax.tree.map(lambda part: lax.all_gather(part, axis), value)  80.7 us
    dynamic_slice x30, local copies, waits for them, and re-layouts, lap(): longer = join(so_far, jax.tree.map(lambda part: part[position], pieces))  58.8 us
    unnamed x1, blocking collectives  44.8 us
    psum x1, blocking collectives, local(): lax.psum((grad_map_query, grad_map_key, grad_gain_attn, grad_gain_mlp), (...  38.5 us
    unnamed x220, local copies, waits for them, and re-layouts  22.5 us
  transfers between devices with their start and end apart: 4, of which 3 were waited for; matrix products, arithmetic and copies ran while one was open for 11% of the time, Pallas kernels for 0%

commit v1 on v0

v1 whole, which is shorter than its diff:
```python
import functools

import jax
import jax.numpy as jnp
from jax import lax
from jax.experimental import pallas as pl
from jax.experimental.pallas import tpu as pltpu
from jax.sharding import PartitionSpec as P

EPSILON = 1e-05
F32 = jnp.float32
BF16 = jnp.bfloat16
CORE, SEQ, MEMBER, PLANE, FLAGS = 0, 1, 2, 3, 4
STATE_ROWS = 72
MIB = 1024 * 1024


def mm(a, b):
    return lax.dot_general(a, b, (((1,), (0,)), ((), ())), preferred_element_type=F32)


def nt(a, b):
    return lax.dot_general(a, b, (((1,), (1,)), ((), ())), preferred_element_type=F32)


def tn(a, b):
    return lax.dot_general(a, b, (((0,), (0,)), ((), ())), preferred_element_type=F32)


def split(v):
    high = v.astype(BF16)
    return high, (v - high.astype(F32)).astype(BF16)


def iota(shape, dim):
    return lax.broadcasted_iota(jnp.int32, shape, dim)


def segment_ones(width):
    shape = (width, width)
    return (iota(shape, 0) // 64 == iota(shape, 1) // 64).astype(BF16)


def segment_sum(v, ones):
    high, low = split(v)
    return mm(high, ones) + mm(low, ones)


def moments(x):
    centre = jnp.mean(x, axis=-1, keepdims=True)
    offsets = x - centre
    variance = jnp.mean(offsets * offsets, axis=-1, keepdims=True)
    scale = lax.rsqrt(variance + EPSILON)
    return offsets * scale, scale


def norm_back(grad, normed, scale, gain):
    dn = grad * gain
    first = jnp.mean(dn, axis=-1, keepdims=True)
    second = jnp.mean(dn * normed, axis=-1, keepdims=True)
    return (dn - first - normed * second) * scale


def fill_maps(scr, map_ref):
    scr[...] = jnp.zeros(scr.shape, scr.dtype)
    for h in range(4):
        m = map_ref[h].astype(F32)
        scr[64 * h : 64 * h + 64, 128 * h : 128 * h + 128] = jnp.concatenate(
            [m, -m], axis=1
        ).astype(scr.dtype)


def features(pre, ones):
    low_half = iota(pre.shape, 1) < 64
    top = jnp.max(jnp.where(low_half, pre, -jnp.inf), axis=1, keepdims=True)
    bottom = jnp.max(jnp.where(low_half, -jnp.inf, pre), axis=1, keepdims=True)
    e = jnp.exp(pre - jnp.where(low_half, top, bottom))
    return e / segment_sum(e, ones)


def features_back(feat, grad, ones):
    weighted = feat * grad
    total = segment_sum(weighted, ones)
    mass = mm(feat.astype(BF16), ones)
    part = weighted - feat * (total / mass)
    return part - pltpu.roll(part, 64, 1)


def whole(shape):
    return pl.BlockSpec(shape, lambda *_: (0,) * len(shape))


def columns(rows, width):
    return pl.BlockSpec((rows, width), lambda j, _: (0, j))


ANYWHERE = pl.BlockSpec(memory_space=pl.ANY)


def run(kernel, scal, tok, grid, ins, outs, scratch=(), limit=48, flops=0):
    def body(*refs):
        sc = refs[0]
        n_in, n_out = len(ins), len(outs)
        kernel(
            sc,
            *refs[1 : 1 + n_in],
            *refs[2 + n_in : 2 + n_in + n_out],
            *refs[3 + n_in + n_out :],
        )

    moved = sum(a.size * a.dtype.itemsize for a, _ in ins)
    result = pl.pallas_call(
        body,
        grid_spec=pltpu.PrefetchScalarGridSpec(
            num_scalar_prefetch=1,
            grid=grid,
            in_specs=[spec for _, spec in ins] + [ANYWHERE],
            out_specs=[spec for _, _, spec in outs] + [ANYWHERE],
            scratch_shapes=list(scratch),
        ),
        out_shape=[jax.ShapeDtypeStruct(shape, dtype) for shape, dtype, _ in outs]
        + [jax.ShapeDtypeStruct((8, 128), F32)],
        compiler_params=pltpu.CompilerParams(vmem_limit_bytes=limit * MIB),
        cost_estimate=pl.CostEstimate(flops=flops, bytes_accessed=moved, transcendentals=0),
    )(scal, *[a for a, _ in ins], tok)
    return list(result[:-1]), result[-1]


def keys_kernel(sc, x_ref, gain_ref, wk_ref, wv_ref, map_ref, mask_ref,
                attn_ref, k_ref, v_ref, fk_ref, p0, p1, p2, p3,
                allow_ref, allow_t_ref, tail_ref, contin_ref,
                map_scr, state_scr):
    j = pl.program_id(0)
    tokens = x_ref.shape[0]
    n_flags = sc.shape[0] - FLAGS
    unit = tokens // n_flags

    def seg(shape, dim):
        place = iota(shape, dim)
        total = jnp.zeros(shape, jnp.int32)
        for u in range(n_flags):
            total = total + jnp.where(place >= unit * u, sc[FLAGS + u], 0)
        return total

    @pl.when(j == 0)
    def _():
        normed, _ = moments(x_ref[...].astype(F32))
        attn_ref[...] = (normed * gain_ref[...]).astype(BF16)
        last = sc[FLAGS]
        for u in range(1, n_flags):
            last = last + sc[FLAGS + u]
        mask_row = mask_ref[...].astype(F32)
        mask_col = jnp.transpose(jnp.broadcast_to(mask_row, (128, tokens)))
        seg_col = seg((tokens, 128), 0)
        tail_ref[...] = jnp.where(seg_col == last, mask_col, 0.0)
        contin_ref[...] = jnp.where(seg_col == 0, 1.0, 0.0)
        square = (tokens, tokens)
        same = seg(square, 0) == seg(square, 1)
        allow_ref[...] = jnp.where(same & (iota(square, 1) <= iota(square, 0)), mask_row, 0.0)
        wide_mask = jnp.concatenate([mask_col] * (tokens // 128), axis=1)
        allow_t_ref[...] = jnp.where(same & (iota(square, 0) <= iota(square, 1)), wide_mask, 0.0)

    fill_maps(map_scr, map_ref)
    attn = attn_ref[...]
    k4 = mm(attn, wk_ref[...]).astype(BF16)
    v4 = mm(attn, wv_ref[...]).astype(BF16)
    k_ref[...] = k4
    v_ref[...] = v4
    pre = mm(k4, map_scr[...])
    ones = segment_ones(128)
    v_t = jnp.transpose(v4.astype(F32)).astype(BF16)
    tail = tail_ref[...]
    row_ones = jnp.ones((16, tokens), BF16)
    for h in range(4):
        feat = features(pre[:, 128 * h : 128 * h + 128], ones).astype(BF16)
        fk_ref[:, 128 * h : 128 * h + 128] = feat
        kept = (feat.astype(F32) * tail).astype(BF16)
        state_scr[4 * j + h, 0:64, :] = mm(v_t[64 * h : 64 * h + 64], kept)
        state_scr[4 * j + h, 64:72, :] = mm(row_ones, kept)[0:8]

    @pl.when(j == pl.num_programs(0) - 1)
    def _():
        for k, piece in enumerate((p0, p1, p2, p3)):
            n = piece.shape[0]
            piece[...] = state_scr[pl.ds((sc[MEMBER] ^ k) * n, n)]


def queries_kernel(sc, attn_ref, wq_ref, map_ref, fk_ref, v_ref, allow_ref,
                   q_ref, fq_ref, nd_ref, map_scr):
    tokens = attn_ref.shape[0]
    half = tokens // 2
    fill_maps(map_scr, map_ref)
    q4 = mm(attn_ref[...], wq_ref[...]).astype(BF16)
    q_ref[...] = q4
    pre = mm(q4, map_scr[...])
    ones = segment_ones(128)
    low_half = iota((tokens, 128), 1) < 64
    for h in range(4):
        lanes = slice(128 * h, 128 * h + 128)
        feat = features(pre[:, lanes], ones).astype(BF16)
        fq_ref[:, lanes] = feat
        fk = fk_ref[:, lanes]
        pair = v_ref[:, 128 * (h // 2) : 128 * (h // 2) + 128].astype(F32)
        if h % 2:
            pair = pltpu.roll(pair, 64, 1)
        wide = jnp.where(low_half, pair, 1.0).astype(BF16)
        first = nt(feat[:half], fk[:half]) * allow_ref[:half, :half]
        nd_ref[:half, lanes] = mm(first.astype(BF16), wide[:half])
        second = nt(feat[half:], fk) * allow_ref[half:, :]
        nd_ref[half:, lanes] = mm(second.astype(BF16), wide)


def plane_sum_kernel(sc, *refs):
    *pieces, out = refs
    total = pieces[0][...]
    for piece in pieces[1:]:
        total = total + piece[...]
    out[...] = total


def scan_kernel(backward, planes, sc, *refs):
    own = refs[:4]
    others = refs[4:-4]
    outs = refs[-4:]
    member, plane = sc[MEMBER], sc[PLANE]
    total = jnp.zeros(own[0].shape, F32)
    for i, other in enumerate(others):
        if planes is None:
            total = total + other[...]
        else:
            there = plane + i + 1 < planes if backward else plane - i - 1 >= 0
            total = total + jnp.where(there, other[...], 0.0)
    for k, out in enumerate(outs):
        value = total
        target = member ^ k
        for i, piece in enumerate(own):
            source = member ^ i
            counts = source > target if backward else source < target
            value = value + jnp.where(counts, piece[...], 0.0)
        out[...] = value


def place_heads(sc, scr, pieces):
    for k, piece in enumerate(pieces):
        n = piece.shape[0]
        scr[pl.ds((sc[MEMBER] ^ k) * n, n)] = piece[...]


def mix_kernel(sc, x_ref, nd_ref, fq_ref, c0, c1, c2, c3, contin_ref, wo_ref, gain_ref,
               mixed_ref, mf_ref, rden_ref, hidden_ref, mlp_ref, carry_scr):
    j = pl.program_id(0)
    tokens = x_ref.shape[0]
    low_half = iota((tokens, 128), 1) < 64

    @pl.when(j == 0)
    def _():
        place_heads(sc, carry_scr, (c0, c1, c2, c3))
        hidden_ref[...] = x_ref[...].astype(F32)

    contin = contin_ref[...]
    for pair in range(2):
        quotients, inverses = [], []
        for side in range(2):
            h = 2 * pair + side
            lanes = slice(128 * h, 128 * h + 128)
            carry = carry_scr[4 * j + h]
            wide = jnp.concatenate([carry[:64], jnp.broadcast_to(carry[64:65], (64, 128))], axis=0)
            high, low = split(wide)
            fq = fq_ref[:, lanes]
            nd = nd_ref[:, lanes] + contin * (nt(fq, high) + nt(fq, low))
            inverse = 1.0 / nd
            turned = pltpu.roll(inverse, 64, 1)
            quotient = nd * turned
            if side:
                quotients.append(pltpu.roll(quotient, 64, 1))
                inverses.append(inverse)
            else:
                quotients.append(quotient)
                inverses.append(turned)
        lanes = slice(128 * pair, 128 * pair + 128)
        mf = jnp.where(low_half, *quotients)
        mf_ref[:, lanes] = mf
        mixed_ref[:, lanes] = mf.astype(BF16)
        rden_ref[:, lanes] = jnp.where(low_half, *inverses)
    hidden_ref[...] += mm(mixed_ref[...], wo_ref[...])

    @pl.when(j == pl.num_programs(0) - 1)
    def _():
        normed, _ = moments(hidden_ref[...])
        mlp_ref[...] = (normed * gain_ref[...]).astype(BF16)


GELU_A, GELU_C = 0.044715, 0.7978845608028654


def mlp_kernel(sc, mlp_ref, cot_ref, mlp_part, cot_part, wf_ref, wp_ref,
               act_ref, gp_ref, send_fc, send_proj, mlp_t, cot_t):
    @pl.when(pl.program_id(0) == 0)
    def _():
        mlp_t[...] = jnp.transpose(mlp_part[...].astype(F32)).astype(BF16)
        cot_t[...] = jnp.transpose(cot_part[...].astype(F32)).astype(BF16)

    u = mm(mlp_ref[...], wf_ref[...])
    square = u * u
    t = jnp.tanh(GELU_C * (u + GELU_A * (u * square)))
    half = 0.5 * (1.0 + t)
    act = (u * half).astype(BF16)
    act_ref[...] = act
    slope = half + (0.5 * GELU_C) * u * (1.0 - t * t) * (1.0 + (3.0 * GELU_A) * square)
    gp = (nt(cot_ref[...], wp_ref[...]) * slope).astype(BF16)
    gp_ref[...] = gp
    send_fc[...] = mm(mlp_t[...], gp)
    send_proj[...] = mm(cot_t[...], act)


def mlp_out_kernel(sc, act_ref, gp_ref, wf_ref, wp_ref, hidden_ref, cot_ref, gain_ref,
                   out_ref, gh_ref, gh_low_ref, gg_ref, back_scr):
    j = pl.program_id(0)

    @pl.when(j == 0)
    def _():
        out_ref[...] = hidden_ref[...]
        back_scr[...] = jnp.zeros(back_scr.shape, F32)

    out_ref[...] += mm(act_ref[...], wp_ref[...])
    back_scr[...] += nt(gp_ref[...], wf_ref[...])

    @pl.when(j == pl.num_programs(0) - 1)
    def _():
        normed, scale = moments(hidden_ref[...])
        grad = back_scr[...]
        gg_ref[...] = jnp.sum(grad * normed, axis=0, keepdims=True)
        gh = cot_ref[...].astype(F32) + norm_back(grad, normed, scale, gain_ref[...])
        gh_ref[...] = gh
        gh_low_ref[...] = gh.astype(BF16)


def numer_back_kernel(sc, gh_ref, wo_ref, mf_ref, rden_ref, fq_ref, contin_ref,
                      gn_ref, gd_ref, gd_t_ref, p0, p1, p2, p3, state_scr):
    j = pl.program_id(0)
    gm = nt(gh_ref[...], wo_ref[...]) * rden_ref[...]
    gn_ref[...] = gm.astype(BF16)
    gd = -segment_sum(gm * mf_ref[...], segment_ones(256))
    gd_ref[...] = gd
    gn_t = jnp.transpose(gm).astype(BF16)
    gd_t = jnp.transpose(gd)
    contin = contin_ref[...]
    for h in range(4):
        rows = gd_t[64 * h : 64 * h + 8]
        gd_t_ref[8 * h : 8 * h + 8, :] = rows
        kept = (fq_ref[:, 128 * h : 128 * h + 128].astype(F32) * contin).astype(BF16)
        state_scr[4 * j + h, 0:64, :] = mm(gn_t[64 * h : 64 * h + 64], kept)
        high, low = split(rows)
        both = jnp.concatenate([high.astype(F32), low.astype(F32)], axis=0).astype(BF16)
        sums = mm(both, kept)
        state_scr[4 * j + h, 64:72, :] = sums[0:8] + sums[8:16]

    @pl.when(j == pl.num_programs(0) - 1)
    def _():
        for k, piece in enumerate((p0, p1, p2, p3)):
            n = piece.shape[0]
            piece[...] = state_scr[pl.ds((sc[MEMBER] ^ k) * n, n)]


def side_rows(state, side):
    zeros = jnp.zeros((64, 128), F32)
    rows = state[:64]
    return jnp.concatenate([zeros, rows] if side else [rows, zeros], axis=0)


def scores_back_kernel(sc, q_ref, fq_ref, fk_ref, v_ref, gn_ref, gd_ref, gd_t_ref,
                       c0, c1, c2, c3, allow_ref, allow_t_ref, contin_ref, map_ref,
                       gq_ref, gfk_ref, gv_ref, gmap_ref, map_scr, carry_scr, d_scr):
    j = pl.program_id(0)
    tokens = q_ref.shape[0]
    half = tokens // 2

    @pl.when(j == 0)
    def _():
        place_heads(sc, carry_scr, (c0, c1, c2, c3))

    fill_maps(map_scr, map_ref)
    ones = segment_ones(128)
    low_half = iota((tokens, 128), 1) < 64
    contin = contin_ref[...]
    for pair in range(2):
        pair_lanes = slice(128 * pair, 128 * pair + 128)
        v_pair = v_ref[:, pair_lanes]
        gn_pair = gn_ref[:, pair_lanes].astype(F32)
        gd_pair = gd_ref[:, pair_lanes]
        gd_turned = pltpu.roll(gd_pair, 64, 1)
        gv_parts = []
        for side in range(2):
            h = 2 * pair + side
            lanes = slice(128 * h, 128 * h + 128)
            mine = ~low_half if side else low_half
            gn = jnp.where(mine, gn_pair, 0.0).astype(BF16)
            gd = jnp.where(mine, gd_pair, gd_turned)
            gd_row = gd_t_ref[8 * h : 8 * h + 1, :]
            fq, fk = fq_ref[:, lanes], fk_ref[:, lanes]
            gd_few = jnp.concatenate([gd] * (half // 128), axis=1)
            gd_many = jnp.concatenate([gd] * (tokens // 128), axis=1)
            g_top = ((nt(gn[:half], v_pair[:half]) + gd_few[:half]) * allow_ref[:half, :half]).astype(BF16)
            g_bot = ((nt(gn[half:], v_pair) + gd_many[half:]) * allow_ref[half:, :]).astype(BF16)
            carry = carry_scr[4 * j + h]
            high, low = split(side_rows(carry, side))
            inter = mm(gn, high) + mm(gn, low) + gd * carry[64:65]
            gfq = jnp.concatenate([mm(g_top, fk[:half]), mm(g_bot, fk)], axis=0) + contin * inter
            d_scr[:, lanes] = features_back(fq.astype(F32), gfq, ones).astype(BF16)

            at_top, at_bot = allow_t_ref[:half, :], allow_t_ref[half:, half:]
            gt_top = ((nt(v_pair[:half], gn) + gd_row) * at_top).astype(BF16)
            gt_bot = ((nt(v_pair[half:], gn[half:]) + gd_row[:, half:]) * at_bot).astype(BF16)
            gfk_ref[:half, lanes] = mm(gt_top, fq)
            gfk_ref[half:, lanes] = mm(gt_bot, fq[half:])
            st_top = (nt(fk[:half], fq) * at_top).astype(BF16)
            st_bot = (nt(fk[half:], fq[half:]) * at_bot).astype(BF16)
            gv_parts.append(jnp.concatenate([mm(st_top, gn), mm(st_bot, gn[half:])], axis=0))
        gv_ref[:, pair_lanes] = gv_parts[0] + gv_parts[1]
    d = d_scr[...]
    gq_ref[...] = (0.5 * nt(d, map_scr[...])).astype(BF16)
    gm = tn(q_ref[...], d)
    for h in range(4):
        gmap_ref[64 * h : 64 * h + 64, :] = gm[64 * h : 64 * h + 64, 128 * h : 128 * h + 128]


def keys_back_kernel(sc, k_ref, fk_ref, v_ref, gfk_ref, gv_ref, u0, u1, u2, u3, tail_ref, map_ref,
                     gk_ref, gvb_ref, gmap_ref, map_scr, up_scr, d_scr):
    j = pl.program_id(0)

    @pl.when(j == 0)
    def _():
        place_heads(sc, up_scr, (u0, u1, u2, u3))

    fill_maps(map_scr, map_ref)
    ones = segment_ones(128)
    tail = tail_ref[...]
    for pair in range(2):
        pair_lanes = slice(128 * pair, 128 * pair + 128)
        v_pair = v_ref[:, pair_lanes]
        gv = gv_ref[:, pair_lanes]
        for side in range(2):
            h = 2 * pair + side
            lanes = slice(128 * h, 128 * h + 128)
            up = up_scr[4 * j + h]
            high, low = split(side_rows(up, side))
            fk = fk_ref[:, lanes]
            key_term = mm(v_pair, high) + mm(v_pair, low) + up[64:65]
            gfk = gfk_ref[:, lanes] + tail * key_term
            gv = gv + tail * (nt(fk, high) + nt(fk, low))
            d_scr[:, lanes] = features_back(fk.astype(F32), gfk, ones).astype(BF16)
        gvb_ref[:, pair_lanes] = gv.astype(BF16)
    d = d_scr[...]
    gk_ref[...] = (0.5 * nt(d, map_scr[...])).astype(BF16)
    gm = tn(k_ref[...], d)
    for h in range(4):
        gmap_ref[64 * h : 64 * h + 64, :] = gm[64 * h : 64 * h + 64, 128 * h : 128 * h + 128]


def inputs_back_kernel(sc, gq_ref, gk_ref, gv_ref, w_ref, x_ref, gh_ref, gain_ref, gg_mlp_ref,
                       gmq_ref, gmk_ref, gx_ref, keep_ref, send_ref, acc, pack):
    j = pl.program_id(0)

    @pl.when(j == 0)
    def _():
        acc[...] = nt(gq_ref[...], w_ref[...])
        rows = gmq_ref.shape[0]
        low_half = iota(gmq_ref.shape, 1) < 64
        pack[:rows, :] = jnp.where(low_half, gmq_ref[...], pltpu.roll(gmk_ref[...], 64, 1))
        pack[rows:, :] = jnp.zeros((pack.shape[0] - rows, 128), F32)

    @pl.when(j == 1)
    def _():
        acc[...] += nt(gk_ref[...], w_ref[...])

    @pl.when(j == 2)
    def _():
        grad = acc[...] + nt(gv_ref[...], w_ref[...])
        normed, scale = moments(x_ref[...].astype(F32))
        gx_ref[...] = gh_ref[...] + norm_back(grad, normed, scale, gain_ref[...])
        gg = jnp.sum(grad * normed, axis=0, keepdims=True)
        rows = gmq_ref.shape[0]
        n = gg.shape[1] // 128
        for i in range(n):
            pack[rows + i : rows + i + 1, :] = gg[:, 128 * i : 128 * i + 128]
            pack[rows + n + i : rows + n + i + 1, :] = gg_mlp_ref[:, 128 * i : 128 * i + 128]
        size = keep_ref.shape[0]
        keep_ref[...] = pack[pl.ds(pl.multiple_of(sc[CORE] * size, 8), size), :]
        send_ref[...] = pack[pl.ds(pl.multiple_of((1 - sc[CORE]) * size, 8), size), :]


def add_kernel(sc, a_ref, b_ref, out_ref):
    out_ref[...] = a_ref[...] + b_ref[...]


def unpack_kernel(sc, mine_ref, other_ref, gmq_ref, gmk_ref, gains_ref, pack):
    size = mine_ref.shape[0]
    pack[pl.ds(pl.multiple_of(sc[CORE] * size, 8), size), :] = mine_ref[...]
    pack[pl.ds(pl.multiple_of((1 - sc[CORE]) * size, 8), size), :] = other_ref[...]
    heads = gmq_ref.shape[0]
    for h in range(heads):
        both = pack[64 * h : 64 * h + 64, :]
        gmq_ref[h] = both[:, :64]
        gmk_ref[h] = both[:, 64:]
    gains_ref[...] = pack[64 * heads :, :]


def send_half_kernel(sc, x_ref, y_ref, out_ref, x_t):
    @pl.when(pl.program_id(0) == 0)
    def _():
        x_t[...] = jnp.transpose(x_ref[...].astype(F32)).astype(BF16)

    out_ref[...] = mm(x_t[...], y_ref[...])


ORDERS = ((0, 1, 2, 3), (1, 0, 2, 3), (2, 3, 0, 1))


def keep_half_kernel(tiles, sc, x_ref, y_ref, r_ref, *rest):
    outs, (x_t, scr) = rest[:6], rest[6:]
    i = pl.program_id(0)

    @pl.when(i == 0)
    def _():
        x_t[...] = jnp.transpose(x_ref[...].astype(F32)).astype(BF16)

    value = mm(x_t[...], y_ref[...]) + r_ref[...]
    rows = value.shape[0] // 16
    half = value.shape[0] // 2
    lo = 0
    for kind, order in enumerate(ORDERS):

        @pl.when((i >= lo) & (i < lo + tiles[kind]))
        def _():
            for g in range(16):
                place = g ^ sc[SEQ]
                spot = 0
                for depth, bit in enumerate(order):
                    spot = spot + (((place >> bit) & 1) << (3 - depth))
                scr[pl.ds(pl.multiple_of(spot * rows, 8), rows), :] = value[rows * g : rows * g + rows]
            outs[2 * kind][...] = scr[half:, :]
            outs[2 * kind + 1][...] = scr[:half, :]

        lo += tiles[kind]


def fold_kernel(plan, sc, *refs):
    n_in = 2 * sum(n for n, _ in plan)
    ins, outs = refs[:n_in], list(refs[n_in:])
    at = 0
    for n, final in plan:
        targets = [outs.pop(0)] if final else [outs.pop(0), outs.pop(0)]
        lane = 0
        for _ in range(n):
            total = ins[at][...] + ins[at + 1][...]
            at += 2
            width = total.shape[1]
            if final:
                targets[0][:, lane : lane + width] = total
            else:
                half = total.shape[0] // 2
                targets[0][:, lane : lane + width] = total[half:]
                targets[1][:, lane : lane + width] = total[:half]
            lane += width


def core_hop(v):
    return lax.ppermute(v, "batch", [(0, 1), (1, 0)])


def local(inputs, w_qkv, w_out, w_fc, w_proj, map_query, map_key, gain_attn, gain_mlp,
          starts, key_mask, cotangent):
    T, D = inputs.shape[1], inputs.shape[2]
    H = map_query.shape[0]
    FF = w_fc.shape[1]
    n_seq = lax.axis_size("seq")
    planes = n_seq // 4
    quads = H // 4
    QW, FW = 4 * 64, 4 * 128
    half_rows = D // 2
    per = H // 4
    core = lax.axis_index("batch").astype(jnp.int32)
    seq = lax.axis_index("seq").astype(jnp.int32)
    scal = jnp.concatenate(
        [jnp.stack([core, seq, seq & 3, seq >> 2]), starts[0].astype(jnp.int32)]
    )
    tok = jnp.zeros((8, 128), F32)
    x, cot = inputs[0], cotangent[0]
    gain_a, gain_m = gain_attn.reshape(1, D), gain_mlp.reshape(1, D)

    def hop(v, bit):
        return lax.ppermute(v, "seq", [(i, i ^ (1 << bit)) for i in range(n_seq)])

    def to_member(v, k):
        return lax.ppermute(v, "seq", [(i, i ^ k) for i in range(n_seq)])

    def shift(v, by):
        return lax.ppermute(v, "seq", [(i, (i + by) % n_seq) for i in range(n_seq)])

    qcol = pl.BlockSpec((T, QW), lambda j, _: (0, j))
    fcol = pl.BlockSpec((T, FW), lambda j, _: (0, j))
    col128 = whole((T, 128))
    square = whole((T, T))
    full = whole((T, D))
    row = whole((1, D))
    maps = pl.BlockSpec((4, 64, 64), lambda j, _: (j, 0, 0))
    piece = (per, STATE_ROWS, 128)
    piece_spec = whole(piece)
    map_scr = pltpu.VMEM((QW, FW), BF16)
    state_scr = pltpu.VMEM((H, STATE_ROWS, 128), F32)

    def w_cols(part):
        return pl.BlockSpec((D, QW), lambda j, _: (0, part * quads + j))

    (attn, k, v, fk, s0, s1, s2, s3, allow, allow_t, tail, contin), tok = run(
        keys_kernel, scal, tok, (quads,),
        [(x, full), (gain_a, row), (w_qkv, w_cols(1)), (w_qkv, w_cols(2)), (map_key, maps),
         (key_mask, whole((1, T)))],
        [((T, D), BF16, full), ((T, D), BF16, qcol), ((T, D), BF16, qcol), ((T, 2 * D), BF16, fcol)]
        + [(piece, F32, piece_spec)] * 4
        + [((T, T), F32, square)] * 2 + [((T, 128), F32, col128)] * 2,
        [map_scr, state_scr],
    )

    def plane_exchange(pieces):
        return [pieces[0]] + [to_member(pieces[k], k) for k in range(1, 4)]

    def plane_total(own, tok):
        (total,), tok = run(
            plane_sum_kernel, scal, tok, (1,), [(p, piece_spec) for p in own],
            [(piece, F32, piece_spec)])
        return total, tok

    def across(total, backward):
        if planes <= 4:
            return [shift(total, (-4 if backward else 4) * i) for i in range(1, planes)]
        every = lax.all_gather(total, "seq").reshape((planes, 4) + piece)
        mine = lax.dynamic_index_in_dim(every, seq & 3, 1, keepdims=False)
        place = jnp.arange(planes)
        want = place > (seq >> 2) if backward else place < (seq >> 2)
        return [jnp.sum(jnp.where(want[:, None, None, None], mine, 0.0), axis=0)]

    def scanned(own, others, backward, tok):
        return run(
            functools.partial(scan_kernel, backward, planes if planes <= 4 else None), scal, tok, (1,),
            [(p, piece_spec) for p in own + others], [(piece, F32, piece_spec)] * 4)

    own = plane_exchange([s0, s1, s2, s3])

    (q, fq, nd), tok = run(
        queries_kernel, scal, tok, (quads,),
        [(attn, full), (w_qkv, w_cols(0)), (map_query, maps), (fk, fcol), (v, qcol), (allow, square)],
        [((T, D), BF16, qcol), ((T, 2 * D), BF16, fcol), ((T, 2 * D), F32, fcol)],
        [map_scr],
    )
    total, tok = plane_total(own, tok)
    others = across(total, False)
    carried, tok = scanned(own, others, False, tok)
    carry = plane_exchange(carried)

    (mixed, mf, rden, hidden, mlp_in), tok = run(
        mix_kernel, scal, tok, (quads,),
        [(x, full), (nd, fcol), (fq, fcol)] + [(c, piece_spec) for c in carry]
        + [(contin, col128), (w_out, pl.BlockSpec((QW, D), lambda j, _: (j, 0))), (gain_m, row)],
        [((T, D), BF16, qcol), ((T, D), F32, qcol), ((T, D), F32, qcol), ((T, D), F32, full),
         ((T, D), BF16, full)],
        [state_scr],
    )

    other_half = pl.BlockSpec((T, half_rows), lambda j, sc: (0, 1 - sc[CORE]))
    this_half = pl.BlockSpec((T, half_rows), lambda j, sc: (0, sc[CORE]))
    half_scr = pltpu.VMEM((half_rows, T), BF16)
    FT = 256
    (act, gp, send_fc, send_proj), tok = run(
        mlp_kernel, scal, tok, (FF // FT,),
        [(mlp_in, full), (cot, full), (mlp_in, other_half), (cot, other_half),
         (w_fc, columns(D, FT)), (w_proj, pl.BlockSpec((FT, D), lambda j, _: (j, 0)))],
        [((T, FF), BF16, columns(T, FT))] * 2 + [((half_rows, FF), F32, columns(half_rows, FT))] * 2,
        [half_scr, half_scr],
    )
    FT = 512
    (output, gh, gh_low, gg_mlp), tok = run(
        mlp_out_kernel, scal, tok, (FF // FT,),
        [(act, columns(T, FT)), (gp, columns(T, FT)), (w_fc, columns(D, FT)),
         (w_proj, pl.BlockSpec((FT, D), lambda j, _: (j, 0))), (hidden, full), (cot, full), (gain_m, row)],
        [((T, D), F32, full), ((T, D), F32, full), ((T, D), BF16, full), ((1, D), F32, row)],
        [pltpu.VMEM((T, D), F32)],
    )
    (gn, gd, gd_t, s0, s1, s2, s3), tok = run(
        numer_back_kernel, scal, tok, (quads,),
        [(gh_low, full), (w_out, pl.BlockSpec((QW, D), lambda j, _: (j, 0))), (mf, qcol), (rden, qcol),
         (fq, fcol), (contin, col128)],
        [((T, D), BF16, qcol), ((T, D), F32, qcol),
         ((8 * H, T), F32, pl.BlockSpec((32, T), lambda j, _: (j, 0)))] + [(piece, F32, piece_spec)] * 4,
        [state_scr],
    )
    own = plane_exchange([s0, s1, s2, s3])

    direct = n_seq == 16

    def send_half(xs, ys, tok):
        if not direct:
            return None, tok
        width = ys.shape[1]
        (out,), tok = run(
            send_half_kernel, scal, tok, (width // 256,), [(xs, other_half), (ys, columns(T, 256))],
            [((half_rows, width), F32, columns(half_rows, 256))], [half_scr])
        return core_hop(out), tok

    def keep_half(xs, ys, received, widths, tile, tok):
        tiles = tuple(w // tile for w in widths)
        out_specs = []
        lo = 0
        for kind in range(3):
            def place(i, _, lo=lo, n=tiles[kind]):
                return (0, jnp.clip(i - lo, 0, n - 1))
            out_specs += [((half_rows // 2, widths[kind]), F32, pl.BlockSpec((half_rows // 2, tile), place))] * 2
            lo += tiles[kind]
        return run(
            functools.partial(keep_half_kernel, tiles), scal, tok, (sum(tiles),),
            [(xs, this_half), (ys, columns(T, tile)), (received, columns(half_rows, tile))],
            out_specs, [half_scr, pltpu.VMEM((half_rows, tile), F32)])

    def fold(plan, pairs, tok):
        ins, outs = [], []
        at = 0
        for n, final in plan:
            width = sum(pairs[at + i][0].shape[1] for i in range(n))
            rows = pairs[at][0].shape[0]
            for i in range(n):
                ins += [(a, whole(a.shape)) for a in pairs[at + i]]
            at += n
            if final:
                outs.append(((rows, width), F32, whole((rows, width))))
            else:
                outs += [((rows // 2, width), F32, whole((rows // 2, width)))] * 2
        return run(functools.partial(fold_kernel, plan), scal, tok, (1,), ins, outs)

    class Reduction:
        def __init__(self, parts):
            sa, self.ka, sb, self.kb, sc_, self.kc = parts
            self.ra, self.rb, self.rc = hop(sa, 0), hop(sb, 1), hop(sc_, 2)
            self.stage = 0

        def step(self, tok):
            if self.stage == 0:
                (sa, self.ka, sb, self.kb, s3_, self.kc), tok = fold(
                    ((1, False),) * 3, [(self.ka, self.ra), (self.kb, self.rb), (self.kc, self.rc)], tok)
                self.ra, self.rb, self.rc = hop(sa, 1), hop(sb, 0), hop(s3_, 3)
            elif self.stage == 1:
                (s, self.k, s3_, self.kc), tok = fold(
                    ((2, False), (1, False)), [(self.ka, self.ra), (self.kb, self.rb), (self.kc, self.rc)], tok)
                self.r, self.rc = hop(s, 2), hop(s3_, 0)
            elif self.stage == 2:
                (s, self.k, s3_, self.kc), tok = fold(
                    ((1, False), (1, False)), [(self.k, self.r), (self.kc, self.rc)], tok)
                self.r, self.rc = hop(s, 3), hop(s3_, 1)
            else:
                (self.result,), tok = fold(((2, True),), [(self.k, self.r), (self.kc, self.rc)], tok)
            self.stage += 1
            return tok

    if direct:
        recv_proj, recv_fc = core_hop(send_proj), core_hop(send_fc)
        recv_out, tok = send_half(mixed, gh_low, tok)
        parts, tok = keep_half(cot, act, recv_proj, (1152, 1152, 768), 384, tok)
        red_proj = Reduction(parts)
        parts, tok = keep_half(mlp_in, gp, recv_fc, (1152, 1152, 768), 384, tok)
        red_fc = Reduction(parts)

    total, tok = plane_total(own, tok)
    others = across(total, True)

    (gq, gfk, gv_f, gmq), tok = run(
        scores_back_kernel, scal, tok, (quads,),
        [(q, qcol), (fq, fcol), (fk, fcol), (v, qcol), (gn, qcol), (gd, qcol),
         (gd_t, pl.BlockSpec((32, T), lambda j, _: (j, 0)))] + [(c, piece_spec) for c in carry]
        + [(allow, square), (allow_t, square), (contin, col128), (map_query, maps)],
        [((T, D), BF16, qcol), ((T, 2 * D), F32, fcol), ((T, D), F32, qcol),
         ((D, 128), F32, pl.BlockSpec((QW, 128), lambda j, _: (j, 0)))],
        [map_scr, state_scr, pltpu.VMEM((T, FW), BF16)],
    )
    carried, tok = scanned(own, others, True, tok)
    upstream = plane_exchange(carried)

    if direct:
        recv_q, tok = send_half(attn, gq, tok)
        tok = red_proj.step(tok)
        parts, tok = keep_half(mixed, gh_low, recv_out, (256, 256, 256), 256, tok)
        red_out = Reduction(parts)

    (gk, gv, gmk), tok = run(
        keys_back_kernel, scal, tok, (quads,),
        [(k, qcol), (fk, fcol), (v, qcol), (gfk, fcol), (gv_f, qcol)] + [(c, piece_spec) for c in upstream]
        + [(tail, col128), (map_key, maps)],
        [((T, D), BF16, qcol), ((T, D), BF16, qcol),
         ((D, 128), F32, pl.BlockSpec((QW, 128), lambda j, _: (j, 0)))],
        [map_scr, state_scr, pltpu.VMEM((T, FW), BF16)],
    )
    if direct:
        recv_k, tok = send_half(attn, gk, tok)
        recv_v, tok = send_half(attn, gv, tok)

    small = D + 16
    small_half = small // 2
    small_spec = whole((small_half, 128))
    (gx, keep, send), tok = run(
        inputs_back_kernel, scal, tok, (3,),
        [(gq, full), (gk, full), (gv, full), (w_qkv, columns(D, D)), (x, full), (gh, full), (gain_a, row),
         (gg_mlp, row), (gmq, whole((D, 128))), (gmk, whole((D, 128)))],
        [((T, D), F32, full)] + [((small_half, 128), F32, small_spec)] * 2,
        [pltpu.VMEM((T, D), F32), pltpu.VMEM((small, 128), F32)],
    )

    def add(a, b, tok):
        (out,), tok = run(add_kernel, scal, tok, (1,), [(a, small_spec), (b, small_spec)],
                          [((small_half, 128), F32, small_spec)])
        return out, tok

    got = core_hop(send)
    if direct:
        parts, tok = keep_half(attn, gq, recv_q, (256, 256, 256), 256, tok)
        red_q = Reduction(parts)
        parts, tok = keep_half(attn, gk, recv_k, (256, 256, 256), 256, tok)
        red_k = Reduction(parts)
        parts, tok = keep_half(attn, gv, recv_v, (256, 256, 256), 256, tok)
        red_v = Reduction(parts)
        mine, tok = add(keep, got, tok)
        got = hop(mine, 0)
        tok = red_fc.step(tok)
        mine, tok = add(mine, got, tok)
        got = hop(mine, 1)
        tok = red_proj.step(tok)
        tok = red_out.step(tok)
        tok = red_q.step(tok)
        tok = red_k.step(tok)
        tok = red_v.step(tok)
        mine, tok = add(mine, got, tok)
        got = hop(mine, 2)
        tok = red_fc.step(tok)
        tok = red_proj.step(tok)
        tok = red_out.step(tok)
        tok = red_q.step(tok)
        tok = red_k.step(tok)
        tok = red_v.step(tok)
        mine, tok = add(mine, got, tok)
        got = hop(mine, 3)
        tok = red_fc.step(tok)
        tok = red_proj.step(tok)
        tok = red_out.step(tok)
        tok = red_q.step(tok)
        tok = red_k.step(tok)
        tok = red_v.step(tok)
        mine, tok = add(mine, got, tok)
        got = core_hop(mine)
        tok = red_fc.step(tok)
        tok = red_out.step(tok)
        tok = red_q.step(tok)
        tok = red_k.step(tok)
        tok = red_v.step(tok)
        grad_w_qkv = jnp.concatenate([red_q.result, red_k.result, red_v.result], axis=1)
        grad_w_out, grad_w_fc = red_out.result, red_fc.result
        grad_proj_rows = red_proj.result
    else:
        mine, tok = add(keep, got, tok)
        mine = lax.psum(mine, "seq")
        got = core_hop(mine)
        summed = lax.psum_scatter(
            jnp.concatenate(
                [tn(attn, gq), tn(attn, gk), tn(attn, gv), tn(mixed, gh_low), tn(mlp_in, gp), tn(cot, act)],
                axis=1,
            ),
            ("batch", "seq"), scatter_dimension=0, tiled=True)
        grad_w_qkv = summed[:, : 3 * D]
        grad_w_out = summed[:, 3 * D : 4 * D]
        grad_w_fc = summed[:, 4 * D : 4 * D + FF]
        grad_proj_rows = summed[:, 4 * D + FF :]

    heads_shape = (H, 64, 64)
    (grad_map_query, grad_map_key, gains), tok = run(
        unpack_kernel, scal, tok, (1,), [(mine, small_spec), (got, small_spec)],
        [(heads_shape, F32, whole(heads_shape))] * 2 + [((16, 128), F32, whole((16, 128)))],
        [pltpu.VMEM((small, 128), F32)])
    n = D // 128
    return (
        output[None],
        gx[None],
        grad_w_qkv,
        grad_w_out,
        grad_w_fc,
        grad_proj_rows.T,
        grad_map_query,
        grad_map_key,
        gains[:n].reshape(D),
        gains[n : 2 * n].reshape(D),
    )


def solution(mesh):
    tokens = P("batch", "seq", None)
    flags = P("batch", "seq")
    rows = P(("batch", "seq"), None)
    return jax.shard_map(
        local,
        mesh=mesh,
        in_specs=(tokens,) + (P(),) * 8 + (flags, flags, tokens),
        out_specs=(tokens, tokens, rows, rows, rows, P(None, ("batch", "seq")), P(), P(), P(), P()),
        check_vma=False,
    )
```

time: 951 us -> 379 us (0.40)
  waiting for transfers between devices: 333 us -> 76.2 us
  other arithmetic: 200 us -> 0.7 us
  blocking collectives: 164 us -> 0 us
  Pallas kernels: 0 us -> 163 us
  starting transfers between devices: 0.59 us -> 108 us
  matrix products: 103 us -> 0 us
  local copies, waits for them, and re-layouts: 120 us -> 23.3 us
  between operations: 16.6 us -> 1.98 us
    reduce_scatter x1 -> x0, waiting for transfers between devices: 199 us -> none  [local(): lax.psum_scatter(jnp.concatenate([column_terms(attn_in, grad_qkv), column...]
    pallas_call x0 -> x53, Pallas kernels: none -> 163 us  [run(): pl.pallas_call(body, grid_spec=pltpu.PrefetchScalarGridSpec(num_scalar_pr...]
    select_n x60 -> x0, other arithmetic: 131 us -> none  [lap(): jnp.where(position < mine, new, old)]
    psum x1 -> x0, waiting for transfers between devices: 130 us -> none  [local(): lax.psum((grad_map_query, grad_map_key, grad_gain_attn, grad_gain_mlp), (...]
    ppermute x0 -> x90, starting transfers between devices: none -> 108 us  [the longest x64 79.9 us: hop(): return lax.ppermute(v, 'seq', [(i, i ^ 1 << bit) for i in range(n_seq)])]
    dot_general x30 -> x0, matrix products: 89 us -> none  [the longest x4 19.3 us: column_terms(): lax.dot_general(left_mat, right_mat, (((0,), (0,)), ((), ())), preferred_...]
    all_gather x2 -> x0, blocking collectives: 80.7 us -> none  [carried_in(): pieces = jax.tree.map(lambda part: lax.all_gather(part, axis), value)]
    ppermute x0 -> x90, waiting for transfers between devices: none -> 76.2 us  [the longest x64 42.5 us: hop(): return lax.ppermute(v, 'seq', [(i, i ^ 1 << bit) for i in range(n_seq)])]
  transfers between devices with their start and end apart: 4 -> 90, of which waited for: 3 -> 29; matrix products, arithmetic and copies ran while one was open for 11% -> 0% of each run, Pallas kernels for 0% -> 33%
where the time goes in v1:
time: 379 us; the launch traced here: 374 us
  Pallas kernels  163 us (43%)
  starting transfers between devices  108 us (28%)
  waiting for transfers between devices  76.2 us (20%)
  local copies, waits for them, and re-layouts  23.3 us (6%)
    pallas_call x53, Pallas kernels, run(): pl.pallas_call(body, grid_spec=pltpu.PrefetchScalarGridSpec(num_scalar_pr...  163 us
    ppermute x64, starting transfers between devices, hop(): return lax.ppermute(v, 'seq', [(i, i ^ 1 << bit) for i in range(n_seq)])  79.9 us
    ppermute x64, waiting for transfers between devices, hop(): return lax.ppermute(v, 'seq', [(i, i ^ 1 << bit) for i in range(n_seq)])  42.5 us
    unnamed x146, local copies, waits for them, and re-layouts  21.3 us
    ppermute x12, waiting for transfers between devices, to_member(): return lax.ppermute(v, 'seq', [(i, i ^ k) for i in range(n_seq)])  19.8 us
    ppermute x12, starting transfers between devices, to_member(): return lax.ppermute(v, 'seq', [(i, i ^ k) for i in range(n_seq)])  15.4 us
    ppermute x6, waiting for transfers between devices, shift(): return lax.ppermute(v, 'seq', [(i, (i + by) % n_seq) for i in range(n_seq)])  13.9 us
    ppermute x6, starting transfers between devices, shift(): return lax.ppermute(v, 'seq', [(i, (i + by) % n_seq) for i in range(n_seq)])  11.7 us
  transfers between devices with their start and end apart: 90, of which 29 were waited for; matrix products, arithmetic and copies ran while one was open for 0% of the time, Pallas kernels for 33%

profile of v1, /device:TPU:0, one launch (start us, length us, event | category | flops | bytes accessed | tf_op | source)
XLA Modules:
  0.0 373.8 jit_solution(9411696503630469799)
XLA Ops:
  4.8 10.3 %shard_map.195 = (bf16[512,768]{1,0:T(8,128)(2,1)S(1)}, bf16[512,768]{1,0:T(8,128)(2,1)S(1)}, bf16[512,768]{1,0:T(8,128)(2,1)S(1)}, bf16[512,1536]{1,0:T(8,128)(...) custom-call(s32[12]{0:T(128)S(1)} %concatenate.6.refs_0_, ...), custom_call_target="tpu_custom_call" | custom-call | bytes 7967744 | tf_op jit(solution)/shard_map/pallas_call | solution.py:112
  16.0 2.9 collective-permute-start
  20.5 11.2 %shard_map.196 = (bf16[512,768]{1,0:T(8,128)(2,1)S(1)}, bf16[512,1536]{1,0:T(8,128)(2,1)S(1)}, f32[512,1536]{1,0:T(8,128)}, f32[8,128]{1,0:T(8,128)S(1)}) custom-call(s32[12]{0:T(128)S(1)} %concatenate.6.refs_0_, bf16[512,768]{1,0:T(8,128)(2,1)S(1)} %get-tuple-element.255.refs_1_, bf16[768,2304]{1,0:T(8,128)(2,1)} %refs_4_.5, ...), custom_call_target="tpu_custom_call" | custom-call | bytes 7831552 | tf_op jit(solution)/shard_map/pallas_call | solution.py:112
  33.4 2.1 collective-permute-start.3
  35.5 2.6 collective-permute-start.4
  39.6 1.9 collective-permute-done.3.refs_5_
  41.5 3.2 collective-permute-done.4.refs_6_
  45.6 1.7 collective-permute-start.6
  50.6 2.6 collective-permute-done.7.refs_6_.refs_10_
  54.4 7.6 %shard_map.199 = (bf16[512,768]{1,0:T(8,128)(2,1)S(1)}, f32[512,768]{1,0:T(8,128)S(1)}, f32[512,768]{1,0:T(8,128)}, f32[512,768]{1,0:T(8,128)}, bf16[512,768]{1,0:T(8,128)(2,1)S(1)}, /*index=5*/f32[8,128]{1,0:T(8,128)S(1)}) custom-call(s32[12]{0:T(128)S(1)} %concatenate.6.refs_0_, bf16[512,768]{1,0:T(8,128)(2,1)S(1)} %bitcast.19, ...), custom_call_target="tpu_custom_call" | custom-call | bytes 7392256 | tf_op jit(solution)/shard_map/pallas_call | solution.py:112
  62.1 18.7 %shard_map.200 = (bf16[512,3072]{1,0:T(8,128)(2,1)S(1)}, bf16[512,3072]{1,0:T(8,128)(2,1)}, f32[384,3072]{1,0:T(8,128)}, f32[384,3072]{1,0:T(8,128)}, f32[8,128]{1,0:T(8,128)S(1)}) custom-call(s32[12]{0:T(128)S(1)} %concatenate.6.refs_0_, bf16[512,768]{1,0:T(8,128)(2,1)S(1)} %get-tuple-element.275.refs_1_.refs_3_, bf16[512,768]{1,0:T(8,128)(2,1)S(1)} %bitcast.14, ...), custom_call_target="tpu_custom_call" | custom-call | bytes 12582912 | tf_op jit(solution)/shard_map/pallas_call | solution.py:112
  80.8 1.7 copy-done.3
  83.0 12.4 %shard_map.201 = (f32[512,768]{1,0:T(8,128)}, f32[512,768]{1,0:T(8,128)S(1)}, bf16[512,768]{1,0:T(8,128)(2,1)S(1)}, f32[1,768]{1,0:T(1,128)S(1)}, f32[8,128]{1,0:T(8,128)S(1)}) custom-call(s32[12]{0:T(128)S(1)} %concatenate.6.refs_0_, bf16[512,3072]{1,0:T(8,128)(2,1)} %copy-done.3, bf16[512,3072]{1,0:T(8,128)(2,1)} %get-tuple-element.278.refs_2_, ...), custom_call_target="tpu_custom_call" | custom-call | bytes 18091008 | tf_op jit(solution)/shard_map/pallas_call | solution.py:112
  95.4 5.8 %shard_map.202 = (bf16[512,768]{1,0:T(8,128)(2,1)S(1)}, f32[512,768]{1,0:T(8,128)S(1)}, f32[96,512]{1,0:T(8,128)S(1)}, f32[3,72,128]{2,1,0:T(8,128)S(1)}, f32[3,...) custom-call(s32[12]{0:T(128)S(1)} %concatenate.6.refs_0_, ...), custom_call_target="tpu_custom_call" | custom-call | bytes 6946816 | tf_op jit(solution)/shard_map/pallas_call | solution.py:112
  103.3 2.9 shard_map.203
  107.8 9.6 %shard_map.204 = (f32[192,1152]{1,0:T(8,128)}, f32[192,1152]{1,0:T(8,128)S(1)}, f32[192,1152]{1,0:T(8,128)}, f32[192,1152]{1,0:T(8,128)S(1)}, f32[192,768]{1,0:T...) custom-call(s32[12]{0:T(128)S(1)} %concatenate.6.refs_0_, bf16[512,768]{1,0:T(8,128)(2,1)S(1)} %bitcast.17, ...), custom_call_target="tpu_custom_call" | custom-call | bytes 8650752 | tf_op jit(solution)/shard_map/pallas_call | solution.py:112
  123.7 2.7 collective-permute-start.23
  126.4 9.7 %shard_map.205 = (f32[192,1152]{1,0:T(8,128)}, f32[192,1152]{1,0:T(8,128)S(1)}, f32[192,1152]{1,0:T(8,128)}, f32[192,1152]{1,0:T(8,128)S(1)}, f32[192,768]{1,0:T...) custom-call(s32[12]{0:T(128)S(1)} %concatenate.6.refs_0_, ...), custom_call_target="tpu_custom_call" | custom-call | bytes 8650752 | tf_op jit(solution)/shard_map/pallas_call | solution.py:112
  138.8 6.2 %collective-permute-done.11.refs_4_ = f32[3,72,128]{2,1,0:T(8,128)S(1)} collective-permute-done((f32[3,72,128]{2,1,0:T(8,128)S(1)}, f32[3,72,128]{2,1,0:T(8,128)S(1)}, u32[]{:S(2)}, u32[]{:S(2)}) %collective-permute-start.11) | collective-permute-done | bytes 110624 | tf_op jit(solution)/shard_map/ppermute | solution.py:595
  145.6 3.3 collective-permute-start.14
  148.9 3.1 collective-permute-done.14.refs_5_
  152.2 5.5 %collective-permute-done.15.refs_6_ = f32[3,72,128]{2,1,0:T(8,128)S(1)} collective-permute-done((f32[3,72,128]{2,1,0:T(8,128)S(1)}, f32[3,72,128]{2,1,0:T(8,128)S(1)}, u32[]{:S(2)}, u32[]{:S(2)}) %collective-permute-start.15) | collective-permute-done | bytes 110624 | tf_op jit(solution)/shard_map/ppermute | solution.py:598
  157.6 2.1 collective-permute-start.16
  161.8 16.5 %shard_map.207 = (bf16[512,768]{1,0:T(8,128)(2,1)S(1)}, f32[512,1536]{1,0:T(8,128)}, f32[512,768]{1,0:T(8,128)}, f32[768,128]{1,0:T(8,128)S(1)}, f32[8,128]{1,0:T(8,128)S(1)}) custom-call(s32[12]{0:T(128)S(1)} %concatenate.6.refs_0_, bf16[512,768]{1,0:T(8,128)(2,1)S(1)} %copy-done.23, bf16[512,1536]{1,0:T(8,128)(2,1)} %copy-done.1, ...), custom_call_target="tpu_custom_call" | custom-call | bytes 10174464 | tf_op jit(solution)/shard_map/pallas_call | solution.py:112
  181.5 3.7 collective-permute-done.17.refs_7_
  185.2 1.9 collective-permute-done.18.refs_8_
  187.6 3.0 collective-permute-start.19
  190.6 2.9 shard_map.209
  195.8 2.0 shard_map.210
  198.6 2.9 shard_map.211
  202.9 2.7 collective-permute-done.19.refs_9_
  205.7 7.5 %shard_map.212 = (bf16[512,768]{1,0:T(8,128)(2,1)S(1)}, bf16[512,768]{1,0:T(8,128)(2,1)S(1)}, f32[768,128]{1,0:T(8,128)S(1)}, f32[8,128]{1,0:T(8,128)S(1)}) custom-call(s32[12]{0:T(128)S(1)} %concatenate.6.refs_0_, bf16[512,768]{1,0:T(8,128)(2,1)S(1)} %copy-done.27, bf16[512,1536]{1,0:T(8,128)(2,1)S(1)} %copy-done, ...), custom_call_target="tpu_custom_call" | custom-call | bytes 8667136 | tf_op jit(solution)/shard_map/pallas_call | solution.py:112
  213.2 2.9 shard_map.213
  216.1 1.7 shard_map.214
  219.8 1.6 collective-permute-start.29
  221.4 6.8 %shard_map.215 = (f32[512,768]{1,0:T(8,128)}, f32[392,128]{1,0:T(8,128)S(1)}, f32[392,128]{1,0:T(8,128)S(1)}, f32[8,128]{1,0:T(8,128)S(1)}) custom-call(s32[12]{0:T(128)S(1)} %concatenate.6.refs_0_, bf16[512,768]{1,0:T(8,128)(2,1)S(1)} %get-tuple-element.303.refs_2_.refs_1_, bf16[512,768]{1,0:T(8,128)(2,1)S(1)} %get-tuple-element.325.refs_2_, ...), custom_call_target="tpu_custom_call" | custom-call | bytes 9050112 | tf_op jit(solution)/shard_map/pallas_call | solution.py:112
  228.7 6.9 %collective-permute-done.30.refs_6_ = f32[192,256]{1,0:T(8,128)S(1)} collective-permute-done((f32[192,256]{1,0:T(8,128)S(1)}, f32[192,256]{1,0:T(8,128)S(1)}, u32[]{:S(2)}, u32[]{:S(2)}) %collective-permute-start.30) | collective-permute-done | bytes 196640 | tf_op jit(solution)/shard_map/ppermute | solution.py:592
  236.7 3.1 collective-permute-start.33
  239.8 2.8 shard_map.216
  245.6 2.9 shard_map.217
  248.5 2.1 shard_map.218
  254.6 1.7 collective-permute-start.57
  256.3 2.3 shard_map.220
  258.7 3.2 collective-permute-start.51
  261.9 1.7 collective-permute-done.56.refs_2_
  264.8 1.6 collective-permute-start.54
  269.0 3.5 collective-permute-done.58.refs_6_
  272.5 2.8 collective-permute-start.49
  279.3 1.6 collective-permute-start.71
  281.8 3.0 collective-permute-done.68.refs_2_
  284.8 2.3 collective-permute-start.73
  288.2 3.5 collective-permute-done.72.refs_4_
  294.3 2.1 collective-permute-done.42.refs_4_
  297.9 4.1 %collective-permute-done.43.refs_6_ = f32[96,256]{1,0:T(8,128)S(1)} collective-permute-done((f32[96,256]{1,0:T(8,128)S(1)}, f32[96,256]{1,0:T(8,128)S(1)}, u32[]{:S(2)}, u32[]{:S(2)}) %collective-permute-start.43) | collective-permute-done | bytes 98336 | tf_op jit(solution)/shard_map/ppermute | solution.py:592
  305.6 3.0 collective-permute-start.46
  309.9 2.0 collective-permute-start.67
  314.0 3.3 collective-permute-start.70
  321.1 3.1 collective-permute-done.70.refs_6_
  324.2 3.4 collective-permute-start.63
  335.1 3.6 collective-permute-done.59.refs_2_
  342.2 2.7 collective-permute-start.82
  356.6 1.7 collective-permute-start.76
  358.3 3.1 collective-permute-done.74.refs_2_
  362.5 1.9 collective-permute-start.87
  (321 shorter events, 106.7 us)
Async XLA Ops:
  16.0 16.8 %collective-permute-start = (f32[3,72,128]{2,1,0:T(8,128)S(1)}, f32[3,72,128]{2,1,0:T(8,128)S(1)}, u32[]{:S(2)}, u32[]{:S(2)}) collective-permute-start(f32[3,72,128]{2,1,0:T(8,128)S(1)} %get-tuple-element.263), channel_id=1, source_target_pairs={{0,1},{1,0},{2,3},{3,2},{4,5},{5,4},{6,7},{7,6},{8,9},{9,8},{10,11... | collective-permute-start | bytes 331784 | tf_op jit(solution)/shard_map/ppermute | solution.py:595
  18.9 13.9 %collective-permute-start.1 = (f32[3,72,128]{2,1,0:T(8,128)S(1)}, f32[3,72,128]{2,1,0:T(8,128)S(1)}, u32[]{:S(2)}, u32[]{:S(2)}) collective-permute-start(f32[3,72,128]{2,1,0:T(8,128)S(1)} %get-tuple-element.264), channel_id=1, source_target_pairs={{0,2},{1,3},{2,0},{3,1},{4,6},{5,7},{6,4},{7,5},{8,10},{9,11},{10,... | collective-permute-start | bytes 331784 | tf_op jit(solution)/shard_map/ppermute | solution.py:595
  20.4 12.4 %collective-permute-start.2 = (f32[3,72,128]{2,1,0:T(8,128)S(1)}, f32[3,72,128]{2,1,0:T(8,128)S(1)}, u32[]{:S(2)}, u32[]{:S(2)}) collective-permute-start(f32[3,72,128]{2,1,0:T(8,128)S(1)} %get-tuple-element.265), channel_id=1, source_target_pairs={{0,3},{1,2},{2,1},{3,0},{4,7},{5,6},{6,5},{7,4},{8,11},{9,10},{10,... | collective-permute-start | bytes 331784 | tf_op jit(solution)/shard_map/ppermute | solution.py:595
  33.4 8.0 %collective-permute-start.3 = (f32[3,72,128]{2,1,0:T(8,128)S(1)}, f32[3,72,128]{2,1,0:T(8,128)S(1)}, u32[]{:S(2)}, u32[]{:S(2)}) collective-permute-start(f32[3,72,128]{2,1,0:T(8,128)S(1)} %get-tuple-element.267), channel_id=1, source_target_pairs={{0,4},{1,5},{2,6},{3,7},{4,8},{5,9},{6,10},{7,11},{8,12},{9,13},{1... | collective-permute-start | bytes 331784 | tf_op jit(solution)/shard_map/ppermute | solution.py:598
  35.5 9.1 %collective-permute-start.4 = (f32[3,72,128]{2,1,0:T(8,128)S(1)}, f32[3,72,128]{2,1,0:T(8,128)S(1)}, u32[]{:S(2)}, u32[]{:S(2)}) collective-permute-start(f32[3,72,128]{2,1,0:T(8,128)S(1)} %get-tuple-element.267), channel_id=1, source_target_pairs={{0,8},{1,9},{2,10},{3,11},{4,12},{5,13},{6,14},{7,15},{8,0},{9,1},... | collective-permute-start | bytes 331784 | tf_op jit(solution)/shard_map/ppermute | solution.py:598
  82.5 25.3 %collective-permute-start.13 = (f32[384,3072]{1,0:T(8,128)}, f32[384,3072]{1,0:T(8,128)}, u32[]{:S(2)}, u32[]{:S(2)}) collective-permute-start(f32[384,3072]{1,0:T(8,128)} %get-tuple-element.296), channel_id=1, source_target_pairs={{0,16},{16,0},{1,17},{17,1},{2,18},{18,2},{3,19},{19,3},{4,20},{20... | collective-permute-start | bytes 14155784 | tf_op jit(solution)/shard_map/ppermute | solution.py:568
  82.5 41.2 %collective-permute-start.12 = (f32[384,3072]{1,0:T(8,128)}, f32[384,3072]{1,0:T(8,128)}, u32[]{:S(2)}, u32[]{:S(2)}) collective-permute-start(f32[384,3072]{1,0:T(8,128)} %get-tuple-element.295), channel_id=1, source_target_pairs={{0,16},{16,0},{1,17},{17,1},{2,18},{18,2},{3,19},{19,3},{4,20},{20... | collective-permute-start | bytes 14155784 | tf_op jit(solution)/shard_map/ppermute | solution.py:568
  106.2 75.0 %collective-permute-start.20 = (f32[384,768]{1,0:T(8,128)}, f32[384,768]{1,0:T(8,128)S(1)}, u32[]{:S(2)}, u32[]{:S(2)}) collective-permute-start(f32[384,768]{1,0:T(8,128)} %get-tuple-element.314), channel_id=1, source_target_pairs={{0,16},{16,0},{1,17},{17,1},{2,18},{18,2},{3,19},{19,3},{4,20},{20... | collective-permute-start | bytes 3538952 | tf_op jit(solution)/shard_map/ppermute | solution.py:568
  106.2 15.4 %collective-permute-start.9 = (f32[3,72,128]{2,1,0:T(8,128)S(1)}, f32[3,72,128]{2,1,0:T(8,128)S(1)}, u32[]{:S(2)}, u32[]{:S(2)}) collective-permute-start(f32[3,72,128]{2,1,0:T(8,128)S(1)} %get-tuple-element.292), channel_id=1, source_target_pairs={{0,1},{1,0},{2,3},{3,2},{4,5},{5,4},{6,7},{7,6},{8,9},{9,8},{10,11... | collective-permute-start | bytes 331784 | tf_op jit(solution)/shard_map/ppermute | solution.py:595
  107.0 15.7 %collective-permute-start.10 = (f32[3,72,128]{2,1,0:T(8,128)S(1)}, f32[3,72,128]{2,1,0:T(8,128)S(1)}, u32[]{:S(2)}, u32[]{:S(2)}) collective-permute-start(f32[3,72,128]{2,1,0:T(8,128)S(1)} %get-tuple-element.293), channel_id=1, source_target_pairs={{0,2},{1,3},{2,0},{3,1},{4,6},{5,7},{6,4},{7,5},{8,10},{9,11},{10,... | collective-permute-start | bytes 331784 | tf_op jit(solution)/shard_map/ppermute | solution.py:595
  120.2 67.4 %collective-permute-start.21 = (f32[192,1152]{1,0:T(8,128)}, f32[192,1152]{1,0:T(8,128)S(1)}, u32[]{:S(2)}, u32[]{:S(2)}) collective-permute-start(f32[192,1152]{1,0:T(8,128)} %get-tuple-element.316), channel_id=1, source_target_pairs={{0,1},{1,0},{2,3},{3,2},{4,5},{5,4},{6,7},{7,6},{8,9},{9,8},{10,11... | collective-permute-start | bytes 2654216 | tf_op jit(solution)/shard_map/ppermute | solution.py:592
  121.6 71.9 %collective-permute-start.22 = (f32[192,1152]{1,0:T(8,128)}, f32[192,1152]{1,0:T(8,128)}, u32[]{:S(2)}, u32[]{:S(2)}) collective-permute-start(f32[192,1152]{1,0:T(8,128)} %get-tuple-element.318), channel_id=1, source_target_pairs={{0,2},{1,3},{2,0},{3,1},{4,6},{5,7},{6,4},{7,5},{8,10},{9,11},{10,... | collective-permute-start | bytes 2654216 | tf_op jit(solution)/shard_map/ppermute | solution.py:592
  122.6 22.4 %collective-permute-start.11 = (f32[3,72,128]{2,1,0:T(8,128)S(1)}, f32[3,72,128]{2,1,0:T(8,128)S(1)}, u32[]{:S(2)}, u32[]{:S(2)}) collective-permute-start(f32[3,72,128]{2,1,0:T(8,128)S(1)} %get-tuple-element.294), channel_id=1, source_target_pairs={{0,3},{1,2},{2,1},{3,0},{4,7},{5,6},{6,5},{7,4},{8,11},{9,10},{10,... | collective-permute-start | bytes 331784 | tf_op jit(solution)/shard_map/ppermute | solution.py:595
  123.7 63.9 %collective-permute-start.23 = (f32[192,768]{1,0:T(8,128)}, f32[192,768]{1,0:T(8,128)S(1)}, u32[]{:S(2)}, u32[]{:S(2)}) collective-permute-start(f32[192,768]{1,0:T(8,128)} %get-tuple-element.320), channel_id=1, source_target_pairs={{0,4},{1,5},{2,6},{3,7},{4,0},{5,1},{6,2},{7,3},{8,12},{9,13},{10,... | collective-permute-start | bytes 1769480 | tf_op jit(solution)/shard_map/ppermute | solution.py:592
  157.6 21.5 %collective-permute-start.16 = (f32[3,72,128]{2,1,0:T(8,128)S(1)}, f32[3,72,128]{2,1,0:T(8,128)S(1)}, u32[]{:S(2)}, u32[]{:S(2)}) collective-permute-start(f32[3,72,128]{2,1,0:T(8,128)S(1)} %get-tuple-element.307), channel_id=1, source_target_pairs={{0,4},{1,5},{2,6},{3,7},{4,8},{5,9},{6,10},{7,11},{8,12},{9,13},{1... | collective-permute-start | bytes 331784 | tf_op jit(solution)/shard_map/ppermute | solution.py:598
  185.2 32.8 %collective-permute-start.40 = (f32[192,768]{1,0:T(8,128)}, f32[192,768]{1,0:T(8,128)S(1)}, u32[]{:S(2)}, u32[]{:S(2)}) collective-permute-start(f32[192,768]{1,0:T(8,128)} %get-tuple-element.368), channel_id=1, source_target_pairs={{0,4},{1,5},{2,6},{3,7},{4,0},{5,1},{6,2},{7,3},{8,12},{9,13},{10,... | collective-permute-start | bytes 1769480 | tf_op jit(solution)/shard_map/ppermute | solution.py:592
  187.1 31.4 %collective-permute-start.38 = (f32[192,1152]{1,0:T(8,128)}, f32[192,1152]{1,0:T(8,128)}, u32[]{:S(2)}, u32[]{:S(2)}) collective-permute-start(f32[192,1152]{1,0:T(8,128)} %get-tuple-element.364), channel_id=1, source_target_pairs={{0,1},{1,0},{2,3},{3,2},{4,5},{5,4},{6,7},{7,6},{8,9},{9,8},{10,11... | collective-permute-start | bytes 2654216 | tf_op jit(solution)/shard_map/ppermute | solution.py:592
  187.5 32.2 %collective-permute-start.39 = (f32[192,1152]{1,0:T(8,128)}, f32[192,1152]{1,0:T(8,128)}, u32[]{:S(2)}, u32[]{:S(2)}) collective-permute-start(f32[192,1152]{1,0:T(8,128)} %get-tuple-element.366), channel_id=1, source_target_pairs={{0,2},{1,3},{2,0},{3,1},{4,6},{5,7},{6,4},{7,5},{8,10},{9,11},{10,... | collective-permute-start | bytes 2654216 | tf_op jit(solution)/shard_map/ppermute | solution.py:592
  187.6 18.1 %collective-permute-start.19 = (f32[3,72,128]{2,1,0:T(8,128)S(1)}, f32[3,72,128]{2,1,0:T(8,128)S(1)}, u32[]{:S(2)}, u32[]{:S(2)}) collective-permute-start(f32[3,72,128]{2,1,0:T(8,128)S(1)} %get-tuple-element.312), channel_id=1, source_target_pairs={{0,3},{1,2},{2,1},{3,0},{4,7},{5,6},{6,5},{7,4},{8,11},{9,10},{10,... | collective-permute-start | bytes 331784 | tf_op jit(solution)/shard_map/ppermute | solution.py:595
  193.5 43.3 %collective-permute-start.24 = (f32[384,768]{1,0:T(8,128)}, f32[384,768]{1,0:T(8,128)S(1)}, u32[]{:S(2)}, u32[]{:S(2)}) collective-permute-start(f32[384,768]{1,0:T(8,128)} %get-tuple-element.335), channel_id=1, source_target_pairs={{0,16},{16,0},{1,17},{17,1},{2,18},{18,2},{3,19},{19,3},{4,20},{20... | collective-permute-start | bytes 3538952 | tf_op jit(solution)/shard_map/ppermute | solution.py:568
  217.9 24.8 %collective-permute-start.35 = (f32[384,768]{1,0:T(8,128)S(1)}, f32[384,768]{1,0:T(8,128)S(1)}, u32[]{:S(2)}, u32[]{:S(2)}) collective-permute-start(f32[384,768]{1,0:T(8,128)S(1)} %get-tuple-element.357), channel_id=1, source_target_pairs={{0,16},{16,0},{1,17},{17,1},{2,18},{18,2},{3,19},{19,3},{4,20},{20... | collective-permute-start | bytes 3538952 | tf_op jit(solution)/shard_map/ppermute | solution.py:568
  218.0 26.1 %collective-permute-start.36 = (f32[384,768]{1,0:T(8,128)}, f32[384,768]{1,0:T(8,128)S(1)}, u32[]{:S(2)}, u32[]{:S(2)}) collective-permute-start(f32[384,768]{1,0:T(8,128)} %get-tuple-element.358), channel_id=1, source_target_pairs={{0,16},{16,0},{1,17},{17,1},{2,18},{18,2},{3,19},{19,3},{4,20},{20... | collective-permute-start | bytes 3538952 | tf_op jit(solution)/shard_map/ppermute | solution.py:568
  218.5 9.8 %collective-permute-start.28 = (f32[192,256]{1,0:T(8,128)}, f32[192,256]{1,0:T(8,128)S(1)}, u32[]{:S(2)}, u32[]{:S(2)}) collective-permute-start(f32[192,256]{1,0:T(8,128)} %get-tuple-element.344), channel_id=1, source_target_pairs={{0,1},{1,0},{2,3},{3,2},{4,5},{5,4},{6,7},{7,6},{8,9},{9,8},{10,11... | collective-permute-start | bytes 589832 | tf_op jit(solution)/shard_map/ppermute | solution.py:592
  219.8 8.5 %collective-permute-start.29 = (f32[192,256]{1,0:T(8,128)}, f32[192,256]{1,0:T(8,128)S(1)}, u32[]{:S(2)}, u32[]{:S(2)}) collective-permute-start(f32[192,256]{1,0:T(8,128)} %get-tuple-element.346), channel_id=1, source_target_pairs={{0,2},{1,3},{2,0},{3,1},{4,6},{5,7},{6,4},{7,5},{8,10},{9,11},{10,... | collective-permute-start | bytes 589832 | tf_op jit(solution)/shard_map/ppermute | solution.py:592
  228.3 7.7 %collective-permute-start.34 = (f32[392,128]{1,0:T(8,128)S(1)}, f32[392,128]{1,0:T(8,128)S(1)}, u32[]{:S(2)}, u32[]{:S(2)}) collective-permute-start(f32[392,128]{1,0:T(8,128)S(1)} %get-tuple-element.356), channel_id=1, source_target_pairs={{0,16},{16,0},{1,17},{17,1},{2,18},{18,2},{3,19},{19,3},{4,20},{20... | collective-permute-start | bytes 602120 | tf_op jit(solution)/shard_map/ppermute | solution.py:568
  235.6 18.1 %collective-permute-start.31 = (f32[96,1152]{1,0:T(8,128)S(1)}, f32[96,1152]{1,0:T(8,128)S(1)}, u32[]{:S(2)}, u32[]{:S(2)}) collective-permute-start(f32[96,1152]{1,0:T(8,128)S(1)} %copy-done.69), channel_id=1, source_target_pairs={{0,2},{1,3},{2,0},{3,1},{4,6},{5,7},{6,4},{7,5},{8,10},{9,11},{10,... | collective-permute-start | bytes 1327112 | tf_op jit(solution)/shard_map/ppermute | solution.py:592
  236.0 17.7 %collective-permute-start.32 = (f32[96,1152]{1,0:T(8,128)S(1)}, f32[96,1152]{1,0:T(8,128)S(1)}, u32[]{:S(2)}, u32[]{:S(2)}) collective-permute-start(f32[96,1152]{1,0:T(8,128)S(1)} %copy-done.67), channel_id=1, source_target_pairs={{0,1},{1,0},{2,3},{3,2},{4,5},{5,4},{6,7},{7,6},{8,9},{9,8},{10,11... | collective-permute-start | bytes 1327112 | tf_op jit(solution)/shard_map/ppermute | solution.py:592
  236.7 15.8 %collective-permute-start.33 = (f32[96,768]{1,0:T(8,128)S(1)}, f32[96,768]{1,0:T(8,128)S(1)}, u32[]{:S(2)}, u32[]{:S(2)}) collective-permute-start(f32[96,768]{1,0:T(8,128)S(1)} %copy-done.71), channel_id=1, source_target_pairs={{0,8},{1,9},{2,10},{3,11},{4,12},{5,13},{6,14},{7,15},{8,0},{9,1},... | collective-permute-start | bytes 884744 | tf_op jit(solution)/shard_map/ppermute | solution.py:592
  242.6 12.0 %collective-permute-start.25 = (f32[192,256]{1,0:T(8,128)S(1)}, f32[192,256]{1,0:T(8,128)S(1)}, u32[]{:S(2)}, u32[]{:S(2)}) collective-permute-start(f32[192,256]{1,0:T(8,128)S(1)} %get-tuple-element.338), channel_id=1, source_target_pairs={{0,1},{1,0},{2,3},{3,2},{4,5},{5,4},{6,7},{7,6},{8,9},{9,8},{10,11... | collective-permute-start | bytes 589832 | tf_op jit(solution)/shard_map/ppermute | solution.py:592
  244.0 14.6 %collective-permute-start.26 = (f32[192,256]{1,0:T(8,128)}, f32[192,256]{1,0:T(8,128)S(1)}, u32[]{:S(2)}, u32[]{:S(2)}) collective-permute-start(f32[192,256]{1,0:T(8,128)} %get-tuple-element.340), channel_id=1, source_target_pairs={{0,2},{1,3},{2,0},{3,1},{4,6},{5,7},{6,4},{7,5},{8,10},{9,11},{10,... | collective-permute-start | bytes 589832 | tf_op jit(solution)/shard_map/ppermute | solution.py:592
  252.5 14.0 %collective-permute-start.37 = (f32[392,128]{1,0:T(8,128)S(1)}, f32[392,128]{1,0:T(8,128)S(1)}, u32[]{:S(2)}, u32[]{:S(2)}) collective-permute-start(f32[392,128]{1,0:T(8,128)S(1)} %get-tuple-element.362.refs_1_), channel_id=1, source_target_pairs={{0,1},{1,0},{2,3},{3,2},{4,5},{5,4},{6,7},{7,6},{8,9},{9,8},{10,11... | collective-permute-start | bytes 602120 | tf_op jit(solution)/shard_map/ppermute | solution.py:592
  253.7 8.1 %collective-permute-start.27 = (f32[192,256]{1,0:T(8,128)S(1)}, f32[192,256]{1,0:T(8,128)S(1)}, u32[]{:S(2)}, u32[]{:S(2)}) collective-permute-start(f32[192,256]{1,0:T(8,128)S(1)} %get-tuple-element.342), channel_id=1, source_target_pairs={{0,4},{1,5},{2,6},{3,7},{4,0},{5,1},{6,2},{7,3},{8,12},{9,13},{10,... | collective-permute-start | bytes 589832 | tf_op jit(solution)/shard_map/ppermute | solution.py:592
  253.7 9.9 %collective-permute-start.56 = (f32[192,256]{1,0:T(8,128)S(1)}, f32[192,256]{1,0:T(8,128)S(1)}, u32[]{:S(2)}, u32[]{:S(2)}) collective-permute-start(f32[192,256]{1,0:T(8,128)S(1)} %get-tuple-element.404), channel_id=1, source_target_pairs={{0,1},{1,0},{2,3},{3,2},{4,5},{5,4},{6,7},{7,6},{8,9},{9,8},{10,11... | collective-permute-start | bytes 589832 | tf_op jit(solution)/shard_map/ppermute | solution.py:592
  254.6 10.2 %collective-permute-start.57 = (f32[192,256]{1,0:T(8,128)}, f32[192,256]{1,0:T(8,128)S(1)}, u32[]{:S(2)}, u32[]{:S(2)}) collective-permute-start(f32[192,256]{1,0:T(8,128)} %get-tuple-element.406), channel_id=1, source_target_pairs={{0,2},{1,3},{2,0},{3,1},{4,6},{5,7},{6,4},{7,5},{8,10},{9,11},{10,... | collective-permute-start | bytes 589832 | tf_op jit(solution)/shard_map/ppermute | solution.py:592
  258.7 22.3 %collective-permute-start.51 = (f32[96,768]{1,0:T(8,128)S(1)}, f32[96,768]{1,0:T(8,128)S(1)}, u32[]{:S(2)}, u32[]{:S(2)}) collective-permute-start(f32[96,768]{1,0:T(8,128)S(1)} %get-tuple-element.395), channel_id=1, source_target_pairs={{0,8},{1,9},{2,10},{3,11},{4,12},{5,13},{6,14},{7,15},{8,0},{9,1},... | collective-permute-start | bytes 884744 | tf_op jit(solution)/shard_map/ppermute | solution.py:592
  261.9 10.6 %collective-permute-start.58 = (f32[192,256]{1,0:T(8,128)}, f32[192,256]{1,0:T(8,128)S(1)}, u32[]{:S(2)}, u32[]{:S(2)}) collective-permute-start(f32[192,256]{1,0:T(8,128)} %get-tuple-element.408), channel_id=1, source_target_pairs={{0,4},{1,5},{2,6},{3,7},{4,0},{5,1},{6,2},{7,3},{8,12},{9,13},{10,... | collective-permute-start | bytes 589832 | tf_op jit(solution)/shard_map/ppermute | solution.py:592
  263.6 12.3 %collective-permute-start.53 = (f32[192,256]{1,0:T(8,128)S(1)}, f32[192,256]{1,0:T(8,128)S(1)}, u32[]{:S(2)}, u32[]{:S(2)}) collective-permute-start(f32[192,256]{1,0:T(8,128)S(1)} %get-tuple-element.398), channel_id=1, source_target_pairs={{0,1},{1,0},{2,3},{3,2},{4,5},{5,4},{6,7},{7,6},{8,9},{9,8},{10,11... | collective-permute-start | bytes 589832 | tf_op jit(solution)/shard_map/ppermute | solution.py:592
  264.8 11.1 %collective-permute-start.54 = (f32[192,256]{1,0:T(8,128)S(1)}, f32[192,256]{1,0:T(8,128)S(1)}, u32[]{:S(2)}, u32[]{:S(2)}) collective-permute-start(f32[192,256]{1,0:T(8,128)S(1)} %get-tuple-element.400), channel_id=1, source_target_pairs={{0,2},{1,3},{2,0},{3,1},{4,6},{5,7},{6,4},{7,5},{8,10},{9,11},{10,... | collective-permute-start | bytes 589832 | tf_op jit(solution)/shard_map/ppermute | solution.py:592
  266.5 10.6 %collective-permute-start.55 = (f32[192,256]{1,0:T(8,128)S(1)}, f32[192,256]{1,0:T(8,128)S(1)}, u32[]{:S(2)}, u32[]{:S(2)}) collective-permute-start(f32[192,256]{1,0:T(8,128)S(1)} %get-tuple-element.402), channel_id=1, source_target_pairs={{0,4},{1,5},{2,6},{3,7},{4,0},{5,1},{6,2},{7,3},{8,12},{9,13},{10,... | collective-permute-start | bytes 589832 | tf_op jit(solution)/shard_map/ppermute | solution.py:592
  272.5 32.0 %collective-permute-start.49 = (f32[96,1152]{1,0:T(8,128)S(1)}, f32[96,1152]{1,0:T(8,128)S(1)}, u32[]{:S(2)}, u32[]{:S(2)}) collective-permute-start(f32[96,1152]{1,0:T(8,128)S(1)} %get-tuple-element.391), channel_id=1, source_target_pairs={{0,2},{1,3},{2,0},{3,1},{4,6},{5,7},{6,4},{7,5},{8,10},{9,11},{10,... | collective-permute-start | bytes 1327112 | tf_op jit(solution)/shard_map/ppermute | solution.py:592
  279.0 26.6 %collective-permute-start.50 = (f32[96,1152]{1,0:T(8,128)S(1)}, f32[96,1152]{1,0:T(8,128)S(1)}, u32[]{:S(2)}, u32[]{:S(2)}) collective-permute-start(f32[96,1152]{1,0:T(8,128)S(1)} %get-tuple-element.393), channel_id=1, source_target_pairs={{0,1},{1,0},{2,3},{3,2},{4,5},{5,4},{6,7},{7,6},{8,9},{9,8},{10,11... | collective-permute-start | bytes 1327112 | tf_op jit(solution)/shard_map/ppermute | solution.py:592
  279.3 7.8 %collective-permute-start.71 = (f32[96,256]{1,0:T(8,128)S(1)}, f32[96,256]{1,0:T(8,128)S(1)}, u32[]{:S(2)}, u32[]{:S(2)}) collective-permute-start(f32[96,256]{1,0:T(8,128)S(1)} %get-tuple-element.440), channel_id=1, source_target_pairs={{0,2},{1,3},{2,0},{3,1},{4,6},{5,7},{6,4},{7,5},{8,10},{9,11},{10,... | collective-permute-start | bytes 294920 | tf_op jit(solution)/shard_map/ppermute | solution.py:592
  280.9 10.8 %collective-permute-start.72 = (f32[96,256]{1,0:T(8,128)S(1)}, f32[96,256]{1,0:T(8,128)S(1)}, u32[]{:S(2)}, u32[]{:S(2)}) collective-permute-start(f32[96,256]{1,0:T(8,128)S(1)} %get-tuple-element.442), channel_id=1, source_target_pairs={{0,1},{1,0},{2,3},{3,2},{4,5},{5,4},{6,7},{7,6},{8,9},{9,8},{10,11... | collective-permute-start | bytes 294920 | tf_op jit(solution)/shard_map/ppermute | solution.py:592
  291.7 22.2 %collective-permute-start.47 = (f32[48,2304]{1,0:T(8,128)S(1)}, f32[48,2304]{1,0:T(8,128)S(1)}, u32[]{:S(2)}, u32[]{:S(2)}) collective-permute-start(f32[48,2304]{1,0:T(8,128)S(1)} %get-tuple-element.387), channel_id=1, source_target_pairs={{0,4},{1,5},{2,6},{3,7},{4,0},{5,1},{6,2},{7,3},{8,12},{9,13},{10,... | collective-permute-start | bytes 1327112 | tf_op jit(solution)/shard_map/ppermute | solution.py:592
  292.7 10.8 %collective-permute-start.52 = (f32[392,128]{1,0:T(8,128)S(1)}, f32[392,128]{1,0:T(8,128)S(1)}, u32[]{:S(2)}, u32[]{:S(2)}) collective-permute-start(f32[392,128]{1,0:T(8,128)S(1)} %get-tuple-element.396.refs_1_), channel_id=1, source_target_pairs={{0,2},{1,3},{2,0},{3,1},{4,6},{5,7},{6,4},{7,5},{8,10},{9,11},{10,... | collective-permute-start | bytes 602120 | tf_op jit(solution)/shard_map/ppermute | solution.py:592
  302.0 7.8 %collective-permute-start.44 = (f32[96,256]{1,0:T(8,128)S(1)}, f32[96,256]{1,0:T(8,128)S(1)}, u32[]{:S(2)}, u32[]{:S(2)}) collective-permute-start(f32[96,256]{1,0:T(8,128)S(1)} %get-tuple-element.381), channel_id=1, source_target_pairs={{0,2},{1,3},{2,0},{3,1},{4,6},{5,7},{6,4},{7,5},{8,10},{9,11},{10,... | collective-permute-start | bytes 294920 | tf_op jit(solution)/shard_map/ppermute | solution.py:592
  304.5 8.8 %collective-permute-start.48 = (f32[48,768]{1,0:T(8,128)S(1)}, f32[48,768]{1,0:T(8,128)S(1)}, u32[]{:S(2)}, u32[]{:S(2)}) collective-permute-start(f32[48,768]{1,0:T(8,128)S(1)} %get-tuple-element.389), channel_id=1, source_target_pairs={{0,1},{1,0},{2,3},{3,2},{4,5},{5,4},{6,7},{7,6},{8,9},{9,8},{10,11... | collective-permute-start | bytes 442376 | tf_op jit(solution)/shard_map/ppermute | solution.py:592
  309.8 32.3 %collective-permute-start.65 = (f32[48,2304]{1,0:T(8,128)S(1)}, f32[48,2304]{1,0:T(8,128)S(1)}, u32[]{:S(2)}, u32[]{:S(2)}) collective-permute-start(f32[48,2304]{1,0:T(8,128)S(1)} %get-tuple-element.429), channel_id=1, source_target_pairs={{0,4},{1,5},{2,6},{3,7},{4,0},{5,1},{6,2},{7,3},{8,12},{9,13},{10,... | collective-permute-start | bytes 1327112 | tf_op jit(solution)/shard_map/ppermute | solution.py:592
  309.9 17.7 %collective-permute-start.67 = (f32[392,128]{1,0:T(8,128)S(1)}, f32[392,128]{1,0:T(8,128)S(1)}, u32[]{:S(2)}, u32[]{:S(2)}) collective-permute-start(f32[392,128]{1,0:T(8,128)S(1)} %get-tuple-element.432.refs_1_), channel_id=1, source_target_pairs={{0,4},{1,5},{2,6},{3,7},{4,0},{5,1},{6,2},{7,3},{8,12},{9,13},{10,... | collective-permute-start | bytes 602120 | tf_op jit(solution)/shard_map/ppermute | solution.py:592
  311.9 12.3 %collective-permute-start.66 = (f32[48,768]{1,0:T(8,128)S(1)}, f32[48,768]{1,0:T(8,128)S(1)}, u32[]{:S(2)}, u32[]{:S(2)}) collective-permute-start(f32[48,768]{1,0:T(8,128)S(1)} %get-tuple-element.431), channel_id=1, source_target_pairs={{0,1},{1,0},{2,3},{3,2},{4,5},{5,4},{6,7},{7,6},{8,9},{9,8},{10,11... | collective-permute-start | bytes 442376 | tf_op jit(solution)/shard_map/ppermute | solution.py:592
  314.0 10.2 %collective-permute-start.70 = (f32[96,256]{1,0:T(8,128)S(1)}, f32[96,256]{1,0:T(8,128)S(1)}, u32[]{:S(2)}, u32[]{:S(2)}) collective-permute-start(f32[96,256]{1,0:T(8,128)S(1)} %get-tuple-element.438), channel_id=1, source_target_pairs={{0,8},{1,9},{2,10},{3,11},{4,12},{5,13},{6,14},{7,15},{8,0},{9,1},... | collective-permute-start | bytes 294920 | tf_op jit(solution)/shard_map/ppermute | solution.py:592
  319.6 9.4 %collective-permute-start.84 = (f32[48,256]{1,0:T(8,128)S(1)}, f32[48,256]{1,0:T(8,128)S(1)}, u32[]{:S(2)}, u32[]{:S(2)}) collective-permute-start(f32[48,256]{1,0:T(8,128)S(1)} %get-tuple-element.472), channel_id=1, source_target_pairs={{0,1},{1,0},{2,3},{3,2},{4,5},{5,4},{6,7},{7,6},{8,9},{9,8},{10,11... | collective-permute-start | bytes 147464 | tf_op jit(solution)/shard_map/ppermute | solution.py:592
  324.2 9.6 %collective-permute-start.64 = (f32[24,768]{1,0:T(8,128)S(1)}, f32[24,768]{1,0:T(8,128)S(1)}, u32[]{:S(2)}, u32[]{:S(2)}) collective-permute-start(f32[24,768]{1,0:T(8,128)S(1)} %get-tuple-element.427), channel_id=1, source_target_pairs={{0,2},{1,3},{2,0},{3,1},{4,6},{5,7},{6,4},{7,5},{8,10},{9,11},{10,... | collective-permute-start | bytes 221192 | tf_op jit(solution)/shard_map/ppermute | solution.py:592
  324.2 21.3 %collective-permute-start.63 = (f32[24,2304]{1,0:T(8,128)S(1)}, f32[24,2304]{1,0:T(8,128)S(1)}, u32[]{:S(2)}, u32[]{:S(2)}) collective-permute-start(f32[24,2304]{1,0:T(8,128)S(1)} %get-tuple-element.425), channel_id=1, source_target_pairs={{0,8},{1,9},{2,10},{3,11},{4,12},{5,13},{6,14},{7,15},{8,0},{9,1},... | collective-permute-start | bytes 663560 | tf_op jit(solution)/shard_map/ppermute | solution.py:592
  331.7 18.9 %collective-permute-start.80 = (f32[392,128]{1,0:T(8,128)S(1)}, f32[392,128]{1,0:T(8,128)S(1)}, u32[]{:S(2)}, u32[]{:S(2)}) collective-permute-start(f32[392,128]{1,0:T(8,128)S(1)} %get-tuple-element.464.refs_1_), channel_id=1, source_target_pairs={{0,8},{1,9},{2,10},{3,11},{4,12},{5,13},{6,14},{7,15},{8,0},{9,1},... | collective-permute-start | bytes 602120 | tf_op jit(solution)/shard_map/ppermute | solution.py:592
  333.8 7.8 %collective-permute-start.61 = (f32[48,512]{1,0:T(8,128)S(1)}, f32[48,512]{1,0:T(8,128)S(1)}, u32[]{:S(2)}, u32[]{:S(2)}) collective-permute-start(f32[48,512]{1,0:T(8,128)S(1)} %get-tuple-element.421), channel_id=1, source_target_pairs={{0,4},{1,5},{2,6},{3,7},{4,0},{5,1},{6,2},{7,3},{8,12},{9,13},{10,... | collective-permute-start | bytes 294920 | tf_op jit(solution)/shard_map/ppermute | solution.py:592
  338.8 10.6 %collective-permute-start.83 = (f32[48,512]{1,0:T(8,128)S(1)}, f32[48,512]{1,0:T(8,128)S(1)}, u32[]{:S(2)}, u32[]{:S(2)}) collective-permute-start(f32[48,512]{1,0:T(8,128)S(1)} %get-tuple-element.470), channel_id=1, source_target_pairs={{0,4},{1,5},{2,6},{3,7},{4,0},{5,1},{6,2},{7,3},{8,12},{9,13},{10,... | collective-permute-start | bytes 294920 | tf_op jit(solution)/shard_map/ppermute | solution.py:592
  341.6 8.4 %collective-permute-start.81 = (f32[48,512]{1,0:T(8,128)S(1)}, f32[48,512]{1,0:T(8,128)S(1)}, u32[]{:S(2)}, u32[]{:S(2)}) collective-permute-start(f32[48,512]{1,0:T(8,128)S(1)} %get-tuple-element.466), channel_id=1, source_target_pairs={{0,4},{1,5},{2,6},{3,7},{4,0},{5,1},{6,2},{7,3},{8,12},{9,13},{10,... | collective-permute-start | bytes 294920 | tf_op jit(solution)/shard_map/ppermute | solution.py:592
  342.2 7.8 %collective-permute-start.82 = (f32[48,256]{1,0:T(8,128)S(1)}, f32[48,256]{1,0:T(8,128)S(1)}, u32[]{:S(2)}, u32[]{:S(2)}) collective-permute-start(f32[48,256]{1,0:T(8,128)S(1)} %get-tuple-element.468), channel_id=1, source_target_pairs={{0,1},{1,0},{2,3},{3,2},{4,5},{5,4},{6,7},{7,6},{8,9},{9,8},{10,11... | collective-permute-start | bytes 147464 | tf_op jit(solution)/shard_map/ppermute | solution.py:592
  345.5 19.8 %collective-permute-start.78 = (f32[24,2304]{1,0:T(8,128)S(1)}, f32[24,2304]{1,0:T(8,128)S(1)}, u32[]{:S(2)}, u32[]{:S(2)}) collective-permute-start(f32[24,2304]{1,0:T(8,128)S(1)} %get-tuple-element.461), channel_id=1, source_target_pairs={{0,8},{1,9},{2,10},{3,11},{4,12},{5,13},{6,14},{7,15},{8,0},{9,1},... | collective-permute-start | bytes 663560 | tf_op jit(solution)/shard_map/ppermute | solution.py:592
  351.2 19.4 %collective-permute-start.89 = (f32[392,128]{1,0:T(8,128)S(1)}, f32[392,128]{1,0:T(8,128)S(1)}, u32[]{:S(2)}, u32[]{:S(2)}) collective-permute-start(f32[392,128]{1,0:T(8,128)S(1)} %get-tuple-element.495.refs_1_), channel_id=1, source_target_pairs={{0,16},{16,0},{1,17},{17,1},{2,18},{18,2},{3,19},{19,3},{4,20},{20... | collective-permute-start | bytes 602120 | tf_op jit(solution)/shard_map/ppermute | solution.py:568
  353.3 11.0 %collective-permute-start.79 = (f32[24,768]{1,0:T(8,128)S(1)}, f32[24,768]{1,0:T(8,128)S(1)}, u32[]{:S(2)}, u32[]{:S(2)}) collective-permute-start(f32[24,768]{1,0:T(8,128)S(1)} %get-tuple-element.463), channel_id=1, source_target_pairs={{0,2},{1,3},{2,0},{3,1},{4,6},{5,7},{6,4},{7,5},{8,10},{9,11},{10,... | collective-permute-start | bytes 221192 | tf_op jit(solution)/shard_map/ppermute | solution.py:592
  361.4 8.0 %collective-permute-start.85 = (f32[24,512]{1,0:T(8,128)S(1)}, f32[24,512]{1,0:T(8,128)S(1)}, u32[]{:S(2)}, u32[]{:S(2)}) collective-permute-start(f32[24,512]{1,0:T(8,128)S(1)} %get-tuple-element.481), channel_id=1, source_target_pairs={{0,8},{1,9},{2,10},{3,11},{4,12},{5,13},{6,14},{7,15},{8,0},{9,1},... | collective-permute-start | bytes 147464 | tf_op jit(solution)/shard_map/ppermute | solution.py:592
  362.5 7.5 %collective-permute-start.87 = (f32[24,512]{1,0:T(8,128)S(1)}, f32[24,512]{1,0:T(8,128)S(1)}, u32[]{:S(2)}, u32[]{:S(2)}) collective-permute-start(f32[24,512]{1,0:T(8,128)S(1)} %get-tuple-element.487), channel_id=1, source_target_pairs={{0,8},{1,9},{2,10},{3,11},{4,12},{5,13},{6,14},{7,15},{8,0},{9,1},... | collective-permute-start | bytes 147464 | tf_op jit(solution)/shard_map/ppermute | solution.py:592
  (99 other events, 907.4 us)

commit v2 on v1

v2 whole, which is shorter than its diff:
```python
import functools

import jax
import jax.numpy as jnp
from jax import lax
from jax.experimental import pallas as pl
from jax.experimental.pallas import tpu as pltpu
from jax.sharding import PartitionSpec as P

EPSILON = 1e-05
F32 = jnp.float32
BF16 = jnp.bfloat16
STATE_ROWS = 72
SMALL_ROWS = 72
MIB = 1024 * 1024


def mm(a, b):
    return lax.dot_general(a, b, (((1,), (0,)), ((), ())), preferred_element_type=F32)


def nt(a, b):
    return lax.dot_general(a, b, (((1,), (1,)), ((), ())), preferred_element_type=F32)


def tn(a, b):
    return lax.dot_general(a, b, (((0,), (0,)), ((), ())), preferred_element_type=F32)


def split(v):
    high = v.astype(BF16)
    return high, (v - high.astype(F32)).astype(BF16)


def iota(shape, dim):
    return lax.broadcasted_iota(jnp.int32, shape, dim)


def segment_ones(width):
    shape = (width, width)
    return (iota(shape, 0) // 64 == iota(shape, 1) // 64).astype(BF16)


def segment_sum(v, ones):
    high, low = split(v)
    return mm(high, ones) + mm(low, ones)


def moments(x):
    centre = jnp.mean(x, axis=-1, keepdims=True)
    offsets = x - centre
    variance = jnp.mean(offsets * offsets, axis=-1, keepdims=True)
    scale = lax.rsqrt(variance + EPSILON)
    return offsets * scale, scale


def norm_back(grad, normed, scale, gain):
    dn = grad * gain
    first = jnp.mean(dn, axis=-1, keepdims=True)
    second = jnp.mean(dn * normed, axis=-1, keepdims=True)
    return (dn - first - normed * second) * scale


def fill_maps(scr, map_ref):
    scr[...] = jnp.zeros(scr.shape, scr.dtype)
    for h in range(4):
        m = map_ref[h].astype(F32)
        scr[64 * h : 64 * h + 64, 128 * h : 128 * h + 128] = jnp.concatenate(
            [m, -m], axis=1
        ).astype(scr.dtype)


def features(pre, ones):
    low_half = iota(pre.shape, 1) < 64
    top = jnp.max(jnp.where(low_half, pre, -jnp.inf), axis=1, keepdims=True)
    bottom = jnp.max(jnp.where(low_half, -jnp.inf, pre), axis=1, keepdims=True)
    e = jnp.exp(pre - jnp.where(low_half, top, bottom))
    return e / segment_sum(e, ones)


def features_back(feat, grad, ones):
    weighted = feat * grad
    total = segment_sum(weighted, ones)
    mass = mm(feat.astype(BF16), ones)
    part = weighted - feat * (total / mass)
    return part - pltpu.roll(part, 64, 1)


def whole(shape):
    return pl.BlockSpec(shape, lambda *_: (0,) * len(shape))


def columns(rows, width):
    return pl.BlockSpec((rows, width), lambda j: (0, j))


ANYWHERE = pl.BlockSpec(memory_space=pl.ANY)


def my_core():
    return lax.axis_index("batch")


def my_seq():
    return lax.axis_index("seq")


def nbytes(shape, dtype):
    total = jnp.dtype(dtype).itemsize
    for n in shape:
        total *= n
    return total


class Held:
    def __init__(self, array):
        self.array, self.shape, self.dtype = array, array.shape, array.dtype


class Near(Held):
    pass


def run(kernel, tok, grid, ins, outs, scratch=(), extra=4, aliases=None, us=1.0):
    n_in, n_out = len(ins), len(outs)
    linked = tok is not None
    outs = [tuple(out) + (False,) * (4 - len(out)) for out in outs]

    def body(*refs):
        kernel(*refs[:n_in], *refs[n_in + linked : n_in + linked + n_out], *refs[n_in + linked + n_out + 1 :])

    held = 0
    arrays = []
    for array, spec in ins:
        near = isinstance(array, Near)
        if spec.block_shape is not None and not near:
            held += (1 if spec.block_shape == array.shape else 2) * nbytes(spec.block_shape, array.dtype)
        if isinstance(array, Held):
            array = pltpu.with_memory_space_constraint(array.array, pltpu.VMEM if near else pltpu.HBM)
        arrays.append(array)
    for shape, dtype, spec, stays in outs:
        if stays is not Near:
            held += (1 if spec.block_shape == shape else 2) * nbytes(spec.block_shape, dtype)
    for item in scratch:
        held += nbytes(item.shape, item.dtype)
    result = pl.pallas_call(
        body,
        grid=grid,
        in_specs=[spec for _, spec in ins] + [ANYWHERE] * linked,
        out_specs=[spec for _, _, spec, _ in outs] + [ANYWHERE],
        scratch_shapes=list(scratch),
        out_shape=[
            pltpu.VMEM(shape, dtype) if stays is Near
            else pltpu.HBM(shape, dtype) if stays else jax.ShapeDtypeStruct(shape, dtype)
            for shape, dtype, _, stays in outs
        ]
        + [jax.ShapeDtypeStruct((8, 128), F32)],
        input_output_aliases=aliases or {},
        cost_estimate=pl.CostEstimate(flops=int(us * 1.15e9), bytes_accessed=0, transcendentals=0),
        compiler_params=pltpu.CompilerParams(vmem_limit_bytes=min(held + extra * MIB, 60 * MIB)),
    )(*arrays, *([tok] if linked else []))
    results = [Near(r) if out[3] is Near else Held(r) if out[3] else r for r, out in zip(result, outs)]
    return results, result[-1]


def keys_kernel(x_ref, gain_ref, wk_ref, wv_ref, map_ref, mask_ref, starts_ref,
                attn_ref, k_ref, v_ref, fk_ref, p0, p1, p2, p3,
                allow_ref, allow_t_ref, tail_ref, contin_ref,
                map_scr, state_scr):
    j = pl.program_id(0)
    tokens = x_ref.shape[0]
    n_flags = starts_ref.shape[1]
    unit = tokens // n_flags

    def seg(shape, dim):
        place = iota(shape, dim)
        total = jnp.zeros(shape, jnp.int32)
        for u in range(n_flags):
            total = total + jnp.where(place >= unit * u, starts_ref[0, u], 0)
        return total

    @pl.when(j == 0)
    def _():
        normed, _ = moments(x_ref[...].astype(F32))
        attn_ref[...] = (normed * gain_ref[...]).astype(BF16)
        last = starts_ref[0, 0]
        for u in range(1, n_flags):
            last = last + starts_ref[0, u]
        mask_row = mask_ref[...].astype(F32)
        mask_col = jnp.transpose(jnp.broadcast_to(mask_row, (128, tokens)))
        seg_col = seg((tokens, 128), 0)
        tail_ref[...] = jnp.where(seg_col == last, mask_col, 0.0)
        contin_ref[...] = jnp.where(seg_col == 0, 1.0, 0.0)
        square = (tokens, tokens)
        same = seg(square, 0) == seg(square, 1)
        allow_ref[...] = jnp.where(same & (iota(square, 1) <= iota(square, 0)), mask_row, 0.0)
        wide_mask = jnp.concatenate([mask_col] * (tokens // 128), axis=1)
        allow_t_ref[...] = jnp.where(same & (iota(square, 0) <= iota(square, 1)), wide_mask, 0.0)

    fill_maps(map_scr, map_ref)
    attn = attn_ref[...]
    k4 = mm(attn, wk_ref[...]).astype(BF16)
    v4 = mm(attn, wv_ref[...]).astype(BF16)
    k_ref[...] = k4
    v_ref[...] = v4
    pre = mm(k4, map_scr[...])
    ones = segment_ones(128)
    v_t = jnp.transpose(v4.astype(F32)).astype(BF16)
    tail = tail_ref[...]
    row_ones = jnp.ones((16, tokens), BF16)
    for h in range(4):
        feat = features(pre[:, 128 * h : 128 * h + 128], ones).astype(BF16)
        fk_ref[:, 128 * h : 128 * h + 128] = feat
        kept = (feat.astype(F32) * tail).astype(BF16)
        state_scr[4 * j + h, 0:64, :] = mm(v_t[64 * h : 64 * h + 64], kept)
        state_scr[4 * j + h, 64:72, :] = mm(row_ones, kept)[0:8]

    @pl.when(j == pl.num_programs(0) - 1)
    def _():
        for k, piece in enumerate((p0, p1, p2, p3)):
            n = piece.shape[0]
            piece[...] = state_scr[pl.ds(((my_seq() & 3) ^ k) * n, n)]


def queries_kernel(attn_ref, wq_ref, map_ref, fk_ref, v_ref, allow_ref,
                   q_ref, fq_ref, nd_ref, map_scr):
    tokens = attn_ref.shape[0]
    half = tokens // 2
    fill_maps(map_scr, map_ref)
    q4 = mm(attn_ref[...], wq_ref[...]).astype(BF16)
    q_ref[...] = q4
    pre = mm(q4, map_scr[...])
    ones = segment_ones(128)
    low_half = iota((tokens, 128), 1) < 64
    for h in range(4):
        lanes = slice(128 * h, 128 * h + 128)
        feat = features(pre[:, lanes], ones).astype(BF16)
        fq_ref[:, lanes] = feat
        fk = fk_ref[:, lanes]
        pair = v_ref[:, 128 * (h // 2) : 128 * (h // 2) + 128].astype(F32)
        if h % 2:
            pair = pltpu.roll(pair, 64, 1)
        wide = jnp.where(low_half, pair, 1.0).astype(BF16)
        first = nt(feat[:half], fk[:half]) * allow_ref[:half, :half]
        nd_ref[:half, lanes] = mm(first.astype(BF16), wide[:half])
        second = nt(feat[half:], fk) * allow_ref[half:, :]
        nd_ref[half:, lanes] = mm(second.astype(BF16), wide)


def plane_sum_kernel(*refs):
    *pieces, out = refs
    total = pieces[0][...]
    for piece in pieces[1:]:
        total = total + piece[...]
    out[...] = total


def scan_kernel(backward, planes, *refs):
    own = refs[:4]
    others = refs[4:-4]
    outs = refs[-4:]
    member, plane = my_seq() & 3, my_seq() >> 2
    total = jnp.zeros(own[0].shape, F32)
    for i, other in enumerate(others):
        if planes is None:
            total = total + other[...]
        else:
            there = plane + i + 1 < planes if backward else plane - i - 1 >= 0
            total = total + jnp.where(there, other[...], 0.0)
    for k, out in enumerate(outs):
        value = total
        target = member ^ k
        for i, piece in enumerate(own):
            source = member ^ i
            counts = source > target if backward else source < target
            value = value + jnp.where(counts, piece[...], 0.0)
        out[...] = value


def place_heads(scr, pieces):
    for k, piece in enumerate(pieces):
        n = piece.shape[0]
        scr[pl.ds(((my_seq() & 3) ^ k) * n, n)] = piece[...]


def mix_kernel(x_ref, nd_ref, fq_ref, c0, c1, c2, c3, contin_ref, wo_ref, gain_ref,
               mixed_ref, mf_ref, rden_ref, hidden_ref, mlp_ref, carry_scr):
    j = pl.program_id(0)
    tokens = x_ref.shape[0]
    low_half = iota((tokens, 128), 1) < 64

    @pl.when(j == 0)
    def _():
        place_heads(carry_scr, (c0, c1, c2, c3))
        hidden_ref[...] = x_ref[...].astype(F32)

    contin = contin_ref[...]
    for pair in range(2):
        quotients, inverses = [], []
        for side in range(2):
            h = 2 * pair + side
            lanes = slice(128 * h, 128 * h + 128)
            carry = carry_scr[4 * j + h]
            wide = jnp.concatenate([carry[:64], jnp.broadcast_to(carry[64:65], (64, 128))], axis=0)
            high, low = split(wide)
            fq = fq_ref[:, lanes]
            nd = nd_ref[:, lanes] + contin * (nt(fq, high) + nt(fq, low))
            inverse = 1.0 / nd
            turned = pltpu.roll(inverse, 64, 1)
            quotient = nd * turned
            if side:
                quotients.append(pltpu.roll(quotient, 64, 1))
                inverses.append(inverse)
            else:
                quotients.append(quotient)
                inverses.append(turned)
        lanes = slice(128 * pair, 128 * pair + 128)
        mf = jnp.where(low_half, *quotients)
        mf_ref[:, lanes] = mf
        mixed_ref[:, lanes] = mf.astype(BF16)
        rden_ref[:, lanes] = jnp.where(low_half, *inverses)
    hidden_ref[...] += mm(mixed_ref[...], wo_ref[...])

    @pl.when(j == pl.num_programs(0) - 1)
    def _():
        normed, _ = moments(hidden_ref[...])
        mlp_ref[...] = (normed * gain_ref[...]).astype(BF16)


GELU_A, GELU_C = 0.044715, 0.7978845608028654


def turn_kernel(kinds, x_ref, out_ref, scr):
    rows, half = out_ref.shape[2] // 16, out_ref.shape[2]
    for side in range(2):
        core = my_core() if side else 1 - my_core()
        turned = jnp.transpose(
            x_ref[:, pl.ds(pl.multiple_of(core * half, 128), half)].astype(F32)
        )
        for at, kind in enumerate(kinds):
            for g in range(16):
                place = g ^ my_seq()
                spot = 0
                for depth, bit in enumerate(ORDERS[kind]):
                    spot = spot + (((place >> bit) & 1) << (3 - depth))
                scr[pl.ds(pl.multiple_of(spot * rows, 8), rows), :] = turned[rows * g : rows * g + rows]
            out_ref[side, at] = scr[...].astype(BF16)


def act_back_kernel(cot_ref, wp_ref, ga_ref):
    ga_ref[...] = nt(cot_ref[...], wp_ref[...])


def mlp_kernel(mlp_ref, ga_ref, mlp_t, cot_t, wf_ref, act_ref, gp_ref, send_ref):
    j = pl.program_id(0)
    tokens = mlp_ref.shape[0]
    step = tokens // 4
    for r in range(4):
        rows = slice(step * r, step * r + step)
        u = mm(mlp_ref[rows, :], wf_ref[...])
        square = u * u
        t = jnp.tanh(GELU_C * (u + GELU_A * (u * square)))
        half = 0.5 * (1.0 + t)
        act_ref[rows, :] = (u * half).astype(BF16)
        slope = half + (0.5 * GELU_C) * u * (1.0 - t * t) * (1.0 + (3.0 * GELU_A) * square)
        gp_ref[rows, :] = (ga_ref[rows, :] * slope).astype(BF16)
    send_ref[0, 0] = mm(cot_t[0, j % 3], act_ref[...])
    send_ref[1, 0] = mm(mlp_t[0, (j + 1) // 2], gp_ref[...])


def mlp_out_kernel(act_ref, gp_ref, wf_ref, wp_ref, part_ref, hidden_ref, cot_ref, gain_ref,
                   out_ref, gh_ref, gh_low_ref, gg_ref, back_scr):
    j = pl.program_id(0)
    out_ref[...] = part_ref[...] + mm(act_ref[...], wp_ref[...])
    back_scr[j] = nt(gp_ref[...], wf_ref[...])

    @pl.when(j == pl.num_programs(0) - 1)
    def _():
        normed, scale = moments(hidden_ref[...])
        grad = jnp.concatenate([back_scr[i] for i in range(back_scr.shape[0])], axis=1)
        gg_ref[...] = jnp.sum(grad * normed, axis=0, keepdims=True)
        gh = cot_ref[...].astype(F32) + norm_back(grad, normed, scale, gain_ref[...])
        gh_ref[...] = gh
        gh_low_ref[...] = gh.astype(BF16)


def numer_back_kernel(gh_ref, wo_ref, mf_ref, rden_ref, fq_ref, contin_ref,
                      gn_ref, gd_ref, gd_t_ref, p0, p1, p2, p3, state_scr):
    j = pl.program_id(0)
    gm = nt(gh_ref[...], wo_ref[...]) * rden_ref[...]
    gn_ref[...] = gm.astype(BF16)
    gd = -segment_sum(gm * mf_ref[...], segment_ones(256))
    gd_ref[...] = gd
    gn_t = jnp.transpose(gm).astype(BF16)
    gd_t = jnp.transpose(gd)
    contin = contin_ref[...]
    for h in range(4):
        rows = gd_t[64 * h : 64 * h + 8]
        gd_t_ref[8 * h : 8 * h + 8, :] = rows
        kept = (fq_ref[:, 128 * h : 128 * h + 128].astype(F32) * contin).astype(BF16)
        state_scr[4 * j + h, 0:64, :] = mm(gn_t[64 * h : 64 * h + 64], kept)
        high, low = split(rows)
        both = jnp.concatenate([high.astype(F32), low.astype(F32)], axis=0).astype(BF16)
        sums = mm(both, kept)
        state_scr[4 * j + h, 64:72, :] = sums[0:8] + sums[8:16]

    @pl.when(j == pl.num_programs(0) - 1)
    def _():
        for k, piece in enumerate((p0, p1, p2, p3)):
            n = piece.shape[0]
            piece[...] = state_scr[pl.ds(((my_seq() & 3) ^ k) * n, n)]


def side_rows(state, side):
    zeros = jnp.zeros((64, 128), F32)
    rows = state[:64]
    return jnp.concatenate([zeros, rows] if side else [rows, zeros], axis=0)


def scores_back_kernel(j, q_ref, fq_ref, fk_ref, v_ref, gn_ref, gd_ref, gd_t_ref,
                       c0, c1, c2, c3, allow_ref, allow_t_ref, contin_ref, map_ref, *rest):
    gq_ref, gfk_ref, gv_ref, gmap_ref, map_scr, carry_scr, d_scr = rest[-7:]
    tokens = q_ref.shape[0]
    half = tokens // 2
    place_heads(carry_scr, (c0, c1, c2, c3))

    fill_maps(map_scr, map_ref)
    ones = segment_ones(128)
    low_half = iota((tokens, 128), 1) < 64
    contin = contin_ref[...]
    for pair in range(2):
        pair_lanes = slice(128 * pair, 128 * pair + 128)
        v_pair = v_ref[:, pair_lanes]
        gn_pair = gn_ref[:, pair_lanes].astype(F32)
        gd_pair = gd_ref[:, pair_lanes]
        gd_turned = pltpu.roll(gd_pair, 64, 1)
        gv_parts = []
        for side in range(2):
            h = 2 * pair + side
            lanes = slice(128 * h, 128 * h + 128)
            mine = ~low_half if side else low_half
            gn = jnp.where(mine, gn_pair, 0.0).astype(BF16)
            gd = jnp.where(mine, gd_pair, gd_turned)
            gd_row = gd_t_ref[8 * h : 8 * h + 1, :]
            fq, fk = fq_ref[:, lanes], fk_ref[:, lanes]
            gd_few = jnp.concatenate([gd] * (half // 128), axis=1)
            gd_many = jnp.concatenate([gd] * (tokens // 128), axis=1)
            g_top = ((nt(gn[:half], v_pair[:half]) + gd_few[:half]) * allow_ref[:half, :half]).astype(BF16)
            g_bot = ((nt(gn[half:], v_pair) + gd_many[half:]) * allow_ref[half:, :]).astype(BF16)
            carry = carry_scr[4 * j + h]
            high, low = split(side_rows(carry, side))
            inter = mm(gn, high) + mm(gn, low) + gd * carry[64:65]
            gfq = jnp.concatenate([mm(g_top, fk[:half]), mm(g_bot, fk)], axis=0) + contin * inter
            d_scr[:, lanes] = features_back(fq.astype(F32), gfq, ones).astype(BF16)

            at_top, at_bot = allow_t_ref[:half, :], allow_t_ref[half:, half:]
            gt_top = ((nt(v_pair[:half], gn) + gd_row) * at_top).astype(BF16)
            gt_bot = ((nt(v_pair[half:], gn[half:]) + gd_row[:, half:]) * at_bot).astype(BF16)
            gfk_ref[:half, lanes] = mm(gt_top, fq)
            gfk_ref[half:, lanes] = mm(gt_bot, fq[half:])
            st_top = (nt(fk[:half], fq) * at_top).astype(BF16)
            st_bot = (nt(fk[half:], fq[half:]) * at_bot).astype(BF16)
            gv_parts.append(jnp.concatenate([mm(st_top, gn), mm(st_bot, gn[half:])], axis=0))
        gv_ref[:, pair_lanes] = gv_parts[0] + gv_parts[1]
    d = d_scr[...]
    gq_ref[...] = (0.5 * nt(d, map_scr[...])).astype(BF16)
    gm = tn(q_ref[...], d)
    for h in range(4):
        gmap_ref[64 * h : 64 * h + 64, :] = gm[64 * h : 64 * h + 64, 128 * h : 128 * h + 128]


def keys_back_kernel(k_ref, fk_ref, v_ref, gfk_ref, gv_ref, u0, u1, u2, u3, tail_ref, map_ref,
                     gk_ref, gvb_ref, gmap_ref, map_scr, up_scr, d_scr):
    j = pl.program_id(0)

    @pl.when(j == 0)
    def _():
        place_heads(up_scr, (u0, u1, u2, u3))

    fill_maps(map_scr, map_ref)
    ones = segment_ones(128)
    tail = tail_ref[...]
    for pair in range(2):
        pair_lanes = slice(128 * pair, 128 * pair + 128)
        v_pair = v_ref[:, pair_lanes]
        gv = gv_ref[:, pair_lanes]
        for side in range(2):
            h = 2 * pair + side
            lanes = slice(128 * h, 128 * h + 128)
            up = up_scr[4 * j + h]
            high, low = split(side_rows(up, side))
            fk = fk_ref[:, lanes]
            key_term = mm(v_pair, high) + mm(v_pair, low) + up[64:65]
            gfk = gfk_ref[:, lanes] + tail * key_term
            gv = gv + tail * (nt(fk, high) + nt(fk, low))
            d_scr[:, lanes] = features_back(fk.astype(F32), gfk, ones).astype(BF16)
        gvb_ref[:, pair_lanes] = gv.astype(BF16)
    d = d_scr[...]
    gk_ref[...] = (0.5 * nt(d, map_scr[...])).astype(BF16)
    gm = tn(k_ref[...], d)
    for h in range(4):
        gmap_ref[64 * h : 64 * h + 64, :] = gm[64 * h : 64 * h + 64, 128 * h : 128 * h + 128]


def inputs_back_kernel(gq_ref, gk_ref, gv_ref, w_ref, x_ref, gh_ref, gain_ref, gg_mlp_ref,
                       gmq_ref, gmk_ref, gx_ref, keep_ref, send_ref, acc, pack):
    j = pl.program_id(0)

    @pl.when(j == 0)
    def _():
        acc[...] = nt(gq_ref[...], w_ref[...])
        rows = gmq_ref.shape[0]
        low_half = iota(gmq_ref.shape, 1) < 64
        pack[:rows, :] = jnp.where(low_half, gmq_ref[...], pltpu.roll(gmk_ref[...], 64, 1))
        pack[rows:, :] = jnp.zeros((pack.shape[0] - rows, 128), F32)

    @pl.when(j == 1)
    def _():
        acc[...] += nt(gk_ref[...], w_ref[...])

    @pl.when(j == 2)
    def _():
        grad = acc[...] + nt(gv_ref[...], w_ref[...])
        normed, scale = moments(x_ref[...].astype(F32))
        gx_ref[...] = gh_ref[...] + norm_back(grad, normed, scale, gain_ref[...])
        gg = jnp.sum(grad * normed, axis=0, keepdims=True)
        rows = gmq_ref.shape[0]
        n = gg.shape[1] // 128
        for i in range(n):
            pack[rows + i : rows + i + 1, :] = gg[:, 128 * i : 128 * i + 128]
            pack[rows + n + i : rows + n + i + 1, :] = gg_mlp_ref[:, 128 * i : 128 * i + 128]
        for out, core in ((keep_ref, my_core()), (send_ref, 1 - my_core())):
            for c in range(n):
                start = core * (n * SMALL_ROWS) + c * SMALL_ROWS
                out[:, 128 * c : 128 * c + 128] = pack[pl.ds(pl.multiple_of(start, 8), SMALL_ROWS), :]


def unpack_kernel(kept_ref, got_ref, other_ref, gmq_ref, gmk_ref, gains_ref, pack):
    n = kept_ref.shape[1] // 128
    for value, core in ((kept_ref[...], my_core()), (other_ref[...], 1 - my_core())):
        for c in range(n):
            start = core * (n * SMALL_ROWS) + c * SMALL_ROWS
            pack[pl.ds(pl.multiple_of(start, 8), SMALL_ROWS), :] = value[:, 128 * c : 128 * c + 128]
    heads = gmq_ref.shape[0]
    for h in range(heads):
        both = pack[64 * h : 64 * h + 64, :]
        gmq_ref[h] = both[:, :64]
        gmk_ref[h] = both[:, 64:]
    gains_ref[...] = pack[64 * heads : 64 * heads + 16, :]


ORDERS = ((0, 1, 2, 3), (1, 2, 0, 3), (2, 0, 1, 3))


def send_kernel(kinds, x_ref, *refs):
    out_ref = refs[-1]
    for i, kind in enumerate(kinds):
        out_ref[i] = mm(x_ref[0, kind], refs[i][...])


def wave_kernel(plan, *refs):
    i = pl.program_id(0)

    @pl.when(i == 0)
    def _():
        for kept, got, at, count, send, base, keep in plan["folds"]:
            rows = refs[kept].shape[0] // count
            half = rows // 2
            for p in range(count):
                total = (refs[kept][rows * p : rows * p + rows, :]
                         + refs[got][at + rows * p : at + rows * p + rows, :])
                refs[send][base + half * p : base + half * p + half, :] = total[half:]
                refs[keep][half * p : half * p + half, :] = total[:half]
        for kept, got, at, out, block in plan["ends"]:
            rows, width = refs[out].shape[0], refs[kept].shape[1]
            first, piece = block
            refs[out][:, width * first : width * first + width] = (
                refs[kept][rows * piece : rows * piece + rows, :]
                + refs[got][at + rows * piece : at + rows * piece + rows, :]
            )
        for kept, got, at, send, base, keep in plan["smalls"]:
            rows = refs[kept].shape[0]
            total = refs[kept][...] + refs[got][at : at + rows, :]
            refs[keep][...] = total
            if send is not None:
                refs[send][base : base + rows, :] = total

    for step, (x, entry, y, r, send, base, keep, at) in enumerate(plan["joins"]):

        @pl.when(i == step)
        def _():
            value = mm(refs[x][1, entry], refs[y][...]) + refs[r][0]
            half = value.shape[0] // 2
            refs[send][base : base + half, :] = value[half:]
            refs[keep][at : at + half, :] = value[:half]


def core_hop(v):
    return lax.ppermute(v, "batch", [(0, 1), (1, 0)])


def local(inputs, w_qkv, w_out, w_fc, w_proj, map_query, map_key, gain_attn, gain_mlp,
          starts, key_mask, cotangent):
    T, D = inputs.shape[1], inputs.shape[2]
    H = map_query.shape[0]
    FF = w_fc.shape[1]
    n_seq = lax.axis_size("seq")
    planes = n_seq // 4
    quads = H // 4
    QW, FW = 4 * 64, 4 * 128
    half_rows = D // 2
    per = H // 4
    seq = lax.axis_index("seq")
    tok = None
    x, cot = inputs[0], cotangent[0]
    gain_a, gain_m = gain_attn.reshape(1, D), gain_mlp.reshape(1, D)
    direct = n_seq == 16

    def hop(v, bit):
        return lax.ppermute(v, "seq", [(i, i ^ (1 << bit)) for i in range(n_seq)])

    def to_member(v, k):
        return lax.ppermute(v, "seq", [(i, i ^ k) for i in range(n_seq)])

    def shift(v, by):
        return lax.ppermute(v, "seq", [(i, (i + by) % n_seq) for i in range(n_seq)])

    qcol = pl.BlockSpec((T, QW), lambda j: (0, j))
    fcol = pl.BlockSpec((T, FW), lambda j: (0, j))
    col128 = whole((T, 128))
    square = whole((T, T))
    full = whole((T, D))
    row = whole((1, D))
    maps = pl.BlockSpec((4, 64, 64), lambda j: (j, 0, 0))
    piece = (per, STATE_ROWS, 128)
    piece_spec = whole(piece)
    map_scr = pltpu.VMEM((QW, FW), BF16)
    state_scr = pltpu.VMEM((H, STATE_ROWS, 128), F32)

    def w_cols(part):
        return pl.BlockSpec((D, QW), lambda j: (0, part * quads + j))

    (attn, k, v, fk, s0, s1, s2, s3, allow, allow_t, tail, contin), tok = run(
        keys_kernel, tok, (quads,),
        [(Held(x), full), (gain_a, row), (Held(w_qkv), w_cols(1)), (Held(w_qkv), w_cols(2)), (Held(map_key), maps),
         (Held(key_mask), whole((1, T))), (starts, pl.BlockSpec(memory_space=pltpu.SMEM))],
        [((T, D), BF16, full), ((T, D), BF16, qcol), ((T, D), BF16, qcol), ((T, 2 * D), BF16, fcol)]
        + [(piece, F32, piece_spec)] * 4
        + [((T, T), F32, square)] * 2 + [((T, 128), F32, col128)] * 2,
        [map_scr, state_scr], us=8.0)

    def plane_exchange(pieces):
        return [pieces[0]] + [to_member(pieces[k], k) for k in range(1, 4)]

    def plane_total(own, tok):
        (total,), tok = run(
            plane_sum_kernel, tok, (1,), [(p, piece_spec) for p in own], [(piece, F32, piece_spec)])
        return total, tok

    def across(total, backward):
        if planes <= 4:
            return [shift(total, (-4 if backward else 4) * i) for i in range(1, planes)]
        every = lax.all_gather(total, "seq").reshape((planes, 4) + piece)
        mine = lax.dynamic_index_in_dim(every, seq & 3, 1, keepdims=False)
        place = jnp.arange(planes)
        want = place > (seq >> 2) if backward else place < (seq >> 2)
        return [jnp.sum(jnp.where(want[:, None, None, None], mine, 0.0), axis=0)]

    def scanned(own, others, backward, tok):
        return run(
            functools.partial(scan_kernel, backward, planes if planes <= 4 else None), tok, (1,),
            [(p, piece_spec) for p in own + others], [(piece, F32, piece_spec)] * 4)

    def turn(x, kinds, tok):
        shape = (2, len(kinds), half_rows, T)
        if not direct:
            return jnp.zeros(shape, BF16), tok
        (out,), tok = run(
            functools.partial(turn_kernel, kinds), tok, (1,), [(x, full)], [(shape, BF16, whole(shape))],
            [pltpu.VMEM((half_rows, T), F32)])
        return out, tok

    own = plane_exchange([s0, s1, s2, s3])

    (q, fq, nd), tok = run(
        queries_kernel, tok, (quads,),
        [(attn, full), (w_qkv, w_cols(0)), (map_query, maps), (fk, fcol), (v, qcol), (allow, square)],
        [((T, D), BF16, qcol), ((T, 2 * D), BF16, fcol), ((T, 2 * D), F32, fcol)],
        [map_scr], us=9.0)
    total, tok = plane_total(own, tok)
    others = across(total, False)
    (ga,), tok = run(
        act_back_kernel, tok, (FF // D,), [(cot, full), (w_proj, pl.BlockSpec((D, D), lambda j: (j, 0)))],
        [((T, FF), F32, columns(T, D), True)], us=4.0)
    carried, tok = scanned(own, others, False, tok)
    carry = plane_exchange(carried)
    cot_t, tok = turn(cot, (0, 1, 2), tok)
    attn_t, tok = turn(attn, (0, 1, 2), tok)

    (mixed, mf, rden, hidden, mlp_in), tok = run(
        mix_kernel, tok, (quads,),
        [(x, full), (nd, fcol), (fq, fcol)] + [(c, piece_spec) for c in carry]
        + [(contin, col128), (w_out, pl.BlockSpec((QW, D), lambda j: (j, 0))), (gain_m, row)],
        [((T, D), BF16, qcol), ((T, D), F32, qcol), ((T, D), F32, qcol), ((T, D), F32, full),
         ((T, D), BF16, full)],
        [state_scr], us=4.5)
    mlp_t, tok = turn(mlp_in, (0, 1, 2), tok)

    n_ff = FF // D
    turned_spec = whole((2, 3, half_rows, T))
    send_shape = (2, n_ff, half_rows, D)
    (act, gp, send_mlp), tok = run(
        mlp_kernel, tok, (n_ff,),
        [(mlp_in, full), (ga, columns(T, D)), (mlp_t, turned_spec), (cot_t, turned_spec), (w_fc, columns(D, D))],
        [((T, FF), BF16, columns(T, D))] * 2
        + [(send_shape, F32, pl.BlockSpec((2, 1, half_rows, D), lambda j: (0, j, 0, 0)))], us=10.0)
    if direct:
        recv_mlp = core_hop(send_mlp).reshape(2 * n_ff, half_rows, D)
    (output, gh, gh_low, gg_mlp), tok = run(
        mlp_out_kernel, tok, (quads,),
        [(act, whole((T, FF))), (gp, whole((T, FF))), (w_fc, pl.BlockSpec((QW, FF), lambda j: (j, 0))),
         (w_proj, columns(FF, QW)), (hidden, qcol), (hidden, full), (cot, full), (gain_m, row)],
        [((T, D), F32, qcol), ((T, D), F32, full), ((T, D), BF16, full), ((1, D), F32, row)],
        [pltpu.VMEM((quads, T, QW), F32)], us=8.0)
    def send_half(x_t, kinds, ys, tok):
        shape = (len(kinds), half_rows, D)
        (out,), tok = run(
            functools.partial(send_kernel, kinds), tok, (1,),
            [(x_t, whole(x_t.shape))] + [(y, full) for y in ys], [(shape, F32, whole(shape))], us=30.0)
        return core_hop(out), tok

    class Group:
        def __init__(self, counts, layout, widths):
            self.counts, self.layout, self.widths = counts, layout, widths
            self.stage, self.small = -1, None

    def wave(folds, join, tok, us=30.0):
        ins, outs, sends = [], [], {}
        plan = {"folds": [], "ends": [], "smalls": [], "joins": []}
        after = []

        def take(array, spec=None):
            for n, (other, other_spec) in enumerate(ins):
                if other is array and spec is None:
                    return n
            ins.append((array, spec or whole(array.shape)))
            return len(ins) - 1

        def place(bit, rows):
            base = sends.get(bit, 0)
            sends[bit] = base + rows
            return base

        def give(shape, put, not_last=True):
            outs.append((shape, F32, whole(shape), not_last and Near))
            after.append((len(outs) - 1, put))
            return ("out", len(outs) - 1)

        steps = 1
        for g in folds:
            g.stage += 1
            if g.stage == 4:
                rows = half_rows // 16
                g.result = [None] * len(g.widths)
                made = []
                for n, width in enumerate(g.widths):
                    def put(array, n=n, g=g):
                        g.result[n] = array
                    made.append(give((rows, width), put, False))
                n = 0
                for kind in range(3):
                    if g.counts[kind] == 0:
                        continue
                    got, at = g.got[kind]
                    for p in range(g.counts[kind]):
                        out, block = g.layout[n]
                        plan["ends"].append((take(g.keeps[kind]), take(got), at, made[out], (block, p)))
                        n += 1
            else:
                old_keeps, g.keeps = g.keeps, [None] * 3
                old_got, g.got = g.got, [None] * 3
                for kind in range(3):
                    if g.counts[kind] == 0:
                        continue
                    bit = ORDERS[kind][g.stage]
                    rows = old_keeps[kind].shape[0] // 2
                    base = place(bit, rows)
                    def put(array, kind=kind, g=g):
                        g.keeps[kind] = array
                    keep = give((rows, D), put)
                    got, at = old_got[kind]
                    plan["folds"].append(
                        (take(old_keeps[kind]), take(got), at, g.counts[kind], ("send", bit), base, keep))
                    g.got[kind] = (bit, base)
            if g.small is not None:
                got, at = g.small_got
                bit = ORDERS[0][g.stage] if g.stage < 4 else None
                base = place(bit, SMALL_ROWS) if g.stage < 4 else 0
                def put(array, g=g):
                    g.small = array
                keep = give(small_shape, put)
                plan["smalls"].append(
                    (take(g.small), take(got), at, ("send", bit) if g.stage < 4 else None, base, keep))
                g.small_got = (bit, base)
        if join is not None:
            g, xs, ys, segments, small = join
            g.stage = 0
            g.keeps, g.got, offset = [None] * 3, [None] * 3, [0, 0, 0]
            at_x = [take(x) for x in xs]
            at_y, at_r = [], []
            for n, (y, r, block, y_block) in enumerate(ys):
                mine = [i for i, seg in enumerate(segments) if seg[2] == n]
                first, count = mine[0], len(mine)
                at_y.append(take(y, pl.BlockSpec(
                    (T, D), lambda i, first=first, count=count, block=y_block:
                    (0, block + jnp.clip(i - first, 0, count - 1)))))
                at_r.append(take(r, pl.BlockSpec(
                    (1, half_rows, D), lambda i, first=first, count=count, block=block:
                    (block + jnp.clip(i - first, 0, count - 1), 0, 0))))
            half = half_rows // 2
            for kind in range(3):
                if g.counts[kind] == 0:
                    continue
                bit = ORDERS[kind][0]
                g.got[kind] = (bit, place(bit, half * g.counts[kind]))
                def put(array, kind=kind, g=g):
                    g.keeps[kind] = array
                g.keeps[kind] = give((half * g.counts[kind], D), put)
            for x, entry, y, kind in segments:
                bit, base = g.got[kind]
                plan["joins"].append(
                    (at_x[x], entry, at_y[y], at_r[y], ("send", bit), base + offset[kind], g.keeps[kind], offset[kind]))
                offset[kind] += half
            steps = len(segments)
            if small is not None:
                bit = ORDERS[0][0]
                base = place(bit, SMALL_ROWS)
                def put(array, g=g):
                    g.small = array
                keep = give(small_shape, put)
                plan["smalls"].append((take(small[0]), take(small[1]), 0, ("send", bit), base, keep))
                g.small, g.small_got = True, (bit, base)
        first_send = len(outs)
        bits = sorted(sends)
        for bit in bits:
            outs.append(((sends[bit], D), F32, whole((sends[bit], D)), Near))
        n_in = len(ins)

        def ref(item):
            if isinstance(item, tuple) and item[0] == "out":
                return n_in + item[1]
            if isinstance(item, tuple) and item[0] == "send":
                return n_in + first_send + bits.index(item[1])
            return item

        plan = {name: tuple(tuple(ref(x) for x in entry) for entry in entries) for name, entries in plan.items()}
        results, tok = run(functools.partial(wave_kernel, plan), tok, (steps,), ins, outs, us=us, extra=9)
        for n, put in after:
            put(results[n])
        moved = {bit: Near(hop(results[first_send + n].array, bit)) for n, bit in enumerate(bits)}
        for g in folds + ([join[0]] if join else []):
            if g.stage < 4:
                g.got = [item and (moved[item[0]], item[1]) for item in g.got]
                if g.small is not None:
                    g.small_got = (moved[g.small_got[0]], g.small_got[1])
        return tok

    small_shape = (SMALL_ROWS, D)
    early = Group((1, 1, 1), [(0, i) for i in range(3)], (3 * D,))
    main = Group((2, 2, 1), [(0, 0)] + [(1, i) for i in range(n_ff)], (D, FF))
    wide = Group((0, 0, 1), [(0, 0)], (D,))
    last = Group((1, 1, 1), [(0, i) for i in range(3)], (3 * D,))
    if direct:
        tok = wave([], (early, [cot_t], [(act, recv_mlp, 0, 0)], [(0, kind, 0, kind) for kind in range(3)], None), tok, 4.0)

    (gn, gd, gd_t, s0, s1, s2, s3), tok = run(
        numer_back_kernel, tok, (quads,),
        [(gh_low, full), (w_out, pl.BlockSpec((QW, D), lambda j: (j, 0))), (mf, qcol), (rden, qcol),
         (fq, fcol), (contin, col128)],
        [((T, D), BF16, qcol), ((T, D), F32, qcol),
         ((8 * H, T), F32, pl.BlockSpec((32, T), lambda j: (j, 0)))] + [(piece, F32, piece_spec)] * 4,
        [state_scr], us=5.0)
    own = plane_exchange([s0, s1, s2, s3])
    if direct:
        tok = wave(
            [early],
            (main, [cot_t, mlp_t], [(act, recv_mlp, n_ff - 1, n_ff - 1), (gp, recv_mlp, n_ff, 0)],
             [(0, 0, 0, 0)] + [(1, kind, 1, kind) for kind in (0, 1, 1, 2)], None), tok, 7.0)
    total, tok = plane_total(own, tok)
    others = across(total, True)

    def fixed(shape, quad):
        return pl.BlockSpec(shape, lambda i: (0, quad))

    def fixed_rows(shape, quad):
        return pl.BlockSpec(shape, lambda i: (quad,) + (0,) * (len(shape) - 1))

    def scores_back(quad, before, tok):
        ins = [(q, fixed((T, QW), quad)), (fq, fixed((T, FW), quad)), (fk, fixed((T, FW), quad)),
               (v, fixed((T, QW), quad)), (gn, fixed((T, QW), quad)), (gd, fixed((T, QW), quad)),
               (gd_t, fixed_rows((32, T), quad))] + [(c, piece_spec) for c in carry]
        ins += [(allow, square), (allow_t, square), (contin, col128), (map_query, fixed_rows((4, 64, 64), quad))]
        aliases = {len(ins) + i: i for i in range(4)} if before else None
        ins += [(a, ANYWHERE) for a in before]
        return run(
            functools.partial(scores_back_kernel, quad), tok, (1,), ins,
            [((T, D), BF16, fixed((T, QW), quad)), ((T, 2 * D), F32, fixed((T, FW), quad)),
             ((T, D), F32, fixed((T, QW), quad)), ((D, 128), F32, fixed_rows((QW, 128), quad))],
            [map_scr, state_scr, pltpu.VMEM((T, FW), BF16)], extra=12, aliases=aliases, us=4.5)

    backs, tok = scores_back(0, [], tok)
    backs, tok = scores_back(1, backs, tok)
    backs, tok = scores_back(2, backs, tok)
    gq, gfk, gv_f, gmq = backs
    carried, tok = scanned(own, others, True, tok)
    upstream = plane_exchange(carried)
    if direct:
        mixed_t, tok = turn(mixed, (2,), tok)
        recv_out, tok = send_half(mixed_t, (0,), [gh_low], tok)
        tok = wave(
            [early, main], (wide, [mixed_t], [(gh_low, recv_out, 0, 0)], [(0, 0, 0, 2)], None), tok, 2.0)

    (gk, gv, gmk), tok = run(
        keys_back_kernel, tok, (quads,),
        [(k, qcol), (fk, fcol), (v, qcol), (gfk, fcol), (gv_f, qcol)] + [(c, piece_spec) for c in upstream]
        + [(tail, col128), (map_key, maps)],
        [((T, D), BF16, qcol), ((T, D), BF16, qcol),
         ((D, 128), F32, pl.BlockSpec((QW, 128), lambda j: (j, 0)))],
        [map_scr, state_scr, pltpu.VMEM((T, FW), BF16)], us=60.0)
    if direct:
        recv_qkv, tok = send_half(attn_t, (0, 1, 2), [gq, gk, gv], tok)

    small_spec = whole(small_shape)
    packed = 2 * SMALL_ROWS * (D // 128)
    (gx, keep, send), tok = run(
        inputs_back_kernel, tok, (3,),
        [(gq, full), (gk, full), (gv, full), (w_qkv, columns(D, D)), (x, full), (gh, full), (gain_a, row),
         (gg_mlp, row), (gmq, whole((D, 128))), (gmk, whole((D, 128)))],
        [((T, D), F32, full)] + [(small_shape, F32, small_spec)] * 2,
        [pltpu.VMEM((T, D), F32), pltpu.VMEM((packed, 128), F32)], us=60.0)

    got = core_hop(send)
    if direct:
        tok = wave(
            [], (last, [attn_t], [(gq, recv_qkv, 0, 0), (gk, recv_qkv, 1, 0), (gv, recv_qkv, 2, 0)],
                 [(0, kind, kind, kind) for kind in range(3)], (keep, got)), tok, 4.0)
        tok = wave([early, main, wide], None, tok)
        tok = wave([last], None, tok)
        tok = wave([early, main, wide], None, tok)
        tok = wave([last], None, tok)
        tok = wave([main, wide], None, tok)
        tok = wave([last], None, tok)
        tok = wave([wide], None, tok)
        tok = wave([last], None, tok)
        mine = last.small.array
        got = core_hop(mine)
        (grad_w_qkv,) = last.result
        proj_last, grad_w_fc = main.result
        (grad_w_out,) = wide.result
        grad_proj_rows = jnp.concatenate([early.result[0], proj_last], axis=1)
    else:
        mine = lax.psum(keep + got, "seq")
        got = core_hop(mine)
        summed = lax.psum_scatter(
            jnp.concatenate(
                [tn(attn, gq), tn(attn, gk), tn(attn, gv), tn(mixed, gh_low), tn(mlp_in, gp), tn(cot, act)],
                axis=1,
            ),
            ("batch", "seq"), scatter_dimension=0, tiled=True)
        grad_w_qkv = summed[:, : 3 * D]
        grad_w_out = summed[:, 3 * D : 4 * D]
        grad_w_fc = summed[:, 4 * D : 4 * D + FF]
        grad_proj_rows = summed[:, 4 * D + FF :]

    heads_shape = (H, 64, 64)
    (grad_map_query, grad_map_key, gains), tok = run(
        unpack_kernel, tok, (1,), [(mine, small_spec), (mine, small_spec), (got, small_spec)],
        [(heads_shape, F32, whole(heads_shape))] * 2 + [((16, 128), F32, whole((16, 128)))],
        [pltpu.VMEM((packed, 128), F32)])
    n = D // 128
    return (
        output[None],
        gx[None],
        grad_w_qkv,
        grad_w_out,
        grad_w_fc,
        grad_proj_rows.T,
        grad_map_query,
        grad_map_key,
        gains[:n].reshape(D),
        gains[n : 2 * n].reshape(D),
    )


def solution(mesh):
    tokens = P("batch", "seq", None)
    flags = P("batch", "seq")
    rows = P(("batch", "seq"), None)
    return jax.shard_map(
        local,
        mesh=mesh,
        in_specs=(tokens,) + (P(),) * 8 + (flags, flags, tokens),
        out_specs=(tokens, tokens, rows, rows, rows, P(None, ("batch", "seq")), P(), P(), P(), P()),
        check_vma=False,
    )
```

time: 379 us -> 269 us (0.71)
  Pallas kernels: 163 us -> 93.9 us
  starting transfers between devices: 108 us -> 48.3 us
  waiting for transfers between devices: 76.2 us -> 98.6 us
    pallas_call x53 -> x35, Pallas kernels: 163 us -> 93.9 us  [run(): pl.pallas_call(body, grid=grid, in_specs=[spec for _, spec in ins] + [ANY...]
    ppermute x64 -> x26, starting transfers between devices: 79.9 us -> 21.1 us  [hop(): return lax.ppermute(v, 'seq', [(i, i ^ 1 << bit) for i in range(n_seq)])]
    ppermute x64 -> x26, waiting for transfers between devices: 42.5 us -> 90.4 us  [hop(): return lax.ppermute(v, 'seq', [(i, i ^ 1 << bit) for i in range(n_seq)])]
    ppermute x12, waiting for transfers between devices: 19.8 us -> 4.33 us  [to_member(): return lax.ppermute(v, 'seq', [(i, i ^ k) for i in range(n_seq)])]
    ppermute x6, waiting for transfers between devices: 13.9 us -> 3.06 us  [shift(): return lax.ppermute(v, 'seq', [(i, (i + by) % n_seq) for i in range(n_seq)])]
    unnamed x146 -> x120, local copies, waits for them, and re-layouts: 21.3 us -> 19.9 us
  transfers between devices with their start and end apart: 90 -> 49, of which waited for: 29 -> 17; matrix products, arithmetic and copies ran while one was open for 0% -> 0% of each run, Pallas kernels for 33% -> 24%
where the time goes in v2:
time: 269 us; the launch traced here: 264 us
  waiting for transfers between devices  98.6 us (37%)
  Pallas kernels  93.9 us (35%)
  starting transfers between devices  48.3 us (18%)
  local copies, waits for them, and re-layouts  21.2 us (8%)
    pallas_call x35, Pallas kernels, run(): pl.pallas_call(body, grid=grid, in_specs=[spec for _, spec in ins] + [ANY...  93.9 us
    ppermute x26, waiting for transfers between devices, hop(): return lax.ppermute(v, 'seq', [(i, i ^ 1 << bit) for i in range(n_seq)])  90.4 us
    ppermute x26, starting transfers between devices, hop(): return lax.ppermute(v, 'seq', [(i, i ^ 1 << bit) for i in range(n_seq)])  21.1 us
    unnamed x120, local copies, waits for them, and re-layouts  19.9 us
    ppermute x12, starting transfers between devices, to_member(): return lax.ppermute(v, 'seq', [(i, i ^ k) for i in range(n_seq)])  16.5 us
    ppermute x6, starting transfers between devices, shift(): return lax.ppermute(v, 'seq', [(i, (i + by) % n_seq) for i in range(n_seq)])  10.6 us
  transfers between devices with their start and end apart: 49, of which 17 were waited for; matrix products, arithmetic and copies ran while one was open for 0% of the time, Pallas kernels for 24%

profile of v2, /device:TPU:0, one launch (start us, length us, event | category | flops | bytes accessed | tf_op | source)
XLA Modules:
  0.0 264.3 jit_solution(14504552758325232302)
XLA Ops:
  2.0 9.3 %shard_map.195 = (bf16[512,768]{1,0:T(8,128)(2,1)S(1)}, bf16[512,768]{1,0:T(8,128)(2,1)S(1)}, bf16[512,768]{1,0:T(8,128)(2,1)S(1)}, bf16[512,1536]{1,0:T(8,128)(...) custom-call(bf16[512,768]{1,0:T(8,128)(2,1)} %bitcast.21, ...), custom_call_target="tpu_custom_call" | custom-call | flops 9200000000 | tf_op jit(solution)/shard_map/pallas_call | solution.py:146
  12.1 3.0 %collective-permute-start = (f32[3,72,128]{2,1,0:T(8,128)S(1)}, f32[3,72,128]{2,1,0:T(8,128)S(1)}, u32[]{:S(2)}, u32[]{:S(2)}) collective-permute-start(f32[3,72,128]{2,1,0:T(8,128)S(1)} %get-tuple-element.200), channel_id=1, source_target_pairs={{0,1},{1,0},{2,3},{3,2},{4,5},{5,4},{6,7},{7,6},{8,9},{9,8},{10,11... | collective-permute-start | bytes 331784 | tf_op jit(solution)/shard_map/ppermute | solution.py:623
  15.1 1.5 collective-permute-start.1
  16.7 8.9 %shard_map.196 = (bf16[512,768]{1,0:T(8,128)(2,1)S(1)}, bf16[512,1536]{1,0:T(8,128)(2,1)S(1)}, f32[512,1536]{1,0:T(8,128)S(1)}, f32[8,128]{1,0:T(8,128)S(1)}) custom-call(bf16[512,768]{1,0:T(8,128)(2,1)S(1)} %get-tuple-element.192.refs_0_, bf16[768,2304]{1,0:T(8,128)(2,1)S(1)} %copy-done.10, bf16[12,64,64]{2,1,0:T(8,128)(2,1)S(1)} %copy-done.17, ...), custom_call_target="tpu_custom_call" | custom-call | flops 10350000128 | tf_op jit(solution)/shard_map/pallas_call | solution.py:146
  26.5 4.1 %collective-permute-start.5 = (f32[3,72,128]{2,1,0:T(8,128)S(1)}, f32[3,72,128]{2,1,0:T(8,128)S(1)}, u32[]{:S(2)}, u32[]{:S(2)}) collective-permute-start(f32[3,72,128]{2,1,0:T(8,128)S(1)} %get-tuple-element.204), channel_id=1, source_target_pairs={{0,12},{1,13},{2,14},{3,15},{4,0},{5,1},{6,2},{7,3},{8,4},{9,5},{1... | collective-permute-start | bytes 331784 | tf_op jit(solution)/shard_map/ppermute | solution.py:626
  30.5 1.2 collective-permute-start.3
  31.7 5.0 %shard_map.198 = (f32[512,3072]{1,0:T(8,128)}, f32[8,128]{1,0:T(8,128)S(1)}) custom-call(bf16[512,768]{1,0:T(8,128)(2,1)S(1)} %bitcast.18, bf16[3072,768]{1,0:T(8,128)(2,1)S(1)} %bitcast.15, f32[8,128]{1,0:T(8,128)S(1)} %get-tuple-element.205.refs_2_), custom_call_target="tpu_custom_call" | custom-call | flops 4600000000 | tf_op jit(solution)/shard_map/pallas_call | solution.py:146
  36.8 3.0 %collective-permute-done.4.refs_5_ = f32[3,72,128]{2,1,0:T(8,128)S(1)} collective-permute-done((f32[3,72,128]{2,1,0:T(8,128)S(1)}, f32[3,72,128]{2,1,0:T(8,128)S(1)}, u32[]{:S(2)}, u32[]{:S(2)}) %collective-permute-start.4) | collective-permute-done | bytes 110624 | tf_op jit(solution)/shard_map/ppermute | solution.py:626
  40.0 1.6 collective-permute-start.6
  41.5 1.5 collective-permute-start.7
  45.1 1.4 copy-done.22
  47.4 1.2 collective-permute-done.8.refs_6_.refs_10_
  48.7 4.6 %shard_map.202 = (bf16[512,768]{1,0:T(8,128)(2,1)S(1)}, f32[512,768]{1,0:T(8,128)S(1)}, f32[512,768]{1,0:T(8,128)S(1)}, f32[512,768]{1,0:T(8,128)S(1)}, bf16[512...) custom-call(bf16[512,768]{1,0:T(8,128)(2,1)S(1)} %bitcast.22, f32[512,1536]{1,0:T(8,128)S(1)} %get-tuple-element.197.refs_1_, ...), custom_call_target="tpu_custom_call" | custom-call | flops 5175000064 | tf_op jit(solution)/shard_map/pallas_call | solution.py:146
  53.3 1.1 copy-done.47
  56.3 12.3 %shard_map.204 = (bf16[512,3072]{1,0:T(8,128)(2,1)S(1)}, bf16[512,3072]{1,0:T(8,128)(2,1)S(1)}, f32[2,4,384,768]{3,2,1,0:T(8,128)}, f32[8,128]{1,0:T(8,128)S(1)}) custom-call(bf16[512,768]{1,0:T(8,128)(2,1)S(1)} %get-tuple-element.215.refs_0_, f32[512,3072]{1,0:T(8,128)} %get-tuple-element.216.refs_1_, ...), custom_call_target="tpu_custom_call" | custom-call | flops 11500000256 | tf_op jit(solution)/shard_map/pallas_call | solution.py:146
  68.7 3.5 %copy-done.8 = bf16[3072,768]{1,0:T(8,128)(2,1)S(1)} copy-done((bf16[3072,768]{1,0:T(8,128)(2,1)S(1)}, bf16[3072,768]{1,0:T(8,128)(2,1)}, u32[]{:S(2)}) %copy-start.8) | copy-done | bytes 4718616
  72.1 2.3 copy-done.9
  74.5 1.1 copy-done.14
  75.6 1.4 copy-done.48
  77.0 7.8 %shard_map.205 = (f32[512,768]{1,0:T(8,128)}, f32[512,768]{1,0:T(8,128)S(1)}, bf16[512,768]{1,0:T(8,128)(2,1)S(1)}, f32[1,768]{1,0:T(1,128)S(1)}, f32[8,128]{1,0:T(8,128)S(1)}) custom-call(bf16[512,3072]{1,0:T(8,128)(2,1)S(1)} %get-tuple-element.221.refs_0_.refs_1_.refs_8_, bf16[512,3072]{1,0:T(8,128)(2,1)S(1)} %get-tuple-element.222.refs_1_.refs_10_, ...), custom_call_target="tpu_custom_call" | custom-call | flops 9200000000 | tf_op jit(solution)/shard_map/pallas_call | solution.py:146
  84.8 1.1 copy-done.49
  86.0 1.7 shard_map.206
  89.3 4.1 %shard_map.207 = (bf16[512,768]{1,0:T(8,128)(2,1)S(1)}, f32[512,768]{1,0:T(8,128)S(1)}, f32[96,512]{1,0:T(8,128)S(1)}, f32[3,72,128]{2,1,0:T(8,128)S(1)}, f32[3,...) custom-call(bf16[512,768]{1,0:T(8,128)(2,1)S(1)} %get-tuple-element.227.refs_, ...), custom_call_target="tpu_custom_call" | custom-call | flops 5750000128 | tf_op jit(solution)/shard_map/pallas_call | solution.py:146
  93.4 1.7 collective-permute-start.10
  95.1 1.0 collective-permute-start.11
  96.1 7.4 %collective-permute-done.13.refs_1_ = f32[192,768]{1,0:T(8,128)S(1)} collective-permute-done((f32[192,768]{1,0:T(8,128)S(1)}, f32[192,768]{1,0:T(8,128)S(1)}, u32[]{:S(2)}, u32[]{:S(2)}) %collective-permute-start.13) | collective-permute-done | bytes 589856 | tf_op jit(solution)/shard_map/ppermute | solution.py:620
  104.5 3.1 %shard_map.208 = (f32[96,768]{1,0:T(8,128)S(1)}, f32[96,768]{1,0:T(8,128)S(1)}, f32[96,768]{1,0:T(8,128)S(1)}, f32[384,768]{1,0:T(8,128)S(1)}, f32[384,768]{1,0:...) custom-call(f32[192,768]{1,0:T(8,128)S(1)} %get-tuple-element.241.re, ...), custom_call_target="tpu_custom_call" | custom-call | flops 8049999872 | tf_op jit(solution)/shard_map/pallas_call | solution.py:146
  107.6 1.6 collective-permute-done.12.refs_3_
  109.4 2.0 collective-permute-start.17
  111.4 3.2 %collective-permute-start.16 = (f32[3,72,128]{2,1,0:T(8,128)S(1)}, f32[3,72,128]{2,1,0:T(8,128)S(1)}, u32[]{:S(2)}, u32[]{:S(2)}) collective-permute-start(f32[3,72,128]{2,1,0:T(8,128)S(1)} %get-tuple-element.264), channel_id=1, source_target_pairs={{0,12},{1,13},{2,14},{3,15},{4,0},{5,1},{6,2},{7,3},{8,4},{9,5},{1... | collective-permute-start | bytes 331784 | tf_op jit(solution)/shard_map/ppermute | solution.py:626
  114.6 1.0 collective-permute-start.22
  116.1 1.2 copy-done.32
  117.3 4.2 %shard_map.210 = (bf16[512,768]{1,0:T(8,128)(2,1)S(1)}, f32[512,1536]{1,0:T(8,128)S(1)}, f32[512,768]{1,0:T(8,128)S(1)}, f32[768,128]{1,0:T(8,128)S(1)}, f32[8,128]{1,0:T(8,128)S(1)}) custom-call(bf16[512,768]{1,0:T(8,128)(2,1)S(1)} %copy-done.36, bf16[512,1536]{1,0:T(8,128)(2,1)S(1)} %copy-done.28, bf16[512,1536]{1,0:T(8,128)(2,1)S(1)} %copy-done.25, ...), custom_call_target="tpu_custom_call" | custom-call | flops 5175000064 | tf_op jit(solution)/shard_map/pallas_call | solution.py:146
  121.5 4.2 %shard_map.211 = (bf16[512,768]{1,0:T(8,128)(2,1)S(1)}, f32[512,1536]{1,0:T(8,128)S(1)}, f32[512,768]{1,0:T(8,128)S(1)}, f32[768,128]{1,0:T(8,128)S(1)}, f32[8,128]{1,0:T(8,128)S(1)}) custom-call(bf16[512,768]{1,0:T(8,128)(2,1)S(1)} %copy-done.36, ...), custom_call_target="tpu_custom_call", output_to_operand_aliasing={{0}: (15, {}), {1}: (16, {}), {2}: (17, {}), {3}: (18, {})} | custom-call | flops 5175000064 | tf_op jit(solution)/shard_map/pallas_call | solution.py:146
  125.8 4.4 %shard_map.212 = (bf16[512,768]{1,0:T(8,128)(2,1)S(1)}, f32[512,1536]{1,0:T(8,128)S(1)}, f32[512,768]{1,0:T(8,128)S(1)}, f32[768,128]{1,0:T(8,128)S(1)}, f32[8,128]{1,0:T(8,128)S(1)}) custom-call(bf16[512,768]{1,0:T(8,128)(2,1)S(1)} %copy-done.36, ...), custom_call_target="tpu_custom_call", output_to_operand_aliasing={{0}: (15, {}), {1}: (16, {}), {2}: (17, {}), {3}: (18, {})} | custom-call | flops 5175000064 | tf_op jit(solution)/shard_map/pallas_call | solution.py:146
  133.1 1.7 collective-permute-start.19
  134.8 20.3 %collective-permute-done.23.refs_3_ = f32[288,768]{1,0:T(8,128)S(1)} collective-permute-done((f32[288,768]{1,0:T(8,128)S(1)}, f32[288,768]{1,0:T(8,128)S(1)}, u32[]{:S(2)}, u32[]{:S(2)}) %collective-permute-start.23) | collective-permute-done | bytes 884768 | tf_op jit(solution)/shard_map/ppermute | solution.py:620
  155.1 1.2 collective-permute-start.20
  156.3 1.9 collective-permute-start.21
  158.2 2.1 shard_map.216
  160.3 1.0 collective-permute-start.33
  162.2 5.8 %shard_map.217 = (bf16[512,768]{1,0:T(8,128)(2,1)S(1)}, bf16[512,768]{1,0:T(8,128)(2,1)S(1)}, f32[768,128]{1,0:T(8,128)S(1)}, f32[8,128]{1,0:T(8,128)S(1)}) custom-call(bf16[512,768]{1,0:T(8,128)(2,1)S(1)} %copy-done.52, bf16[512,1536]{1,0:T(8,128)(2,1)S(1)} %copy-done.25, bf16[512,768]{1,0:T(8,128)(2,1)S(1)} %copy-done.34, ...), custom_call_target="tpu_custom_call" | custom-call | flops 69000003584 | tf_op jit(solution)/shard_map/pallas_call | solution.py:146
  168.1 1.1 shard_map.218
  170.8 4.6 %shard_map.219 = (f32[512,768]{1,0:T(8,128)}, f32[72,768]{1,0:T(8,128)S(1)}, f32[72,768]{1,0:T(8,128)S(1)}, f32[8,128]{1,0:T(8,128)S(1)}) custom-call(bf16[512,768]{1,0:T(8,128)(2,1)S(1)} %get-tuple-element.260.refs_1_.refs_0_, bf16[512,768]{1,0:T(8,128)(2,1)S(1)} %get-tuple-element.287.refs_2_.refs_1_.refs_3_, ...), custom_call_target="tpu_custom_call" | custom-call | flops 69000003584 | tf_op jit(solution)/shard_map/pallas_call | solution.py:146
  175.4 2.0 collective-permute-start.32
  177.4 1.5 shard_map.220
  178.9 1.1 collective-permute-start.29
  180.7 7.5 %collective-permute-done.32.refs_3_ = f32[144,768]{1,0:T(8,128)S(1)} collective-permute-done((f32[144,768]{1,0:T(8,128)S(1)}, f32[144,768]{1,0:T(8,128)S(1)}, u32[]{:S(2)}, u32[]{:S(2)}) %collective-permute-start.32) | collective-permute-done | bytes 442400 | tf_op jit(solution)/shard_map/ppermute | solution.py:620
  188.2 1.7 collective-permute-start.28
  190.0 3.8 %collective-permute-done.31.refs_1_ = f32[432,768]{1,0:T(8,128)} collective-permute-done((f32[432,768]{1,0:T(8,128)}, f32[432,768]{1,0:T(8,128)}, u32[]{:S(2)}, u32[]{:S(2)}) %collective-permute-start.31) | collective-permute-done | bytes 1327136 | tf_op jit(solution)/shard_map/ppermute | solution.py:620
  193.7 1.8 shard_map.221
  195.6 1.1 collective-permute-start.40
  197.9 13.2 %collective-permute-done.30.refs_5_ = f32[192,768]{1,0:T(8,128)S(1)} collective-permute-done((f32[192,768]{1,0:T(8,128)S(1)}, f32[192,768]{1,0:T(8,128)S(1)}, u32[]{:S(2)}, u32[]{:S(2)}) %collective-permute-start.30) | collective-permute-done | bytes 589856 | tf_op jit(solution)/shard_map/ppermute | solution.py:620
  211.9 1.5 collective-permute-start.36
  213.4 1.0 collective-permute-start.34
  214.4 2.9 %collective-permute-done.38.refs_5_ = f32[96,768]{1,0:T(8,128)S(1)} collective-permute-done((f32[96,768]{1,0:T(8,128)S(1)}, f32[96,768]{1,0:T(8,128)S(1)}, u32[]{:S(2)}, u32[]{:S(2)}) %collective-permute-start.38) | collective-permute-done | bytes 294944 | tf_op jit(solution)/shard_map/ppermute | solution.py:620
  217.3 7.8 %collective-permute-done.39.refs_7_ = f32[192,768]{1,0:T(8,128)S(1)} collective-permute-done((f32[192,768]{1,0:T(8,128)S(1)}, f32[192,768]{1,0:T(8,128)S(1)}, u32[]{:S(2)}, u32[]{:S(2)}) %collective-permute-start.39) | collective-permute-done | bytes 589856 | tf_op jit(solution)/shard_map/ppermute | solution.py:620
  225.2 1.1 collective-permute-start.45
  226.3 3.5 %collective-permute-done.36.refs_5_ = f32[96,768]{1,0:T(8,128)S(1)} collective-permute-done((f32[96,768]{1,0:T(8,128)S(1)}, f32[96,768]{1,0:T(8,128)S(1)}, u32[]{:S(2)}, u32[]{:S(2)}) %collective-permute-start.36) | collective-permute-done | bytes 294944 | tf_op jit(solution)/shard_map/ppermute | solution.py:620
  231.8 12.4 %collective-permute-done.44.refs_1_ = f32[120,768]{1,0:T(8,128)S(1)} collective-permute-done((f32[120,768]{1,0:T(8,128)S(1)}, f32[120,768]{1,0:T(8,128)S(1)}, u32[]{:S(2)}, u32[]{:S(2)}) %collective-permute-start.44) | collective-permute-done | bytes 368672 | tf_op jit(solution)/shard_map/ppermute | solution.py:620
  245.1 3.0 %collective-permute-start.46 = (f32[144,768]{1,0:T(8,128)S(1)}, f32[144,768]{1,0:T(8,128)S(1)}, u32[]{:S(2)}, u32[]{:S(2)}) collective-permute-start(f32[144,768]{1,0:T(8,128)S(1)} %get-tuple-element.356), channel_id=1, source_target_pairs={{0,8},{1,9},{2,10},{3,11},{4,12},{5,13},{6,14},{7,15},{8,0},{9,1},... | collective-permute-start | bytes 1327112 | tf_op jit(solution)/shard_map/ppermute | solution.py:620
  248.0 5.8 %collective-permute-done.47.refs_1_ = f32[24,768]{1,0:T(8,128)S(1)} collective-permute-done((f32[24,768]{1,0:T(8,128)S(1)}, f32[24,768]{1,0:T(8,128)S(1)}, u32[]{:S(2)}, u32[]{:S(2)}) %collective-permute-start.47) | collective-permute-done | bytes 73760 | tf_op jit(solution)/shard_map/ppermute | solution.py:620
  254.5 5.8 %collective-permute-done.46.refs_1_ = f32[144,768]{1,0:T(8,128)S(1)} collective-permute-done((f32[144,768]{1,0:T(8,128)S(1)}, f32[144,768]{1,0:T(8,128)S(1)}, u32[]{:S(2)}, u32[]{:S(2)}) %collective-permute-start.46) | collective-permute-done | bytes 442400 | tf_op jit(solution)/shard_map/ppermute | solution.py:620
  262.5 1.0 shard_map.229
  (195 shorter events, 25.6 us)
Async XLA Ops:
  2.0 14.7 %copy-start.10 = (bf16[768,2304]{1,0:T(8,128)(2,1)S(1)}, bf16[768,2304]{1,0:T(8,128)(2,1)}, u32[]{:S(2)}) copy-start(bf16[768,2304]{1,0:T(8,128)(2,1)} %refs_3_.5) | copy-start | bytes 10616836
  2.0 14.7 %copy-start.17 = (bf16[12,64,64]{2,1,0:T(8,128)(2,1)S(1)}, bf16[12,64,64]{2,1,0:T(8,128)(2,1)}, u32[]{:S(2)}) copy-start(bf16[12,64,64]{2,1,0:T(8,128)(2,1)} %refs_14_.5) | copy-start | bytes 294916
  2.0 29.7 %slice-start = ((s8[4718592]{0:T(1024)(128)(4,1)}), s8[4194304]{0:T(1024)(128)(4,1)S(1)}, s32[]{:S(2)}) async-start(s8[4718592]{0:T(1024)(128)(4,1)} %bitcast.14), calls=%async_computation | async-start | bytes 8388608
  12.1 13.5 %copy-start.24 = (bf16[512,1536]{1,0:T(8,128)(2,1)}, bf16[512,1536]{1,0:T(8,128)(2,1)S(1)}, u32[]{:S(2)}) copy-start(bf16[512,1536]{1,0:T(8,128)(2,1)S(1)} %get-tuple-element.193.refs_3_.refs_2_.refs_1_) | copy-start | bytes 4718596
  12.1 13.5 %copy-start.29 = (f32[512,512]{1,0:T(8,128)}, f32[512,512]{1,0:T(8,128)S(1)}, u32[]{:S(2)}) copy-start(f32[512,512]{1,0:T(8,128)S(1)} %get-tuple-element.195.refs_5_.refs_11_) | copy-start | bytes 3145732
  12.1 13.5 %copy-start.31 = (f32[512,512]{1,0:T(8,128)}, f32[512,512]{1,0:T(8,128)S(1)}, u32[]{:S(2)}) copy-start(f32[512,512]{1,0:T(8,128)S(1)} %get-tuple-element.236.refs_12_) | copy-start | bytes 3145732
  12.1 13.5 %copy-start.33 = (bf16[512,768]{1,0:T(8,128)(2,1)}, bf16[512,768]{1,0:T(8,128)(2,1)S(1)}, u32[]{:S(2)}) copy-start(bf16[512,768]{1,0:T(8,128)(2,1)S(1)} %get-tuple-element.194.refs_4_.refs_3_.refs_2_) | copy-start | bytes 2359300
  12.1 13.5 %copy-start.51 = (bf16[512,768]{1,0:T(8,128)(2,1)}, bf16[512,768]{1,0:T(8,128)(2,1)S(1)}, u32[]{:S(2)}) copy-start(bf16[512,768]{1,0:T(8,128)(2,1)S(1)} %get-tuple-element.261.refs_0_) | copy-start | bytes 2359300
  12.1 77.2 %copy-start.39 = (f32[512,128]{1,0:T(8,128)}, f32[512,128]{1,0:T(8,128)S(1)}, u32[]{:S(2)}) copy-start(f32[512,128]{1,0:T(8,128)S(1)} %get-tuple-element.211.refs_7_.refs_5_.refs_13_) | copy-start | bytes 786436
  12.1 13.5 %collective-permute-start = (f32[3,72,128]{2,1,0:T(8,128)S(1)}, f32[3,72,128]{2,1,0:T(8,128)S(1)}, u32[]{:S(2)}, u32[]{:S(2)}) collective-permute-start(f32[3,72,128]{2,1,0:T(8,128)S(1)} %get-tuple-element.200), channel_id=1, source_target_pairs={{0,1},{1,0},{2,3},{3,2},{4,5},{5,4},{6,7},{7,6},{8,9},{9,8},{10,11... | collective-permute-start | bytes 331784 | tf_op jit(solution)/shard_map/ppermute | solution.py:623
  15.1 10.5 %collective-permute-start.1 = (f32[3,72,128]{2,1,0:T(8,128)S(1)}, f32[3,72,128]{2,1,0:T(8,128)S(1)}, u32[]{:S(2)}, u32[]{:S(2)}) collective-permute-start(f32[3,72,128]{2,1,0:T(8,128)S(1)} %get-tuple-element.201), channel_id=1, source_target_pairs={{0,2},{1,3},{2,0},{3,1},{4,6},{5,7},{6,4},{7,5},{8,10},{9,11},{10,... | collective-permute-start | bytes 331784 | tf_op jit(solution)/shard_map/ppermute | solution.py:623
  16.6 9.0 %collective-permute-start.2 = (f32[3,72,128]{2,1,0:T(8,128)S(1)}, f32[3,72,128]{2,1,0:T(8,128)S(1)}, u32[]{:S(2)}, u32[]{:S(2)}) collective-permute-start(f32[3,72,128]{2,1,0:T(8,128)S(1)} %get-tuple-element.202), channel_id=1, source_target_pairs={{0,3},{1,2},{2,1},{3,0},{4,7},{5,6},{6,5},{7,4},{8,11},{9,10},{10,... | collective-permute-start | bytes 331784 | tf_op jit(solution)/shard_map/ppermute | solution.py:623
  16.7 15.1 %slice-start.1 = ((s8[4718592]{0:T(1024)(128)(4,1)}), s8[524288]{0:T(1024)(128)(4,1)S(1)}, s32[]{:S(2)}) async-start(s8[4718592]{0:T(1024)(128)(4,1)} %bitcast.14), calls=%async_computation.1 | async-start | bytes 1048576
  25.6 23.1 %copy-start.26 = (bf16[512,1536]{1,0:T(8,128)(2,1)}, bf16[512,1536]{1,0:T(8,128)(2,1)S(1)}, u32[]{:S(2)}) copy-start(bf16[512,1536]{1,0:T(8,128)(2,1)S(1)} %get-tuple-element.198.refs_2_.refs_4_.refs_1_) | copy-start | bytes 4718596
  26.5 10.3 %collective-permute-start.5 = (f32[3,72,128]{2,1,0:T(8,128)S(1)}, f32[3,72,128]{2,1,0:T(8,128)S(1)}, u32[]{:S(2)}, u32[]{:S(2)}) collective-permute-start(f32[3,72,128]{2,1,0:T(8,128)S(1)} %get-tuple-element.204), channel_id=1, source_target_pairs={{0,12},{1,13},{2,14},{3,15},{4,0},{5,1},{6,2},{7,3},{8,4},{9,5},{1... | collective-permute-start | bytes 331784 | tf_op jit(solution)/shard_map/ppermute | solution.py:626
  30.5 9.3 %collective-permute-start.4 = (f32[3,72,128]{2,1,0:T(8,128)S(1)}, f32[3,72,128]{2,1,0:T(8,128)S(1)}, u32[]{:S(2)}, u32[]{:S(2)}) collective-permute-start(f32[3,72,128]{2,1,0:T(8,128)S(1)} %get-tuple-element.204), channel_id=1, source_target_pairs={{0,8},{1,9},{2,10},{3,11},{4,12},{5,13},{6,14},{7,15},{8,0},{9,1},... | collective-permute-start | bytes 331784 | tf_op jit(solution)/shard_map/ppermute | solution.py:626
  30.5 9.3 %collective-permute-start.3 = (f32[3,72,128]{2,1,0:T(8,128)S(1)}, f32[3,72,128]{2,1,0:T(8,128)S(1)}, u32[]{:S(2)}, u32[]{:S(2)}) collective-permute-start(f32[3,72,128]{2,1,0:T(8,128)S(1)} %get-tuple-element.204), channel_id=1, source_target_pairs={{0,4},{1,5},{2,6},{3,7},{4,8},{5,9},{6,10},{7,11},{8,12},{9,13},{1... | collective-permute-start | bytes 331784 | tf_op jit(solution)/shard_map/ppermute | solution.py:626
  40.0 6.6 %collective-permute-start.6 = (f32[3,72,128]{2,1,0:T(8,128)S(1)}, f32[3,72,128]{2,1,0:T(8,128)S(1)}, u32[]{:S(2)}, u32[]{:S(2)}) collective-permute-start(f32[3,72,128]{2,1,0:T(8,128)S(1)} %get-tuple-element.208), channel_id=1, source_target_pairs={{0,1},{1,0},{2,3},{3,2},{4,5},{5,4},{6,7},{7,6},{8,9},{9,8},{10,11... | collective-permute-start | bytes 331784 | tf_op jit(solution)/shard_map/ppermute | solution.py:623
  41.5 5.9 %collective-permute-start.7 = (f32[3,72,128]{2,1,0:T(8,128)S(1)}, f32[3,72,128]{2,1,0:T(8,128)S(1)}, u32[]{:S(2)}, u32[]{:S(2)}) collective-permute-start(f32[3,72,128]{2,1,0:T(8,128)S(1)} %get-tuple-element.209), channel_id=1, source_target_pairs={{0,2},{1,3},{2,0},{3,1},{4,6},{5,7},{6,4},{7,5},{8,10},{9,11},{10,... | collective-permute-start | bytes 331784 | tf_op jit(solution)/shard_map/ppermute | solution.py:623
  43.0 5.6 %collective-permute-start.8 = (f32[3,72,128]{2,1,0:T(8,128)S(1)}, f32[3,72,128]{2,1,0:T(8,128)S(1)}, u32[]{:S(2)}, u32[]{:S(2)}) collective-permute-start(f32[3,72,128]{2,1,0:T(8,128)S(1)} %get-tuple-element.210), channel_id=1, source_target_pairs={{0,3},{1,2},{2,1},{3,0},{4,7},{5,6},{6,5},{7,4},{8,11},{9,10},{10,... | collective-permute-start | bytes 331784 | tf_op jit(solution)/shard_map/ppermute | solution.py:623
  56.3 12.3 %copy-start.2 = (bf16[2,3,384,512]{3,2,1,0:T(8,128)(2,1)}, bf16[2,3,384,512]{3,2,1,0:T(8,128)(2,1)S(1)}, u32[]{:S(2)}) copy-start(bf16[2,3,384,512]{3,2,1,0:T(8,128)(2,1)S(1)} %get-tuple-element.218.refs_2_.refs_7_) | copy-start | bytes 7077892
  68.6 16.2 %copy-start = (bf16[512,3072]{1,0:T(8,128)(2,1)}, bf16[512,3072]{1,0:T(8,128)(2,1)S(1)}, u32[]{:S(2)}) copy-start(bf16[512,3072]{1,0:T(8,128)(2,1)S(1)} %get-tuple-element.222.refs_1_.refs_10_) | copy-start | bytes 9437188
  68.6 17.3 %collective-permute-start.9 = (f32[2,4,384,768]{3,2,1,0:T(8,128)}, f32[2,4,384,768]{3,2,1,0:T(8,128)S(1)}, u32[]{:S(2)}, u32[]{:S(2)}) collective-permute-start(f32[2,4,384,768]{3,2,1,0:T(8,128)} %get-tuple-element.230), channel_id=1, source_target_pairs={{0,16},{16,0},{1,17},{17,1},{2,18},{18,2},{3,19},{19,3},{4,20},{20... | collective-permute-start | bytes 28311560 | tf_op jit(solution)/shard_map/ppermute | solution.py:599
  87.7 15.8 %collective-permute-start.13 = (f32[192,768]{1,0:T(8,128)S(1)}, f32[192,768]{1,0:T(8,128)S(1)}, u32[]{:S(2)}, u32[]{:S(2)}) collective-permute-start(f32[192,768]{1,0:T(8,128)S(1)} %get-tuple-element.242), channel_id=1, source_target_pairs={{0,1},{1,0},{2,3},{3,2},{4,5},{5,4},{6,7},{7,6},{8,9},{9,8},{10,11... | collective-permute-start | bytes 1769480 | tf_op jit(solution)/shard_map/ppermute | solution.py:620
  88.4 16.0 %collective-permute-start.14 = (f32[192,768]{1,0:T(8,128)S(1)}, f32[192,768]{1,0:T(8,128)S(1)}, u32[]{:S(2)}, u32[]{:S(2)}) collective-permute-start(f32[192,768]{1,0:T(8,128)S(1)} %get-tuple-element.244), channel_id=1, source_target_pairs={{0,2},{1,3},{2,0},{3,1},{4,6},{5,7},{6,4},{7,5},{8,10},{9,11},{10,... | collective-permute-start | bytes 1769480 | tf_op jit(solution)/shard_map/ppermute | solution.py:620
  89.2 15.2 %collective-permute-start.15 = (f32[192,768]{1,0:T(8,128)S(1)}, f32[192,768]{1,0:T(8,128)S(1)}, u32[]{:S(2)}, u32[]{:S(2)}) collective-permute-start(f32[192,768]{1,0:T(8,128)S(1)} %get-tuple-element.246), channel_id=1, source_target_pairs={{0,4},{1,5},{2,6},{3,7},{4,0},{5,1},{6,2},{7,3},{8,12},{9,13},{10,... | collective-permute-start | bytes 1769480 | tf_op jit(solution)/shard_map/ppermute | solution.py:620
  89.3 15.1 %copy-start.1 = (bf16[512,3072]{1,0:T(8,128)(2,1)S(1)}, bf16[512,3072]{1,0:T(8,128)(2,1)}, u32[]{:S(2)}) copy-start(bf16[512,3072]{1,0:T(8,128)(2,1)} %copy-done) | copy-start | bytes 9437188
  89.3 15.1 %copy-start.3 = (bf16[2,3,384,512]{3,2,1,0:T(8,128)(2,1)S(1)}, bf16[2,3,384,512]{3,2,1,0:T(8,128)(2,1)}, u32[]{:S(2)}) copy-start(bf16[2,3,384,512]{3,2,1,0:T(8,128)(2,1)} %copy-done.2) | copy-start | bytes 7077892
  93.4 14.2 %collective-permute-start.10 = (f32[3,72,128]{2,1,0:T(8,128)S(1)}, f32[3,72,128]{2,1,0:T(8,128)S(1)}, u32[]{:S(2)}, u32[]{:S(2)}) collective-permute-start(f32[3,72,128]{2,1,0:T(8,128)S(1)} %get-tuple-element.238), channel_id=1, source_target_pairs={{0,1},{1,0},{2,3},{3,2},{4,5},{5,4},{6,7},{7,6},{8,9},{9,8},{10,11... | collective-permute-start | bytes 331784 | tf_op jit(solution)/shard_map/ppermute | solution.py:623
  95.1 12.5 %collective-permute-start.11 = (f32[3,72,128]{2,1,0:T(8,128)S(1)}, f32[3,72,128]{2,1,0:T(8,128)S(1)}, u32[]{:S(2)}, u32[]{:S(2)}) collective-permute-start(f32[3,72,128]{2,1,0:T(8,128)S(1)} %get-tuple-element.239), channel_id=1, source_target_pairs={{0,2},{1,3},{2,0},{3,1},{4,6},{5,7},{6,4},{7,5},{8,10},{9,11},{10,... | collective-permute-start | bytes 331784 | tf_op jit(solution)/shard_map/ppermute | solution.py:623
  103.5 5.6 %collective-permute-start.12 = (f32[3,72,128]{2,1,0:T(8,128)S(1)}, f32[3,72,128]{2,1,0:T(8,128)S(1)}, u32[]{:S(2)}, u32[]{:S(2)}) collective-permute-start(f32[3,72,128]{2,1,0:T(8,128)S(1)} %get-tuple-element.240), channel_id=1, source_target_pairs={{0,3},{1,2},{2,1},{3,0},{4,7},{5,6},{6,5},{7,4},{8,11},{9,10},{10,... | collective-permute-start | bytes 331784 | tf_op jit(solution)/shard_map/ppermute | solution.py:623
  109.2 20.9 %collective-permute-start.18 = (f32[3,72,128]{2,1,0:T(8,128)S(1)}, f32[3,72,128]{2,1,0:T(8,128)S(1)}, u32[]{:S(2)}, u32[]{:S(2)}) collective-permute-start(f32[3,72,128]{2,1,0:T(8,128)S(1)} %get-tuple-element.264), channel_id=1, source_target_pairs={{0,4},{1,5},{2,6},{3,7},{4,8},{5,9},{6,10},{7,11},{8,12},{9,13},{1... | collective-permute-start | bytes 331784 | tf_op jit(solution)/shard_map/ppermute | solution.py:626
  109.4 20.8 %collective-permute-start.17 = (f32[3,72,128]{2,1,0:T(8,128)S(1)}, f32[3,72,128]{2,1,0:T(8,128)S(1)}, u32[]{:S(2)}, u32[]{:S(2)}) collective-permute-start(f32[3,72,128]{2,1,0:T(8,128)S(1)} %get-tuple-element.264), channel_id=1, source_target_pairs={{0,8},{1,9},{2,10},{3,11},{4,12},{5,13},{6,14},{7,15},{8,0},{9,1},... | collective-permute-start | bytes 331784 | tf_op jit(solution)/shard_map/ppermute | solution.py:626
  111.4 18.8 %collective-permute-start.16 = (f32[3,72,128]{2,1,0:T(8,128)S(1)}, f32[3,72,128]{2,1,0:T(8,128)S(1)}, u32[]{:S(2)}, u32[]{:S(2)}) collective-permute-start(f32[3,72,128]{2,1,0:T(8,128)S(1)} %get-tuple-element.264), channel_id=1, source_target_pairs={{0,12},{1,13},{2,14},{3,15},{4,0},{5,1},{6,2},{7,3},{8,4},{9,5},{1... | collective-permute-start | bytes 331784 | tf_op jit(solution)/shard_map/ppermute | solution.py:626
  114.6 43.6 %collective-permute-start.22 = (f32[480,768]{1,0:T(8,128)S(1)}, f32[480,768]{1,0:T(8,128)S(1)}, u32[]{:S(2)}, u32[]{:S(2)}) collective-permute-start(f32[480,768]{1,0:T(8,128)S(1)} %get-tuple-element.272), channel_id=1, source_target_pairs={{0,2},{1,3},{2,0},{3,1},{4,6},{5,7},{6,4},{7,5},{8,10},{9,11},{10,... | collective-permute-start | bytes 4423688 | tf_op jit(solution)/shard_map/ppermute | solution.py:620
  115.6 42.6 %collective-permute-start.24 = (f32[480,768]{1,0:T(8,128)S(1)}, f32[480,768]{1,0:T(8,128)S(1)}, u32[]{:S(2)}, u32[]{:S(2)}) collective-permute-start(f32[480,768]{1,0:T(8,128)S(1)} %get-tuple-element.276), channel_id=1, source_target_pairs={{0,1},{1,0},{2,3},{3,2},{4,5},{5,4},{6,7},{7,6},{8,9},{9,8},{10,11... | collective-permute-start | bytes 4423688 | tf_op jit(solution)/shard_map/ppermute | solution.py:620
  132.9 23.4 %collective-permute-start.25 = (f32[1,384,768]{2,1,0:T(8,128)S(1)}, f32[1,384,768]{2,1,0:T(8,128)S(1)}, u32[]{:S(2)}, u32[]{:S(2)}) collective-permute-start(f32[1,384,768]{2,1,0:T(8,128)S(1)} %get-tuple-element.284), channel_id=1, source_target_pairs={{0,16},{16,0},{1,17},{17,1},{2,18},{18,2},{3,19},{19,3},{4,20},{20... | collective-permute-start | bytes 3538952 | tf_op jit(solution)/shard_map/ppermute | solution.py:599
  133.0 22.1 %collective-permute-start.23 = (f32[288,768]{1,0:T(8,128)S(1)}, f32[288,768]{1,0:T(8,128)S(1)}, u32[]{:S(2)}, u32[]{:S(2)}) collective-permute-start(f32[288,768]{1,0:T(8,128)S(1)} %get-tuple-element.274), channel_id=1, source_target_pairs={{0,4},{1,5},{2,6},{3,7},{4,0},{5,1},{6,2},{7,3},{8,12},{9,13},{10,... | collective-permute-start | bytes 2654216 | tf_op jit(solution)/shard_map/ppermute | solution.py:620
  133.1 28.5 %collective-permute-start.19 = (f32[3,72,128]{2,1,0:T(8,128)S(1)}, f32[3,72,128]{2,1,0:T(8,128)S(1)}, u32[]{:S(2)}, u32[]{:S(2)}) collective-permute-start(f32[3,72,128]{2,1,0:T(8,128)S(1)} %get-tuple-element.267), channel_id=1, source_target_pairs={{0,1},{1,0},{2,3},{3,2},{4,5},{5,4},{6,7},{7,6},{8,9},{9,8},{10,11... | collective-permute-start | bytes 331784 | tf_op jit(solution)/shard_map/ppermute | solution.py:623
  155.1 7.1 %collective-permute-start.20 = (f32[3,72,128]{2,1,0:T(8,128)S(1)}, f32[3,72,128]{2,1,0:T(8,128)S(1)}, u32[]{:S(2)}, u32[]{:S(2)}) collective-permute-start(f32[3,72,128]{2,1,0:T(8,128)S(1)} %get-tuple-element.268), channel_id=1, source_target_pairs={{0,2},{1,3},{2,0},{3,1},{4,6},{5,7},{6,4},{7,5},{8,10},{9,11},{10,... | collective-permute-start | bytes 331784 | tf_op jit(solution)/shard_map/ppermute | solution.py:623
  156.3 5.9 %collective-permute-start.21 = (f32[3,72,128]{2,1,0:T(8,128)S(1)}, f32[3,72,128]{2,1,0:T(8,128)S(1)}, u32[]{:S(2)}, u32[]{:S(2)}) collective-permute-start(f32[3,72,128]{2,1,0:T(8,128)S(1)} %get-tuple-element.269), channel_id=1, source_target_pairs={{0,3},{1,2},{2,1},{3,0},{4,7},{5,6},{6,5},{7,4},{8,11},{9,10},{10,... | collective-permute-start | bytes 331784 | tf_op jit(solution)/shard_map/ppermute | solution.py:623
  160.3 29.6 %collective-permute-start.33 = (f32[240,768]{1,0:T(8,128)}, f32[240,768]{1,0:T(8,128)}, u32[]{:S(2)}, u32[]{:S(2)}) collective-permute-start(f32[240,768]{1,0:T(8,128)} %get-tuple-element.313), channel_id=1, source_target_pairs={{0,2},{1,3},{2,0},{3,1},{4,6},{5,7},{6,4},{7,5},{8,10},{9,11},{10,... | collective-permute-start | bytes 2211848 | tf_op jit(solution)/shard_map/ppermute | solution.py:620
  161.4 32.4 %collective-permute-start.31 = (f32[432,768]{1,0:T(8,128)}, f32[432,768]{1,0:T(8,128)}, u32[]{:S(2)}, u32[]{:S(2)}) collective-permute-start(f32[432,768]{1,0:T(8,128)} %get-tuple-element.309), channel_id=1, source_target_pairs={{0,4},{1,5},{2,6},{3,7},{4,0},{5,1},{6,2},{7,3},{8,12},{9,13},{10,... | collective-permute-start | bytes 3981320 | tf_op jit(solution)/shard_map/ppermute | solution.py:620
  169.2 8.2 %collective-permute-start.26 = (f32[3,384,768]{2,1,0:T(8,128)S(1)}, f32[3,384,768]{2,1,0:T(8,128)S(1)}, u32[]{:S(2)}, u32[]{:S(2)}) collective-permute-start(f32[3,384,768]{2,1,0:T(8,128)S(1)} %get-tuple-element.297), channel_id=1, source_target_pairs={{0,16},{16,0},{1,17},{17,1},{2,18},{18,2},{3,19},{19,3},{4,20},{20... | collective-permute-start | bytes 10616840 | tf_op jit(solution)/shard_map/ppermute | solution.py:599
  175.4 2.0 collective-permute-start.27
  175.4 12.8 %collective-permute-start.32 = (f32[144,768]{1,0:T(8,128)S(1)}, f32[144,768]{1,0:T(8,128)S(1)}, u32[]{:S(2)}, u32[]{:S(2)}) collective-permute-start(f32[144,768]{1,0:T(8,128)S(1)} %get-tuple-element.311), channel_id=1, source_target_pairs={{0,1},{1,0},{2,3},{3,2},{4,5},{5,4},{6,7},{7,6},{8,9},{9,8},{10,11... | collective-permute-start | bytes 1327112 | tf_op jit(solution)/shard_map/ppermute | solution.py:620
  178.9 18.7 %collective-permute-start.29 = (f32[192,768]{1,0:T(8,128)S(1)}, f32[192,768]{1,0:T(8,128)S(1)}, u32[]{:S(2)}, u32[]{:S(2)}) collective-permute-start(f32[192,768]{1,0:T(8,128)S(1)} %get-tuple-element.304), channel_id=1, source_target_pairs={{0,2},{1,3},{2,0},{3,1},{4,6},{5,7},{6,4},{7,5},{8,10},{9,11},{10,... | collective-permute-start | bytes 1769480 | tf_op jit(solution)/shard_map/ppermute | solution.py:620
  180.0 31.0 %collective-permute-start.30 = (f32[192,768]{1,0:T(8,128)S(1)}, f32[192,768]{1,0:T(8,128)S(1)}, u32[]{:S(2)}, u32[]{:S(2)}) collective-permute-start(f32[192,768]{1,0:T(8,128)S(1)} %get-tuple-element.306), channel_id=1, source_target_pairs={{0,4},{1,5},{2,6},{3,7},{4,0},{5,1},{6,2},{7,3},{8,12},{9,13},{10,... | collective-permute-start | bytes 1769480 | tf_op jit(solution)/shard_map/ppermute | solution.py:620
  188.2 23.4 %collective-permute-start.28 = (f32[264,768]{1,0:T(8,128)S(1)}, f32[264,768]{1,0:T(8,128)S(1)}, u32[]{:S(2)}, u32[]{:S(2)}) collective-permute-start(f32[264,768]{1,0:T(8,128)S(1)} %get-tuple-element.302), channel_id=1, source_target_pairs={{0,1},{1,0},{2,3},{3,2},{4,5},{5,4},{6,7},{7,6},{8,9},{9,8},{10,11... | collective-permute-start | bytes 2433032 | tf_op jit(solution)/shard_map/ppermute | solution.py:620
  195.6 16.4 %collective-permute-start.40 = (f32[48,768]{1,0:T(8,128)S(1)}, f32[48,768]{1,0:T(8,128)S(1)}, u32[]{:S(2)}, u32[]{:S(2)}) collective-permute-start(f32[48,768]{1,0:T(8,128)S(1)} %get-tuple-element.336), channel_id=1, source_target_pairs={{0,2},{1,3},{2,0},{3,1},{4,6},{5,7},{6,4},{7,5},{8,10},{9,11},{10,... | collective-permute-start | bytes 442376 | tf_op jit(solution)/shard_map/ppermute | solution.py:620
  196.6 16.8 %collective-permute-start.37 = (f32[72,768]{1,0:T(8,128)S(1)}, f32[72,768]{1,0:T(8,128)S(1)}, u32[]{:S(2)}, u32[]{:S(2)}) collective-permute-start(f32[72,768]{1,0:T(8,128)S(1)} %get-tuple-element.328), channel_id=1, source_target_pairs={{0,8},{1,9},{2,10},{3,11},{4,12},{5,13},{6,14},{7,15},{8,0},{9,1},... | collective-permute-start | bytes 663560 | tf_op jit(solution)/shard_map/ppermute | solution.py:620
  197.6 19.8 %collective-permute-start.38 = (f32[96,768]{1,0:T(8,128)S(1)}, f32[96,768]{1,0:T(8,128)S(1)}, u32[]{:S(2)}, u32[]{:S(2)}) collective-permute-start(f32[96,768]{1,0:T(8,128)S(1)} %get-tuple-element.332), channel_id=1, source_target_pairs={{0,4},{1,5},{2,6},{3,7},{4,0},{5,1},{6,2},{7,3},{8,12},{9,13},{10,... | collective-permute-start | bytes 884744 | tf_op jit(solution)/shard_map/ppermute | solution.py:620
  211.0 14.1 %collective-permute-start.39 = (f32[192,768]{1,0:T(8,128)S(1)}, f32[192,768]{1,0:T(8,128)S(1)}, u32[]{:S(2)}, u32[]{:S(2)}) collective-permute-start(f32[192,768]{1,0:T(8,128)S(1)} %get-tuple-element.334), channel_id=1, source_target_pairs={{0,1},{1,0},{2,3},{3,2},{4,5},{5,4},{6,7},{7,6},{8,9},{9,8},{10,11... | collective-permute-start | bytes 1769480 | tf_op jit(solution)/shard_map/ppermute | solution.py:620
  211.9 14.4 %collective-permute-start.35 = (f32[96,768]{1,0:T(8,128)S(1)}, f32[96,768]{1,0:T(8,128)S(1)}, u32[]{:S(2)}, u32[]{:S(2)}) collective-permute-start(f32[96,768]{1,0:T(8,128)S(1)} %get-tuple-element.323), channel_id=1, source_target_pairs={{0,4},{1,5},{2,6},{3,7},{4,0},{5,1},{6,2},{7,3},{8,12},{9,13},{10,... | collective-permute-start | bytes 884744 | tf_op jit(solution)/shard_map/ppermute | solution.py:620
  211.9 17.9 %collective-permute-start.36 = (f32[96,768]{1,0:T(8,128)S(1)}, f32[96,768]{1,0:T(8,128)S(1)}, u32[]{:S(2)}, u32[]{:S(2)}) collective-permute-start(f32[96,768]{1,0:T(8,128)S(1)} %get-tuple-element.325), channel_id=1, source_target_pairs={{0,1},{1,0},{2,3},{3,2},{4,5},{5,4},{6,7},{7,6},{8,9},{9,8},{10,11... | collective-permute-start | bytes 884744 | tf_op jit(solution)/shard_map/ppermute | solution.py:620
  213.4 16.4 %collective-permute-start.34 = (f32[168,768]{1,0:T(8,128)S(1)}, f32[168,768]{1,0:T(8,128)S(1)}, u32[]{:S(2)}, u32[]{:S(2)}) collective-permute-start(f32[168,768]{1,0:T(8,128)S(1)} %get-tuple-element.321), channel_id=1, source_target_pairs={{0,2},{1,3},{2,0},{3,1},{4,6},{5,7},{6,4},{7,5},{8,10},{9,11},{10,... | collective-permute-start | bytes 1548296 | tf_op jit(solution)/shard_map/ppermute | solution.py:620
  225.2 6.5 %collective-permute-start.45 = (f32[48,768]{1,0:T(8,128)S(1)}, f32[48,768]{1,0:T(8,128)S(1)}, u32[]{:S(2)}, u32[]{:S(2)}) collective-permute-start(f32[48,768]{1,0:T(8,128)S(1)} %get-tuple-element.352), channel_id=1, source_target_pairs={{0,2},{1,3},{2,0},{3,1},{4,6},{5,7},{6,4},{7,5},{8,10},{9,11},{10,... | collective-permute-start | bytes 442376 | tf_op jit(solution)/shard_map/ppermute | solution.py:620
  226.3 17.9 %collective-permute-start.44 = (f32[120,768]{1,0:T(8,128)S(1)}, f32[120,768]{1,0:T(8,128)S(1)}, u32[]{:S(2)}, u32[]{:S(2)}) collective-permute-start(f32[120,768]{1,0:T(8,128)S(1)} %get-tuple-element.348), channel_id=1, source_target_pairs={{0,8},{1,9},{2,10},{3,11},{4,12},{5,13},{6,14},{7,15},{8,0},{9,1},... | collective-permute-start | bytes 1105928 | tf_op jit(solution)/shard_map/ppermute | solution.py:620
  230.0 15.0 %collective-permute-start.42 = (f32[48,768]{1,0:T(8,128)S(1)}, f32[48,768]{1,0:T(8,128)S(1)}, u32[]{:S(2)}, u32[]{:S(2)}) collective-permute-start(f32[48,768]{1,0:T(8,128)S(1)} %get-tuple-element.343), channel_id=1, source_target_pairs={{0,1},{1,0},{2,3},{3,2},{4,5},{5,4},{6,7},{7,6},{8,9},{9,8},{10,11... | collective-permute-start | bytes 442376 | tf_op jit(solution)/shard_map/ppermute | solution.py:620
  230.6 14.3 %collective-permute-start.43 = (f32[48,768]{1,0:T(8,128)S(1)}, f32[48,768]{1,0:T(8,128)S(1)}, u32[]{:S(2)}, u32[]{:S(2)}) collective-permute-start(f32[48,768]{1,0:T(8,128)S(1)} %get-tuple-element.345), channel_id=1, source_target_pairs={{0,2},{1,3},{2,0},{3,1},{4,6},{5,7},{6,4},{7,5},{8,10},{9,11},{10,... | collective-permute-start | bytes 442376 | tf_op jit(solution)/shard_map/ppermute | solution.py:620
  231.5 13.4 %collective-permute-start.41 = (f32[120,768]{1,0:T(8,128)S(1)}, f32[120,768]{1,0:T(8,128)S(1)}, u32[]{:S(2)}, u32[]{:S(2)}) collective-permute-start(f32[120,768]{1,0:T(8,128)S(1)} %get-tuple-element.341), channel_id=1, source_target_pairs={{0,4},{1,5},{2,6},{3,7},{4,0},{5,1},{6,2},{7,3},{8,12},{9,13},{10,... | collective-permute-start | bytes 1105928 | tf_op jit(solution)/shard_map/ppermute | solution.py:620
  245.0 8.9 %collective-permute-start.47 = (f32[24,768]{1,0:T(8,128)S(1)}, f32[24,768]{1,0:T(8,128)S(1)}, u32[]{:S(2)}, u32[]{:S(2)}) collective-permute-start(f32[24,768]{1,0:T(8,128)S(1)} %get-tuple-element.361), channel_id=1, source_target_pairs={{0,8},{1,9},{2,10},{3,11},{4,12},{5,13},{6,14},{7,15},{8,0},{9,1},... | collective-permute-start | bytes 221192 | tf_op jit(solution)/shard_map/ppermute | solution.py:620
  245.1 15.3 %collective-permute-start.46 = (f32[144,768]{1,0:T(8,128)S(1)}, f32[144,768]{1,0:T(8,128)S(1)}, u32[]{:S(2)}, u32[]{:S(2)}) collective-permute-start(f32[144,768]{1,0:T(8,128)S(1)} %get-tuple-element.356), channel_id=1, source_target_pairs={{0,8},{1,9},{2,10},{3,11},{4,12},{5,13},{6,14},{7,15},{8,0},{9,1},... | collective-permute-start | bytes 1327112 | tf_op jit(solution)/shard_map/ppermute | solution.py:620
  261.1 1.5 collective-permute-start.48
  (45 other events, 198.7 us)

commit v3 on v2

--- a/solution.py
+++ b/solution.py
@@ -70,19 +70,25 @@
         ).astype(scr.dtype)
 
 
-def features(pre, ones):
+def half_sums(v, low_half):
+    top = jnp.sum(jnp.where(low_half, v, 0.0), axis=1, keepdims=True)
+    bottom = jnp.sum(jnp.where(low_half, 0.0, v), axis=1, keepdims=True)
+    return jnp.where(low_half, top, bottom)
+
+
+def features(pre):
     low_half = iota(pre.shape, 1) < 64
     top = jnp.max(jnp.where(low_half, pre, -jnp.inf), axis=1, keepdims=True)
     bottom = jnp.max(jnp.where(low_half, -jnp.inf, pre), axis=1, keepdims=True)
     e = jnp.exp(pre - jnp.where(low_half, top, bottom))
-    return e / segment_sum(e, ones)
+    return e / half_sums(e, low_half)
 
 
 def features_back(feat, grad, ones):
+    low_half = iota(feat.shape, 1) < 64
     weighted = feat * grad
-    total = segment_sum(weighted, ones)
     mass = mm(feat.astype(BF16), ones)
-    part = weighted - feat * (total / mass)
+    part = weighted - feat * (half_sums(weighted, low_half) / mass)
     return part - pltpu.roll(part, 64, 1)
 
 
@@ -133,13 +139,13 @@
     arrays = []
     for array, spec in ins:
         near = isinstance(array, Near)
-        if spec.block_shape is not None and not near:
+        if spec.block_shape is not None and not (near and spec.block_shape == array.shape):
             held += (1 if spec.block_shape == array.shape else 2) * nbytes(spec.block_shape, array.dtype)
         if isinstance(array, Held):
             array = pltpu.with_memory_space_constraint(array.array, pltpu.VMEM if near else pltpu.HBM)
         arrays.append(array)
     for shape, dtype, spec, stays in outs:
-        if stays is not Near:
+        if not (stays is Near and spec.block_shape == shape):
             held += (1 if spec.block_shape == shape else 2) * nbytes(spec.block_shape, dtype)
     for item in scratch:
         held += nbytes(item.shape, item.dtype)
@@ -209,11 +215,11 @@
     tail = tail_ref[...]
     row_ones = jnp.ones((16, tokens), BF16)
     for h in range(4):
-        feat = features(pre[:, 128 * h : 128 * h + 128], ones).astype(BF16)
+        feat = features(pre[:, 128 * h : 128 * h + 128]).astype(BF16)
         fk_ref[:, 128 * h : 128 * h + 128] = feat
         kept = (feat.astype(F32) * tail).astype(BF16)
-        state_scr[4 * j + h, 0:64, :] = mm(v_t[64 * h : 64 * h + 64], kept)
-        state_scr[4 * j + h, 64:72, :] = mm(row_ones, kept)[0:8]
+        rows = jnp.concatenate([v_t[64 * h : 64 * h + 64], row_ones], axis=0)
+        state_scr[4 * j + h] = mm(rows, kept)[0:STATE_ROWS]
 
     @pl.when(j == pl.num_programs(0) - 1)
     def _():
@@ -234,7 +240,7 @@
     low_half = iota((tokens, 128), 1) < 64
     for h in range(4):
         lanes = slice(128 * h, 128 * h + 128)
-        feat = features(pre[:, lanes], ones).astype(BF16)
+        feat = features(pre[:, lanes]).astype(BF16)
         fq_ref[:, lanes] = feat
         fk = fk_ref[:, lanes]
         pair = v_ref[:, 128 * (h // 2) : 128 * (h // 2) + 128].astype(F32)
@@ -275,6 +281,28 @@
             counts = source > target if backward else source < target
             value = value + jnp.where(counts, piece[...], 0.0)
         out[...] = value
+
+
+def later_kernel(planes, own0, own1, own2, own3, *refs):
+    own, others, (mine, x_pair, y_one) = (own0, own1, own2, own3), refs[:-3], refs[-3:]
+    member, plane = my_seq() & 3, my_seq() >> 2
+    total = jnp.zeros(own0.shape, F32)
+    for i, other in enumerate(others):
+        if planes is None:
+            total = total + other[...]
+        else:
+            total = total + jnp.where(plane + i + 1 < planes, other[...], 0.0)
+    n = own0.shape[0]
+    for k in range(4):
+        value = total
+        for i, piece in enumerate(own):
+            value = value + jnp.where((member ^ i) > (member ^ k), piece[...], 0.0)
+        if k == 0:
+            mine[...] = value
+        elif k == 2:
+            y_one[...] = value
+        else:
+            x_pair[n * (k // 2) : n * (k // 2) + n] = value
 
 
 def place_heads(scr, pieces):
@@ -348,12 +376,15 @@
 
 
 def act_back_kernel(cot_ref, wp_ref, ga_ref):
-    ga_ref[...] = nt(cot_ref[...], wp_ref[...])
+    width = wp_ref.shape[0]
+    start = pl.multiple_of(pl.program_id(0) * width, 128)
+    ga_ref[:, pl.ds(start, width)] = nt(cot_ref[...], wp_ref[...])
 
 
 def mlp_kernel(mlp_ref, ga_ref, mlp_t, cot_t, wf_ref, act_ref, gp_ref, send_ref):
     j = pl.program_id(0)
-    tokens = mlp_ref.shape[0]
+    tokens, width = mlp_ref.shape[0], wf_ref.shape[1]
+    lanes = slice(0, width)
     step = tokens // 4
     for r in range(4):
         rows = slice(step * r, step * r + step)
@@ -361,11 +392,11 @@
         square = u * u
         t = jnp.tanh(GELU_C * (u + GELU_A * (u * square)))
         half = 0.5 * (1.0 + t)
-        act_ref[rows, :] = (u * half).astype(BF16)
+        act_ref[rows, lanes] = (u * half).astype(BF16)
         slope = half + (0.5 * GELU_C) * u * (1.0 - t * t) * (1.0 + (3.0 * GELU_A) * square)
-        gp_ref[rows, :] = (ga_ref[rows, :] * slope).astype(BF16)
-    send_ref[0, 0] = mm(cot_t[0, j % 3], act_ref[...])
-    send_ref[1, 0] = mm(mlp_t[0, (j + 1) // 2], gp_ref[...])
+        gp_ref[rows, lanes] = (ga_ref[rows, lanes] * slope).astype(BF16)
+    send_ref[0, 0] = mm(cot_t[0, j % 3], act_ref[:, lanes])
+    send_ref[1, 0] = mm(mlp_t[0, (j + 1) // 2], gp_ref[:, lanes])
 
 
 def mlp_out_kernel(act_ref, gp_ref, wf_ref, wp_ref, part_ref, hidden_ref, cot_ref, gain_ref,
@@ -398,11 +429,11 @@
         rows = gd_t[64 * h : 64 * h + 8]
         gd_t_ref[8 * h : 8 * h + 8, :] = rows
         kept = (fq_ref[:, 128 * h : 128 * h + 128].astype(F32) * contin).astype(BF16)
-        state_scr[4 * j + h, 0:64, :] = mm(gn_t[64 * h : 64 * h + 64], kept)
         high, low = split(rows)
         both = jnp.concatenate([high.astype(F32), low.astype(F32)], axis=0).astype(BF16)
-        sums = mm(both, kept)
-        state_scr[4 * j + h, 64:72, :] = sums[0:8] + sums[8:16]
+        sums = mm(jnp.concatenate([gn_t[64 * h : 64 * h + 64], both], axis=0), kept)
+        state_scr[4 * j + h, 0:64, :] = sums[0:64]
+        state_scr[4 * j + h, 64:72, :] = sums[64:72] + sums[72:80]
 
     @pl.when(j == pl.num_programs(0) - 1)
     def _():
@@ -535,7 +566,11 @@
                 out[:, 128 * c : 128 * c + 128] = pack[pl.ds(pl.multiple_of(start, 8), SMALL_ROWS), :]
 
 
-def unpack_kernel(kept_ref, got_ref, other_ref, gmq_ref, gmk_ref, gains_ref, pack):
+def add_kernel(a_ref, b_ref, out_ref):
+    out_ref[...] = a_ref[...] + b_ref[...]
+
+
+def unpack_kernel(kept_ref, other_ref, gmq_ref, gmk_ref, gains_ref, pack):
     n = kept_ref.shape[1] // 128
     for value, core in ((kept_ref[...], my_core()), (other_ref[...], 1 - my_core())):
         for c in range(n):
@@ -550,6 +585,7 @@
 
 
 ORDERS = ((0, 1, 2, 3), (1, 2, 0, 3), (2, 0, 1, 3))
+SMALL_ORDER = (3, 0, 1, 2)
 
 
 def send_kernel(kinds, x_ref, *refs):
@@ -571,6 +607,8 @@
                          + refs[got][at + rows * p : at + rows * p + rows, :])
                 refs[send][base + half * p : base + half * p + half, :] = total[half:]
                 refs[keep][half * p : half * p + half, :] = total[:half]
+        for whence, out in plan["copies"]:
+            refs[out][:, : refs[whence].shape[1]] = refs[whence][...]
         for kept, got, at, out, block in plan["ends"]:
             rows, width = refs[out].shape[0], refs[kept].shape[1]
             first, piece = block
@@ -582,8 +620,7 @@
             rows = refs[kept].shape[0]
             total = refs[kept][...] + refs[got][at : at + rows, :]
             refs[keep][...] = total
-            if send is not None:
-                refs[send][base : base + rows, :] = total
+            refs[send][base : base + rows, :] = total
 
     for step, (x, entry, y, r, send, base, keep, at) in enumerate(plan["joins"]):
 
@@ -671,6 +708,15 @@
             functools.partial(scan_kernel, backward, planes if planes <= 4 else None), tok, (1,),
             [(p, piece_spec) for p in own + others], [(piece, F32, piece_spec)] * 4)
 
+    def later(own, others, tok):
+        pair = (2 * per,) + piece[1:]
+        (mine, x_pair, y_one), tok = run(
+            functools.partial(later_kernel, planes if planes <= 4 else None), tok, (1,),
+            [(p, piece_spec) for p in own + others],
+            [(piece, F32, piece_spec), (pair, F32, whole(pair)), (piece, F32, piece_spec)])
+        x_pair, y_one = to_member(x_pair, 1), to_member(y_one, 2)
+        return [mine, x_pair, y_one, to_member(x_pair[per:], 2)], tok
+
     def turn(x, kinds, tok):
         shape = (2, len(kinds), half_rows, T)
         if not direct:
@@ -691,7 +737,7 @@
     others = across(total, False)
     (ga,), tok = run(
         act_back_kernel, tok, (FF // D,), [(cot, full), (w_proj, pl.BlockSpec((D, D), lambda j: (j, 0)))],
-        [((T, FF), F32, columns(T, D), True)], us=4.0)
+        [((T, FF), F32, whole((T, FF)), Near)], us=4.0)
     carried, tok = scanned(own, others, False, tok)
     carry = plane_exchange(carried)
     cot_t, tok = turn(cot, (0, 1, 2), tok)
@@ -711,15 +757,15 @@
     send_shape = (2, n_ff, half_rows, D)
     (act, gp, send_mlp), tok = run(
         mlp_kernel, tok, (n_ff,),
-        [(mlp_in, full), (ga, columns(T, D)), (mlp_t, turned_spec), (cot_t, turned_spec), (w_fc, columns(D, D))],
-        [((T, FF), BF16, columns(T, D))] * 2
-        + [(send_shape, F32, pl.BlockSpec((2, 1, half_rows, D), lambda j: (0, j, 0, 0)))], us=10.0)
+        [(mlp_in, full), (ga, columns(T, D)), (mlp_t, turned_spec), (cot_t, turned_spec), (Held(w_fc), columns(D, D))],
+        [((T, FF), BF16, columns(T, D), Near)] * 2
+        + [(send_shape, F32, pl.BlockSpec((2, 1, half_rows, D), lambda j: (0, j, 0, 0)), True)], us=10.0)
     if direct:
-        recv_mlp = core_hop(send_mlp).reshape(2 * n_ff, half_rows, D)
+        recv_mlp = core_hop(send_mlp.array).reshape(2 * n_ff, half_rows, D)
     (output, gh, gh_low, gg_mlp), tok = run(
         mlp_out_kernel, tok, (quads,),
-        [(act, whole((T, FF))), (gp, whole((T, FF))), (w_fc, pl.BlockSpec((QW, FF), lambda j: (j, 0))),
-         (w_proj, columns(FF, QW)), (hidden, qcol), (hidden, full), (cot, full), (gain_m, row)],
+        [(act, whole((T, FF))), (gp, whole((T, FF))), (Held(w_fc), pl.BlockSpec((QW, FF), lambda j: (j, 0))),
+         (Held(w_proj), columns(FF, QW)), (hidden, qcol), (hidden, full), (Held(cot), full), (gain_m, row)],
         [((T, D), F32, qcol), ((T, D), F32, full), ((T, D), BF16, full), ((1, D), F32, row)],
         [pltpu.VMEM((quads, T, QW), F32)], us=8.0)
     def send_half(x_t, kinds, ys, tok):
@@ -736,7 +782,7 @@
 
     def wave(folds, join, tok, us=30.0):
         ins, outs, sends = [], [], {}
-        plan = {"folds": [], "ends": [], "smalls": [], "joins": []}
+        plan = {"folds": [], "ends": [], "smalls": [], "joins": [], "copies": []}
         after = []
 
         def take(array, spec=None):
@@ -763,6 +809,8 @@
                 rows = half_rows // 16
                 g.result = [None] * len(g.widths)
                 made = []
+                if g is main:
+                    plan["copies"] = [(take(early.result[0]), ("out", len(outs)))]
                 for n, width in enumerate(g.widths):
                     def put(array, n=n, g=g):
                         g.result[n] = array
@@ -792,15 +840,14 @@
                     plan["folds"].append(
                         (take(old_keeps[kind]), take(got), at, g.counts[kind], ("send", bit), base, keep))
                     g.got[kind] = (bit, base)
-            if g.small is not None:
+            if g.small is not None and g.stage < 4:
                 got, at = g.small_got
-                bit = ORDERS[0][g.stage] if g.stage < 4 else None
-                base = place(bit, SMALL_ROWS) if g.stage < 4 else 0
+                bit = SMALL_ORDER[g.stage]
+                base = place(bit, SMALL_ROWS)
                 def put(array, g=g):
                     g.small = array
                 keep = give(small_shape, put)
-                plan["smalls"].append(
-                    (take(g.small), take(got), at, ("send", bit) if g.stage < 4 else None, base, keep))
+                plan["smalls"].append((take(g.small), take(got), at, ("send", bit), base, keep))
                 g.small_got = (bit, base)
         if join is not None:
             g, xs, ys, segments, small = join
@@ -833,7 +880,7 @@
                 offset[kind] += half
             steps = len(segments)
             if small is not None:
-                bit = ORDERS[0][0]
+                bit = SMALL_ORDER[0]
                 base = place(bit, SMALL_ROWS)
                 def put(array, g=g):
                     g.small = array
@@ -867,8 +914,8 @@
 
     small_shape = (SMALL_ROWS, D)
     early = Group((1, 1, 1), [(0, i) for i in range(3)], (3 * D,))
-    main = Group((2, 2, 1), [(0, 0)] + [(1, i) for i in range(n_ff)], (D, FF))
-    wide = Group((0, 0, 1), [(0, 0)], (D,))
+    main = Group((2, 2, 1), [(0, n_ff - 1)] + [(1, i) for i in range(n_ff)], (FF, FF))
+    wide = Group((1, 0, 0), [(0, 0)], (D,))
     last = Group((1, 1, 1), [(0, i) for i in range(3)], (3 * D,))
     if direct:
         tok = wave([], (early, [cot_t], [(act, recv_mlp, 0, 0)], [(0, kind, 0, kind) for kind in range(3)], None), tok, 4.0)
@@ -912,13 +959,12 @@
     backs, tok = scores_back(1, backs, tok)
     backs, tok = scores_back(2, backs, tok)
     gq, gfk, gv_f, gmq = backs
-    carried, tok = scanned(own, others, True, tok)
-    upstream = plane_exchange(carried)
+    upstream, tok = later(own, others, tok)
     if direct:
-        mixed_t, tok = turn(mixed, (2,), tok)
+        mixed_t, tok = turn(mixed, (0,), tok)
         recv_out, tok = send_half(mixed_t, (0,), [gh_low], tok)
         tok = wave(
-            [early, main], (wide, [mixed_t], [(gh_low, recv_out, 0, 0)], [(0, 0, 0, 2)], None), tok, 2.0)
+            [early, main], (wide, [mixed_t], [(gh_low, recv_out, 0, 0)], [(0, 0, 0, 0)], None), tok, 2.0)
 
     (gk, gv, gmk), tok = run(
         keys_back_kernel, tok, (quads,),
@@ -950,20 +996,20 @@
         tok = wave([last], None, tok)
         tok = wave([main, wide], None, tok)
         tok = wave([last], None, tok)
-        tok = wave([wide], None, tok)
-        tok = wave([last], None, tok)
-        mine = last.small.array
-        got = core_hop(mine)
+        (mine,), tok = run(
+            add_kernel, tok, (1,), [(last.small, small_spec), (last.small_got[0], small_spec)],
+            [(small_shape, F32, small_spec, Near)], us=0.1)
+        got = core_hop(mine.array)
+        tok = wave([wide, last], None, tok)
         (grad_w_qkv,) = last.result
-        proj_last, grad_w_fc = main.result
+        grad_proj_rows, grad_w_fc = main.result
         (grad_w_out,) = wide.result
-        grad_proj_rows = jnp.concatenate([early.result[0], proj_last], axis=1)
     else:
         mine = lax.psum(keep + got, "seq")
         got = core_hop(mine)
         summed = lax.psum_scatter(
             jnp.concatenate(
-                [tn(attn, gq), tn(attn, gk), tn(attn, gv), tn(mixed, gh_low), tn(mlp_in, gp), tn(cot, act)],
+                [tn(attn, gq), tn(attn, gk), tn(attn, gv), tn(mixed, gh_low), tn(mlp_in, gp.array), tn(cot, act.array)],
                 axis=1,
             ),
             ("batch", "seq"), scatter_dimension=0, tiled=True)
@@ -974,9 +1020,9 @@
 
     heads_shape = (H, 64, 64)
     (grad_map_query, grad_map_key, gains), tok = run(
-        unpack_kernel, tok, (1,), [(mine, small_spec), (mine, small_spec), (got, small_spec)],
+        unpack_kernel, tok, (1,), [(mine, small_spec), (got, small_spec)],
         [(heads_shape, F32, whole(heads_shape))] * 2 + [((16, 128), F32, whole((16, 128)))],
-        [pltpu.VMEM((packed, 128), F32)])
+        [pltpu.VMEM((packed, 128), F32)], us=0.1)
     n = D // 128
     return (
         output[None],

time: 269 us -> 244 us (0.907)
  waiting for transfers between devices: 98.6 us -> 82.4 us
  local copies, waits for them, and re-layouts: 21.2 us -> 10.1 us
  starting transfers between devices: 48.3 us -> 54.2 us
    ppermute x26 -> x28, waiting for transfers between devices: 90.4 us -> 49.4 us  [hop(): return lax.ppermute(v, 'seq', [(i, i ^ 1 << bit) for i in range(n_seq)])]
    ppermute x12, waiting for transfers between devices: 4.33 us -> 22.7 us  [to_member(): return lax.ppermute(v, 'seq', [(i, i ^ k) for i in range(n_seq)])]
    unnamed x120 -> x84, local copies, waits for them, and re-layouts: 19.9 us -> 8.79 us
    ppermute x26 -> x28, starting transfers between devices: 21.1 us -> 27.8 us  [hop(): return lax.ppermute(v, 'seq', [(i, i ^ 1 << bit) for i in range(n_seq)])]
    ppermute x5, waiting for transfers between devices: 0.75 us -> 5.51 us  [core_hop(): return lax.ppermute(v, 'batch', [(0, 1), (1, 0)])]
  transfers between devices with their start and end apart: 49 -> 51, of which waited for: 17 -> 20; matrix products, arithmetic and copies ran while one was open for 0% -> 0% of each run, Pallas kernels for 24% -> 26%
where the time goes in v3:
time: 244 us; the launch traced here: 240 us
  Pallas kernels  91.3 us (37%)
  waiting for transfers between devices  82.4 us (34%)
  starting transfers between devices  54.2 us (22%)
  local copies, waits for them, and re-layouts  10.1 us (4%)
    pallas_call x35, Pallas kernels, run(): pl.pallas_call(body, grid=grid, in_specs=[spec for _, spec in ins] + [ANY...  91.3 us
    ppermute x28, waiting for transfers between devices, hop(): return lax.ppermute(v, 'seq', [(i, i ^ 1 << bit) for i in range(n_seq)])  49.4 us
    ppermute x28, starting transfers between devices, hop(): return lax.ppermute(v, 'seq', [(i, i ^ 1 << bit) for i in range(n_seq)])  27.8 us
    ppermute x12, waiting for transfers between devices, to_member(): return lax.ppermute(v, 'seq', [(i, i ^ k) for i in range(n_seq)])  22.7 us
    ppermute x12, starting transfers between devices, to_member(): return lax.ppermute(v, 'seq', [(i, i ^ k) for i in range(n_seq)])  15.5 us
    ppermute x6, starting transfers between devices, shift(): return lax.ppermute(v, 'seq', [(i, (i + by) % n_seq) for i in range(n_seq)])  10.6 us
    unnamed x84, local copies, waits for them, and re-layouts  8.79 us
    ppermute x5, waiting for transfers between devices, core_hop(): return lax.ppermute(v, 'batch', [(0, 1), (1, 0)])  5.51 us
  transfers between devices with their start and end apart: 51, of which 20 were waited for; matrix products, arithmetic and copies ran while one was open for 0% of the time, Pallas kernels for 26%

profile of v3, /device:TPU:0, one launch (start us, length us, event | category | flops | bytes accessed | tf_op | source)
XLA Modules:
  0.0 239.6 jit_solution(1718660925037787265)
XLA Ops:
  2.0 8.8 %shard_map.195 = (bf16[512,768]{1,0:T(8,128)(2,1)S(1)}, bf16[512,768]{1,0:T(8,128)(2,1)S(1)}, bf16[512,768]{1,0:T(8,128)(2,1)S(1)}, bf16[512,1536]{1,0:T(8,128)(...) custom-call(bf16[512,768]{1,0:T(8,128)(2,1)} %bitcast.18, ...), custom_call_target="tpu_custom_call" | custom-call | flops 9200000000 | tf_op jit(solution)/shard_map/pallas_call | solution.py:152
  10.9 3.0 %collective-permute-start = (f32[3,72,128]{2,1,0:T(8,128)S(1)}, f32[3,72,128]{2,1,0:T(8,128)S(1)}, u32[]{:S(2)}, u32[]{:S(2)}) collective-permute-start(f32[3,72,128]{2,1,0:T(8,128)S(1)} %get-tuple-element.201), channel_id=1, source_target_pairs={{0,1},{1,0},{2,3},{3,2},{4,5},{5,4},{6,7},{7,6},{8,9},{9,8},{10,11... | collective-permute-start | bytes 331784 | tf_op jit(solution)/shard_map/ppermute | solution.py:660
  13.9 1.5 collective-permute-start.1
  15.5 8.0 %shard_map.196 = (bf16[512,768]{1,0:T(8,128)(2,1)S(1)}, bf16[512,1536]{1,0:T(8,128)(2,1)S(1)}, f32[512,1536]{1,0:T(8,128)S(1)}, f32[8,128]{1,0:T(8,128)S(1)}) custom-call(bf16[512,768]{1,0:T(8,128)(2,1)S(1)} %get-tuple-element.193.refs_0_, bf16[768,2304]{1,0:T(8,128)(2,1)S(1)} %copy-done.4, bf16[12,64,64]{2,1,0:T(8,128)(2,1)S(1)} %copy-done.10, ...), custom_call_target="tpu_custom_call" | custom-call | flops 10350000128 | tf_op jit(solution)/shard_map/pallas_call | solution.py:152
  24.6 4.1 %collective-permute-start.5 = (f32[3,72,128]{2,1,0:T(8,128)S(1)}, f32[3,72,128]{2,1,0:T(8,128)S(1)}, u32[]{:S(2)}, u32[]{:S(2)}) collective-permute-start(f32[3,72,128]{2,1,0:T(8,128)S(1)} %get-tuple-element.205), channel_id=1, source_target_pairs={{0,12},{1,13},{2,14},{3,15},{4,0},{5,1},{6,2},{7,3},{8,4},{9,5},{1... | collective-permute-start | bytes 331784 | tf_op jit(solution)/shard_map/ppermute | solution.py:663
  28.6 1.2 collective-permute-start.3
  29.8 3.3 %shard_map.198 = (f32[512,3072]{1,0:T(8,128)S(1)}, f32[8,128]{1,0:T(8,128)S(1)}) custom-call(bf16[512,768]{1,0:T(8,128)(2,1)S(1)} %bitcast.16, bf16[3072,768]{1,0:T(8,128)(2,1)S(1)} %bitcast.14, f32[8,128]{1,0:T(8,128)S(1)} %get-tuple-element.206.refs_2_), custom_call_target="tpu_custom_call" | custom-call | flops 4600000000 | tf_op jit(solution)/shard_map/pallas_call | solution.py:152
  33.1 4.8 %collective-permute-done.4.refs_5_ = f32[3,72,128]{2,1,0:T(8,128)S(1)} collective-permute-done((f32[3,72,128]{2,1,0:T(8,128)S(1)}, f32[3,72,128]{2,1,0:T(8,128)S(1)}, u32[]{:S(2)}, u32[]{:S(2)}) %collective-permute-start.4) | collective-permute-done | bytes 110624 | tf_op jit(solution)/shard_map/ppermute | solution.py:663
  38.0 1.6 collective-permute-start.6
  39.6 1.5 collective-permute-start.7
  43.2 1.5 copy-done.13
  45.5 1.2 collective-permute-done.8.refs_6_.refs_10_
  46.8 4.6 %shard_map.202 = (bf16[512,768]{1,0:T(8,128)(2,1)S(1)}, f32[512,768]{1,0:T(8,128)S(1)}, f32[512,768]{1,0:T(8,128)S(1)}, f32[512,768]{1,0:T(8,128)S(1)}, bf16[512...) custom-call(bf16[512,768]{1,0:T(8,128)(2,1)S(1)} %bitcast.19, f32[512,1536]{1,0:T(8,128)S(1)} %get-tuple-element.198.refs_1_, ...), custom_call_target="tpu_custom_call" | custom-call | flops 5175000064 | tf_op jit(solution)/shard_map/pallas_call | solution.py:152
  53.2 12.2 %shard_map.204 = (bf16[512,3072]{1,0:T(8,128)(2,1)S(1)}, bf16[512,3072]{1,0:T(8,128)(2,1)S(1)}, f32[2,4,384,768]{3,2,1,0:T(8,128)}, f32[8,128]{1,0:T(8,128)S(1)}) custom-call(bf16[512,768]{1,0:T(8,128)(2,1)S(1)} %get-tuple-element.216.refs_0_, f32[512,3072]{1,0:T(8,128)S(1)} %get-tuple-element.217.refs_1_, ...), custom_call_target="tpu_custom_call" | custom-call | flops 11500000256 | tf_op jit(solution)/shard_map/pallas_call | solution.py:152
  65.5 9.7 %shard_map.205 = (f32[512,768]{1,0:T(8,128)}, f32[512,768]{1,0:T(8,128)S(1)}, bf16[512,768]{1,0:T(8,128)(2,1)S(1)}, f32[1,768]{1,0:T(1,128)S(1)}, f32[8,128]{1,0:T(8,128)S(1)}) custom-call(bf16[512,3072]{1,0:T(8,128)(2,1)S(1)} %get-tuple-element.222.refs_0_.refs_1_.refs_8_, bf16[512,3072]{1,0:T(8,128)(2,1)S(1)} %get-tuple-element.223.refs_1_.refs_10_, ...), custom_call_target="tpu_custom_call" | custom-call | flops 9200000000 | tf_op jit(solution)/shard_map/pallas_call | solution.py:152
  75.1 1.1 copy-done.35
  76.3 4.0 %collective-permute-done.9 = f32[2,4,384,768]{3,2,1,0:T(8,128)S(1)} collective-permute-done((f32[2,4,384,768]{3,2,1,0:T(8,128)}, f32[2,4,384,768]{3,2,1,0:T(8,128)S(1)}, u32[]{:S(2)}, u32[]{:S(2)}) %collective-permute-start.9) | collective-permute-done | bytes 9437216 | tf_op jit(solution)/shard_map/ppermute | solution.py:636
  80.3 1.7 shard_map.206
  83.6 4.1 %shard_map.207 = (bf16[512,768]{1,0:T(8,128)(2,1)S(1)}, f32[512,768]{1,0:T(8,128)S(1)}, f32[96,512]{1,0:T(8,128)S(1)}, f32[3,72,128]{2,1,0:T(8,128)S(1)}, f32[3,...) custom-call(bf16[512,768]{1,0:T(8,128)(2,1)S(1)} %get-tuple-element.228.refs_, ...), custom_call_target="tpu_custom_call" | custom-call | flops 5750000128 | tf_op jit(solution)/shard_map/pallas_call | solution.py:152
  88.5 1.6 collective-permute-start.10
  90.2 1.0 collective-permute-start.11
  91.2 7.1 %collective-permute-done.13.refs_1_ = f32[192,768]{1,0:T(8,128)S(1)} collective-permute-done((f32[192,768]{1,0:T(8,128)S(1)}, f32[192,768]{1,0:T(8,128)S(1)}, u32[]{:S(2)}, u32[]{:S(2)}) %collective-permute-start.13) | collective-permute-done | bytes 589856 | tf_op jit(solution)/shard_map/ppermute | solution.py:657
  99.2 3.1 %shard_map.208 = (f32[96,768]{1,0:T(8,128)S(1)}, f32[96,768]{1,0:T(8,128)S(1)}, f32[96,768]{1,0:T(8,128)S(1)}, f32[384,768]{1,0:T(8,128)S(1)}, f32[384,768]{1,0:...) custom-call(f32[192,768]{1,0:T(8,128)S(1)} %get-tuple-element.242.re, ...), custom_call_target="tpu_custom_call" | custom-call | flops 8049999872 | tf_op jit(solution)/shard_map/pallas_call | solution.py:152
  102.3 1.6 collective-permute-done.12.refs_3_
  104.1 2.0 collective-permute-start.17
  106.1 3.2 %collective-permute-start.16 = (f32[3,72,128]{2,1,0:T(8,128)S(1)}, f32[3,72,128]{2,1,0:T(8,128)S(1)}, u32[]{:S(2)}, u32[]{:S(2)}) collective-permute-start(f32[3,72,128]{2,1,0:T(8,128)S(1)} %get-tuple-element.265), channel_id=1, source_target_pairs={{0,12},{1,13},{2,14},{3,15},{4,0},{5,1},{6,2},{7,3},{8,4},{9,5},{1... | collective-permute-start | bytes 331784 | tf_op jit(solution)/shard_map/ppermute | solution.py:663
  109.3 1.0 collective-permute-start.22
  110.8 3.9 %shard_map.210 = (bf16[512,768]{1,0:T(8,128)(2,1)S(1)}, f32[512,1536]{1,0:T(8,128)S(1)}, f32[512,768]{1,0:T(8,128)S(1)}, f32[768,128]{1,0:T(8,128)S(1)}, f32[8,128]{1,0:T(8,128)S(1)}) custom-call(bf16[512,768]{1,0:T(8,128)(2,1)S(1)} %copy-done.26, bf16[512,1536]{1,0:T(8,128)(2,1)S(1)} %copy-done.18, bf16[512,1536]{1,0:T(8,128)(2,1)S(1)} %copy-done.16, ...), custom_call_target="tpu_custom_call" | custom-call | flops 5175000064 | tf_op jit(solution)/shard_map/pallas_call | solution.py:152
  114.6 3.9 %shard_map.211 = (bf16[512,768]{1,0:T(8,128)(2,1)S(1)}, f32[512,1536]{1,0:T(8,128)S(1)}, f32[512,768]{1,0:T(8,128)S(1)}, f32[768,128]{1,0:T(8,128)S(1)}, f32[8,128]{1,0:T(8,128)S(1)}) custom-call(bf16[512,768]{1,0:T(8,128)(2,1)S(1)} %copy-done.26, ...), custom_call_target="tpu_custom_call", output_to_operand_aliasing={{0}: (15, {}), {1}: (16, {}), {2}: (17, {}), {3}: (18, {})} | custom-call | flops 5175000064 | tf_op jit(solution)/shard_map/pallas_call | solution.py:152
  118.5 3.9 %shard_map.212 = (bf16[512,768]{1,0:T(8,128)(2,1)S(1)}, f32[512,1536]{1,0:T(8,128)S(1)}, f32[512,768]{1,0:T(8,128)S(1)}, f32[768,128]{1,0:T(8,128)S(1)}, f32[8,128]{1,0:T(8,128)S(1)}) custom-call(bf16[512,768]{1,0:T(8,128)(2,1)S(1)} %copy-done.26, ...), custom_call_target="tpu_custom_call", output_to_operand_aliasing={{0}: (15, {}), {1}: (16, {}), {2}: (17, {}), {3}: (18, {})} | custom-call | flops 5175000064 | tf_op jit(solution)/shard_map/pallas_call | solution.py:152
  124.7 1.7 collective-permute-start.19
  126.4 19.0 %collective-permute-done.19.refs_6_ = f32[6,72,128]{2,1,0:T(8,128)S(1)} collective-permute-done((f32[6,72,128]{2,1,0:T(8,128)S(1)}, f32[6,72,128]{2,1,0:T(8,128)S(1)}, u32[]{:S(2)}, u32[]{:S(2)}) %collective-permute-start.19) | collective-permute-done | bytes 221216 | tf_op jit(solution)/shard_map/ppermute | solution.py:660
  145.5 1.0 collective-permute-start.20
  146.7 1.2 collective-permute-start.21
  148.0 2.2 shard_map.216
  151.2 1.6 collective-permute-start.27
  152.9 6.1 %shard_map.217 = (bf16[512,768]{1,0:T(8,128)(2,1)S(1)}, bf16[512,768]{1,0:T(8,128)(2,1)S(1)}, f32[768,128]{1,0:T(8,128)S(1)}, f32[8,128]{1,0:T(8,128)S(1)}) custom-call(bf16[512,768]{1,0:T(8,128)(2,1)S(1)} %copy-done.38, bf16[512,1536]{1,0:T(8,128)(2,1)S(1)} %copy-done.16, bf16[512,768]{1,0:T(8,128)(2,1)S(1)} %copy-done.24, ...), custom_call_target="tpu_custom_call" | custom-call | flops 69000003584 | tf_op jit(solution)/shard_map/pallas_call | solution.py:152
  159.1 1.1 shard_map.218
  161.8 4.6 %shard_map.219 = (f32[512,768]{1,0:T(8,128)}, f32[72,768]{1,0:T(8,128)S(1)}, f32[72,768]{1,0:T(8,128)S(1)}, f32[8,128]{1,0:T(8,128)S(1)}) custom-call(bf16[512,768]{1,0:T(8,128)(2,1)S(1)} %get-tuple-element.261.refs_1_.refs_0_, bf16[512,768]{1,0:T(8,128)(2,1)S(1)} %get-tuple-element.287.refs_2_.refs_1_.refs_3_, ...), custom_call_target="tpu_custom_call" | custom-call | flops 69000003584 | tf_op jit(solution)/shard_map/pallas_call | solution.py:152
  166.4 1.5 collective-permute-done.30.refs_8_
  167.9 1.5 shard_map.220
  169.4 1.0 collective-permute-start.38
  170.9 1.1 collective-permute-start.36
  172.0 1.8 collective-permute-start.37
  173.7 3.6 %collective-permute-done.27.refs_3_ = f32[336,768]{1,0:T(8,128)} collective-permute-done((f32[336,768]{1,0:T(8,128)}, f32[336,768]{1,0:T(8,128)}, u32[]{:S(2)}, u32[]{:S(2)}) %collective-permute-start.27) | collective-permute-done | bytes 1032224 | tf_op jit(solution)/shard_map/ppermute | solution.py:657
  177.3 2.0 shard_map.221
  179.5 3.9 %collective-permute-done.38.refs_7_ = f32[72,768]{1,0:T(8,128)S(1)} collective-permute-done((f32[72,768]{1,0:T(8,128)S(1)}, f32[72,768]{1,0:T(8,128)S(1)}, u32[]{:S(2)}, u32[]{:S(2)}) %collective-permute-start.38) | collective-permute-done | bytes 221216 | tf_op jit(solution)/shard_map/ppermute | solution.py:657
  183.5 4.4 %collective-permute-done.35.refs_1_ = f32[192,768]{1,0:T(8,128)S(1)} collective-permute-done((f32[192,768]{1,0:T(8,128)S(1)}, f32[192,768]{1,0:T(8,128)S(1)}, u32[]{:S(2)}, u32[]{:S(2)}) %collective-permute-start.35) | collective-permute-done | bytes 589856 | tf_op jit(solution)/shard_map/ppermute | solution.py:657
  187.8 1.6 collective-permute-start.33
  189.5 1.0 collective-permute-start.34
  190.5 6.0 %collective-permute-done.37.refs_5_ = f32[192,768]{1,0:T(8,128)S(1)} collective-permute-done((f32[192,768]{1,0:T(8,128)S(1)}, f32[192,768]{1,0:T(8,128)S(1)}, u32[]{:S(2)}, u32[]{:S(2)}) %collective-permute-start.37) | collective-permute-done | bytes 589856 | tf_op jit(solution)/shard_map/ppermute | solution.py:657
  196.7 1.0 collective-permute-start.41
  197.8 5.0 %collective-permute-done.32.refs_5_ = f32[96,768]{1,0:T(8,128)S(1)} collective-permute-done((f32[96,768]{1,0:T(8,128)S(1)}, f32[96,768]{1,0:T(8,128)S(1)}, u32[]{:S(2)}, u32[]{:S(2)}) %collective-permute-start.32) | collective-permute-done | bytes 294944 | tf_op jit(solution)/shard_map/ppermute | solution.py:657
  202.8 1.6 collective-permute-start.43
  204.6 4.5 %collective-permute-start.39 = (f32[120,768]{1,0:T(8,128)S(1)}, f32[120,768]{1,0:T(8,128)S(1)}, u32[]{:S(2)}, u32[]{:S(2)}) collective-permute-start(f32[120,768]{1,0:T(8,128)S(1)} %get-tuple-element.335), channel_id=1, source_target_pairs={{0,8},{1,9},{2,10},{3,11},{4,12},{5,13},{6,14},{7,15},{8,0},{9,1},... | collective-permute-start | bytes 1105928 | tf_op jit(solution)/shard_map/ppermute | solution.py:657
  209.0 5.8 %collective-permute-done.42.refs_3_ = f32[96,768]{1,0:T(8,128)S(1)} collective-permute-done((f32[96,768]{1,0:T(8,128)S(1)}, f32[96,768]{1,0:T(8,128)S(1)}, u32[]{:S(2)}, u32[]{:S(2)}) %collective-permute-start.42) | collective-permute-done | bytes 294944 | tf_op jit(solution)/shard_map/ppermute | solution.py:657
  215.0 1.4 collective-permute-start.46
  217.9 4.5 %collective-permute-done.39.refs_2_ = f32[120,768]{1,0:T(8,128)S(1)} collective-permute-done((f32[120,768]{1,0:T(8,128)S(1)}, f32[120,768]{1,0:T(8,128)S(1)}, u32[]{:S(2)}, u32[]{:S(2)}) %collective-permute-start.39) | collective-permute-done | bytes 368672 | tf_op jit(solution)/shard_map/ppermute | solution.py:657
  224.1 2.0 collective-permute-start.49
  226.1 1.8 collective-permute-start.48
  227.9 1.1 collective-permute-start.44
  229.0 1.3 collective-permute-done.49.refs_1_
  230.4 6.6 %collective-permute-done.44.refs_1_ = f32[24,768]{1,0:T(8,128)S(1)} collective-permute-done((f32[24,768]{1,0:T(8,128)S(1)}, f32[24,768]{1,0:T(8,128)S(1)}, u32[]{:S(2)}, u32[]{:S(2)}) %collective-permute-start.44) | collective-permute-done | bytes 73760 | tf_op jit(solution)/shard_map/ppermute | solution.py:657
  237.8 1.0 shard_map.229
  (162 shorter events, 22.4 us)
Async XLA Ops:
  2.0 13.5 %copy-start.4 = (bf16[768,2304]{1,0:T(8,128)(2,1)S(1)}, bf16[768,2304]{1,0:T(8,128)(2,1)}, u32[]{:S(2)}) copy-start(bf16[768,2304]{1,0:T(8,128)(2,1)} %refs_3_.5) | copy-start | bytes 10616836
  2.0 13.5 %copy-start.10 = (bf16[12,64,64]{2,1,0:T(8,128)(2,1)S(1)}, bf16[12,64,64]{2,1,0:T(8,128)(2,1)}, u32[]{:S(2)}) copy-start(bf16[12,64,64]{2,1,0:T(8,128)(2,1)} %refs_14_.5) | copy-start | bytes 294916
  2.0 27.8 %slice-start = ((s8[4718592]{0:T(1024)(128)(4,1)}), s8[4194304]{0:T(1024)(128)(4,1)S(1)}, s32[]{:S(2)}) async-start(s8[4718592]{0:T(1024)(128)(4,1)} %bitcast.13), calls=%async_computation | async-start | bytes 8388608
  10.9 12.7 %copy-start.15 = (bf16[512,1536]{1,0:T(8,128)(2,1)}, bf16[512,1536]{1,0:T(8,128)(2,1)S(1)}, u32[]{:S(2)}) copy-start(bf16[512,1536]{1,0:T(8,128)(2,1)S(1)} %get-tuple-element.194.refs_3_.refs_2_.refs_1_) | copy-start | bytes 4718596
  10.9 12.7 %copy-start.19 = (f32[512,512]{1,0:T(8,128)}, f32[512,512]{1,0:T(8,128)S(1)}, u32[]{:S(2)}) copy-start(f32[512,512]{1,0:T(8,128)S(1)} %get-tuple-element.196.refs_5_.refs_11_) | copy-start | bytes 3145732
  10.9 12.7 %copy-start.21 = (f32[512,512]{1,0:T(8,128)}, f32[512,512]{1,0:T(8,128)S(1)}, u32[]{:S(2)}) copy-start(f32[512,512]{1,0:T(8,128)S(1)} %get-tuple-element.237.refs_12_) | copy-start | bytes 3145732
  10.9 12.7 %copy-start.23 = (bf16[512,768]{1,0:T(8,128)(2,1)}, bf16[512,768]{1,0:T(8,128)(2,1)S(1)}, u32[]{:S(2)}) copy-start(bf16[512,768]{1,0:T(8,128)(2,1)S(1)} %get-tuple-element.195.refs_4_.refs_3_.refs_2_) | copy-start | bytes 2359300
  10.9 12.7 %copy-start.37 = (bf16[512,768]{1,0:T(8,128)(2,1)}, bf16[512,768]{1,0:T(8,128)(2,1)S(1)}, u32[]{:S(2)}) copy-start(bf16[512,768]{1,0:T(8,128)(2,1)S(1)} %get-tuple-element.262.refs_0_) | copy-start | bytes 2359300
  10.9 12.7 %collective-permute-start = (f32[3,72,128]{2,1,0:T(8,128)S(1)}, f32[3,72,128]{2,1,0:T(8,128)S(1)}, u32[]{:S(2)}, u32[]{:S(2)}) collective-permute-start(f32[3,72,128]{2,1,0:T(8,128)S(1)} %get-tuple-element.201), channel_id=1, source_target_pairs={{0,1},{1,0},{2,3},{3,2},{4,5},{5,4},{6,7},{7,6},{8,9},{9,8},{10,11... | collective-permute-start | bytes 331784 | tf_op jit(solution)/shard_map/ppermute | solution.py:660
  13.9 9.7 %collective-permute-start.1 = (f32[3,72,128]{2,1,0:T(8,128)S(1)}, f32[3,72,128]{2,1,0:T(8,128)S(1)}, u32[]{:S(2)}, u32[]{:S(2)}) collective-permute-start(f32[3,72,128]{2,1,0:T(8,128)S(1)} %get-tuple-element.202), channel_id=1, source_target_pairs={{0,2},{1,3},{2,0},{3,1},{4,6},{5,7},{6,4},{7,5},{8,10},{9,11},{10,... | collective-permute-start | bytes 331784 | tf_op jit(solution)/shard_map/ppermute | solution.py:660
  15.4 8.2 %collective-permute-start.2 = (f32[3,72,128]{2,1,0:T(8,128)S(1)}, f32[3,72,128]{2,1,0:T(8,128)S(1)}, u32[]{:S(2)}, u32[]{:S(2)}) collective-permute-start(f32[3,72,128]{2,1,0:T(8,128)S(1)} %get-tuple-element.203), channel_id=1, source_target_pairs={{0,3},{1,2},{2,1},{3,0},{4,7},{5,6},{6,5},{7,4},{8,11},{9,10},{10,... | collective-permute-start | bytes 331784 | tf_op jit(solution)/shard_map/ppermute | solution.py:660
  15.5 14.3 %slice-start.1 = ((s8[4718592]{0:T(1024)(128)(4,1)}), s8[524288]{0:T(1024)(128)(4,1)S(1)}, s32[]{:S(2)}) async-start(s8[4718592]{0:T(1024)(128)(4,1)} %bitcast.13), calls=%async_computation.1 | async-start | bytes 1048576
  23.6 60.0 %copy-start.17 = (bf16[512,1536]{1,0:T(8,128)(2,1)}, bf16[512,1536]{1,0:T(8,128)(2,1)S(1)}, u32[]{:S(2)}) copy-start(bf16[512,1536]{1,0:T(8,128)(2,1)S(1)} %get-tuple-element.199.refs_2_.refs_4_.refs_1_) | copy-start | bytes 4718596
  24.6 8.5 %collective-permute-start.5 = (f32[3,72,128]{2,1,0:T(8,128)S(1)}, f32[3,72,128]{2,1,0:T(8,128)S(1)}, u32[]{:S(2)}, u32[]{:S(2)}) collective-permute-start(f32[3,72,128]{2,1,0:T(8,128)S(1)} %get-tuple-element.205), channel_id=1, source_target_pairs={{0,12},{1,13},{2,14},{3,15},{4,0},{5,1},{6,2},{7,3},{8,4},{9,5},{1... | collective-permute-start | bytes 331784 | tf_op jit(solution)/shard_map/ppermute | solution.py:663
  28.6 9.3 %collective-permute-start.4 = (f32[3,72,128]{2,1,0:T(8,128)S(1)}, f32[3,72,128]{2,1,0:T(8,128)S(1)}, u32[]{:S(2)}, u32[]{:S(2)}) collective-permute-start(f32[3,72,128]{2,1,0:T(8,128)S(1)} %get-tuple-element.205), channel_id=1, source_target_pairs={{0,8},{1,9},{2,10},{3,11},{4,12},{5,13},{6,14},{7,15},{8,0},{9,1},... | collective-permute-start | bytes 331784 | tf_op jit(solution)/shard_map/ppermute | solution.py:663
  28.6 9.3 %collective-permute-start.3 = (f32[3,72,128]{2,1,0:T(8,128)S(1)}, f32[3,72,128]{2,1,0:T(8,128)S(1)}, u32[]{:S(2)}, u32[]{:S(2)}) collective-permute-start(f32[3,72,128]{2,1,0:T(8,128)S(1)} %get-tuple-element.205), channel_id=1, source_target_pairs={{0,4},{1,5},{2,6},{3,7},{4,8},{5,9},{6,10},{7,11},{8,12},{9,13},{1... | collective-permute-start | bytes 331784 | tf_op jit(solution)/shard_map/ppermute | solution.py:663
  38.0 6.7 %collective-permute-start.6 = (f32[3,72,128]{2,1,0:T(8,128)S(1)}, f32[3,72,128]{2,1,0:T(8,128)S(1)}, u32[]{:S(2)}, u32[]{:S(2)}) collective-permute-start(f32[3,72,128]{2,1,0:T(8,128)S(1)} %get-tuple-element.209), channel_id=1, source_target_pairs={{0,1},{1,0},{2,3},{3,2},{4,5},{5,4},{6,7},{7,6},{8,9},{9,8},{10,11... | collective-permute-start | bytes 331784 | tf_op jit(solution)/shard_map/ppermute | solution.py:660
  39.6 5.9 %collective-permute-start.7 = (f32[3,72,128]{2,1,0:T(8,128)S(1)}, f32[3,72,128]{2,1,0:T(8,128)S(1)}, u32[]{:S(2)}, u32[]{:S(2)}) collective-permute-start(f32[3,72,128]{2,1,0:T(8,128)S(1)} %get-tuple-element.210), channel_id=1, source_target_pairs={{0,2},{1,3},{2,0},{3,1},{4,6},{5,7},{6,4},{7,5},{8,10},{9,11},{10,... | collective-permute-start | bytes 331784 | tf_op jit(solution)/shard_map/ppermute | solution.py:660
  41.1 5.6 %collective-permute-start.8 = (f32[3,72,128]{2,1,0:T(8,128)S(1)}, f32[3,72,128]{2,1,0:T(8,128)S(1)}, u32[]{:S(2)}, u32[]{:S(2)}) collective-permute-start(f32[3,72,128]{2,1,0:T(8,128)S(1)} %get-tuple-element.211), channel_id=1, source_target_pairs={{0,3},{1,2},{2,1},{3,0},{4,7},{5,6},{6,5},{7,4},{8,11},{9,10},{10,... | collective-permute-start | bytes 331784 | tf_op jit(solution)/shard_map/ppermute | solution.py:660
  53.2 12.2 %copy-start = (bf16[2,3,384,512]{3,2,1,0:T(8,128)(2,1)}, bf16[2,3,384,512]{3,2,1,0:T(8,128)(2,1)S(1)}, u32[]{:S(2)}) copy-start(bf16[2,3,384,512]{3,2,1,0:T(8,128)(2,1)S(1)} %get-tuple-element.219.refs_2_.refs_7_) | copy-start | bytes 7077892
  53.2 12.2 %copy-start.34 = (f32[512,768]{1,0:T(8,128)S(1)}, f32[512,768]{1,0:T(8,128)}, u32[]{:S(2)}) copy-start(f32[512,768]{1,0:T(8,128)} %copy-done.33) | copy-start | bytes 4718596
  65.4 14.9 %collective-permute-start.9 = (f32[2,4,384,768]{3,2,1,0:T(8,128)}, f32[2,4,384,768]{3,2,1,0:T(8,128)S(1)}, u32[]{:S(2)}, u32[]{:S(2)}) collective-permute-start(f32[2,4,384,768]{3,2,1,0:T(8,128)} %get-tuple-element.231), channel_id=1, source_target_pairs={{0,16},{16,0},{1,17},{17,1},{2,18},{18,2},{3,19},{19,3},{4,20},{20... | collective-permute-start | bytes 28311560 | tf_op jit(solution)/shard_map/ppermute | solution.py:636
  82.0 16.2 %collective-permute-start.13 = (f32[192,768]{1,0:T(8,128)S(1)}, f32[192,768]{1,0:T(8,128)S(1)}, u32[]{:S(2)}, u32[]{:S(2)}) collective-permute-start(f32[192,768]{1,0:T(8,128)S(1)} %get-tuple-element.243), channel_id=1, source_target_pairs={{0,1},{1,0},{2,3},{3,2},{4,5},{5,4},{6,7},{7,6},{8,9},{9,8},{10,11... | collective-permute-start | bytes 1769480 | tf_op jit(solution)/shard_map/ppermute | solution.py:657
  82.7 16.4 %collective-permute-start.14 = (f32[192,768]{1,0:T(8,128)S(1)}, f32[192,768]{1,0:T(8,128)S(1)}, u32[]{:S(2)}, u32[]{:S(2)}) collective-permute-start(f32[192,768]{1,0:T(8,128)S(1)} %get-tuple-element.245), channel_id=1, source_target_pairs={{0,2},{1,3},{2,0},{3,1},{4,6},{5,7},{6,4},{7,5},{8,10},{9,11},{10,... | collective-permute-start | bytes 1769480 | tf_op jit(solution)/shard_map/ppermute | solution.py:657
  83.5 15.6 %collective-permute-start.15 = (f32[192,768]{1,0:T(8,128)S(1)}, f32[192,768]{1,0:T(8,128)S(1)}, u32[]{:S(2)}, u32[]{:S(2)}) collective-permute-start(f32[192,768]{1,0:T(8,128)S(1)} %get-tuple-element.247), channel_id=1, source_target_pairs={{0,4},{1,5},{2,6},{3,7},{4,0},{5,1},{6,2},{7,3},{8,12},{9,13},{10,... | collective-permute-start | bytes 1769480 | tf_op jit(solution)/shard_map/ppermute | solution.py:657
  83.6 15.6 %copy-start.1 = (bf16[2,3,384,512]{3,2,1,0:T(8,128)(2,1)S(1)}, bf16[2,3,384,512]{3,2,1,0:T(8,128)(2,1)}, u32[]{:S(2)}) copy-start(bf16[2,3,384,512]{3,2,1,0:T(8,128)(2,1)} %copy-done) | copy-start | bytes 7077892
  88.5 13.7 %collective-permute-start.10 = (f32[3,72,128]{2,1,0:T(8,128)S(1)}, f32[3,72,128]{2,1,0:T(8,128)S(1)}, u32[]{:S(2)}, u32[]{:S(2)}) collective-permute-start(f32[3,72,128]{2,1,0:T(8,128)S(1)} %get-tuple-element.239), channel_id=1, source_target_pairs={{0,1},{1,0},{2,3},{3,2},{4,5},{5,4},{6,7},{7,6},{8,9},{9,8},{10,11... | collective-permute-start | bytes 331784 | tf_op jit(solution)/shard_map/ppermute | solution.py:660
  90.2 12.1 %collective-permute-start.11 = (f32[3,72,128]{2,1,0:T(8,128)S(1)}, f32[3,72,128]{2,1,0:T(8,128)S(1)}, u32[]{:S(2)}, u32[]{:S(2)}) collective-permute-start(f32[3,72,128]{2,1,0:T(8,128)S(1)} %get-tuple-element.240), channel_id=1, source_target_pairs={{0,2},{1,3},{2,0},{3,1},{4,6},{5,7},{6,4},{7,5},{8,10},{9,11},{10,... | collective-permute-start | bytes 331784 | tf_op jit(solution)/shard_map/ppermute | solution.py:660
  98.2 5.6 %collective-permute-start.12 = (f32[3,72,128]{2,1,0:T(8,128)S(1)}, f32[3,72,128]{2,1,0:T(8,128)S(1)}, u32[]{:S(2)}, u32[]{:S(2)}) collective-permute-start(f32[3,72,128]{2,1,0:T(8,128)S(1)} %get-tuple-element.241), channel_id=1, source_target_pairs={{0,3},{1,2},{2,1},{3,0},{4,7},{5,6},{6,5},{7,4},{8,11},{9,10},{10,... | collective-permute-start | bytes 331784 | tf_op jit(solution)/shard_map/ppermute | solution.py:660
  103.9 18.4 %collective-permute-start.18 = (f32[3,72,128]{2,1,0:T(8,128)S(1)}, f32[3,72,128]{2,1,0:T(8,128)S(1)}, u32[]{:S(2)}, u32[]{:S(2)}) collective-permute-start(f32[3,72,128]{2,1,0:T(8,128)S(1)} %get-tuple-element.265), channel_id=1, source_target_pairs={{0,4},{1,5},{2,6},{3,7},{4,8},{5,9},{6,10},{7,11},{8,12},{9,13},{1... | collective-permute-start | bytes 331784 | tf_op jit(solution)/shard_map/ppermute | solution.py:663
  104.1 18.3 %collective-permute-start.17 = (f32[3,72,128]{2,1,0:T(8,128)S(1)}, f32[3,72,128]{2,1,0:T(8,128)S(1)}, u32[]{:S(2)}, u32[]{:S(2)}) collective-permute-start(f32[3,72,128]{2,1,0:T(8,128)S(1)} %get-tuple-element.265), channel_id=1, source_target_pairs={{0,8},{1,9},{2,10},{3,11},{4,12},{5,13},{6,14},{7,15},{8,0},{9,1},... | collective-permute-start | bytes 331784 | tf_op jit(solution)/shard_map/ppermute | solution.py:663
  106.1 16.3 %collective-permute-start.16 = (f32[3,72,128]{2,1,0:T(8,128)S(1)}, f32[3,72,128]{2,1,0:T(8,128)S(1)}, u32[]{:S(2)}, u32[]{:S(2)}) collective-permute-start(f32[3,72,128]{2,1,0:T(8,128)S(1)} %get-tuple-element.265), channel_id=1, source_target_pairs={{0,12},{1,13},{2,14},{3,15},{4,0},{5,1},{6,2},{7,3},{8,4},{9,5},{1... | collective-permute-start | bytes 331784 | tf_op jit(solution)/shard_map/ppermute | solution.py:663
  109.3 38.6 %collective-permute-start.22 = (f32[480,768]{1,0:T(8,128)S(1)}, f32[480,768]{1,0:T(8,128)S(1)}, u32[]{:S(2)}, u32[]{:S(2)}) collective-permute-start(f32[480,768]{1,0:T(8,128)S(1)} %get-tuple-element.272), channel_id=1, source_target_pairs={{0,2},{1,3},{2,0},{3,1},{4,6},{5,7},{6,4},{7,5},{8,10},{9,11},{10,... | collective-permute-start | bytes 4423688 | tf_op jit(solution)/shard_map/ppermute | solution.py:657
  110.3 37.6 %collective-permute-start.24 = (f32[480,768]{1,0:T(8,128)S(1)}, f32[480,768]{1,0:T(8,128)S(1)}, u32[]{:S(2)}, u32[]{:S(2)}) collective-permute-start(f32[480,768]{1,0:T(8,128)S(1)} %get-tuple-element.276), channel_id=1, source_target_pairs={{0,1},{1,0},{2,3},{3,2},{4,5},{5,4},{6,7},{7,6},{8,9},{9,8},{10,11... | collective-permute-start | bytes 4423688 | tf_op jit(solution)/shard_map/ppermute | solution.py:657
  124.4 23.5 %collective-permute-start.25 = (f32[1,384,768]{2,1,0:T(8,128)S(1)}, f32[1,384,768]{2,1,0:T(8,128)S(1)}, u32[]{:S(2)}, u32[]{:S(2)}) collective-permute-start(f32[1,384,768]{2,1,0:T(8,128)S(1)} %get-tuple-element.284), channel_id=1, source_target_pairs={{0,16},{16,0},{1,17},{17,1},{2,18},{18,2},{3,19},{19,3},{4,20},{20... | collective-permute-start | bytes 3538952 | tf_op jit(solution)/shard_map/ppermute | solution.py:636
  124.5 22.2 %collective-permute-start.23 = (f32[288,768]{1,0:T(8,128)S(1)}, f32[288,768]{1,0:T(8,128)S(1)}, u32[]{:S(2)}, u32[]{:S(2)}) collective-permute-start(f32[288,768]{1,0:T(8,128)S(1)} %get-tuple-element.274), channel_id=1, source_target_pairs={{0,4},{1,5},{2,6},{3,7},{4,0},{5,1},{6,2},{7,3},{8,12},{9,13},{10,... | collective-permute-start | bytes 2654216 | tf_op jit(solution)/shard_map/ppermute | solution.py:657
  124.7 20.8 %collective-permute-start.19 = (f32[6,72,128]{2,1,0:T(8,128)S(1)}, f32[6,72,128]{2,1,0:T(8,128)S(1)}, u32[]{:S(2)}, u32[]{:S(2)}) collective-permute-start(f32[6,72,128]{2,1,0:T(8,128)S(1)} %get-tuple-element.268), channel_id=1, source_target_pairs={{0,1},{1,0},{2,3},{3,2},{4,5},{5,4},{6,7},{7,6},{8,9},{9,8},{10,11... | collective-permute-start | bytes 663560 | tf_op jit(solution)/shard_map/ppermute | solution.py:660
  145.5 7.4 %collective-permute-start.20 = (f32[3,72,128]{2,1,0:T(8,128)S(1)}, f32[3,72,128]{2,1,0:T(8,128)S(1)}, u32[]{:S(2)}, u32[]{:S(2)}) collective-permute-start(f32[3,72,128]{2,1,0:T(8,128)S(1)} %get-tuple-element.269), channel_id=1, source_target_pairs={{0,2},{1,3},{2,0},{3,1},{4,6},{5,7},{6,4},{7,5},{8,10},{9,11},{10,... | collective-permute-start | bytes 331784 | tf_op jit(solution)/shard_map/ppermute | solution.py:660
  146.7 6.2 %collective-permute-start.21 = (f32[3,72,128]{2,1,0:T(8,128)S(1)}, f32[3,72,128]{2,1,0:T(8,128)S(1)}, u32[]{:S(2)}, u32[]{:S(2)}) collective-permute-start(f32[3,72,128]{2,1,0:T(8,128)S(1)} %slice.12), channel_id=1, source_target_pairs={{0,2},{1,3},{2,0},{3,1},{4,6},{5,7},{6,4},{7,5},{8,10},{9,11},{10,... | collective-permute-start | bytes 331784 | tf_op jit(solution)/shard_map/ppermute | solution.py:660
  150.1 20.8 %collective-permute-start.26 = (f32[240,768]{1,0:T(8,128)}, f32[240,768]{1,0:T(8,128)}, u32[]{:S(2)}, u32[]{:S(2)}) collective-permute-start(f32[240,768]{1,0:T(8,128)} %get-tuple-element.298), channel_id=1, source_target_pairs={{0,4},{1,5},{2,6},{3,7},{4,0},{5,1},{6,2},{7,3},{8,12},{9,13},{10,... | collective-permute-start | bytes 2211848 | tf_op jit(solution)/shard_map/ppermute | solution.py:657
  150.4 21.6 %collective-permute-start.28 = (f32[240,768]{1,0:T(8,128)}, f32[240,768]{1,0:T(8,128)}, u32[]{:S(2)}, u32[]{:S(2)}) collective-permute-start(f32[240,768]{1,0:T(8,128)} %get-tuple-element.302), channel_id=1, source_target_pairs={{0,2},{1,3},{2,0},{3,1},{4,6},{5,7},{6,4},{7,5},{8,10},{9,11},{10,... | collective-permute-start | bytes 2211848 | tf_op jit(solution)/shard_map/ppermute | solution.py:657
  151.2 26.1 %collective-permute-start.27 = (f32[336,768]{1,0:T(8,128)}, f32[336,768]{1,0:T(8,128)}, u32[]{:S(2)}, u32[]{:S(2)}) collective-permute-start(f32[336,768]{1,0:T(8,128)} %get-tuple-element.300), channel_id=1, source_target_pairs={{0,1},{1,0},{2,3},{3,2},{4,5},{5,4},{6,7},{7,6},{8,9},{9,8},{10,11... | collective-permute-start | bytes 3096584 | tf_op jit(solution)/shard_map/ppermute | solution.py:657
  160.2 7.7 %collective-permute-start.29 = (f32[3,384,768]{2,1,0:T(8,128)S(1)}, f32[3,384,768]{2,1,0:T(8,128)S(1)}, u32[]{:S(2)}, u32[]{:S(2)}) collective-permute-start(f32[3,384,768]{2,1,0:T(8,128)S(1)} %get-tuple-element.307), channel_id=1, source_target_pairs={{0,16},{16,0},{1,17},{17,1},{2,18},{18,2},{3,19},{19,3},{4,20},{20... | collective-permute-start | bytes 10616840 | tf_op jit(solution)/shard_map/ppermute | solution.py:636
  166.4 1.5 collective-permute-start.30
  169.4 14.1 %collective-permute-start.38 = (f32[72,768]{1,0:T(8,128)S(1)}, f32[72,768]{1,0:T(8,128)S(1)}, u32[]{:S(2)}, u32[]{:S(2)}) collective-permute-start(f32[72,768]{1,0:T(8,128)S(1)} %get-tuple-element.330), channel_id=1, source_target_pairs={{0,8},{1,9},{2,10},{3,11},{4,12},{5,13},{6,14},{7,15},{8,0},{9,1},... | collective-permute-start | bytes 663560 | tf_op jit(solution)/shard_map/ppermute | solution.py:657
  170.4 17.4 %collective-permute-start.35 = (f32[192,768]{1,0:T(8,128)S(1)}, f32[192,768]{1,0:T(8,128)S(1)}, u32[]{:S(2)}, u32[]{:S(2)}) collective-permute-start(f32[192,768]{1,0:T(8,128)S(1)} %get-tuple-element.324), channel_id=1, source_target_pairs={{0,1},{1,0},{2,3},{3,2},{4,5},{5,4},{6,7},{7,6},{8,9},{9,8},{10,11... | collective-permute-start | bytes 1769480 | tf_op jit(solution)/shard_map/ppermute | solution.py:657
  170.9 18.5 %collective-permute-start.36 = (f32[192,768]{1,0:T(8,128)S(1)}, f32[192,768]{1,0:T(8,128)S(1)}, u32[]{:S(2)}, u32[]{:S(2)}) collective-permute-start(f32[192,768]{1,0:T(8,128)S(1)} %get-tuple-element.326), channel_id=1, source_target_pairs={{0,2},{1,3},{2,0},{3,1},{4,6},{5,7},{6,4},{7,5},{8,10},{9,11},{10,... | collective-permute-start | bytes 1769480 | tf_op jit(solution)/shard_map/ppermute | solution.py:657
  172.0 24.5 %collective-permute-start.37 = (f32[192,768]{1,0:T(8,128)S(1)}, f32[192,768]{1,0:T(8,128)S(1)}, u32[]{:S(2)}, u32[]{:S(2)}) collective-permute-start(f32[192,768]{1,0:T(8,128)S(1)} %get-tuple-element.328), channel_id=1, source_target_pairs={{0,4},{1,5},{2,6},{3,7},{4,0},{5,1},{6,2},{7,3},{8,12},{9,13},{10,... | collective-permute-start | bytes 1769480 | tf_op jit(solution)/shard_map/ppermute | solution.py:657
  179.3 18.5 %collective-permute-start.31 = (f32[72,768]{1,0:T(8,128)S(1)}, f32[72,768]{1,0:T(8,128)S(1)}, u32[]{:S(2)}, u32[]{:S(2)}) collective-permute-start(f32[72,768]{1,0:T(8,128)S(1)} %get-tuple-element.313), channel_id=1, source_target_pairs={{0,8},{1,9},{2,10},{3,11},{4,12},{5,13},{6,14},{7,15},{8,0},{9,1},... | collective-permute-start | bytes 663560 | tf_op jit(solution)/shard_map/ppermute | solution.py:657
  183.5 19.3 %collective-permute-start.32 = (f32[96,768]{1,0:T(8,128)S(1)}, f32[96,768]{1,0:T(8,128)S(1)}, u32[]{:S(2)}, u32[]{:S(2)}) collective-permute-start(f32[96,768]{1,0:T(8,128)S(1)} %get-tuple-element.317), channel_id=1, source_target_pairs={{0,4},{1,5},{2,6},{3,7},{4,0},{5,1},{6,2},{7,3},{8,12},{9,13},{10,... | collective-permute-start | bytes 884744 | tf_op jit(solution)/shard_map/ppermute | solution.py:657
  187.8 16.5 %collective-permute-start.33 = (f32[96,768]{1,0:T(8,128)S(1)}, f32[96,768]{1,0:T(8,128)S(1)}, u32[]{:S(2)}, u32[]{:S(2)}) collective-permute-start(f32[96,768]{1,0:T(8,128)S(1)} %get-tuple-element.319), channel_id=1, source_target_pairs={{0,1},{1,0},{2,3},{3,2},{4,5},{5,4},{6,7},{7,6},{8,9},{9,8},{10,11... | collective-permute-start | bytes 884744 | tf_op jit(solution)/shard_map/ppermute | solution.py:657
  189.5 14.9 %collective-permute-start.34 = (f32[144,768]{1,0:T(8,128)S(1)}, f32[144,768]{1,0:T(8,128)S(1)}, u32[]{:S(2)}, u32[]{:S(2)}) collective-permute-start(f32[144,768]{1,0:T(8,128)S(1)} %get-tuple-element.321), channel_id=1, source_target_pairs={{0,2},{1,3},{2,0},{3,1},{4,6},{5,7},{6,4},{7,5},{8,10},{9,11},{10,... | collective-permute-start | bytes 1327112 | tf_op jit(solution)/shard_map/ppermute | solution.py:657
  196.7 12.3 %collective-permute-start.41 = (f32[96,768]{1,0:T(8,128)S(1)}, f32[96,768]{1,0:T(8,128)S(1)}, u32[]{:S(2)}, u32[]{:S(2)}) collective-permute-start(f32[96,768]{1,0:T(8,128)S(1)} %get-tuple-element.341), channel_id=1, source_target_pairs={{0,2},{1,3},{2,0},{3,1},{4,6},{5,7},{6,4},{7,5},{8,10},{9,11},{10,... | collective-permute-start | bytes 884744 | tf_op jit(solution)/shard_map/ppermute | solution.py:657
  197.7 17.1 %collective-permute-start.42 = (f32[96,768]{1,0:T(8,128)S(1)}, f32[96,768]{1,0:T(8,128)S(1)}, u32[]{:S(2)}, u32[]{:S(2)}) collective-permute-start(f32[96,768]{1,0:T(8,128)S(1)} %get-tuple-element.343), channel_id=1, source_target_pairs={{0,4},{1,5},{2,6},{3,7},{4,0},{5,1},{6,2},{7,3},{8,12},{9,13},{10,... | collective-permute-start | bytes 884744 | tf_op jit(solution)/shard_map/ppermute | solution.py:657
  202.8 12.0 %collective-permute-start.43 = (f32[168,768]{1,0:T(8,128)S(1)}, f32[168,768]{1,0:T(8,128)S(1)}, u32[]{:S(2)}, u32[]{:S(2)}) collective-permute-start(f32[168,768]{1,0:T(8,128)S(1)} %get-tuple-element.345), channel_id=1, source_target_pairs={{0,1},{1,0},{2,3},{3,2},{4,5},{5,4},{6,7},{7,6},{8,9},{9,8},{10,11... | collective-permute-start | bytes 1548296 | tf_op jit(solution)/shard_map/ppermute | solution.py:657
  204.5 13.5 %collective-permute-start.40 = (f32[48,768]{1,0:T(8,128)S(1)}, f32[48,768]{1,0:T(8,128)S(1)}, u32[]{:S(2)}, u32[]{:S(2)}) collective-permute-start(f32[48,768]{1,0:T(8,128)S(1)} %get-tuple-element.339), channel_id=1, source_target_pairs={{0,4},{1,5},{2,6},{3,7},{4,0},{5,1},{6,2},{7,3},{8,12},{9,13},{10,... | collective-permute-start | bytes 442376 | tf_op jit(solution)/shard_map/ppermute | solution.py:657
  204.6 17.9 %collective-permute-start.39 = (f32[120,768]{1,0:T(8,128)S(1)}, f32[120,768]{1,0:T(8,128)S(1)}, u32[]{:S(2)}, u32[]{:S(2)}) collective-permute-start(f32[120,768]{1,0:T(8,128)S(1)} %get-tuple-element.335), channel_id=1, source_target_pairs={{0,8},{1,9},{2,10},{3,11},{4,12},{5,13},{6,14},{7,15},{8,0},{9,1},... | collective-permute-start | bytes 1105928 | tf_op jit(solution)/shard_map/ppermute | solution.py:657
  214.9 8.5 %collective-permute-start.45 = (f32[48,768]{1,0:T(8,128)S(1)}, f32[48,768]{1,0:T(8,128)S(1)}, u32[]{:S(2)}, u32[]{:S(2)}) collective-permute-start(f32[48,768]{1,0:T(8,128)S(1)} %get-tuple-element.352), channel_id=1, source_target_pairs={{0,4},{1,5},{2,6},{3,7},{4,0},{5,1},{6,2},{7,3},{8,12},{9,13},{10,... | collective-permute-start | bytes 442376 | tf_op jit(solution)/shard_map/ppermute | solution.py:657
  215.0 8.4 %collective-permute-start.46 = (f32[48,768]{1,0:T(8,128)S(1)}, f32[48,768]{1,0:T(8,128)S(1)}, u32[]{:S(2)}, u32[]{:S(2)}) collective-permute-start(f32[48,768]{1,0:T(8,128)S(1)} %get-tuple-element.354), channel_id=1, source_target_pairs={{0,1},{1,0},{2,3},{3,2},{4,5},{5,4},{6,7},{7,6},{8,9},{9,8},{10,11... | collective-permute-start | bytes 442376 | tf_op jit(solution)/shard_map/ppermute | solution.py:657
  216.5 7.5 %collective-permute-start.47 = (f32[120,768]{1,0:T(8,128)S(1)}, f32[120,768]{1,0:T(8,128)S(1)}, u32[]{:S(2)}, u32[]{:S(2)}) collective-permute-start(f32[120,768]{1,0:T(8,128)S(1)} %get-tuple-element.356), channel_id=1, source_target_pairs={{0,2},{1,3},{2,0},{3,1},{4,6},{5,7},{6,4},{7,5},{8,10},{9,11},{10,... | collective-permute-start | bytes 1105928 | tf_op jit(solution)/shard_map/ppermute | solution.py:657
  224.1 6.3 %collective-permute-start.49 = (f32[72,768]{1,0:T(8,128)S(1)}, f32[72,768]{1,0:T(8,128)S(1)}, u32[]{:S(2)}, u32[]{:S(2)}) collective-permute-start(f32[72,768]{1,0:T(8,128)S(1)} %get-tuple-element.364), channel_id=1, source_target_pairs={{0,4},{1,5},{2,6},{3,7},{4,0},{5,1},{6,2},{7,3},{8,12},{9,13},{10,... | collective-permute-start | bytes 663560 | tf_op jit(solution)/shard_map/ppermute | solution.py:657
  226.1 11.0 %collective-permute-start.48 = (f32[72,768]{1,0:T(8,128)S(1)}, f32[72,768]{1,0:T(8,128)S(1)}, u32[]{:S(2)}, u32[]{:S(2)}) collective-permute-start(f32[72,768]{1,0:T(8,128)S(1)} %get-tuple-element.360), channel_id=1, source_target_pairs={{0,8},{1,9},{2,10},{3,11},{4,12},{5,13},{6,14},{7,15},{8,0},{9,1},... | collective-permute-start | bytes 663560 | tf_op jit(solution)/shard_map/ppermute | solution.py:657
  227.9 9.1 %collective-permute-start.44 = (f32[24,768]{1,0:T(8,128)S(1)}, f32[24,768]{1,0:T(8,128)S(1)}, u32[]{:S(2)}, u32[]{:S(2)}) collective-permute-start(f32[24,768]{1,0:T(8,128)S(1)} %get-tuple-element.350), channel_id=1, source_target_pairs={{0,8},{1,9},{2,10},{3,11},{4,12},{5,13},{6,14},{7,15},{8,0},{9,1},... | collective-permute-start | bytes 221192 | tf_op jit(solution)/shard_map/ppermute | solution.py:657
  230.4 7.4 %collective-permute-start.50 = (f32[72,768]{1,0:T(8,128)S(1)}, f32[72,768]{1,0:T(8,128)S(1)}, u32[]{:S(2)}, u32[]{:S(2)}) collective-permute-start(f32[72,768]{1,0:T(8,128)S(1)} %get-tuple-element.371.refs_0_), channel_id=1, source_target_pairs={{0,16},{16,0},{1,17},{17,1},{2,18},{18,2},{3,19},{19,3},{4,20},{20... | collective-permute-start | bytes 663560 | tf_op jit(solution)/shard_map/ppermute | solution.py:636
  (29 other events, 137.2 us)

commit v4 on v3

--- a/solution.py
+++ b/solution.py
@@ -127,7 +127,7 @@
     pass
 
 
-def run(kernel, tok, grid, ins, outs, scratch=(), extra=4, aliases=None, us=1.0):
+def run(kernel, tok, grid, ins, outs, scratch=(), extra=3, aliases=None, us=1.0):
     n_in, n_out = len(ins), len(outs)
     linked = tok is not None
     outs = [tuple(out) + (False,) * (4 - len(out)) for out in outs]
@@ -188,7 +188,7 @@
     @pl.when(j == 0)
     def _():
         normed, _ = moments(x_ref[...].astype(F32))
-        attn_ref[...] = (normed * gain_ref[...]).astype(BF16)
+        attn_ref[...] = (normed * gain_ref[...].reshape(1, -1)).astype(BF16)
         last = starts_ref[0, 0]
         for u in range(1, n_flags):
             last = last + starts_ref[0, u]
@@ -352,7 +352,7 @@
     @pl.when(j == pl.num_programs(0) - 1)
     def _():
         normed, _ = moments(hidden_ref[...])
-        mlp_ref[...] = (normed * gain_ref[...]).astype(BF16)
+        mlp_ref[...] = (normed * gain_ref[...].reshape(1, -1)).astype(BF16)
 
 
 GELU_A, GELU_C = 0.044715, 0.7978845608028654
@@ -410,7 +410,7 @@
         normed, scale = moments(hidden_ref[...])
         grad = jnp.concatenate([back_scr[i] for i in range(back_scr.shape[0])], axis=1)
         gg_ref[...] = jnp.sum(grad * normed, axis=0, keepdims=True)
-        gh = cot_ref[...].astype(F32) + norm_back(grad, normed, scale, gain_ref[...])
+        gh = cot_ref[...].astype(F32) + norm_back(grad, normed, scale, gain_ref[...].reshape(1, -1))
         gh_ref[...] = gh
         gh_low_ref[...] = gh.astype(BF16)
 
@@ -553,7 +553,7 @@
     def _():
         grad = acc[...] + nt(gv_ref[...], w_ref[...])
         normed, scale = moments(x_ref[...].astype(F32))
-        gx_ref[...] = gh_ref[...] + norm_back(grad, normed, scale, gain_ref[...])
+        gx_ref[...] = gh_ref[...] + norm_back(grad, normed, scale, gain_ref[...].reshape(1, -1))
         gg = jnp.sum(grad * normed, axis=0, keepdims=True)
         rows = gmq_ref.shape[0]
         n = gg.shape[1] // 128
@@ -650,7 +650,7 @@
     seq = lax.axis_index("seq")
     tok = None
     x, cot = inputs[0], cotangent[0]
-    gain_a, gain_m = gain_attn.reshape(1, D), gain_mlp.reshape(1, D)
+    gain_a, gain_m = gain_attn, gain_mlp
     direct = n_seq == 16
 
     def hop(v, bit):
@@ -668,6 +668,7 @@
     square = whole((T, T))
     full = whole((T, D))
     row = whole((1, D))
+    line = whole((D,))
     maps = pl.BlockSpec((4, 64, 64), lambda j: (j, 0, 0))
     piece = (per, STATE_ROWS, 128)
     piece_spec = whole(piece)
@@ -679,7 +680,7 @@
 
     (attn, k, v, fk, s0, s1, s2, s3, allow, allow_t, tail, contin), tok = run(
         keys_kernel, tok, (quads,),
-        [(Held(x), full), (gain_a, row), (Held(w_qkv), w_cols(1)), (Held(w_qkv), w_cols(2)), (Held(map_key), maps),
+        [(Held(x), full), (Held(gain_a), line), (Held(w_qkv), w_cols(1)), (Held(w_qkv), w_cols(2)), (Held(map_key), maps),
          (Held(key_mask), whole((1, T))), (starts, pl.BlockSpec(memory_space=pltpu.SMEM))],
         [((T, D), BF16, full), ((T, D), BF16, qcol), ((T, D), BF16, qcol), ((T, 2 * D), BF16, fcol)]
         + [(piece, F32, piece_spec)] * 4
@@ -746,7 +747,7 @@
     (mixed, mf, rden, hidden, mlp_in), tok = run(
         mix_kernel, tok, (quads,),
         [(x, full), (nd, fcol), (fq, fcol)] + [(c, piece_spec) for c in carry]
-        + [(contin, col128), (w_out, pl.BlockSpec((QW, D), lambda j: (j, 0))), (gain_m, row)],
+        + [(contin, col128), (w_out, pl.BlockSpec((QW, D), lambda j: (j, 0))), (Held(gain_m), line)],
         [((T, D), BF16, qcol), ((T, D), F32, qcol), ((T, D), F32, qcol), ((T, D), F32, full),
          ((T, D), BF16, full)],
         [state_scr], us=4.5)
@@ -765,7 +766,7 @@
     (output, gh, gh_low, gg_mlp), tok = run(
         mlp_out_kernel, tok, (quads,),
         [(act, whole((T, FF))), (gp, whole((T, FF))), (Held(w_fc), pl.BlockSpec((QW, FF), lambda j: (j, 0))),
-         (Held(w_proj), columns(FF, QW)), (hidden, qcol), (hidden, full), (Held(cot), full), (gain_m, row)],
+         (Held(w_proj), columns(FF, QW)), (hidden, qcol), (hidden, full), (Held(cot), full), (Held(gain_m), line)],
         [((T, D), F32, qcol), ((T, D), F32, full), ((T, D), BF16, full), ((1, D), F32, row)],
         [pltpu.VMEM((quads, T, QW), F32)], us=8.0)
     def send_half(x_t, kinds, ys, tok):
@@ -901,7 +902,7 @@
             return item
 
         plan = {name: tuple(tuple(ref(x) for x in entry) for entry in entries) for name, entries in plan.items()}
-        results, tok = run(functools.partial(wave_kernel, plan), tok, (steps,), ins, outs, us=us, extra=9)
+        results, tok = run(functools.partial(wave_kernel, plan), tok, (steps,), ins, outs, us=us, extra=6)
         for n, put in after:
             put(results[n])
         moved = {bit: Near(hop(results[first_send + n].array, bit)) for n, bit in enumerate(bits)}
@@ -953,7 +954,7 @@
             functools.partial(scores_back_kernel, quad), tok, (1,), ins,
             [((T, D), BF16, fixed((T, QW), quad)), ((T, 2 * D), F32, fixed((T, FW), quad)),
              ((T, D), F32, fixed((T, QW), quad)), ((D, 128), F32, fixed_rows((QW, 128), quad))],
-            [map_scr, state_scr, pltpu.VMEM((T, FW), BF16)], extra=12, aliases=aliases, us=4.5)
+            [map_scr, state_scr, pltpu.VMEM((T, FW), BF16)], extra=7, aliases=aliases, us=4.5)
 
     backs, tok = scores_back(0, [], tok)
     backs, tok = scores_back(1, backs, tok)
@@ -980,7 +981,7 @@
     packed = 2 * SMALL_ROWS * (D // 128)
     (gx, keep, send), tok = run(
         inputs_back_kernel, tok, (3,),
-        [(gq, full), (gk, full), (gv, full), (w_qkv, columns(D, D)), (x, full), (gh, full), (gain_a, row),
+        [(gq, full), (gk, full), (gv, full), (w_qkv, columns(D, D)), (x, full), (gh, full), (Held(gain_a), line),
          (gg_mlp, row), (gmq, whole((D, 128))), (gmk, whole((D, 128)))],
         [((T, D), F32, full)] + [(small_shape, F32, small_spec)] * 2,
         [pltpu.VMEM((T, D), F32), pltpu.VMEM((packed, 128), F32)], us=60.0)

time: 244 us -> 242 us (level)
  local copies, waits for them, and re-layouts: 10.1 us -> 7.38 us
    unnamed x84 -> x64, local copies, waits for them, and re-layouts: 8.79 us -> 6.77 us
where the time goes in v4:
time: 242 us; the launch traced here: 238 us
  Pallas kernels  91.2 us (38%)
  waiting for transfers between devices  83.5 us (35%)
  starting transfers between devices  54.2 us (22%)
  local copies, waits for them, and re-layouts  7.38 us (3%)
    pallas_call x35, Pallas kernels, run(): pl.pallas_call(body, grid=grid, in_specs=[spec for _, spec in ins] + [ANY...  91.2 us
    ppermute x28, waiting for transfers between devices, hop(): return lax.ppermute(v, 'seq', [(i, i ^ 1 << bit) for i in range(n_seq)])  50.4 us
    ppermute x28, starting transfers between devices, hop(): return lax.ppermute(v, 'seq', [(i, i ^ 1 << bit) for i in range(n_seq)])  27.6 us
    ppermute x12, waiting for transfers between devices, to_member(): return lax.ppermute(v, 'seq', [(i, i ^ k) for i in range(n_seq)])  22.8 us
    ppermute x12, starting transfers between devices, to_member(): return lax.ppermute(v, 'seq', [(i, i ^ k) for i in range(n_seq)])  15.6 us
    ppermute x6, starting transfers between devices, shift(): return lax.ppermute(v, 'seq', [(i, (i + by) % n_seq) for i in range(n_seq)])  10.6 us
    unnamed x64, local copies, waits for them, and re-layouts  6.77 us
    ppermute x5, waiting for transfers between devices, core_hop(): return lax.ppermute(v, 'batch', [(0, 1), (1, 0)])  5.5 us
  transfers between devices with their start and end apart: 51, of which 20 were waited for; matrix products, arithmetic and copies ran while one was open for 0% of the time, Pallas kernels for 26%

profile of v4, /device:TPU:0, one launch (start us, length us, event | category | flops | bytes accessed | tf_op | source)
XLA Modules:
  0.0 237.7 jit_solution(13915033135197095889)
XLA Ops:
  1.3 8.9 %shard_map.195 = (bf16[512,768]{1,0:T(8,128)(2,1)S(1)}, bf16[512,768]{1,0:T(8,128)(2,1)S(1)}, bf16[512,768]{1,0:T(8,128)(2,1)S(1)}, bf16[512,1536]{1,0:T(8,128)(...) custom-call(bf16[512,768]{1,0:T(8,128)(2,1)} %bitcast.18, ...), custom_call_target="tpu_custom_call" | custom-call | flops 9200000000 | tf_op jit(solution)/shard_map/pallas_call | solution.py:152
  10.2 3.0 %collective-permute-start = (f32[3,72,128]{2,1,0:T(8,128)S(1)}, f32[3,72,128]{2,1,0:T(8,128)S(1)}, u32[]{:S(2)}, u32[]{:S(2)}) collective-permute-start(f32[3,72,128]{2,1,0:T(8,128)S(1)} %get-tuple-element.201), channel_id=1, source_target_pairs={{0,1},{1,0},{2,3},{3,2},{4,5},{5,4},{6,7},{7,6},{8,9},{9,8},{10,11... | collective-permute-start | bytes 331784 | tf_op jit(solution)/shard_map/ppermute | solution.py:660
  13.2 1.5 collective-permute-start.1
  14.8 8.0 %shard_map.196 = (bf16[512,768]{1,0:T(8,128)(2,1)S(1)}, bf16[512,1536]{1,0:T(8,128)(2,1)S(1)}, f32[512,1536]{1,0:T(8,128)S(1)}, f32[8,128]{1,0:T(8,128)S(1)}) custom-call(bf16[512,768]{1,0:T(8,128)(2,1)S(1)} %get-tuple-element.193.refs_0_, bf16[768,2304]{1,0:T(8,128)(2,1)S(1)} %copy-done, bf16[12,64,64]{2,1,0:T(8,128)(2,1)S(1)} %copy-done.6, ...), custom_call_target="tpu_custom_call" | custom-call | flops 10350000128 | tf_op jit(solution)/shard_map/pallas_call | solution.py:152
  23.7 4.1 %collective-permute-start.5 = (f32[3,72,128]{2,1,0:T(8,128)S(1)}, f32[3,72,128]{2,1,0:T(8,128)S(1)}, u32[]{:S(2)}, u32[]{:S(2)}) collective-permute-start(f32[3,72,128]{2,1,0:T(8,128)S(1)} %get-tuple-element.205), channel_id=1, source_target_pairs={{0,12},{1,13},{2,14},{3,15},{4,0},{5,1},{6,2},{7,3},{8,4},{9,5},{1... | collective-permute-start | bytes 331784 | tf_op jit(solution)/shard_map/ppermute | solution.py:663
  27.8 1.2 collective-permute-start.3
  28.9 3.3 %shard_map.198 = (f32[512,3072]{1,0:T(8,128)S(1)}, f32[8,128]{1,0:T(8,128)S(1)}) custom-call(bf16[512,768]{1,0:T(8,128)(2,1)S(1)} %bitcast.16, bf16[3072,768]{1,0:T(8,128)(2,1)S(1)} %bitcast.14, f32[8,128]{1,0:T(8,128)S(1)} %get-tuple-element.206.refs_2_), custom_call_target="tpu_custom_call" | custom-call | flops 4600000000 | tf_op jit(solution)/shard_map/pallas_call | solution.py:152
  32.2 4.8 %collective-permute-done.4.refs_5_ = f32[3,72,128]{2,1,0:T(8,128)S(1)} collective-permute-done((f32[3,72,128]{2,1,0:T(8,128)S(1)}, f32[3,72,128]{2,1,0:T(8,128)S(1)}, u32[]{:S(2)}, u32[]{:S(2)}) %collective-permute-start.4) | collective-permute-done | bytes 110624 | tf_op jit(solution)/shard_map/ppermute | solution.py:663
  37.1 1.6 collective-permute-start.6
  38.7 1.5 collective-permute-start.7
  42.3 1.5 copy-done.9
  44.6 1.2 collective-permute-done.8.refs_6_.refs_10_
  45.9 5.0 %shard_map.202 = (bf16[512,768]{1,0:T(8,128)(2,1)S(1)}, f32[512,768]{1,0:T(8,128)S(1)}, f32[512,768]{1,0:T(8,128)S(1)}, f32[512,768]{1,0:T(8,128)S(1)}, bf16[512...) custom-call(bf16[512,768]{1,0:T(8,128)(2,1)S(1)} %bitcast.19, f32[512,1536]{1,0:T(8,128)S(1)} %get-tuple-element.198.refs_1_, ...), custom_call_target="tpu_custom_call" | custom-call | flops 5175000064 | tf_op jit(solution)/shard_map/pallas_call | solution.py:152
  51.8 11.3 %shard_map.204 = (bf16[512,3072]{1,0:T(8,128)(2,1)S(1)}, bf16[512,3072]{1,0:T(8,128)(2,1)S(1)}, f32[2,4,384,768]{3,2,1,0:T(8,128)}, f32[8,128]{1,0:T(8,128)S(1)}) custom-call(bf16[512,768]{1,0:T(8,128)(2,1)S(1)} %get-tuple-element.216.refs_0_, f32[512,3072]{1,0:T(8,128)S(1)} %get-tuple-element.217.refs_1_, ...), custom_call_target="tpu_custom_call" | custom-call | flops 11500000256 | tf_op jit(solution)/shard_map/pallas_call | solution.py:152
  63.1 9.7 %shard_map.205 = (f32[512,768]{1,0:T(8,128)}, f32[512,768]{1,0:T(8,128)S(1)}, bf16[512,768]{1,0:T(8,128)(2,1)S(1)}, f32[1,768]{1,0:T(1,128)S(1)}, f32[8,128]{1,0:T(8,128)S(1)}) custom-call(bf16[512,3072]{1,0:T(8,128)(2,1)S(1)} %get-tuple-element.222.refs_0_.refs_1_.refs_8_, bf16[512,3072]{1,0:T(8,128)(2,1)S(1)} %get-tuple-element.223.refs_1_.refs_10_, ...), custom_call_target="tpu_custom_call" | custom-call | flops 9200000000 | tf_op jit(solution)/shard_map/pallas_call | solution.py:152
  72.8 1.2 copy-done.26
  73.9 4.0 %collective-permute-done.9 = f32[2,4,384,768]{3,2,1,0:T(8,128)S(1)} collective-permute-done((f32[2,4,384,768]{3,2,1,0:T(8,128)}, f32[2,4,384,768]{3,2,1,0:T(8,128)S(1)}, u32[]{:S(2)}, u32[]{:S(2)}) %collective-permute-start.9) | collective-permute-done | bytes 9437216 | tf_op jit(solution)/shard_map/ppermute | solution.py:636
  78.0 1.7 shard_map.206
  81.2 4.1 %shard_map.207 = (bf16[512,768]{1,0:T(8,128)(2,1)S(1)}, f32[512,768]{1,0:T(8,128)S(1)}, f32[96,512]{1,0:T(8,128)S(1)}, f32[3,72,128]{2,1,0:T(8,128)S(1)}, f32[3,...) custom-call(bf16[512,768]{1,0:T(8,128)(2,1)S(1)} %get-tuple-element.228.refs_, ...), custom_call_target="tpu_custom_call" | custom-call | flops 5750000128 | tf_op jit(solution)/shard_map/pallas_call | solution.py:152
  85.3 1.7 collective-permute-start.10
  87.0 1.0 collective-permute-start.11
  88.0 7.9 %collective-permute-done.13.refs_1_ = f32[192,768]{1,0:T(8,128)S(1)} collective-permute-done((f32[192,768]{1,0:T(8,128)S(1)}, f32[192,768]{1,0:T(8,128)S(1)}, u32[]{:S(2)}, u32[]{:S(2)}) %collective-permute-start.13) | collective-permute-done | bytes 589856 | tf_op jit(solution)/shard_map/ppermute | solution.py:657
  96.8 3.1 %shard_map.208 = (f32[96,768]{1,0:T(8,128)S(1)}, f32[96,768]{1,0:T(8,128)S(1)}, f32[96,768]{1,0:T(8,128)S(1)}, f32[384,768]{1,0:T(8,128)S(1)}, f32[384,768]{1,0:...) custom-call(f32[192,768]{1,0:T(8,128)S(1)} %get-tuple-element.242.re, ...), custom_call_target="tpu_custom_call" | custom-call | flops 8049999872 | tf_op jit(solution)/shard_map/pallas_call | solution.py:152
  99.9 1.6 collective-permute-done.12.refs_3_
  101.7 2.0 collective-permute-start.17
  103.7 3.2 %collective-permute-start.16 = (f32[3,72,128]{2,1,0:T(8,128)S(1)}, f32[3,72,128]{2,1,0:T(8,128)S(1)}, u32[]{:S(2)}, u32[]{:S(2)}) collective-permute-start(f32[3,72,128]{2,1,0:T(8,128)S(1)} %get-tuple-element.265), channel_id=1, source_target_pairs={{0,12},{1,13},{2,14},{3,15},{4,0},{5,1},{6,2},{7,3},{8,4},{9,5},{1... | collective-permute-start | bytes 331784 | tf_op jit(solution)/shard_map/ppermute | solution.py:663
  106.9 1.0 collective-permute-start.22
  108.4 3.8 %shard_map.210 = (bf16[512,768]{1,0:T(8,128)(2,1)S(1)}, f32[512,1536]{1,0:T(8,128)S(1)}, f32[512,768]{1,0:T(8,128)S(1)}, f32[768,128]{1,0:T(8,128)S(1)}, f32[8,128]{1,0:T(8,128)S(1)}) custom-call(bf16[512,768]{1,0:T(8,128)(2,1)S(1)} %copy-done.23, bf16[512,1536]{1,0:T(8,128)(2,1)S(1)} %copy-done.14, bf16[512,1536]{1,0:T(8,128)(2,1)S(1)} %copy-done.12, ...), custom_call_target="tpu_custom_call" | custom-call | flops 5175000064 | tf_op jit(solution)/shard_map/pallas_call | solution.py:152
  112.3 3.8 %shard_map.211 = (bf16[512,768]{1,0:T(8,128)(2,1)S(1)}, f32[512,1536]{1,0:T(8,128)S(1)}, f32[512,768]{1,0:T(8,128)S(1)}, f32[768,128]{1,0:T(8,128)S(1)}, f32[8,128]{1,0:T(8,128)S(1)}) custom-call(bf16[512,768]{1,0:T(8,128)(2,1)S(1)} %copy-done.23, ...), custom_call_target="tpu_custom_call", output_to_operand_aliasing={{0}: (15, {}), {1}: (16, {}), {2}: (17, {}), {3}: (18, {})} | custom-call | flops 5175000064 | tf_op jit(solution)/shard_map/pallas_call | solution.py:152
  116.1 3.9 %shard_map.212 = (bf16[512,768]{1,0:T(8,128)(2,1)S(1)}, f32[512,1536]{1,0:T(8,128)S(1)}, f32[512,768]{1,0:T(8,128)S(1)}, f32[768,128]{1,0:T(8,128)S(1)}, f32[8,128]{1,0:T(8,128)S(1)}) custom-call(bf16[512,768]{1,0:T(8,128)(2,1)S(1)} %copy-done.23, ...), custom_call_target="tpu_custom_call", output_to_operand_aliasing={{0}: (15, {}), {1}: (16, {}), {2}: (17, {}), {3}: (18, {})} | custom-call | flops 5175000064 | tf_op jit(solution)/shard_map/pallas_call | solution.py:152
  122.3 1.7 collective-permute-start.19
  124.0 19.1 %collective-permute-done.19.refs_6_ = f32[6,72,128]{2,1,0:T(8,128)S(1)} collective-permute-done((f32[6,72,128]{2,1,0:T(8,128)S(1)}, f32[6,72,128]{2,1,0:T(8,128)S(1)}, u32[]{:S(2)}, u32[]{:S(2)}) %collective-permute-start.19) | collective-permute-done | bytes 221216 | tf_op jit(solution)/shard_map/ppermute | solution.py:660
  143.1 1.0 collective-permute-start.20
  144.3 1.2 collective-permute-start.21
  145.6 2.2 shard_map.216
  148.8 1.6 collective-permute-start.27
  150.5 6.1 %shard_map.217 = (bf16[512,768]{1,0:T(8,128)(2,1)S(1)}, bf16[512,768]{1,0:T(8,128)(2,1)S(1)}, f32[768,128]{1,0:T(8,128)S(1)}, f32[8,128]{1,0:T(8,128)S(1)}) custom-call(bf16[512,768]{1,0:T(8,128)(2,1)S(1)} %copy-done.29, bf16[512,1536]{1,0:T(8,128)(2,1)S(1)} %copy-done.12, bf16[512,768]{1,0:T(8,128)(2,1)S(1)} %copy-done.21, ...), custom_call_target="tpu_custom_call" | custom-call | flops 69000003584 | tf_op jit(solution)/shard_map/pallas_call | solution.py:152
  156.6 1.1 shard_map.218
  159.3 5.2 %shard_map.219 = (f32[512,768]{1,0:T(8,128)}, f32[72,768]{1,0:T(8,128)S(1)}, f32[72,768]{1,0:T(8,128)S(1)}, f32[8,128]{1,0:T(8,128)S(1)}) custom-call(bf16[512,768]{1,0:T(8,128)(2,1)S(1)} %get-tuple-element.261.refs_1_.refs_0_, bf16[512,768]{1,0:T(8,128)(2,1)S(1)} %get-tuple-element.287.refs_2_.refs_1_.refs_3_, ...), custom_call_target="tpu_custom_call" | custom-call | flops 69000003584 | tf_op jit(solution)/shard_map/pallas_call | solution.py:152
  164.5 1.5 collective-permute-done.30.refs_8_
  166.0 1.5 shard_map.220
  167.5 1.0 collective-permute-start.38
  169.1 1.1 collective-permute-start.36
  170.2 1.7 collective-permute-start.37
  171.8 2.8 %collective-permute-done.27.refs_3_ = f32[336,768]{1,0:T(8,128)} collective-permute-done((f32[336,768]{1,0:T(8,128)}, f32[336,768]{1,0:T(8,128)}, u32[]{:S(2)}, u32[]{:S(2)}) %collective-permute-start.27) | collective-permute-done | bytes 1032224 | tf_op jit(solution)/shard_map/ppermute | solution.py:657
  174.6 1.9 shard_map.221
  176.6 5.0 %collective-permute-done.38.refs_7_ = f32[72,768]{1,0:T(8,128)S(1)} collective-permute-done((f32[72,768]{1,0:T(8,128)S(1)}, f32[72,768]{1,0:T(8,128)S(1)}, u32[]{:S(2)}, u32[]{:S(2)}) %collective-permute-start.38) | collective-permute-done | bytes 221216 | tf_op jit(solution)/shard_map/ppermute | solution.py:657
  181.6 3.8 %collective-permute-done.35.refs_1_ = f32[192,768]{1,0:T(8,128)S(1)} collective-permute-done((f32[192,768]{1,0:T(8,128)S(1)}, f32[192,768]{1,0:T(8,128)S(1)}, u32[]{:S(2)}, u32[]{:S(2)}) %collective-permute-start.35) | collective-permute-done | bytes 589856 | tf_op jit(solution)/shard_map/ppermute | solution.py:657
  185.4 1.6 collective-permute-start.33
  187.0 1.0 collective-permute-start.34
  188.0 6.6 %collective-permute-done.37.refs_5_ = f32[192,768]{1,0:T(8,128)S(1)} collective-permute-done((f32[192,768]{1,0:T(8,128)S(1)}, f32[192,768]{1,0:T(8,128)S(1)}, u32[]{:S(2)}, u32[]{:S(2)}) %collective-permute-start.37) | collective-permute-done | bytes 589856 | tf_op jit(solution)/shard_map/ppermute | solution.py:657
  194.8 1.2 collective-permute-start.41
  196.0 4.9 %collective-permute-done.32.refs_5_ = f32[96,768]{1,0:T(8,128)S(1)} collective-permute-done((f32[96,768]{1,0:T(8,128)S(1)}, f32[96,768]{1,0:T(8,128)S(1)}, u32[]{:S(2)}, u32[]{:S(2)}) %collective-permute-start.32) | collective-permute-done | bytes 294944 | tf_op jit(solution)/shard_map/ppermute | solution.py:657
  200.9 1.7 collective-permute-start.43
  202.9 4.3 %collective-permute-start.39 = (f32[120,768]{1,0:T(8,128)S(1)}, f32[120,768]{1,0:T(8,128)S(1)}, u32[]{:S(2)}, u32[]{:S(2)}) collective-permute-start(f32[120,768]{1,0:T(8,128)S(1)} %get-tuple-element.335), channel_id=1, source_target_pairs={{0,8},{1,9},{2,10},{3,11},{4,12},{5,13},{6,14},{7,15},{8,0},{9,1},... | collective-permute-start | bytes 1105928 | tf_op jit(solution)/shard_map/ppermute | solution.py:657
  207.2 5.8 %collective-permute-done.42.refs_3_ = f32[96,768]{1,0:T(8,128)S(1)} collective-permute-done((f32[96,768]{1,0:T(8,128)S(1)}, f32[96,768]{1,0:T(8,128)S(1)}, u32[]{:S(2)}, u32[]{:S(2)}) %collective-permute-start.42) | collective-permute-done | bytes 294944 | tf_op jit(solution)/shard_map/ppermute | solution.py:657
  213.1 1.6 collective-permute-start.46
  216.1 4.6 %collective-permute-done.39.refs_2_ = f32[120,768]{1,0:T(8,128)S(1)} collective-permute-done((f32[120,768]{1,0:T(8,128)S(1)}, f32[120,768]{1,0:T(8,128)S(1)}, u32[]{:S(2)}, u32[]{:S(2)}) %collective-permute-start.39) | collective-permute-done | bytes 368672 | tf_op jit(solution)/shard_map/ppermute | solution.py:657
  222.4 2.0 collective-permute-start.49
  224.4 1.5 collective-permute-start.48
  225.9 1.4 collective-permute-start.44
  227.3 1.1 collective-permute-done.49.refs_1_
  228.6 6.6 %collective-permute-done.44.refs_1_ = f32[24,768]{1,0:T(8,128)S(1)} collective-permute-done((f32[24,768]{1,0:T(8,128)S(1)}, f32[24,768]{1,0:T(8,128)S(1)}, u32[]{:S(2)}, u32[]{:S(2)}) %collective-permute-start.44) | collective-permute-done | bytes 73760 | tf_op jit(solution)/shard_map/ppermute | solution.py:657
  235.9 1.0 shard_map.229
  (140 shorter events, 19.5 us)
Async XLA Ops:
  1.3 13.5 %copy-start = (bf16[768,2304]{1,0:T(8,128)(2,1)S(1)}, bf16[768,2304]{1,0:T(8,128)(2,1)}, u32[]{:S(2)}) copy-start(bf16[768,2304]{1,0:T(8,128)(2,1)} %refs_3_.5) | copy-start | bytes 10616836
  1.3 13.5 %copy-start.6 = (bf16[12,64,64]{2,1,0:T(8,128)(2,1)S(1)}, bf16[12,64,64]{2,1,0:T(8,128)(2,1)}, u32[]{:S(2)}) copy-start(bf16[12,64,64]{2,1,0:T(8,128)(2,1)} %refs_14_.5) | copy-start | bytes 294916
  1.3 27.6 %slice-start = ((s8[4718592]{0:T(1024)(128)(4,1)}), s8[4194304]{0:T(1024)(128)(4,1)S(1)}, s32[]{:S(2)}) async-start(s8[4718592]{0:T(1024)(128)(4,1)} %bitcast.13), calls=%async_computation | async-start | bytes 8388608
  10.2 12.6 %copy-start.11 = (bf16[512,1536]{1,0:T(8,128)(2,1)}, bf16[512,1536]{1,0:T(8,128)(2,1)S(1)}, u32[]{:S(2)}) copy-start(bf16[512,1536]{1,0:T(8,128)(2,1)S(1)} %get-tuple-element.194.refs_3_.refs_2_.refs_1_) | copy-start | bytes 4718596
  10.2 12.6 %copy-start.15 = (f32[512,512]{1,0:T(8,128)}, f32[512,512]{1,0:T(8,128)S(1)}, u32[]{:S(2)}) copy-start(f32[512,512]{1,0:T(8,128)S(1)} %get-tuple-element.196.refs_5_.refs_11_) | copy-start | bytes 3145732
  10.2 12.6 %copy-start.17 = (f32[512,512]{1,0:T(8,128)}, f32[512,512]{1,0:T(8,128)S(1)}, u32[]{:S(2)}) copy-start(f32[512,512]{1,0:T(8,128)S(1)} %get-tuple-element.237.refs_12_) | copy-start | bytes 3145732
  10.2 12.6 %copy-start.19 = (bf16[512,768]{1,0:T(8,128)(2,1)}, bf16[512,768]{1,0:T(8,128)(2,1)S(1)}, u32[]{:S(2)}) copy-start(bf16[512,768]{1,0:T(8,128)(2,1)S(1)} %get-tuple-element.195.refs_4_.refs_3_.refs_2_) | copy-start | bytes 2359300
  10.2 12.6 %copy-start.28 = (bf16[512,768]{1,0:T(8,128)(2,1)}, bf16[512,768]{1,0:T(8,128)(2,1)S(1)}, u32[]{:S(2)}) copy-start(bf16[512,768]{1,0:T(8,128)(2,1)S(1)} %get-tuple-element.262.refs_0_) | copy-start | bytes 2359300
  10.2 12.6 %collective-permute-start = (f32[3,72,128]{2,1,0:T(8,128)S(1)}, f32[3,72,128]{2,1,0:T(8,128)S(1)}, u32[]{:S(2)}, u32[]{:S(2)}) collective-permute-start(f32[3,72,128]{2,1,0:T(8,128)S(1)} %get-tuple-element.201), channel_id=1, source_target_pairs={{0,1},{1,0},{2,3},{3,2},{4,5},{5,4},{6,7},{7,6},{8,9},{9,8},{10,11... | collective-permute-start | bytes 331784 | tf_op jit(solution)/shard_map/ppermute | solution.py:660
  13.2 9.6 %collective-permute-start.1 = (f32[3,72,128]{2,1,0:T(8,128)S(1)}, f32[3,72,128]{2,1,0:T(8,128)S(1)}, u32[]{:S(2)}, u32[]{:S(2)}) collective-permute-start(f32[3,72,128]{2,1,0:T(8,128)S(1)} %get-tuple-element.202), channel_id=1, source_target_pairs={{0,2},{1,3},{2,0},{3,1},{4,6},{5,7},{6,4},{7,5},{8,10},{9,11},{10,... | collective-permute-start | bytes 331784 | tf_op jit(solution)/shard_map/ppermute | solution.py:660
  14.8 8.1 %collective-permute-start.2 = (f32[3,72,128]{2,1,0:T(8,128)S(1)}, f32[3,72,128]{2,1,0:T(8,128)S(1)}, u32[]{:S(2)}, u32[]{:S(2)}) collective-permute-start(f32[3,72,128]{2,1,0:T(8,128)S(1)} %get-tuple-element.203), channel_id=1, source_target_pairs={{0,3},{1,2},{2,1},{3,0},{4,7},{5,6},{6,5},{7,4},{8,11},{9,10},{10,... | collective-permute-start | bytes 331784 | tf_op jit(solution)/shard_map/ppermute | solution.py:660
  14.8 14.1 %slice-start.1 = ((s8[4718592]{0:T(1024)(128)(4,1)}), s8[524288]{0:T(1024)(128)(4,1)S(1)}, s32[]{:S(2)}) async-start(s8[4718592]{0:T(1024)(128)(4,1)} %bitcast.13), calls=%async_computation.1 | async-start | bytes 1048576
  22.8 58.4 %copy-start.13 = (bf16[512,1536]{1,0:T(8,128)(2,1)}, bf16[512,1536]{1,0:T(8,128)(2,1)S(1)}, u32[]{:S(2)}) copy-start(bf16[512,1536]{1,0:T(8,128)(2,1)S(1)} %get-tuple-element.199.refs_2_.refs_4_.refs_1_) | copy-start | bytes 4718596
  23.7 8.5 %collective-permute-start.5 = (f32[3,72,128]{2,1,0:T(8,128)S(1)}, f32[3,72,128]{2,1,0:T(8,128)S(1)}, u32[]{:S(2)}, u32[]{:S(2)}) collective-permute-start(f32[3,72,128]{2,1,0:T(8,128)S(1)} %get-tuple-element.205), channel_id=1, source_target_pairs={{0,12},{1,13},{2,14},{3,15},{4,0},{5,1},{6,2},{7,3},{8,4},{9,5},{1... | collective-permute-start | bytes 331784 | tf_op jit(solution)/shard_map/ppermute | solution.py:663
  27.8 9.3 %collective-permute-start.4 = (f32[3,72,128]{2,1,0:T(8,128)S(1)}, f32[3,72,128]{2,1,0:T(8,128)S(1)}, u32[]{:S(2)}, u32[]{:S(2)}) collective-permute-start(f32[3,72,128]{2,1,0:T(8,128)S(1)} %get-tuple-element.205), channel_id=1, source_target_pairs={{0,8},{1,9},{2,10},{3,11},{4,12},{5,13},{6,14},{7,15},{8,0},{9,1},... | collective-permute-start | bytes 331784 | tf_op jit(solution)/shard_map/ppermute | solution.py:663
  27.8 9.3 %collective-permute-start.3 = (f32[3,72,128]{2,1,0:T(8,128)S(1)}, f32[3,72,128]{2,1,0:T(8,128)S(1)}, u32[]{:S(2)}, u32[]{:S(2)}) collective-permute-start(f32[3,72,128]{2,1,0:T(8,128)S(1)} %get-tuple-element.205), channel_id=1, source_target_pairs={{0,4},{1,5},{2,6},{3,7},{4,8},{5,9},{6,10},{7,11},{8,12},{9,13},{1... | collective-permute-start | bytes 331784 | tf_op jit(solution)/shard_map/ppermute | solution.py:663
  37.1 6.7 %collective-permute-start.6 = (f32[3,72,128]{2,1,0:T(8,128)S(1)}, f32[3,72,128]{2,1,0:T(8,128)S(1)}, u32[]{:S(2)}, u32[]{:S(2)}) collective-permute-start(f32[3,72,128]{2,1,0:T(8,128)S(1)} %get-tuple-element.209), channel_id=1, source_target_pairs={{0,1},{1,0},{2,3},{3,2},{4,5},{5,4},{6,7},{7,6},{8,9},{9,8},{10,11... | collective-permute-start | bytes 331784 | tf_op jit(solution)/shard_map/ppermute | solution.py:660
  38.7 5.9 %collective-permute-start.7 = (f32[3,72,128]{2,1,0:T(8,128)S(1)}, f32[3,72,128]{2,1,0:T(8,128)S(1)}, u32[]{:S(2)}, u32[]{:S(2)}) collective-permute-start(f32[3,72,128]{2,1,0:T(8,128)S(1)} %get-tuple-element.210), channel_id=1, source_target_pairs={{0,2},{1,3},{2,0},{3,1},{4,6},{5,7},{6,4},{7,5},{8,10},{9,11},{10,... | collective-permute-start | bytes 331784 | tf_op jit(solution)/shard_map/ppermute | solution.py:660
  40.2 5.6 %collective-permute-start.8 = (f32[3,72,128]{2,1,0:T(8,128)S(1)}, f32[3,72,128]{2,1,0:T(8,128)S(1)}, u32[]{:S(2)}, u32[]{:S(2)}) collective-permute-start(f32[3,72,128]{2,1,0:T(8,128)S(1)} %get-tuple-element.211), channel_id=1, source_target_pairs={{0,3},{1,2},{2,1},{3,0},{4,7},{5,6},{6,5},{7,4},{8,11},{9,10},{10,... | collective-permute-start | bytes 331784 | tf_op jit(solution)/shard_map/ppermute | solution.py:660
  63.1 14.9 %collective-permute-start.9 = (f32[2,4,384,768]{3,2,1,0:T(8,128)}, f32[2,4,384,768]{3,2,1,0:T(8,128)S(1)}, u32[]{:S(2)}, u32[]{:S(2)}) collective-permute-start(f32[2,4,384,768]{3,2,1,0:T(8,128)} %get-tuple-element.231), channel_id=1, source_target_pairs={{0,16},{16,0},{1,17},{17,1},{2,18},{18,2},{3,19},{19,3},{4,20},{20... | collective-permute-start | bytes 28311560 | tf_op jit(solution)/shard_map/ppermute | solution.py:636
  79.6 16.2 %collective-permute-start.13 = (f32[192,768]{1,0:T(8,128)S(1)}, f32[192,768]{1,0:T(8,128)S(1)}, u32[]{:S(2)}, u32[]{:S(2)}) collective-permute-start(f32[192,768]{1,0:T(8,128)S(1)} %get-tuple-element.243), channel_id=1, source_target_pairs={{0,1},{1,0},{2,3},{3,2},{4,5},{5,4},{6,7},{7,6},{8,9},{9,8},{10,11... | collective-permute-start | bytes 1769480 | tf_op jit(solution)/shard_map/ppermute | solution.py:657
  80.3 16.4 %collective-permute-start.14 = (f32[192,768]{1,0:T(8,128)S(1)}, f32[192,768]{1,0:T(8,128)S(1)}, u32[]{:S(2)}, u32[]{:S(2)}) collective-permute-start(f32[192,768]{1,0:T(8,128)S(1)} %get-tuple-element.245), channel_id=1, source_target_pairs={{0,2},{1,3},{2,0},{3,1},{4,6},{5,7},{6,4},{7,5},{8,10},{9,11},{10,... | collective-permute-start | bytes 1769480 | tf_op jit(solution)/shard_map/ppermute | solution.py:657
  81.2 15.6 %collective-permute-start.15 = (f32[192,768]{1,0:T(8,128)S(1)}, f32[192,768]{1,0:T(8,128)S(1)}, u32[]{:S(2)}, u32[]{:S(2)}) collective-permute-start(f32[192,768]{1,0:T(8,128)S(1)} %get-tuple-element.247), channel_id=1, source_target_pairs={{0,4},{1,5},{2,6},{3,7},{4,0},{5,1},{6,2},{7,3},{8,12},{9,13},{10,... | collective-permute-start | bytes 1769480 | tf_op jit(solution)/shard_map/ppermute | solution.py:657
  85.3 14.6 %collective-permute-start.10 = (f32[3,72,128]{2,1,0:T(8,128)S(1)}, f32[3,72,128]{2,1,0:T(8,128)S(1)}, u32[]{:S(2)}, u32[]{:S(2)}) collective-permute-start(f32[3,72,128]{2,1,0:T(8,128)S(1)} %get-tuple-element.239), channel_id=1, source_target_pairs={{0,1},{1,0},{2,3},{3,2},{4,5},{5,4},{6,7},{7,6},{8,9},{9,8},{10,11... | collective-permute-start | bytes 331784 | tf_op jit(solution)/shard_map/ppermute | solution.py:660
  87.0 12.9 %collective-permute-start.11 = (f32[3,72,128]{2,1,0:T(8,128)S(1)}, f32[3,72,128]{2,1,0:T(8,128)S(1)}, u32[]{:S(2)}, u32[]{:S(2)}) collective-permute-start(f32[3,72,128]{2,1,0:T(8,128)S(1)} %get-tuple-element.240), channel_id=1, source_target_pairs={{0,2},{1,3},{2,0},{3,1},{4,6},{5,7},{6,4},{7,5},{8,10},{9,11},{10,... | collective-permute-start | bytes 331784 | tf_op jit(solution)/shard_map/ppermute | solution.py:660
  95.9 5.6 %collective-permute-start.12 = (f32[3,72,128]{2,1,0:T(8,128)S(1)}, f32[3,72,128]{2,1,0:T(8,128)S(1)}, u32[]{:S(2)}, u32[]{:S(2)}) collective-permute-start(f32[3,72,128]{2,1,0:T(8,128)S(1)} %get-tuple-element.241), channel_id=1, source_target_pairs={{0,3},{1,2},{2,1},{3,0},{4,7},{5,6},{6,5},{7,4},{8,11},{9,10},{10,... | collective-permute-start | bytes 331784 | tf_op jit(solution)/shard_map/ppermute | solution.py:660
  96.8 11.6 %copy-start.18 = (f32[512,512]{1,0:T(8,128)S(1)}, f32[512,512]{1,0:T(8,128)}, u32[]{:S(2)}) copy-start(f32[512,512]{1,0:T(8,128)} %copy-done.17) | copy-start | bytes 3145732
  96.8 11.6 %copy-start.20 = (bf16[512,768]{1,0:T(8,128)(2,1)S(1)}, bf16[512,768]{1,0:T(8,128)(2,1)}, u32[]{:S(2)}) copy-start(bf16[512,768]{1,0:T(8,128)(2,1)} %copy-done.19) | copy-start | bytes 2359300
  96.8 11.6 %copy-start.23 = (bf16[512,768]{1,0:T(8,128)(2,1)S(1)}, bf16[512,768]{1,0:T(8,128)(2,1)}, u32[]{:S(2)}) copy-start(bf16[512,768]{1,0:T(8,128)(2,1)} %copy-done.22) | copy-start | bytes 2359300
  101.6 18.4 %collective-permute-start.18 = (f32[3,72,128]{2,1,0:T(8,128)S(1)}, f32[3,72,128]{2,1,0:T(8,128)S(1)}, u32[]{:S(2)}, u32[]{:S(2)}) collective-permute-start(f32[3,72,128]{2,1,0:T(8,128)S(1)} %get-tuple-element.265), channel_id=1, source_target_pairs={{0,4},{1,5},{2,6},{3,7},{4,8},{5,9},{6,10},{7,11},{8,12},{9,13},{1... | collective-permute-start | bytes 331784 | tf_op jit(solution)/shard_map/ppermute | solution.py:663
  101.7 18.3 %collective-permute-start.17 = (f32[3,72,128]{2,1,0:T(8,128)S(1)}, f32[3,72,128]{2,1,0:T(8,128)S(1)}, u32[]{:S(2)}, u32[]{:S(2)}) collective-permute-start(f32[3,72,128]{2,1,0:T(8,128)S(1)} %get-tuple-element.265), channel_id=1, source_target_pairs={{0,8},{1,9},{2,10},{3,11},{4,12},{5,13},{6,14},{7,15},{8,0},{9,1},... | collective-permute-start | bytes 331784 | tf_op jit(solution)/shard_map/ppermute | solution.py:663
  103.7 16.3 %collective-permute-start.16 = (f32[3,72,128]{2,1,0:T(8,128)S(1)}, f32[3,72,128]{2,1,0:T(8,128)S(1)}, u32[]{:S(2)}, u32[]{:S(2)}) collective-permute-start(f32[3,72,128]{2,1,0:T(8,128)S(1)} %get-tuple-element.265), channel_id=1, source_target_pairs={{0,12},{1,13},{2,14},{3,15},{4,0},{5,1},{6,2},{7,3},{8,4},{9,5},{1... | collective-permute-start | bytes 331784 | tf_op jit(solution)/shard_map/ppermute | solution.py:663
  106.9 38.6 %collective-permute-start.22 = (f32[480,768]{1,0:T(8,128)S(1)}, f32[480,768]{1,0:T(8,128)S(1)}, u32[]{:S(2)}, u32[]{:S(2)}) collective-permute-start(f32[480,768]{1,0:T(8,128)S(1)} %get-tuple-element.272), channel_id=1, source_target_pairs={{0,2},{1,3},{2,0},{3,1},{4,6},{5,7},{6,4},{7,5},{8,10},{9,11},{10,... | collective-permute-start | bytes 4423688 | tf_op jit(solution)/shard_map/ppermute | solution.py:657
  108.0 37.5 %collective-permute-start.24 = (f32[480,768]{1,0:T(8,128)S(1)}, f32[480,768]{1,0:T(8,128)S(1)}, u32[]{:S(2)}, u32[]{:S(2)}) collective-permute-start(f32[480,768]{1,0:T(8,128)S(1)} %get-tuple-element.276), channel_id=1, source_target_pairs={{0,1},{1,0},{2,3},{3,2},{4,5},{5,4},{6,7},{7,6},{8,9},{9,8},{10,11... | collective-permute-start | bytes 4423688 | tf_op jit(solution)/shard_map/ppermute | solution.py:657
  122.0 23.5 %collective-permute-start.25 = (f32[1,384,768]{2,1,0:T(8,128)S(1)}, f32[1,384,768]{2,1,0:T(8,128)S(1)}, u32[]{:S(2)}, u32[]{:S(2)}) collective-permute-start(f32[1,384,768]{2,1,0:T(8,128)S(1)} %get-tuple-element.284), channel_id=1, source_target_pairs={{0,16},{16,0},{1,17},{17,1},{2,18},{18,2},{3,19},{19,3},{4,20},{20... | collective-permute-start | bytes 3538952 | tf_op jit(solution)/shard_map/ppermute | solution.py:636
  122.3 22.1 %collective-permute-start.23 = (f32[288,768]{1,0:T(8,128)S(1)}, f32[288,768]{1,0:T(8,128)S(1)}, u32[]{:S(2)}, u32[]{:S(2)}) collective-permute-start(f32[288,768]{1,0:T(8,128)S(1)} %get-tuple-element.274), channel_id=1, source_target_pairs={{0,4},{1,5},{2,6},{3,7},{4,0},{5,1},{6,2},{7,3},{8,12},{9,13},{10,... | collective-permute-start | bytes 2654216 | tf_op jit(solution)/shard_map/ppermute | solution.py:657
  122.3 20.8 %collective-permute-start.19 = (f32[6,72,128]{2,1,0:T(8,128)S(1)}, f32[6,72,128]{2,1,0:T(8,128)S(1)}, u32[]{:S(2)}, u32[]{:S(2)}) collective-permute-start(f32[6,72,128]{2,1,0:T(8,128)S(1)} %get-tuple-element.268), channel_id=1, source_target_pairs={{0,1},{1,0},{2,3},{3,2},{4,5},{5,4},{6,7},{7,6},{8,9},{9,8},{10,11... | collective-permute-start | bytes 663560 | tf_op jit(solution)/shard_map/ppermute | solution.py:660
  143.1 7.3 %collective-permute-start.20 = (f32[3,72,128]{2,1,0:T(8,128)S(1)}, f32[3,72,128]{2,1,0:T(8,128)S(1)}, u32[]{:S(2)}, u32[]{:S(2)}) collective-permute-start(f32[3,72,128]{2,1,0:T(8,128)S(1)} %get-tuple-element.269), channel_id=1, source_target_pairs={{0,2},{1,3},{2,0},{3,1},{4,6},{5,7},{6,4},{7,5},{8,10},{9,11},{10,... | collective-permute-start | bytes 331784 | tf_op jit(solution)/shard_map/ppermute | solution.py:660
  144.3 6.1 %collective-permute-start.21 = (f32[3,72,128]{2,1,0:T(8,128)S(1)}, f32[3,72,128]{2,1,0:T(8,128)S(1)}, u32[]{:S(2)}, u32[]{:S(2)}) collective-permute-start(f32[3,72,128]{2,1,0:T(8,128)S(1)} %slice.12), channel_id=1, source_target_pairs={{0,2},{1,3},{2,0},{3,1},{4,6},{5,7},{6,4},{7,5},{8,10},{9,11},{10,... | collective-permute-start | bytes 331784 | tf_op jit(solution)/shard_map/ppermute | solution.py:660
  147.7 21.4 %collective-permute-start.26 = (f32[240,768]{1,0:T(8,128)}, f32[240,768]{1,0:T(8,128)}, u32[]{:S(2)}, u32[]{:S(2)}) collective-permute-start(f32[240,768]{1,0:T(8,128)} %get-tuple-element.298), channel_id=1, source_target_pairs={{0,4},{1,5},{2,6},{3,7},{4,0},{5,1},{6,2},{7,3},{8,12},{9,13},{10,... | collective-permute-start | bytes 2211848 | tf_op jit(solution)/shard_map/ppermute | solution.py:657
  148.0 22.2 %collective-permute-start.28 = (f32[240,768]{1,0:T(8,128)}, f32[240,768]{1,0:T(8,128)}, u32[]{:S(2)}, u32[]{:S(2)}) collective-permute-start(f32[240,768]{1,0:T(8,128)} %get-tuple-element.302), channel_id=1, source_target_pairs={{0,2},{1,3},{2,0},{3,1},{4,6},{5,7},{6,4},{7,5},{8,10},{9,11},{10,... | collective-permute-start | bytes 2211848 | tf_op jit(solution)/shard_map/ppermute | solution.py:657
  148.8 25.8 %collective-permute-start.27 = (f32[336,768]{1,0:T(8,128)}, f32[336,768]{1,0:T(8,128)}, u32[]{:S(2)}, u32[]{:S(2)}) collective-permute-start(f32[336,768]{1,0:T(8,128)} %get-tuple-element.300), channel_id=1, source_target_pairs={{0,1},{1,0},{2,3},{3,2},{4,5},{5,4},{6,7},{7,6},{8,9},{9,8},{10,11... | collective-permute-start | bytes 3096584 | tf_op jit(solution)/shard_map/ppermute | solution.py:657
  157.7 8.3 %collective-permute-start.29 = (f32[3,384,768]{2,1,0:T(8,128)S(1)}, f32[3,384,768]{2,1,0:T(8,128)S(1)}, u32[]{:S(2)}, u32[]{:S(2)}) collective-permute-start(f32[3,384,768]{2,1,0:T(8,128)S(1)} %get-tuple-element.307), channel_id=1, source_target_pairs={{0,16},{16,0},{1,17},{17,1},{2,18},{18,2},{3,19},{19,3},{4,20},{20... | collective-permute-start | bytes 10616840 | tf_op jit(solution)/shard_map/ppermute | solution.py:636
  164.5 1.5 collective-permute-start.30
  167.5 14.1 %collective-permute-start.38 = (f32[72,768]{1,0:T(8,128)S(1)}, f32[72,768]{1,0:T(8,128)S(1)}, u32[]{:S(2)}, u32[]{:S(2)}) collective-permute-start(f32[72,768]{1,0:T(8,128)S(1)} %get-tuple-element.330), channel_id=1, source_target_pairs={{0,8},{1,9},{2,10},{3,11},{4,12},{5,13},{6,14},{7,15},{8,0},{9,1},... | collective-permute-start | bytes 663560 | tf_op jit(solution)/shard_map/ppermute | solution.py:657
  168.5 16.9 %collective-permute-start.35 = (f32[192,768]{1,0:T(8,128)S(1)}, f32[192,768]{1,0:T(8,128)S(1)}, u32[]{:S(2)}, u32[]{:S(2)}) collective-permute-start(f32[192,768]{1,0:T(8,128)S(1)} %get-tuple-element.324), channel_id=1, source_target_pairs={{0,1},{1,0},{2,3},{3,2},{4,5},{5,4},{6,7},{7,6},{8,9},{9,8},{10,11... | collective-permute-start | bytes 1769480 | tf_op jit(solution)/shard_map/ppermute | solution.py:657
  169.1 17.9 %collective-permute-start.36 = (f32[192,768]{1,0:T(8,128)S(1)}, f32[192,768]{1,0:T(8,128)S(1)}, u32[]{:S(2)}, u32[]{:S(2)}) collective-permute-start(f32[192,768]{1,0:T(8,128)S(1)} %get-tuple-element.326), channel_id=1, source_target_pairs={{0,2},{1,3},{2,0},{3,1},{4,6},{5,7},{6,4},{7,5},{8,10},{9,11},{10,... | collective-permute-start | bytes 1769480 | tf_op jit(solution)/shard_map/ppermute | solution.py:657
  170.2 24.4 %collective-permute-start.37 = (f32[192,768]{1,0:T(8,128)S(1)}, f32[192,768]{1,0:T(8,128)S(1)}, u32[]{:S(2)}, u32[]{:S(2)}) collective-permute-start(f32[192,768]{1,0:T(8,128)S(1)} %get-tuple-element.328), channel_id=1, source_target_pairs={{0,4},{1,5},{2,6},{3,7},{4,0},{5,1},{6,2},{7,3},{8,12},{9,13},{10,... | collective-permute-start | bytes 1769480 | tf_op jit(solution)/shard_map/ppermute | solution.py:657
  176.5 19.5 %collective-permute-start.31 = (f32[72,768]{1,0:T(8,128)S(1)}, f32[72,768]{1,0:T(8,128)S(1)}, u32[]{:S(2)}, u32[]{:S(2)}) collective-permute-start(f32[72,768]{1,0:T(8,128)S(1)} %get-tuple-element.313), channel_id=1, source_target_pairs={{0,8},{1,9},{2,10},{3,11},{4,12},{5,13},{6,14},{7,15},{8,0},{9,1},... | collective-permute-start | bytes 663560 | tf_op jit(solution)/shard_map/ppermute | solution.py:657
  181.6 19.4 %collective-permute-start.32 = (f32[96,768]{1,0:T(8,128)S(1)}, f32[96,768]{1,0:T(8,128)S(1)}, u32[]{:S(2)}, u32[]{:S(2)}) collective-permute-start(f32[96,768]{1,0:T(8,128)S(1)} %get-tuple-element.317), channel_id=1, source_target_pairs={{0,4},{1,5},{2,6},{3,7},{4,0},{5,1},{6,2},{7,3},{8,12},{9,13},{10,... | collective-permute-start | bytes 884744 | tf_op jit(solution)/shard_map/ppermute | solution.py:657
  185.4 17.3 %collective-permute-start.33 = (f32[96,768]{1,0:T(8,128)S(1)}, f32[96,768]{1,0:T(8,128)S(1)}, u32[]{:S(2)}, u32[]{:S(2)}) collective-permute-start(f32[96,768]{1,0:T(8,128)S(1)} %get-tuple-element.319), channel_id=1, source_target_pairs={{0,1},{1,0},{2,3},{3,2},{4,5},{5,4},{6,7},{7,6},{8,9},{9,8},{10,11... | collective-permute-start | bytes 884744 | tf_op jit(solution)/shard_map/ppermute | solution.py:657
  187.0 15.6 %collective-permute-start.34 = (f32[144,768]{1,0:T(8,128)S(1)}, f32[144,768]{1,0:T(8,128)S(1)}, u32[]{:S(2)}, u32[]{:S(2)}) collective-permute-start(f32[144,768]{1,0:T(8,128)S(1)} %get-tuple-element.321), channel_id=1, source_target_pairs={{0,2},{1,3},{2,0},{3,1},{4,6},{5,7},{6,4},{7,5},{8,10},{9,11},{10,... | collective-permute-start | bytes 1327112 | tf_op jit(solution)/shard_map/ppermute | solution.py:657
  194.8 12.3 %collective-permute-start.41 = (f32[96,768]{1,0:T(8,128)S(1)}, f32[96,768]{1,0:T(8,128)S(1)}, u32[]{:S(2)}, u32[]{:S(2)}) collective-permute-start(f32[96,768]{1,0:T(8,128)S(1)} %get-tuple-element.341), channel_id=1, source_target_pairs={{0,2},{1,3},{2,0},{3,1},{4,6},{5,7},{6,4},{7,5},{8,10},{9,11},{10,... | collective-permute-start | bytes 884744 | tf_op jit(solution)/shard_map/ppermute | solution.py:657
  196.0 16.9 %collective-permute-start.42 = (f32[96,768]{1,0:T(8,128)S(1)}, f32[96,768]{1,0:T(8,128)S(1)}, u32[]{:S(2)}, u32[]{:S(2)}) collective-permute-start(f32[96,768]{1,0:T(8,128)S(1)} %get-tuple-element.343), channel_id=1, source_target_pairs={{0,4},{1,5},{2,6},{3,7},{4,0},{5,1},{6,2},{7,3},{8,12},{9,13},{10,... | collective-permute-start | bytes 884744 | tf_op jit(solution)/shard_map/ppermute | solution.py:657
  200.9 12.0 %collective-permute-start.43 = (f32[168,768]{1,0:T(8,128)S(1)}, f32[168,768]{1,0:T(8,128)S(1)}, u32[]{:S(2)}, u32[]{:S(2)}) collective-permute-start(f32[168,768]{1,0:T(8,128)S(1)} %get-tuple-element.345), channel_id=1, source_target_pairs={{0,1},{1,0},{2,3},{3,2},{4,5},{5,4},{6,7},{7,6},{8,9},{9,8},{10,11... | collective-permute-start | bytes 1548296 | tf_op jit(solution)/shard_map/ppermute | solution.py:657
  202.8 13.3 %collective-permute-start.40 = (f32[48,768]{1,0:T(8,128)S(1)}, f32[48,768]{1,0:T(8,128)S(1)}, u32[]{:S(2)}, u32[]{:S(2)}) collective-permute-start(f32[48,768]{1,0:T(8,128)S(1)} %get-tuple-element.339), channel_id=1, source_target_pairs={{0,4},{1,5},{2,6},{3,7},{4,0},{5,1},{6,2},{7,3},{8,12},{9,13},{10,... | collective-permute-start | bytes 442376 | tf_op jit(solution)/shard_map/ppermute | solution.py:657
  202.9 17.7 %collective-permute-start.39 = (f32[120,768]{1,0:T(8,128)S(1)}, f32[120,768]{1,0:T(8,128)S(1)}, u32[]{:S(2)}, u32[]{:S(2)}) collective-permute-start(f32[120,768]{1,0:T(8,128)S(1)} %get-tuple-element.335), channel_id=1, source_target_pairs={{0,8},{1,9},{2,10},{3,11},{4,12},{5,13},{6,14},{7,15},{8,0},{9,1},... | collective-permute-start | bytes 1105928 | tf_op jit(solution)/shard_map/ppermute | solution.py:657
  213.1 8.4 %collective-permute-start.45 = (f32[48,768]{1,0:T(8,128)S(1)}, f32[48,768]{1,0:T(8,128)S(1)}, u32[]{:S(2)}, u32[]{:S(2)}) collective-permute-start(f32[48,768]{1,0:T(8,128)S(1)} %get-tuple-element.352), channel_id=1, source_target_pairs={{0,4},{1,5},{2,6},{3,7},{4,0},{5,1},{6,2},{7,3},{8,12},{9,13},{10,... | collective-permute-start | bytes 442376 | tf_op jit(solution)/shard_map/ppermute | solution.py:657
  213.1 8.4 %collective-permute-start.46 = (f32[48,768]{1,0:T(8,128)S(1)}, f32[48,768]{1,0:T(8,128)S(1)}, u32[]{:S(2)}, u32[]{:S(2)}) collective-permute-start(f32[48,768]{1,0:T(8,128)S(1)} %get-tuple-element.354), channel_id=1, source_target_pairs={{0,1},{1,0},{2,3},{3,2},{4,5},{5,4},{6,7},{7,6},{8,9},{9,8},{10,11... | collective-permute-start | bytes 442376 | tf_op jit(solution)/shard_map/ppermute | solution.py:657
  214.8 7.5 %collective-permute-start.47 = (f32[120,768]{1,0:T(8,128)S(1)}, f32[120,768]{1,0:T(8,128)S(1)}, u32[]{:S(2)}, u32[]{:S(2)}) collective-permute-start(f32[120,768]{1,0:T(8,128)S(1)} %get-tuple-element.356), channel_id=1, source_target_pairs={{0,2},{1,3},{2,0},{3,1},{4,6},{5,7},{6,4},{7,5},{8,10},{9,11},{10,... | collective-permute-start | bytes 1105928 | tf_op jit(solution)/shard_map/ppermute | solution.py:657
  222.4 6.1 %collective-permute-start.49 = (f32[72,768]{1,0:T(8,128)S(1)}, f32[72,768]{1,0:T(8,128)S(1)}, u32[]{:S(2)}, u32[]{:S(2)}) collective-permute-start(f32[72,768]{1,0:T(8,128)S(1)} %get-tuple-element.364), channel_id=1, source_target_pairs={{0,4},{1,5},{2,6},{3,7},{4,0},{5,1},{6,2},{7,3},{8,12},{9,13},{10,... | collective-permute-start | bytes 663560 | tf_op jit(solution)/shard_map/ppermute | solution.py:657
  224.4 10.8 %collective-permute-start.48 = (f32[72,768]{1,0:T(8,128)S(1)}, f32[72,768]{1,0:T(8,128)S(1)}, u32[]{:S(2)}, u32[]{:S(2)}) collective-permute-start(f32[72,768]{1,0:T(8,128)S(1)} %get-tuple-element.360), channel_id=1, source_target_pairs={{0,8},{1,9},{2,10},{3,11},{4,12},{5,13},{6,14},{7,15},{8,0},{9,1},... | collective-permute-start | bytes 663560 | tf_op jit(solution)/shard_map/ppermute | solution.py:657
  225.9 9.3 %collective-permute-start.44 = (f32[24,768]{1,0:T(8,128)S(1)}, f32[24,768]{1,0:T(8,128)S(1)}, u32[]{:S(2)}, u32[]{:S(2)}) collective-permute-start(f32[24,768]{1,0:T(8,128)S(1)} %get-tuple-element.350), channel_id=1, source_target_pairs={{0,8},{1,9},{2,10},{3,11},{4,12},{5,13},{6,14},{7,15},{8,0},{9,1},... | collective-permute-start | bytes 221192 | tf_op jit(solution)/shard_map/ppermute | solution.py:657
  228.5 7.4 %collective-permute-start.50 = (f32[72,768]{1,0:T(8,128)S(1)}, f32[72,768]{1,0:T(8,128)S(1)}, u32[]{:S(2)}, u32[]{:S(2)}) collective-permute-start(f32[72,768]{1,0:T(8,128)S(1)} %get-tuple-element.371.refs_0_), channel_id=1, source_target_pairs={{0,16},{16,0},{1,17},{17,1},{2,18},{18,2},{3,19},{19,3},{4,20},{20... | collective-permute-start | bytes 663560 | tf_op jit(solution)/shard_map/ppermute | solution.py:636
  (19 other events, 69.3 us)

commit v5 on v4

--- a/solution.py
+++ b/solution.py
@@ -923,7 +923,7 @@
 
     (gn, gd, gd_t, s0, s1, s2, s3), tok = run(
         numer_back_kernel, tok, (quads,),
-        [(gh_low, full), (w_out, pl.BlockSpec((QW, D), lambda j: (j, 0))), (mf, qcol), (rden, qcol),
+        [(gh_low, full), (Held(w_out), pl.BlockSpec((QW, D), lambda j: (j, 0))), (mf, qcol), (rden, qcol),
          (fq, fcol), (contin, col128)],
         [((T, D), BF16, qcol), ((T, D), F32, qcol),
          ((8 * H, T), F32, pl.BlockSpec((32, T), lambda j: (j, 0)))] + [(piece, F32, piece_spec)] * 4,
@@ -981,7 +981,7 @@
     packed = 2 * SMALL_ROWS * (D // 128)
     (gx, keep, send), tok = run(
         inputs_back_kernel, tok, (3,),
-        [(gq, full), (gk, full), (gv, full), (w_qkv, columns(D, D)), (x, full), (gh, full), (Held(gain_a), line),
+        [(gq, full), (gk, full), (gv, full), (Held(w_qkv), columns(D, D)), (Held(x), full), (gh, full), (Held(gain_a), line),
          (gg_mlp, row), (gmq, whole((D, 128))), (gmk, whole((D, 128)))],
         [((T, D), F32, full)] + [(small_shape, F32, small_spec)] * 2,
         [pltpu.VMEM((T, D), F32), pltpu.VMEM((packed, 128), F32)], us=60.0)

time: 242 us -> 243 us (level)
  transfers between devices with their start and end apart: 51 -> 51, of which waited for: 20 -> 20; matrix products, arithmetic and copies ran while one was open for 0% -> 0% of each run, Pallas kernels for 26% -> 27%
where the time goes in v5:
time: 243 us; the launch traced here: 238 us
  Pallas kernels  93.1 us (38%)
  waiting for transfers between devices  82.3 us (34%)
  starting transfers between devices  54.6 us (22%)
  local copies, waits for them, and re-layouts  6.61 us (3%)
    pallas_call x35, Pallas kernels, run(): pl.pallas_call(body, grid=grid, in_specs=[spec for _, spec in ins] + [ANY...  93.1 us
    ppermute x28, waiting for transfers between devices, hop(): return lax.ppermute(v, 'seq', [(i, i ^ 1 << bit) for i in range(n_seq)])  49.4 us
    ppermute x28, starting transfers between devices, hop(): return lax.ppermute(v, 'seq', [(i, i ^ 1 << bit) for i in range(n_seq)])  27.9 us
    ppermute x12, waiting for transfers between devices, to_member(): return lax.ppermute(v, 'seq', [(i, i ^ k) for i in range(n_seq)])  22.8 us
    ppermute x12, starting transfers between devices, to_member(): return lax.ppermute(v, 'seq', [(i, i ^ k) for i in range(n_seq)])  15.6 us
    ppermute x6, starting transfers between devices, shift(): return lax.ppermute(v, 'seq', [(i, (i + by) % n_seq) for i in range(n_seq)])  10.5 us
    unnamed x64, local copies, waits for them, and re-layouts  6 us
    ppermute x5, waiting for transfers between devices, core_hop(): return lax.ppermute(v, 'batch', [(0, 1), (1, 0)])  5.25 us
  transfers between devices with their start and end apart: 51, of which 20 were waited for; matrix products, arithmetic and copies ran while one was open for 0% of the time, Pallas kernels for 27%

profile of v5, /device:TPU:0, one launch (start us, length us, event | category | flops | bytes accessed | tf_op | source)
XLA Modules:
  0.0 238.0 jit_solution(3634494071873140065)
XLA Ops:
  1.3 8.9 %shard_map.195 = (bf16[512,768]{1,0:T(8,128)(2,1)S(1)}, bf16[512,768]{1,0:T(8,128)(2,1)S(1)}, bf16[512,768]{1,0:T(8,128)(2,1)S(1)}, bf16[512,1536]{1,0:T(8,128)(...) custom-call(bf16[512,768]{1,0:T(8,128)(2,1)} %bitcast.18, ...), custom_call_target="tpu_custom_call" | custom-call | flops 9200000000 | tf_op jit(solution)/shard_map/pallas_call | solution.py:152
  10.2 3.0 %collective-permute-start = (f32[3,72,128]{2,1,0:T(8,128)S(1)}, f32[3,72,128]{2,1,0:T(8,128)S(1)}, u32[]{:S(2)}, u32[]{:S(2)}) collective-permute-start(f32[3,72,128]{2,1,0:T(8,128)S(1)} %get-tuple-element.201), channel_id=1, source_target_pairs={{0,1},{1,0},{2,3},{3,2},{4,5},{5,4},{6,7},{7,6},{8,9},{9,8},{10,11... | collective-permute-start | bytes 331784 | tf_op jit(solution)/shard_map/ppermute | solution.py:660
  13.2 1.5 collective-permute-start.1
  14.8 8.0 %shard_map.196 = (bf16[512,768]{1,0:T(8,128)(2,1)S(1)}, bf16[512,1536]{1,0:T(8,128)(2,1)S(1)}, f32[512,1536]{1,0:T(8,128)S(1)}, f32[8,128]{1,0:T(8,128)S(1)}) custom-call(bf16[512,768]{1,0:T(8,128)(2,1)S(1)} %get-tuple-element.193.refs_0_, bf16[768,2304]{1,0:T(8,128)(2,1)S(1)} %copy-done, bf16[12,64,64]{2,1,0:T(8,128)(2,1)S(1)} %copy-done.4, ...), custom_call_target="tpu_custom_call" | custom-call | flops 10350000128 | tf_op jit(solution)/shard_map/pallas_call | solution.py:152
  23.8 4.0 %collective-permute-start.5 = (f32[3,72,128]{2,1,0:T(8,128)S(1)}, f32[3,72,128]{2,1,0:T(8,128)S(1)}, u32[]{:S(2)}, u32[]{:S(2)}) collective-permute-start(f32[3,72,128]{2,1,0:T(8,128)S(1)} %get-tuple-element.205), channel_id=1, source_target_pairs={{0,12},{1,13},{2,14},{3,15},{4,0},{5,1},{6,2},{7,3},{8,4},{9,5},{1... | collective-permute-start | bytes 331784 | tf_op jit(solution)/shard_map/ppermute | solution.py:663
  27.8 1.2 collective-permute-start.3
  29.0 3.3 %shard_map.198 = (f32[512,3072]{1,0:T(8,128)S(1)}, f32[8,128]{1,0:T(8,128)S(1)}) custom-call(bf16[512,768]{1,0:T(8,128)(2,1)S(1)} %bitcast.16, bf16[3072,768]{1,0:T(8,128)(2,1)S(1)} %bitcast.14, f32[8,128]{1,0:T(8,128)S(1)} %get-tuple-element.206.refs_2_), custom_call_target="tpu_custom_call" | custom-call | flops 4600000000 | tf_op jit(solution)/shard_map/pallas_call | solution.py:152
  32.3 4.8 %collective-permute-done.4.refs_5_ = f32[3,72,128]{2,1,0:T(8,128)S(1)} collective-permute-done((f32[3,72,128]{2,1,0:T(8,128)S(1)}, f32[3,72,128]{2,1,0:T(8,128)S(1)}, u32[]{:S(2)}, u32[]{:S(2)}) %collective-permute-start.4) | collective-permute-done | bytes 110624 | tf_op jit(solution)/shard_map/ppermute | solution.py:663
  37.2 1.6 collective-permute-start.6
  38.8 1.5 collective-permute-start.7
  42.4 1.5 copy-done.7
  44.7 1.2 collective-permute-done.8.refs_6_.refs_10_
  46.0 5.0 %shard_map.202 = (bf16[512,768]{1,0:T(8,128)(2,1)S(1)}, f32[512,768]{1,0:T(8,128)S(1)}, f32[512,768]{1,0:T(8,128)S(1)}, f32[512,768]{1,0:T(8,128)S(1)}, bf16[512...) custom-call(bf16[512,768]{1,0:T(8,128)(2,1)S(1)} %bitcast.20, f32[512,1536]{1,0:T(8,128)S(1)} %get-tuple-element.198.refs_1_, ...), custom_call_target="tpu_custom_call" | custom-call | flops 5175000064 | tf_op jit(solution)/shard_map/pallas_call | solution.py:152
  52.4 11.3 %shard_map.204 = (bf16[512,3072]{1,0:T(8,128)(2,1)S(1)}, bf16[512,3072]{1,0:T(8,128)(2,1)S(1)}, f32[2,4,384,768]{3,2,1,0:T(8,128)}, f32[8,128]{1,0:T(8,128)S(1)}) custom-call(bf16[512,768]{1,0:T(8,128)(2,1)S(1)} %get-tuple-element.216.refs_0_, f32[512,3072]{1,0:T(8,128)S(1)} %get-tuple-element.217.refs_1_, ...), custom_call_target="tpu_custom_call" | custom-call | flops 11500000256 | tf_op jit(solution)/shard_map/pallas_call | solution.py:152
  63.7 9.7 %shard_map.205 = (f32[512,768]{1,0:T(8,128)}, f32[512,768]{1,0:T(8,128)S(1)}, bf16[512,768]{1,0:T(8,128)(2,1)S(1)}, f32[1,768]{1,0:T(1,128)S(1)}, f32[8,128]{1,0:T(8,128)S(1)}) custom-call(bf16[512,3072]{1,0:T(8,128)(2,1)S(1)} %get-tuple-element.222.refs_0_.refs_1_.refs_8_, bf16[512,3072]{1,0:T(8,128)(2,1)S(1)} %get-tuple-element.223.refs_1_.refs_10_, ...), custom_call_target="tpu_custom_call" | custom-call | flops 9200000000 | tf_op jit(solution)/shard_map/pallas_call | solution.py:152
  73.4 1.2 copy-done.26
  74.5 4.0 %collective-permute-done.9 = f32[2,4,384,768]{3,2,1,0:T(8,128)S(1)} collective-permute-done((f32[2,4,384,768]{3,2,1,0:T(8,128)}, f32[2,4,384,768]{3,2,1,0:T(8,128)S(1)}, u32[]{:S(2)}, u32[]{:S(2)}) %collective-permute-start.9) | collective-permute-done | bytes 9437216 | tf_op jit(solution)/shard_map/ppermute | solution.py:636
  78.5 1.7 shard_map.206
  81.8 4.9 %shard_map.207 = (bf16[512,768]{1,0:T(8,128)(2,1)S(1)}, f32[512,768]{1,0:T(8,128)S(1)}, f32[96,512]{1,0:T(8,128)S(1)}, f32[3,72,128]{2,1,0:T(8,128)S(1)}, f32[3,...) custom-call(bf16[512,768]{1,0:T(8,128)(2,1)S(1)} %get-tuple-element.228.refs_, ...), custom_call_target="tpu_custom_call" | custom-call | flops 5750000128 | tf_op jit(solution)/shard_map/pallas_call | solution.py:152
  86.7 1.7 collective-permute-start.10
  88.4 1.0 collective-permute-start.11
  89.4 7.1 %collective-permute-done.13.refs_1_ = f32[192,768]{1,0:T(8,128)S(1)} collective-permute-done((f32[192,768]{1,0:T(8,128)S(1)}, f32[192,768]{1,0:T(8,128)S(1)}, u32[]{:S(2)}, u32[]{:S(2)}) %collective-permute-start.13) | collective-permute-done | bytes 589856 | tf_op jit(solution)/shard_map/ppermute | solution.py:657
  97.4 3.1 %shard_map.208 = (f32[96,768]{1,0:T(8,128)S(1)}, f32[96,768]{1,0:T(8,128)S(1)}, f32[96,768]{1,0:T(8,128)S(1)}, f32[384,768]{1,0:T(8,128)S(1)}, f32[384,768]{1,0:...) custom-call(f32[192,768]{1,0:T(8,128)S(1)} %get-tuple-element.242.re, ...), custom_call_target="tpu_custom_call" | custom-call | flops 8049999872 | tf_op jit(solution)/shard_map/pallas_call | solution.py:152
  100.5 1.6 collective-permute-done.12.refs_3_
  102.3 2.0 collective-permute-start.17
  104.3 3.2 %collective-permute-start.16 = (f32[3,72,128]{2,1,0:T(8,128)S(1)}, f32[3,72,128]{2,1,0:T(8,128)S(1)}, u32[]{:S(2)}, u32[]{:S(2)}) collective-permute-start(f32[3,72,128]{2,1,0:T(8,128)S(1)} %get-tuple-element.265), channel_id=1, source_target_pairs={{0,12},{1,13},{2,14},{3,15},{4,0},{5,1},{6,2},{7,3},{8,4},{9,5},{1... | collective-permute-start | bytes 331784 | tf_op jit(solution)/shard_map/ppermute | solution.py:663
  107.5 1.0 collective-permute-start.22
  109.0 3.8 %shard_map.210 = (bf16[512,768]{1,0:T(8,128)(2,1)S(1)}, f32[512,1536]{1,0:T(8,128)S(1)}, f32[512,768]{1,0:T(8,128)S(1)}, f32[768,128]{1,0:T(8,128)S(1)}, f32[8,128]{1,0:T(8,128)S(1)}) custom-call(bf16[512,768]{1,0:T(8,128)(2,1)S(1)} %copy-done.21, bf16[512,1536]{1,0:T(8,128)(2,1)S(1)} %copy-done.12, bf16[512,1536]{1,0:T(8,128)(2,1)S(1)} %copy-done.10, ...), custom_call_target="tpu_custom_call" | custom-call | flops 5175000064 | tf_op jit(solution)/shard_map/pallas_call | solution.py:152
  112.8 3.8 %shard_map.211 = (bf16[512,768]{1,0:T(8,128)(2,1)S(1)}, f32[512,1536]{1,0:T(8,128)S(1)}, f32[512,768]{1,0:T(8,128)S(1)}, f32[768,128]{1,0:T(8,128)S(1)}, f32[8,128]{1,0:T(8,128)S(1)}) custom-call(bf16[512,768]{1,0:T(8,128)(2,1)S(1)} %copy-done.21, ...), custom_call_target="tpu_custom_call", output_to_operand_aliasing={{0}: (15, {}), {1}: (16, {}), {2}: (17, {}), {3}: (18, {})} | custom-call | flops 5175000064 | tf_op jit(solution)/shard_map/pallas_call | solution.py:152
  116.7 3.9 %shard_map.212 = (bf16[512,768]{1,0:T(8,128)(2,1)S(1)}, f32[512,1536]{1,0:T(8,128)S(1)}, f32[512,768]{1,0:T(8,128)S(1)}, f32[768,128]{1,0:T(8,128)S(1)}, f32[8,128]{1,0:T(8,128)S(1)}) custom-call(bf16[512,768]{1,0:T(8,128)(2,1)S(1)} %copy-done.21, ...), custom_call_target="tpu_custom_call", output_to_operand_aliasing={{0}: (15, {}), {1}: (16, {}), {2}: (17, {}), {3}: (18, {})} | custom-call | flops 5175000064 | tf_op jit(solution)/shard_map/pallas_call | solution.py:152
  122.9 1.7 collective-permute-start.19
  124.6 19.1 %collective-permute-done.19.refs_6_ = f32[6,72,128]{2,1,0:T(8,128)S(1)} collective-permute-done((f32[6,72,128]{2,1,0:T(8,128)S(1)}, f32[6,72,128]{2,1,0:T(8,128)S(1)}, u32[]{:S(2)}, u32[]{:S(2)}) %collective-permute-start.19) | collective-permute-done | bytes 221216 | tf_op jit(solution)/shard_map/ppermute | solution.py:660
  143.7 1.0 collective-permute-start.20
  144.9 1.2 collective-permute-start.21
  146.1 2.2 shard_map.216
  149.4 1.6 collective-permute-start.27
  151.0 6.1 %shard_map.217 = (bf16[512,768]{1,0:T(8,128)(2,1)S(1)}, bf16[512,768]{1,0:T(8,128)(2,1)S(1)}, f32[768,128]{1,0:T(8,128)S(1)}, f32[8,128]{1,0:T(8,128)S(1)}) custom-call(bf16[512,768]{1,0:T(8,128)(2,1)S(1)} %copy-done.29, bf16[512,1536]{1,0:T(8,128)(2,1)S(1)} %copy-done.10, bf16[512,768]{1,0:T(8,128)(2,1)S(1)} %copy-done.19, ...), custom_call_target="tpu_custom_call" | custom-call | flops 69000003584 | tf_op jit(solution)/shard_map/pallas_call | solution.py:152
  157.1 1.1 shard_map.218
  158.5 6.2 %shard_map.219 = (f32[512,768]{1,0:T(8,128)}, f32[72,768]{1,0:T(8,128)S(1)}, f32[72,768]{1,0:T(8,128)S(1)}, f32[8,128]{1,0:T(8,128)S(1)}) custom-call(bf16[512,768]{1,0:T(8,128)(2,1)S(1)} %get-tuple-element.261.refs_1_.refs_0_, bf16[512,768]{1,0:T(8,128)(2,1)S(1)} %get-tuple-element.287.refs_2_.refs_1_.refs_3_, ...), custom_call_target="tpu_custom_call" | custom-call | flops 69000003584 | tf_op jit(solution)/shard_map/pallas_call | solution.py:152
  165.0 1.2 collective-permute-done.30.refs_8_
  166.3 1.5 shard_map.220
  167.8 1.0 collective-permute-start.38
  169.4 1.1 collective-permute-start.36
  170.5 1.7 collective-permute-start.37
  172.2 3.2 %collective-permute-done.27.refs_3_ = f32[336,768]{1,0:T(8,128)} collective-permute-done((f32[336,768]{1,0:T(8,128)}, f32[336,768]{1,0:T(8,128)}, u32[]{:S(2)}, u32[]{:S(2)}) %collective-permute-start.27) | collective-permute-done | bytes 1032224 | tf_op jit(solution)/shard_map/ppermute | solution.py:657
  175.3 1.9 shard_map.221
  177.4 4.5 %collective-permute-done.38.refs_7_ = f32[72,768]{1,0:T(8,128)S(1)} collective-permute-done((f32[72,768]{1,0:T(8,128)S(1)}, f32[72,768]{1,0:T(8,128)S(1)}, u32[]{:S(2)}, u32[]{:S(2)}) %collective-permute-start.38) | collective-permute-done | bytes 221216 | tf_op jit(solution)/shard_map/ppermute | solution.py:657
  181.8 4.1 %collective-permute-done.35.refs_1_ = f32[192,768]{1,0:T(8,128)S(1)} collective-permute-done((f32[192,768]{1,0:T(8,128)S(1)}, f32[192,768]{1,0:T(8,128)S(1)}, u32[]{:S(2)}, u32[]{:S(2)}) %collective-permute-start.35) | collective-permute-done | bytes 589856 | tf_op jit(solution)/shard_map/ppermute | solution.py:657
  186.0 1.6 collective-permute-start.33
  187.6 1.0 collective-permute-start.34
  188.6 6.4 %collective-permute-done.37.refs_5_ = f32[192,768]{1,0:T(8,128)S(1)} collective-permute-done((f32[192,768]{1,0:T(8,128)S(1)}, f32[192,768]{1,0:T(8,128)S(1)}, u32[]{:S(2)}, u32[]{:S(2)}) %collective-permute-start.37) | collective-permute-done | bytes 589856 | tf_op jit(solution)/shard_map/ppermute | solution.py:657
  195.2 1.2 collective-permute-start.41
  196.4 4.9 %collective-permute-done.32.refs_5_ = f32[96,768]{1,0:T(8,128)S(1)} collective-permute-done((f32[96,768]{1,0:T(8,128)S(1)}, f32[96,768]{1,0:T(8,128)S(1)}, u32[]{:S(2)}, u32[]{:S(2)}) %collective-permute-start.32) | collective-permute-done | bytes 294944 | tf_op jit(solution)/shard_map/ppermute | solution.py:657
  201.2 1.7 collective-permute-start.43
  203.2 4.4 %collective-permute-start.39 = (f32[120,768]{1,0:T(8,128)S(1)}, f32[120,768]{1,0:T(8,128)S(1)}, u32[]{:S(2)}, u32[]{:S(2)}) collective-permute-start(f32[120,768]{1,0:T(8,128)S(1)} %get-tuple-element.335), channel_id=1, source_target_pairs={{0,8},{1,9},{2,10},{3,11},{4,12},{5,13},{6,14},{7,15},{8,0},{9,1},... | collective-permute-start | bytes 1105928 | tf_op jit(solution)/shard_map/ppermute | solution.py:657
  207.6 5.6 %collective-permute-done.42.refs_3_ = f32[96,768]{1,0:T(8,128)S(1)} collective-permute-done((f32[96,768]{1,0:T(8,128)S(1)}, f32[96,768]{1,0:T(8,128)S(1)}, u32[]{:S(2)}, u32[]{:S(2)}) %collective-permute-start.42) | collective-permute-done | bytes 294944 | tf_op jit(solution)/shard_map/ppermute | solution.py:657
  213.4 1.7 collective-permute-start.46
  216.4 4.7 %collective-permute-done.39.refs_2_ = f32[120,768]{1,0:T(8,128)S(1)} collective-permute-done((f32[120,768]{1,0:T(8,128)S(1)}, f32[120,768]{1,0:T(8,128)S(1)}, u32[]{:S(2)}, u32[]{:S(2)}) %collective-permute-start.39) | collective-permute-done | bytes 368672 | tf_op jit(solution)/shard_map/ppermute | solution.py:657
  222.7 2.0 collective-permute-start.49
  224.7 1.6 collective-permute-start.48
  226.3 1.3 collective-permute-start.44
  227.6 1.2 collective-permute-done.49.refs_1_
  229.0 6.5 %collective-permute-done.44.refs_1_ = f32[24,768]{1,0:T(8,128)S(1)} collective-permute-done((f32[24,768]{1,0:T(8,128)S(1)}, f32[24,768]{1,0:T(8,128)S(1)}, u32[]{:S(2)}, u32[]{:S(2)}) %collective-permute-start.44) | collective-permute-done | bytes 73760 | tf_op jit(solution)/shard_map/ppermute | solution.py:657
  236.3 1.0 shard_map.229
  (140 shorter events, 18.9 us)
Async XLA Ops:
  1.3 13.5 %copy-start = (bf16[768,2304]{1,0:T(8,128)(2,1)S(1)}, bf16[768,2304]{1,0:T(8,128)(2,1)}, u32[]{:S(2)}) copy-start(bf16[768,2304]{1,0:T(8,128)(2,1)} %refs_3_.5) | copy-start | bytes 10616836
  1.3 13.5 %copy-start.4 = (bf16[12,64,64]{2,1,0:T(8,128)(2,1)S(1)}, bf16[12,64,64]{2,1,0:T(8,128)(2,1)}, u32[]{:S(2)}) copy-start(bf16[12,64,64]{2,1,0:T(8,128)(2,1)} %refs_14_.5) | copy-start | bytes 294916
  1.3 27.7 %slice-start = ((s8[4718592]{0:T(1024)(128)(4,1)}), s8[4194304]{0:T(1024)(128)(4,1)S(1)}, s32[]{:S(2)}) async-start(s8[4718592]{0:T(1024)(128)(4,1)} %bitcast.13), calls=%async_computation | async-start | bytes 8388608
  10.2 12.7 %copy-start.9 = (bf16[512,1536]{1,0:T(8,128)(2,1)}, bf16[512,1536]{1,0:T(8,128)(2,1)S(1)}, u32[]{:S(2)}) copy-start(bf16[512,1536]{1,0:T(8,128)(2,1)S(1)} %get-tuple-element.194.refs_3_.refs_2_.refs_1_) | copy-start | bytes 4718596
  10.2 12.7 %copy-start.13 = (f32[512,512]{1,0:T(8,128)}, f32[512,512]{1,0:T(8,128)S(1)}, u32[]{:S(2)}) copy-start(f32[512,512]{1,0:T(8,128)S(1)} %get-tuple-element.196.refs_5_.refs_11_) | copy-start | bytes 3145732
  10.2 12.7 %copy-start.15 = (f32[512,512]{1,0:T(8,128)}, f32[512,512]{1,0:T(8,128)S(1)}, u32[]{:S(2)}) copy-start(f32[512,512]{1,0:T(8,128)S(1)} %get-tuple-element.237.refs_12_) | copy-start | bytes 3145732
  10.2 12.7 %copy-start.17 = (bf16[512,768]{1,0:T(8,128)(2,1)}, bf16[512,768]{1,0:T(8,128)(2,1)S(1)}, u32[]{:S(2)}) copy-start(bf16[512,768]{1,0:T(8,128)(2,1)S(1)} %get-tuple-element.195.refs_4_.refs_3_.refs_2_) | copy-start | bytes 2359300
  10.2 12.7 %copy-start.28 = (bf16[512,768]{1,0:T(8,128)(2,1)}, bf16[512,768]{1,0:T(8,128)(2,1)S(1)}, u32[]{:S(2)}) copy-start(bf16[512,768]{1,0:T(8,128)(2,1)S(1)} %get-tuple-element.262.refs_0_) | copy-start | bytes 2359300
  10.2 12.7 %collective-permute-start = (f32[3,72,128]{2,1,0:T(8,128)S(1)}, f32[3,72,128]{2,1,0:T(8,128)S(1)}, u32[]{:S(2)}, u32[]{:S(2)}) collective-permute-start(f32[3,72,128]{2,1,0:T(8,128)S(1)} %get-tuple-element.201), channel_id=1, source_target_pairs={{0,1},{1,0},{2,3},{3,2},{4,5},{5,4},{6,7},{7,6},{8,9},{9,8},{10,11... | collective-permute-start | bytes 331784 | tf_op jit(solution)/shard_map/ppermute | solution.py:660
  13.2 9.7 %collective-permute-start.1 = (f32[3,72,128]{2,1,0:T(8,128)S(1)}, f32[3,72,128]{2,1,0:T(8,128)S(1)}, u32[]{:S(2)}, u32[]{:S(2)}) collective-permute-start(f32[3,72,128]{2,1,0:T(8,128)S(1)} %get-tuple-element.202), channel_id=1, source_target_pairs={{0,2},{1,3},{2,0},{3,1},{4,6},{5,7},{6,4},{7,5},{8,10},{9,11},{10,... | collective-permute-start | bytes 331784 | tf_op jit(solution)/shard_map/ppermute | solution.py:660
  14.8 8.2 %collective-permute-start.2 = (f32[3,72,128]{2,1,0:T(8,128)S(1)}, f32[3,72,128]{2,1,0:T(8,128)S(1)}, u32[]{:S(2)}, u32[]{:S(2)}) collective-permute-start(f32[3,72,128]{2,1,0:T(8,128)S(1)} %get-tuple-element.203), channel_id=1, source_target_pairs={{0,3},{1,2},{2,1},{3,0},{4,7},{5,6},{6,5},{7,4},{8,11},{9,10},{10,... | collective-permute-start | bytes 331784 | tf_op jit(solution)/shard_map/ppermute | solution.py:660
  14.8 14.2 %slice-start.1 = ((s8[4718592]{0:T(1024)(128)(4,1)}), s8[524288]{0:T(1024)(128)(4,1)S(1)}, s32[]{:S(2)}) async-start(s8[4718592]{0:T(1024)(128)(4,1)} %bitcast.13), calls=%async_computation.1 | async-start | bytes 1048576
  22.9 58.9 %copy-start.11 = (bf16[512,1536]{1,0:T(8,128)(2,1)}, bf16[512,1536]{1,0:T(8,128)(2,1)S(1)}, u32[]{:S(2)}) copy-start(bf16[512,1536]{1,0:T(8,128)(2,1)S(1)} %get-tuple-element.199.refs_2_.refs_4_.refs_1_) | copy-start | bytes 4718596
  23.8 8.5 %collective-permute-start.5 = (f32[3,72,128]{2,1,0:T(8,128)S(1)}, f32[3,72,128]{2,1,0:T(8,128)S(1)}, u32[]{:S(2)}, u32[]{:S(2)}) collective-permute-start(f32[3,72,128]{2,1,0:T(8,128)S(1)} %get-tuple-element.205), channel_id=1, source_target_pairs={{0,12},{1,13},{2,14},{3,15},{4,0},{5,1},{6,2},{7,3},{8,4},{9,5},{1... | collective-permute-start | bytes 331784 | tf_op jit(solution)/shard_map/ppermute | solution.py:663
  27.8 9.3 %collective-permute-start.4 = (f32[3,72,128]{2,1,0:T(8,128)S(1)}, f32[3,72,128]{2,1,0:T(8,128)S(1)}, u32[]{:S(2)}, u32[]{:S(2)}) collective-permute-start(f32[3,72,128]{2,1,0:T(8,128)S(1)} %get-tuple-element.205), channel_id=1, source_target_pairs={{0,8},{1,9},{2,10},{3,11},{4,12},{5,13},{6,14},{7,15},{8,0},{9,1},... | collective-permute-start | bytes 331784 | tf_op jit(solution)/shard_map/ppermute | solution.py:663
  27.8 9.3 %collective-permute-start.3 = (f32[3,72,128]{2,1,0:T(8,128)S(1)}, f32[3,72,128]{2,1,0:T(8,128)S(1)}, u32[]{:S(2)}, u32[]{:S(2)}) collective-permute-start(f32[3,72,128]{2,1,0:T(8,128)S(1)} %get-tuple-element.205), channel_id=1, source_target_pairs={{0,4},{1,5},{2,6},{3,7},{4,8},{5,9},{6,10},{7,11},{8,12},{9,13},{1... | collective-permute-start | bytes 331784 | tf_op jit(solution)/shard_map/ppermute | solution.py:663
  37.2 6.7 %collective-permute-start.6 = (f32[3,72,128]{2,1,0:T(8,128)S(1)}, f32[3,72,128]{2,1,0:T(8,128)S(1)}, u32[]{:S(2)}, u32[]{:S(2)}) collective-permute-start(f32[3,72,128]{2,1,0:T(8,128)S(1)} %get-tuple-element.209), channel_id=1, source_target_pairs={{0,1},{1,0},{2,3},{3,2},{4,5},{5,4},{6,7},{7,6},{8,9},{9,8},{10,11... | collective-permute-start | bytes 331784 | tf_op jit(solution)/shard_map/ppermute | solution.py:660
  38.8 5.9 %collective-permute-start.7 = (f32[3,72,128]{2,1,0:T(8,128)S(1)}, f32[3,72,128]{2,1,0:T(8,128)S(1)}, u32[]{:S(2)}, u32[]{:S(2)}) collective-permute-start(f32[3,72,128]{2,1,0:T(8,128)S(1)} %get-tuple-element.210), channel_id=1, source_target_pairs={{0,2},{1,3},{2,0},{3,1},{4,6},{5,7},{6,4},{7,5},{8,10},{9,11},{10,... | collective-permute-start | bytes 331784 | tf_op jit(solution)/shard_map/ppermute | solution.py:660
  40.3 5.6 %collective-permute-start.8 = (f32[3,72,128]{2,1,0:T(8,128)S(1)}, f32[3,72,128]{2,1,0:T(8,128)S(1)}, u32[]{:S(2)}, u32[]{:S(2)}) collective-permute-start(f32[3,72,128]{2,1,0:T(8,128)S(1)} %get-tuple-element.211), channel_id=1, source_target_pairs={{0,3},{1,2},{2,1},{3,0},{4,7},{5,6},{6,5},{7,4},{8,11},{9,10},{10,... | collective-permute-start | bytes 331784 | tf_op jit(solution)/shard_map/ppermute | solution.py:660
  63.7 14.9 %collective-permute-start.9 = (f32[2,4,384,768]{3,2,1,0:T(8,128)}, f32[2,4,384,768]{3,2,1,0:T(8,128)S(1)}, u32[]{:S(2)}, u32[]{:S(2)}) collective-permute-start(f32[2,4,384,768]{3,2,1,0:T(8,128)} %get-tuple-element.231), channel_id=1, source_target_pairs={{0,16},{16,0},{1,17},{17,1},{2,18},{18,2},{3,19},{19,3},{4,20},{20... | collective-permute-start | bytes 28311560 | tf_op jit(solution)/shard_map/ppermute | solution.py:636
  80.2 16.2 %collective-permute-start.13 = (f32[192,768]{1,0:T(8,128)S(1)}, f32[192,768]{1,0:T(8,128)S(1)}, u32[]{:S(2)}, u32[]{:S(2)}) collective-permute-start(f32[192,768]{1,0:T(8,128)S(1)} %get-tuple-element.243), channel_id=1, source_target_pairs={{0,1},{1,0},{2,3},{3,2},{4,5},{5,4},{6,7},{7,6},{8,9},{9,8},{10,11... | collective-permute-start | bytes 1769480 | tf_op jit(solution)/shard_map/ppermute | solution.py:657
  80.9 16.4 %collective-permute-start.14 = (f32[192,768]{1,0:T(8,128)S(1)}, f32[192,768]{1,0:T(8,128)S(1)}, u32[]{:S(2)}, u32[]{:S(2)}) collective-permute-start(f32[192,768]{1,0:T(8,128)S(1)} %get-tuple-element.245), channel_id=1, source_target_pairs={{0,2},{1,3},{2,0},{3,1},{4,6},{5,7},{6,4},{7,5},{8,10},{9,11},{10,... | collective-permute-start | bytes 1769480 | tf_op jit(solution)/shard_map/ppermute | solution.py:657
  81.8 15.6 %collective-permute-start.15 = (f32[192,768]{1,0:T(8,128)S(1)}, f32[192,768]{1,0:T(8,128)S(1)}, u32[]{:S(2)}, u32[]{:S(2)}) collective-permute-start(f32[192,768]{1,0:T(8,128)S(1)} %get-tuple-element.247), channel_id=1, source_target_pairs={{0,4},{1,5},{2,6},{3,7},{4,0},{5,1},{6,2},{7,3},{8,12},{9,13},{10,... | collective-permute-start | bytes 1769480 | tf_op jit(solution)/shard_map/ppermute | solution.py:657
  86.7 13.8 %collective-permute-start.10 = (f32[3,72,128]{2,1,0:T(8,128)S(1)}, f32[3,72,128]{2,1,0:T(8,128)S(1)}, u32[]{:S(2)}, u32[]{:S(2)}) collective-permute-start(f32[3,72,128]{2,1,0:T(8,128)S(1)} %get-tuple-element.239), channel_id=1, source_target_pairs={{0,1},{1,0},{2,3},{3,2},{4,5},{5,4},{6,7},{7,6},{8,9},{9,8},{10,11... | collective-permute-start | bytes 331784 | tf_op jit(solution)/shard_map/ppermute | solution.py:660
  88.4 12.1 %collective-permute-start.11 = (f32[3,72,128]{2,1,0:T(8,128)S(1)}, f32[3,72,128]{2,1,0:T(8,128)S(1)}, u32[]{:S(2)}, u32[]{:S(2)}) collective-permute-start(f32[3,72,128]{2,1,0:T(8,128)S(1)} %get-tuple-element.240), channel_id=1, source_target_pairs={{0,2},{1,3},{2,0},{3,1},{4,6},{5,7},{6,4},{7,5},{8,10},{9,11},{10,... | collective-permute-start | bytes 331784 | tf_op jit(solution)/shard_map/ppermute | solution.py:660
  96.5 5.6 %collective-permute-start.12 = (f32[3,72,128]{2,1,0:T(8,128)S(1)}, f32[3,72,128]{2,1,0:T(8,128)S(1)}, u32[]{:S(2)}, u32[]{:S(2)}) collective-permute-start(f32[3,72,128]{2,1,0:T(8,128)S(1)} %get-tuple-element.241), channel_id=1, source_target_pairs={{0,3},{1,2},{2,1},{3,0},{4,7},{5,6},{6,5},{7,4},{8,11},{9,10},{10,... | collective-permute-start | bytes 331784 | tf_op jit(solution)/shard_map/ppermute | solution.py:660
  97.4 11.6 %copy-start.16 = (f32[512,512]{1,0:T(8,128)S(1)}, f32[512,512]{1,0:T(8,128)}, u32[]{:S(2)}) copy-start(f32[512,512]{1,0:T(8,128)} %copy-done.15) | copy-start | bytes 3145732
  97.4 11.6 %copy-start.18 = (bf16[512,768]{1,0:T(8,128)(2,1)S(1)}, bf16[512,768]{1,0:T(8,128)(2,1)}, u32[]{:S(2)}) copy-start(bf16[512,768]{1,0:T(8,128)(2,1)} %copy-done.17) | copy-start | bytes 2359300
  97.4 11.6 %copy-start.21 = (bf16[512,768]{1,0:T(8,128)(2,1)S(1)}, bf16[512,768]{1,0:T(8,128)(2,1)}, u32[]{:S(2)}) copy-start(bf16[512,768]{1,0:T(8,128)(2,1)} %copy-done.20) | copy-start | bytes 2359300
  102.2 18.4 %collective-permute-start.18 = (f32[3,72,128]{2,1,0:T(8,128)S(1)}, f32[3,72,128]{2,1,0:T(8,128)S(1)}, u32[]{:S(2)}, u32[]{:S(2)}) collective-permute-start(f32[3,72,128]{2,1,0:T(8,128)S(1)} %get-tuple-element.265), channel_id=1, source_target_pairs={{0,4},{1,5},{2,6},{3,7},{4,8},{5,9},{6,10},{7,11},{8,12},{9,13},{1... | collective-permute-start | bytes 331784 | tf_op jit(solution)/shard_map/ppermute | solution.py:663
  102.3 18.3 %collective-permute-start.17 = (f32[3,72,128]{2,1,0:T(8,128)S(1)}, f32[3,72,128]{2,1,0:T(8,128)S(1)}, u32[]{:S(2)}, u32[]{:S(2)}) collective-permute-start(f32[3,72,128]{2,1,0:T(8,128)S(1)} %get-tuple-element.265), channel_id=1, source_target_pairs={{0,8},{1,9},{2,10},{3,11},{4,12},{5,13},{6,14},{7,15},{8,0},{9,1},... | collective-permute-start | bytes 331784 | tf_op jit(solution)/shard_map/ppermute | solution.py:663
  104.3 16.3 %collective-permute-start.16 = (f32[3,72,128]{2,1,0:T(8,128)S(1)}, f32[3,72,128]{2,1,0:T(8,128)S(1)}, u32[]{:S(2)}, u32[]{:S(2)}) collective-permute-start(f32[3,72,128]{2,1,0:T(8,128)S(1)} %get-tuple-element.265), channel_id=1, source_target_pairs={{0,12},{1,13},{2,14},{3,15},{4,0},{5,1},{6,2},{7,3},{8,4},{9,5},{1... | collective-permute-start | bytes 331784 | tf_op jit(solution)/shard_map/ppermute | solution.py:663
  107.5 38.6 %collective-permute-start.22 = (f32[480,768]{1,0:T(8,128)S(1)}, f32[480,768]{1,0:T(8,128)S(1)}, u32[]{:S(2)}, u32[]{:S(2)}) collective-permute-start(f32[480,768]{1,0:T(8,128)S(1)} %get-tuple-element.272), channel_id=1, source_target_pairs={{0,2},{1,3},{2,0},{3,1},{4,6},{5,7},{6,4},{7,5},{8,10},{9,11},{10,... | collective-permute-start | bytes 4423688 | tf_op jit(solution)/shard_map/ppermute | solution.py:657
  108.5 37.6 %collective-permute-start.24 = (f32[480,768]{1,0:T(8,128)S(1)}, f32[480,768]{1,0:T(8,128)S(1)}, u32[]{:S(2)}, u32[]{:S(2)}) collective-permute-start(f32[480,768]{1,0:T(8,128)S(1)} %get-tuple-element.276), channel_id=1, source_target_pairs={{0,1},{1,0},{2,3},{3,2},{4,5},{5,4},{6,7},{7,6},{8,9},{9,8},{10,11... | collective-permute-start | bytes 4423688 | tf_op jit(solution)/shard_map/ppermute | solution.py:657
  122.6 23.5 %collective-permute-start.25 = (f32[1,384,768]{2,1,0:T(8,128)S(1)}, f32[1,384,768]{2,1,0:T(8,128)S(1)}, u32[]{:S(2)}, u32[]{:S(2)}) collective-permute-start(f32[1,384,768]{2,1,0:T(8,128)S(1)} %get-tuple-element.284), channel_id=1, source_target_pairs={{0,16},{16,0},{1,17},{17,1},{2,18},{18,2},{3,19},{19,3},{4,20},{20... | collective-permute-start | bytes 3538952 | tf_op jit(solution)/shard_map/ppermute | solution.py:636
  122.8 22.1 %collective-permute-start.23 = (f32[288,768]{1,0:T(8,128)S(1)}, f32[288,768]{1,0:T(8,128)S(1)}, u32[]{:S(2)}, u32[]{:S(2)}) collective-permute-start(f32[288,768]{1,0:T(8,128)S(1)} %get-tuple-element.274), channel_id=1, source_target_pairs={{0,4},{1,5},{2,6},{3,7},{4,0},{5,1},{6,2},{7,3},{8,12},{9,13},{10,... | collective-permute-start | bytes 2654216 | tf_op jit(solution)/shard_map/ppermute | solution.py:657
  122.9 20.8 %collective-permute-start.19 = (f32[6,72,128]{2,1,0:T(8,128)S(1)}, f32[6,72,128]{2,1,0:T(8,128)S(1)}, u32[]{:S(2)}, u32[]{:S(2)}) collective-permute-start(f32[6,72,128]{2,1,0:T(8,128)S(1)} %get-tuple-element.268), channel_id=1, source_target_pairs={{0,1},{1,0},{2,3},{3,2},{4,5},{5,4},{6,7},{7,6},{8,9},{9,8},{10,11... | collective-permute-start | bytes 663560 | tf_op jit(solution)/shard_map/ppermute | solution.py:660
  143.7 7.3 %collective-permute-start.20 = (f32[3,72,128]{2,1,0:T(8,128)S(1)}, f32[3,72,128]{2,1,0:T(8,128)S(1)}, u32[]{:S(2)}, u32[]{:S(2)}) collective-permute-start(f32[3,72,128]{2,1,0:T(8,128)S(1)} %get-tuple-element.269), channel_id=1, source_target_pairs={{0,2},{1,3},{2,0},{3,1},{4,6},{5,7},{6,4},{7,5},{8,10},{9,11},{10,... | collective-permute-start | bytes 331784 | tf_op jit(solution)/shard_map/ppermute | solution.py:660
  144.9 6.1 %collective-permute-start.21 = (f32[3,72,128]{2,1,0:T(8,128)S(1)}, f32[3,72,128]{2,1,0:T(8,128)S(1)}, u32[]{:S(2)}, u32[]{:S(2)}) collective-permute-start(f32[3,72,128]{2,1,0:T(8,128)S(1)} %slice.12), channel_id=1, source_target_pairs={{0,2},{1,3},{2,0},{3,1},{4,6},{5,7},{6,4},{7,5},{8,10},{9,11},{10,... | collective-permute-start | bytes 331784 | tf_op jit(solution)/shard_map/ppermute | solution.py:660
  148.3 21.1 %collective-permute-start.26 = (f32[240,768]{1,0:T(8,128)}, f32[240,768]{1,0:T(8,128)}, u32[]{:S(2)}, u32[]{:S(2)}) collective-permute-start(f32[240,768]{1,0:T(8,128)} %get-tuple-element.298), channel_id=1, source_target_pairs={{0,4},{1,5},{2,6},{3,7},{4,0},{5,1},{6,2},{7,3},{8,12},{9,13},{10,... | collective-permute-start | bytes 2211848 | tf_op jit(solution)/shard_map/ppermute | solution.py:657
  148.6 21.9 %collective-permute-start.28 = (f32[240,768]{1,0:T(8,128)}, f32[240,768]{1,0:T(8,128)}, u32[]{:S(2)}, u32[]{:S(2)}) collective-permute-start(f32[240,768]{1,0:T(8,128)} %get-tuple-element.302), channel_id=1, source_target_pairs={{0,2},{1,3},{2,0},{3,1},{4,6},{5,7},{6,4},{7,5},{8,10},{9,11},{10,... | collective-permute-start | bytes 2211848 | tf_op jit(solution)/shard_map/ppermute | solution.py:657
  149.4 25.9 %collective-permute-start.27 = (f32[336,768]{1,0:T(8,128)}, f32[336,768]{1,0:T(8,128)}, u32[]{:S(2)}, u32[]{:S(2)}) collective-permute-start(f32[336,768]{1,0:T(8,128)} %get-tuple-element.300), channel_id=1, source_target_pairs={{0,1},{1,0},{2,3},{3,2},{4,5},{5,4},{6,7},{7,6},{8,9},{9,8},{10,11... | collective-permute-start | bytes 3096584 | tf_op jit(solution)/shard_map/ppermute | solution.py:657
  158.2 8.0 %collective-permute-start.29 = (f32[3,384,768]{2,1,0:T(8,128)S(1)}, f32[3,384,768]{2,1,0:T(8,128)S(1)}, u32[]{:S(2)}, u32[]{:S(2)}) collective-permute-start(f32[3,384,768]{2,1,0:T(8,128)S(1)} %get-tuple-element.307), channel_id=1, source_target_pairs={{0,16},{16,0},{1,17},{17,1},{2,18},{18,2},{3,19},{19,3},{4,20},{20... | collective-permute-start | bytes 10616840 | tf_op jit(solution)/shard_map/ppermute | solution.py:636
  164.8 1.5 collective-permute-start.30
  167.8 14.1 %collective-permute-start.38 = (f32[72,768]{1,0:T(8,128)S(1)}, f32[72,768]{1,0:T(8,128)S(1)}, u32[]{:S(2)}, u32[]{:S(2)}) collective-permute-start(f32[72,768]{1,0:T(8,128)S(1)} %get-tuple-element.330), channel_id=1, source_target_pairs={{0,8},{1,9},{2,10},{3,11},{4,12},{5,13},{6,14},{7,15},{8,0},{9,1},... | collective-permute-start | bytes 663560 | tf_op jit(solution)/shard_map/ppermute | solution.py:657
  168.8 17.2 %collective-permute-start.35 = (f32[192,768]{1,0:T(8,128)S(1)}, f32[192,768]{1,0:T(8,128)S(1)}, u32[]{:S(2)}, u32[]{:S(2)}) collective-permute-start(f32[192,768]{1,0:T(8,128)S(1)} %get-tuple-element.324), channel_id=1, source_target_pairs={{0,1},{1,0},{2,3},{3,2},{4,5},{5,4},{6,7},{7,6},{8,9},{9,8},{10,11... | collective-permute-start | bytes 1769480 | tf_op jit(solution)/shard_map/ppermute | solution.py:657
  169.4 18.2 %collective-permute-start.36 = (f32[192,768]{1,0:T(8,128)S(1)}, f32[192,768]{1,0:T(8,128)S(1)}, u32[]{:S(2)}, u32[]{:S(2)}) collective-permute-start(f32[192,768]{1,0:T(8,128)S(1)} %get-tuple-element.326), channel_id=1, source_target_pairs={{0,2},{1,3},{2,0},{3,1},{4,6},{5,7},{6,4},{7,5},{8,10},{9,11},{10,... | collective-permute-start | bytes 1769480 | tf_op jit(solution)/shard_map/ppermute | solution.py:657
  170.5 24.4 %collective-permute-start.37 = (f32[192,768]{1,0:T(8,128)S(1)}, f32[192,768]{1,0:T(8,128)S(1)}, u32[]{:S(2)}, u32[]{:S(2)}) collective-permute-start(f32[192,768]{1,0:T(8,128)S(1)} %get-tuple-element.328), channel_id=1, source_target_pairs={{0,4},{1,5},{2,6},{3,7},{4,0},{5,1},{6,2},{7,3},{8,12},{9,13},{10,... | collective-permute-start | bytes 1769480 | tf_op jit(solution)/shard_map/ppermute | solution.py:657
  177.2 19.1 %collective-permute-start.31 = (f32[72,768]{1,0:T(8,128)S(1)}, f32[72,768]{1,0:T(8,128)S(1)}, u32[]{:S(2)}, u32[]{:S(2)}) collective-permute-start(f32[72,768]{1,0:T(8,128)S(1)} %get-tuple-element.313), channel_id=1, source_target_pairs={{0,8},{1,9},{2,10},{3,11},{4,12},{5,13},{6,14},{7,15},{8,0},{9,1},... | collective-permute-start | bytes 663560 | tf_op jit(solution)/shard_map/ppermute | solution.py:657
  181.8 19.4 %collective-permute-start.32 = (f32[96,768]{1,0:T(8,128)S(1)}, f32[96,768]{1,0:T(8,128)S(1)}, u32[]{:S(2)}, u32[]{:S(2)}) collective-permute-start(f32[96,768]{1,0:T(8,128)S(1)} %get-tuple-element.317), channel_id=1, source_target_pairs={{0,4},{1,5},{2,6},{3,7},{4,0},{5,1},{6,2},{7,3},{8,12},{9,13},{10,... | collective-permute-start | bytes 884744 | tf_op jit(solution)/shard_map/ppermute | solution.py:657
  186.0 17.0 %collective-permute-start.33 = (f32[96,768]{1,0:T(8,128)S(1)}, f32[96,768]{1,0:T(8,128)S(1)}, u32[]{:S(2)}, u32[]{:S(2)}) collective-permute-start(f32[96,768]{1,0:T(8,128)S(1)} %get-tuple-element.319), channel_id=1, source_target_pairs={{0,1},{1,0},{2,3},{3,2},{4,5},{5,4},{6,7},{7,6},{8,9},{9,8},{10,11... | collective-permute-start | bytes 884744 | tf_op jit(solution)/shard_map/ppermute | solution.py:657
  187.6 15.4 %collective-permute-start.34 = (f32[144,768]{1,0:T(8,128)S(1)}, f32[144,768]{1,0:T(8,128)S(1)}, u32[]{:S(2)}, u32[]{:S(2)}) collective-permute-start(f32[144,768]{1,0:T(8,128)S(1)} %get-tuple-element.321), channel_id=1, source_target_pairs={{0,2},{1,3},{2,0},{3,1},{4,6},{5,7},{6,4},{7,5},{8,10},{9,11},{10,... | collective-permute-start | bytes 1327112 | tf_op jit(solution)/shard_map/ppermute | solution.py:657
  195.2 12.4 %collective-permute-start.41 = (f32[96,768]{1,0:T(8,128)S(1)}, f32[96,768]{1,0:T(8,128)S(1)}, u32[]{:S(2)}, u32[]{:S(2)}) collective-permute-start(f32[96,768]{1,0:T(8,128)S(1)} %get-tuple-element.341), channel_id=1, source_target_pairs={{0,2},{1,3},{2,0},{3,1},{4,6},{5,7},{6,4},{7,5},{8,10},{9,11},{10,... | collective-permute-start | bytes 884744 | tf_op jit(solution)/shard_map/ppermute | solution.py:657
  196.4 16.9 %collective-permute-start.42 = (f32[96,768]{1,0:T(8,128)S(1)}, f32[96,768]{1,0:T(8,128)S(1)}, u32[]{:S(2)}, u32[]{:S(2)}) collective-permute-start(f32[96,768]{1,0:T(8,128)S(1)} %get-tuple-element.343), channel_id=1, source_target_pairs={{0,4},{1,5},{2,6},{3,7},{4,0},{5,1},{6,2},{7,3},{8,12},{9,13},{10,... | collective-permute-start | bytes 884744 | tf_op jit(solution)/shard_map/ppermute | solution.py:657
  201.2 12.0 %collective-permute-start.43 = (f32[168,768]{1,0:T(8,128)S(1)}, f32[168,768]{1,0:T(8,128)S(1)}, u32[]{:S(2)}, u32[]{:S(2)}) collective-permute-start(f32[168,768]{1,0:T(8,128)S(1)} %get-tuple-element.345), channel_id=1, source_target_pairs={{0,1},{1,0},{2,3},{3,2},{4,5},{5,4},{6,7},{7,6},{8,9},{9,8},{10,11... | collective-permute-start | bytes 1548296 | tf_op jit(solution)/shard_map/ppermute | solution.py:657
  203.1 13.3 %collective-permute-start.40 = (f32[48,768]{1,0:T(8,128)S(1)}, f32[48,768]{1,0:T(8,128)S(1)}, u32[]{:S(2)}, u32[]{:S(2)}) collective-permute-start(f32[48,768]{1,0:T(8,128)S(1)} %get-tuple-element.339), channel_id=1, source_target_pairs={{0,4},{1,5},{2,6},{3,7},{4,0},{5,1},{6,2},{7,3},{8,12},{9,13},{10,... | collective-permute-start | bytes 442376 | tf_op jit(solution)/shard_map/ppermute | solution.py:657
  203.2 17.9 %collective-permute-start.39 = (f32[120,768]{1,0:T(8,128)S(1)}, f32[120,768]{1,0:T(8,128)S(1)}, u32[]{:S(2)}, u32[]{:S(2)}) collective-permute-start(f32[120,768]{1,0:T(8,128)S(1)} %get-tuple-element.335), channel_id=1, source_target_pairs={{0,8},{1,9},{2,10},{3,11},{4,12},{5,13},{6,14},{7,15},{8,0},{9,1},... | collective-permute-start | bytes 1105928 | tf_op jit(solution)/shard_map/ppermute | solution.py:657
  213.4 8.6 %collective-permute-start.45 = (f32[48,768]{1,0:T(8,128)S(1)}, f32[48,768]{1,0:T(8,128)S(1)}, u32[]{:S(2)}, u32[]{:S(2)}) collective-permute-start(f32[48,768]{1,0:T(8,128)S(1)} %get-tuple-element.352), channel_id=1, source_target_pairs={{0,4},{1,5},{2,6},{3,7},{4,0},{5,1},{6,2},{7,3},{8,12},{9,13},{10,... | collective-permute-start | bytes 442376 | tf_op jit(solution)/shard_map/ppermute | solution.py:657
  213.4 8.5 %collective-permute-start.46 = (f32[48,768]{1,0:T(8,128)S(1)}, f32[48,768]{1,0:T(8,128)S(1)}, u32[]{:S(2)}, u32[]{:S(2)}) collective-permute-start(f32[48,768]{1,0:T(8,128)S(1)} %get-tuple-element.354), channel_id=1, source_target_pairs={{0,1},{1,0},{2,3},{3,2},{4,5},{5,4},{6,7},{7,6},{8,9},{9,8},{10,11... | collective-permute-start | bytes 442376 | tf_op jit(solution)/shard_map/ppermute | solution.py:657
  215.1 7.5 %collective-permute-start.47 = (f32[120,768]{1,0:T(8,128)S(1)}, f32[120,768]{1,0:T(8,128)S(1)}, u32[]{:S(2)}, u32[]{:S(2)}) collective-permute-start(f32[120,768]{1,0:T(8,128)S(1)} %get-tuple-element.356), channel_id=1, source_target_pairs={{0,2},{1,3},{2,0},{3,1},{4,6},{5,7},{6,4},{7,5},{8,10},{9,11},{10,... | collective-permute-start | bytes 1105928 | tf_op jit(solution)/shard_map/ppermute | solution.py:657
  222.7 6.2 %collective-permute-start.49 = (f32[72,768]{1,0:T(8,128)S(1)}, f32[72,768]{1,0:T(8,128)S(1)}, u32[]{:S(2)}, u32[]{:S(2)}) collective-permute-start(f32[72,768]{1,0:T(8,128)S(1)} %get-tuple-element.364), channel_id=1, source_target_pairs={{0,4},{1,5},{2,6},{3,7},{4,0},{5,1},{6,2},{7,3},{8,12},{9,13},{10,... | collective-permute-start | bytes 663560 | tf_op jit(solution)/shard_map/ppermute | solution.py:657
  224.7 10.8 %collective-permute-start.48 = (f32[72,768]{1,0:T(8,128)S(1)}, f32[72,768]{1,0:T(8,128)S(1)}, u32[]{:S(2)}, u32[]{:S(2)}) collective-permute-start(f32[72,768]{1,0:T(8,128)S(1)} %get-tuple-element.360), channel_id=1, source_target_pairs={{0,8},{1,9},{2,10},{3,11},{4,12},{5,13},{6,14},{7,15},{8,0},{9,1},... | collective-permute-start | bytes 663560 | tf_op jit(solution)/shard_map/ppermute | solution.py:657
  226.3 9.2 %collective-permute-start.44 = (f32[24,768]{1,0:T(8,128)S(1)}, f32[24,768]{1,0:T(8,128)S(1)}, u32[]{:S(2)}, u32[]{:S(2)}) collective-permute-start(f32[24,768]{1,0:T(8,128)S(1)} %get-tuple-element.350), channel_id=1, source_target_pairs={{0,8},{1,9},{2,10},{3,11},{4,12},{5,13},{6,14},{7,15},{8,0},{9,1},... | collective-permute-start | bytes 221192 | tf_op jit(solution)/shard_map/ppermute | solution.py:657
  228.9 7.3 %collective-permute-start.50 = (f32[72,768]{1,0:T(8,128)S(1)}, f32[72,768]{1,0:T(8,128)S(1)}, u32[]{:S(2)}, u32[]{:S(2)}) collective-permute-start(f32[72,768]{1,0:T(8,128)S(1)} %get-tuple-element.371.refs_0_), channel_id=1, source_target_pairs={{0,16},{16,0},{1,17},{17,1},{2,18},{18,2},{3,19},{19,3},{4,20},{20... | collective-permute-start | bytes 663560 | tf_op jit(solution)/shard_map/ppermute | solution.py:636
  (19 other events, 68.5 us)

commit v6 on v4

--- a/solution.py
+++ b/solution.py
@@ -70,6 +70,11 @@
         ).astype(scr.dtype)
 
 
+def inverse_of(v):
+    guess = pl.reciprocal(v, approx=True)
+    return guess * (2.0 - v * guess)
+
+
 def half_sums(v, low_half):
     top = jnp.sum(jnp.where(low_half, v, 0.0), axis=1, keepdims=True)
     bottom = jnp.sum(jnp.where(low_half, 0.0, v), axis=1, keepdims=True)
@@ -81,14 +86,14 @@
     top = jnp.max(jnp.where(low_half, pre, -jnp.inf), axis=1, keepdims=True)
     bottom = jnp.max(jnp.where(low_half, -jnp.inf, pre), axis=1, keepdims=True)
     e = jnp.exp(pre - jnp.where(low_half, top, bottom))
-    return e / half_sums(e, low_half)
+    return e * inverse_of(half_sums(e, low_half))
 
 
 def features_back(feat, grad, ones):
     low_half = iota(feat.shape, 1) < 64
     weighted = feat * grad
     mass = mm(feat.astype(BF16), ones)
-    part = weighted - feat * (half_sums(weighted, low_half) / mass)
+    part = weighted - feat * (half_sums(weighted, low_half) * inverse_of(mass))
     return part - pltpu.roll(part, 64, 1)
 
 
@@ -333,7 +338,7 @@
             high, low = split(wide)
             fq = fq_ref[:, lanes]
             nd = nd_ref[:, lanes] + contin * (nt(fq, high) + nt(fq, low))
-            inverse = 1.0 / nd
+            inverse = inverse_of(nd)
             turned = pltpu.roll(inverse, 64, 1)
             quotient = nd * turned
             if side:

time: 242 us -> 243 us (level)
  no operation moved by 1% of the time
where the time goes in v6:
time: 243 us; the launch traced here: 238 us
  Pallas kernels  91.6 us (38%)
  waiting for transfers between devices  83.3 us (34%)
  starting transfers between devices  54.4 us (22%)
  local copies, waits for them, and re-layouts  7.38 us (3%)
    pallas_call x35, Pallas kernels, run(): pl.pallas_call(body, grid=grid, in_specs=[spec for _, spec in ins] + [ANY...  91.6 us
    ppermute x28, waiting for transfers between devices, hop(): return lax.ppermute(v, 'seq', [(i, i ^ 1 << bit) for i in range(n_seq)])  50.3 us
    ppermute x28, starting transfers between devices, hop(): return lax.ppermute(v, 'seq', [(i, i ^ 1 << bit) for i in range(n_seq)])  27.8 us
    ppermute x12, waiting for transfers between devices, to_member(): return lax.ppermute(v, 'seq', [(i, i ^ k) for i in range(n_seq)])  22.7 us
    ppermute x12, starting transfers between devices, to_member(): return lax.ppermute(v, 'seq', [(i, i ^ k) for i in range(n_seq)])  15.7 us
    ppermute x6, starting transfers between devices, shift(): return lax.ppermute(v, 'seq', [(i, (i + by) % n_seq) for i in range(n_seq)])  10.6 us
    unnamed x64, local copies, waits for them, and re-layouts  6.77 us
    ppermute x5, waiting for transfers between devices, core_hop(): return lax.ppermute(v, 'batch', [(0, 1), (1, 0)])  5.5 us
  transfers between devices with their start and end apart: 51, of which 20 were waited for; matrix products, arithmetic and copies ran while one was open for 0% of the time, Pallas kernels for 26%

profile of v6, /device:TPU:0, one launch (start us, length us, event | category | flops | bytes accessed | tf_op | source)
XLA Modules:
  0.0 238.1 jit_solution(12815535851043078188)
XLA Ops:
  1.3 8.9 %shard_map.195 = (bf16[512,768]{1,0:T(8,128)(2,1)S(1)}, bf16[512,768]{1,0:T(8,128)(2,1)S(1)}, bf16[512,768]{1,0:T(8,128)(2,1)S(1)}, bf16[512,1536]{1,0:T(8,128)(...) custom-call(bf16[512,768]{1,0:T(8,128)(2,1)} %bitcast.18, ...), custom_call_target="tpu_custom_call" | custom-call | flops 9200000000 | tf_op jit(solution)/shard_map/pallas_call | solution.py:157
  10.3 3.0 %collective-permute-start = (f32[3,72,128]{2,1,0:T(8,128)S(1)}, f32[3,72,128]{2,1,0:T(8,128)S(1)}, u32[]{:S(2)}, u32[]{:S(2)}) collective-permute-start(f32[3,72,128]{2,1,0:T(8,128)S(1)} %get-tuple-element.201), channel_id=1, source_target_pairs={{0,1},{1,0},{2,3},{3,2},{4,5},{5,4},{6,7},{7,6},{8,9},{9,8},{10,11... | collective-permute-start | bytes 331784 | tf_op jit(solution)/shard_map/ppermute | solution.py:665
  13.3 1.5 collective-permute-start.1
  14.8 8.1 %shard_map.196 = (bf16[512,768]{1,0:T(8,128)(2,1)S(1)}, bf16[512,1536]{1,0:T(8,128)(2,1)S(1)}, f32[512,1536]{1,0:T(8,128)S(1)}, f32[8,128]{1,0:T(8,128)S(1)}) custom-call(bf16[512,768]{1,0:T(8,128)(2,1)S(1)} %get-tuple-element.193.refs_0_, bf16[768,2304]{1,0:T(8,128)(2,1)S(1)} %copy-done, bf16[12,64,64]{2,1,0:T(8,128)(2,1)S(1)} %copy-done.6, ...), custom_call_target="tpu_custom_call" | custom-call | flops 10350000128 | tf_op jit(solution)/shard_map/pallas_call | solution.py:157
  23.9 4.0 %collective-permute-start.5 = (f32[3,72,128]{2,1,0:T(8,128)S(1)}, f32[3,72,128]{2,1,0:T(8,128)S(1)}, u32[]{:S(2)}, u32[]{:S(2)}) collective-permute-start(f32[3,72,128]{2,1,0:T(8,128)S(1)} %get-tuple-element.205), channel_id=1, source_target_pairs={{0,12},{1,13},{2,14},{3,15},{4,0},{5,1},{6,2},{7,3},{8,4},{9,5},{1... | collective-permute-start | bytes 331784 | tf_op jit(solution)/shard_map/ppermute | solution.py:668
  27.9 1.2 collective-permute-start.3
  29.1 3.3 %shard_map.198 = (f32[512,3072]{1,0:T(8,128)S(1)}, f32[8,128]{1,0:T(8,128)S(1)}) custom-call(bf16[512,768]{1,0:T(8,128)(2,1)S(1)} %bitcast.16, bf16[3072,768]{1,0:T(8,128)(2,1)S(1)} %bitcast.14, f32[8,128]{1,0:T(8,128)S(1)} %get-tuple-element.206.refs_2_), custom_call_target="tpu_custom_call" | custom-call | flops 4600000000 | tf_op jit(solution)/shard_map/pallas_call | solution.py:157
  32.4 4.8 %collective-permute-done.4.refs_5_ = f32[3,72,128]{2,1,0:T(8,128)S(1)} collective-permute-done((f32[3,72,128]{2,1,0:T(8,128)S(1)}, f32[3,72,128]{2,1,0:T(8,128)S(1)}, u32[]{:S(2)}, u32[]{:S(2)}) %collective-permute-start.4) | collective-permute-done | bytes 110624 | tf_op jit(solution)/shard_map/ppermute | solution.py:668
  37.3 1.6 collective-permute-start.6
  38.9 1.5 collective-permute-start.7
  42.5 1.5 copy-done.9
  44.8 1.2 collective-permute-done.8.refs_6_.refs_10_
  46.0 5.1 %shard_map.202 = (bf16[512,768]{1,0:T(8,128)(2,1)S(1)}, f32[512,768]{1,0:T(8,128)S(1)}, f32[512,768]{1,0:T(8,128)S(1)}, f32[512,768]{1,0:T(8,128)S(1)}, bf16[512...) custom-call(bf16[512,768]{1,0:T(8,128)(2,1)S(1)} %bitcast.19, f32[512,1536]{1,0:T(8,128)S(1)} %get-tuple-element.198.refs_1_, ...), custom_call_target="tpu_custom_call" | custom-call | flops 5175000064 | tf_op jit(solution)/shard_map/pallas_call | solution.py:157
  52.0 11.3 %shard_map.204 = (bf16[512,3072]{1,0:T(8,128)(2,1)S(1)}, bf16[512,3072]{1,0:T(8,128)(2,1)S(1)}, f32[2,4,384,768]{3,2,1,0:T(8,128)}, f32[8,128]{1,0:T(8,128)S(1)}) custom-call(bf16[512,768]{1,0:T(8,128)(2,1)S(1)} %get-tuple-element.216.refs_0_, f32[512,3072]{1,0:T(8,128)S(1)} %get-tuple-element.217.refs_1_, ...), custom_call_target="tpu_custom_call" | custom-call | flops 11500000256 | tf_op jit(solution)/shard_map/pallas_call | solution.py:157
  63.3 9.7 %shard_map.205 = (f32[512,768]{1,0:T(8,128)}, f32[512,768]{1,0:T(8,128)S(1)}, bf16[512,768]{1,0:T(8,128)(2,1)S(1)}, f32[1,768]{1,0:T(1,128)S(1)}, f32[8,128]{1,0:T(8,128)S(1)}) custom-call(bf16[512,3072]{1,0:T(8,128)(2,1)S(1)} %get-tuple-element.222.refs_0_.refs_1_.refs_8_, bf16[512,3072]{1,0:T(8,128)(2,1)S(1)} %get-tuple-element.223.refs_1_.refs_10_, ...), custom_call_target="tpu_custom_call" | custom-call | flops 9200000000 | tf_op jit(solution)/shard_map/pallas_call | solution.py:157
  73.0 1.2 copy-done.26
  74.2 4.0 %collective-permute-done.9 = f32[2,4,384,768]{3,2,1,0:T(8,128)S(1)} collective-permute-done((f32[2,4,384,768]{3,2,1,0:T(8,128)}, f32[2,4,384,768]{3,2,1,0:T(8,128)S(1)}, u32[]{:S(2)}, u32[]{:S(2)}) %collective-permute-start.9) | collective-permute-done | bytes 9437216 | tf_op jit(solution)/shard_map/ppermute | solution.py:641
  78.2 1.7 shard_map.206
  81.4 4.1 %shard_map.207 = (bf16[512,768]{1,0:T(8,128)(2,1)S(1)}, f32[512,768]{1,0:T(8,128)S(1)}, f32[96,512]{1,0:T(8,128)S(1)}, f32[3,72,128]{2,1,0:T(8,128)S(1)}, f32[3,...) custom-call(bf16[512,768]{1,0:T(8,128)(2,1)S(1)} %get-tuple-element.228.refs_, ...), custom_call_target="tpu_custom_call" | custom-call | flops 5750000128 | tf_op jit(solution)/shard_map/pallas_call | solution.py:157
  85.5 1.7 collective-permute-start.10
  87.2 1.0 collective-permute-start.11
  88.2 7.9 %collective-permute-done.13.refs_1_ = f32[192,768]{1,0:T(8,128)S(1)} collective-permute-done((f32[192,768]{1,0:T(8,128)S(1)}, f32[192,768]{1,0:T(8,128)S(1)}, u32[]{:S(2)}, u32[]{:S(2)}) %collective-permute-start.13) | collective-permute-done | bytes 589856 | tf_op jit(solution)/shard_map/ppermute | solution.py:662
  97.0 3.1 %shard_map.208 = (f32[96,768]{1,0:T(8,128)S(1)}, f32[96,768]{1,0:T(8,128)S(1)}, f32[96,768]{1,0:T(8,128)S(1)}, f32[384,768]{1,0:T(8,128)S(1)}, f32[384,768]{1,0:...) custom-call(f32[192,768]{1,0:T(8,128)S(1)} %get-tuple-element.242.re, ...), custom_call_target="tpu_custom_call" | custom-call | flops 8049999872 | tf_op jit(solution)/shard_map/pallas_call | solution.py:157
  100.1 1.6 collective-permute-done.12.refs_3_
  101.9 2.0 collective-permute-start.17
  103.9 3.2 %collective-permute-start.16 = (f32[3,72,128]{2,1,0:T(8,128)S(1)}, f32[3,72,128]{2,1,0:T(8,128)S(1)}, u32[]{:S(2)}, u32[]{:S(2)}) collective-permute-start(f32[3,72,128]{2,1,0:T(8,128)S(1)} %get-tuple-element.265), channel_id=1, source_target_pairs={{0,12},{1,13},{2,14},{3,15},{4,0},{5,1},{6,2},{7,3},{8,4},{9,5},{1... | collective-permute-start | bytes 331784 | tf_op jit(solution)/shard_map/ppermute | solution.py:668
  107.2 1.0 collective-permute-start.22
  108.6 3.9 %shard_map.210 = (bf16[512,768]{1,0:T(8,128)(2,1)S(1)}, f32[512,1536]{1,0:T(8,128)S(1)}, f32[512,768]{1,0:T(8,128)S(1)}, f32[768,128]{1,0:T(8,128)S(1)}, f32[8,128]{1,0:T(8,128)S(1)}) custom-call(bf16[512,768]{1,0:T(8,128)(2,1)S(1)} %copy-done.23, bf16[512,1536]{1,0:T(8,128)(2,1)S(1)} %copy-done.14, bf16[512,1536]{1,0:T(8,128)(2,1)S(1)} %copy-done.12, ...), custom_call_target="tpu_custom_call" | custom-call | flops 5175000064 | tf_op jit(solution)/shard_map/pallas_call | solution.py:157
  112.5 3.9 %shard_map.211 = (bf16[512,768]{1,0:T(8,128)(2,1)S(1)}, f32[512,1536]{1,0:T(8,128)S(1)}, f32[512,768]{1,0:T(8,128)S(1)}, f32[768,128]{1,0:T(8,128)S(1)}, f32[8,128]{1,0:T(8,128)S(1)}) custom-call(bf16[512,768]{1,0:T(8,128)(2,1)S(1)} %copy-done.23, ...), custom_call_target="tpu_custom_call", output_to_operand_aliasing={{0}: (15, {}), {1}: (16, {}), {2}: (17, {}), {3}: (18, {})} | custom-call | flops 5175000064 | tf_op jit(solution)/shard_map/pallas_call | solution.py:157
  116.4 3.9 %shard_map.212 = (bf16[512,768]{1,0:T(8,128)(2,1)S(1)}, f32[512,1536]{1,0:T(8,128)S(1)}, f32[512,768]{1,0:T(8,128)S(1)}, f32[768,128]{1,0:T(8,128)S(1)}, f32[8,128]{1,0:T(8,128)S(1)}) custom-call(bf16[512,768]{1,0:T(8,128)(2,1)S(1)} %copy-done.23, ...), custom_call_target="tpu_custom_call", output_to_operand_aliasing={{0}: (15, {}), {1}: (16, {}), {2}: (17, {}), {3}: (18, {})} | custom-call | flops 5175000064 | tf_op jit(solution)/shard_map/pallas_call | solution.py:157
  120.5 1.0 copy-done.25
  122.6 1.7 collective-permute-start.19
  124.4 19.0 %collective-permute-done.19.refs_6_ = f32[6,72,128]{2,1,0:T(8,128)S(1)} collective-permute-done((f32[6,72,128]{2,1,0:T(8,128)S(1)}, f32[6,72,128]{2,1,0:T(8,128)S(1)}, u32[]{:S(2)}, u32[]{:S(2)}) %collective-permute-start.19) | collective-permute-done | bytes 221216 | tf_op jit(solution)/shard_map/ppermute | solution.py:665
  143.4 1.0 collective-permute-start.20
  144.6 1.2 collective-permute-start.21
  145.9 2.2 shard_map.216
  149.1 1.7 collective-permute-start.27
  150.8 6.1 %shard_map.217 = (bf16[512,768]{1,0:T(8,128)(2,1)S(1)}, bf16[512,768]{1,0:T(8,128)(2,1)S(1)}, f32[768,128]{1,0:T(8,128)S(1)}, f32[8,128]{1,0:T(8,128)S(1)}) custom-call(bf16[512,768]{1,0:T(8,128)(2,1)S(1)} %copy-done.29, bf16[512,1536]{1,0:T(8,128)(2,1)S(1)} %copy-done.12, bf16[512,768]{1,0:T(8,128)(2,1)S(1)} %copy-done.21, ...), custom_call_target="tpu_custom_call" | custom-call | flops 69000003584 | tf_op jit(solution)/shard_map/pallas_call | solution.py:157
  157.0 1.1 shard_map.218
  159.7 5.2 %shard_map.219 = (f32[512,768]{1,0:T(8,128)}, f32[72,768]{1,0:T(8,128)S(1)}, f32[72,768]{1,0:T(8,128)S(1)}, f32[8,128]{1,0:T(8,128)S(1)}) custom-call(bf16[512,768]{1,0:T(8,128)(2,1)S(1)} %get-tuple-element.261.refs_1_.refs_0_, bf16[512,768]{1,0:T(8,128)(2,1)S(1)} %get-tuple-element.287.refs_2_.refs_1_.refs_3_, ...), custom_call_target="tpu_custom_call" | custom-call | flops 69000003584 | tf_op jit(solution)/shard_map/pallas_call | solution.py:157
  164.9 1.5 collective-permute-done.30.refs_8_
  166.3 1.5 shard_map.220
  167.8 1.0 collective-permute-start.38
  169.3 1.1 collective-permute-start.36
  170.4 1.8 collective-permute-start.37
  172.2 2.7 %collective-permute-done.27.refs_3_ = f32[336,768]{1,0:T(8,128)} collective-permute-done((f32[336,768]{1,0:T(8,128)}, f32[336,768]{1,0:T(8,128)}, u32[]{:S(2)}, u32[]{:S(2)}) %collective-permute-start.27) | collective-permute-done | bytes 1032224 | tf_op jit(solution)/shard_map/ppermute | solution.py:662
  174.9 1.9 shard_map.221
  177.0 4.9 %collective-permute-done.38.refs_7_ = f32[72,768]{1,0:T(8,128)S(1)} collective-permute-done((f32[72,768]{1,0:T(8,128)S(1)}, f32[72,768]{1,0:T(8,128)S(1)}, u32[]{:S(2)}, u32[]{:S(2)}) %collective-permute-start.38) | collective-permute-done | bytes 221216 | tf_op jit(solution)/shard_map/ppermute | solution.py:662
  181.9 3.8 %collective-permute-done.35.refs_1_ = f32[192,768]{1,0:T(8,128)S(1)} collective-permute-done((f32[192,768]{1,0:T(8,128)S(1)}, f32[192,768]{1,0:T(8,128)S(1)}, u32[]{:S(2)}, u32[]{:S(2)}) %collective-permute-start.35) | collective-permute-done | bytes 589856 | tf_op jit(solution)/shard_map/ppermute | solution.py:662
  185.7 1.7 collective-permute-start.33
  187.4 1.0 collective-permute-start.34
  188.4 6.5 %collective-permute-done.37.refs_5_ = f32[192,768]{1,0:T(8,128)S(1)} collective-permute-done((f32[192,768]{1,0:T(8,128)S(1)}, f32[192,768]{1,0:T(8,128)S(1)}, u32[]{:S(2)}, u32[]{:S(2)}) %collective-permute-start.37) | collective-permute-done | bytes 589856 | tf_op jit(solution)/shard_map/ppermute | solution.py:662
  195.1 1.0 collective-permute-start.41
  196.3 4.9 %collective-permute-done.32.refs_5_ = f32[96,768]{1,0:T(8,128)S(1)} collective-permute-done((f32[96,768]{1,0:T(8,128)S(1)}, f32[96,768]{1,0:T(8,128)S(1)}, u32[]{:S(2)}, u32[]{:S(2)}) %collective-permute-start.32) | collective-permute-done | bytes 294944 | tf_op jit(solution)/shard_map/ppermute | solution.py:662
  201.2 1.6 collective-permute-start.43
  203.0 4.5 %collective-permute-start.39 = (f32[120,768]{1,0:T(8,128)S(1)}, f32[120,768]{1,0:T(8,128)S(1)}, u32[]{:S(2)}, u32[]{:S(2)}) collective-permute-start(f32[120,768]{1,0:T(8,128)S(1)} %get-tuple-element.335), channel_id=1, source_target_pairs={{0,8},{1,9},{2,10},{3,11},{4,12},{5,13},{6,14},{7,15},{8,0},{9,1},... | collective-permute-start | bytes 1105928 | tf_op jit(solution)/shard_map/ppermute | solution.py:662
  207.5 5.7 %collective-permute-done.42.refs_3_ = f32[96,768]{1,0:T(8,128)S(1)} collective-permute-done((f32[96,768]{1,0:T(8,128)S(1)}, f32[96,768]{1,0:T(8,128)S(1)}, u32[]{:S(2)}, u32[]{:S(2)}) %collective-permute-start.42) | collective-permute-done | bytes 294944 | tf_op jit(solution)/shard_map/ppermute | solution.py:662
  213.4 1.5 collective-permute-start.46
  216.4 4.6 %collective-permute-done.39.refs_2_ = f32[120,768]{1,0:T(8,128)S(1)} collective-permute-done((f32[120,768]{1,0:T(8,128)S(1)}, f32[120,768]{1,0:T(8,128)S(1)}, u32[]{:S(2)}, u32[]{:S(2)}) %collective-permute-start.39) | collective-permute-done | bytes 368672 | tf_op jit(solution)/shard_map/ppermute | solution.py:662
  222.5 2.0 collective-permute-start.49
  224.5 2.0 collective-permute-start.48
  227.4 1.4 collective-permute-done.49.refs_1_
  228.9 6.6 %collective-permute-done.44.refs_1_ = f32[24,768]{1,0:T(8,128)S(1)} collective-permute-done((f32[24,768]{1,0:T(8,128)S(1)}, f32[24,768]{1,0:T(8,128)S(1)}, u32[]{:S(2)}, u32[]{:S(2)}) %collective-permute-start.44) | collective-permute-done | bytes 73760 | tf_op jit(solution)/shard_map/ppermute | solution.py:662
  236.3 1.0 shard_map.229
  (140 shorter events, 19.6 us)
Async XLA Ops:
  1.3 13.5 %copy-start = (bf16[768,2304]{1,0:T(8,128)(2,1)S(1)}, bf16[768,2304]{1,0:T(8,128)(2,1)}, u32[]{:S(2)}) copy-start(bf16[768,2304]{1,0:T(8,128)(2,1)} %refs_3_.5) | copy-start | bytes 10616836
  1.3 13.5 %copy-start.6 = (bf16[12,64,64]{2,1,0:T(8,128)(2,1)S(1)}, bf16[12,64,64]{2,1,0:T(8,128)(2,1)}, u32[]{:S(2)}) copy-start(bf16[12,64,64]{2,1,0:T(8,128)(2,1)} %refs_14_.5) | copy-start | bytes 294916
  1.3 27.8 %slice-start = ((s8[4718592]{0:T(1024)(128)(4,1)}), s8[4194304]{0:T(1024)(128)(4,1)S(1)}, s32[]{:S(2)}) async-start(s8[4718592]{0:T(1024)(128)(4,1)} %bitcast.13), calls=%async_computation | async-start | bytes 8388608
  10.2 12.7 %copy-start.11 = (bf16[512,1536]{1,0:T(8,128)(2,1)}, bf16[512,1536]{1,0:T(8,128)(2,1)S(1)}, u32[]{:S(2)}) copy-start(bf16[512,1536]{1,0:T(8,128)(2,1)S(1)} %get-tuple-element.194.refs_3_.refs_2_.refs_1_) | copy-start | bytes 4718596
  10.2 12.7 %copy-start.15 = (f32[512,512]{1,0:T(8,128)}, f32[512,512]{1,0:T(8,128)S(1)}, u32[]{:S(2)}) copy-start(f32[512,512]{1,0:T(8,128)S(1)} %get-tuple-element.196.refs_5_.refs_11_) | copy-start | bytes 3145732
  10.2 12.7 %copy-start.17 = (f32[512,512]{1,0:T(8,128)}, f32[512,512]{1,0:T(8,128)S(1)}, u32[]{:S(2)}) copy-start(f32[512,512]{1,0:T(8,128)S(1)} %get-tuple-element.237.refs_12_) | copy-start | bytes 3145732
  10.2 12.7 %copy-start.19 = (bf16[512,768]{1,0:T(8,128)(2,1)}, bf16[512,768]{1,0:T(8,128)(2,1)S(1)}, u32[]{:S(2)}) copy-start(bf16[512,768]{1,0:T(8,128)(2,1)S(1)} %get-tuple-element.195.refs_4_.refs_3_.refs_2_) | copy-start | bytes 2359300
  10.2 12.7 %copy-start.28 = (bf16[512,768]{1,0:T(8,128)(2,1)}, bf16[512,768]{1,0:T(8,128)(2,1)S(1)}, u32[]{:S(2)}) copy-start(bf16[512,768]{1,0:T(8,128)(2,1)S(1)} %get-tuple-element.262.refs_0_) | copy-start | bytes 2359300
  10.3 12.7 %collective-permute-start = (f32[3,72,128]{2,1,0:T(8,128)S(1)}, f32[3,72,128]{2,1,0:T(8,128)S(1)}, u32[]{:S(2)}, u32[]{:S(2)}) collective-permute-start(f32[3,72,128]{2,1,0:T(8,128)S(1)} %get-tuple-element.201), channel_id=1, source_target_pairs={{0,1},{1,0},{2,3},{3,2},{4,5},{5,4},{6,7},{7,6},{8,9},{9,8},{10,11... | collective-permute-start | bytes 331784 | tf_op jit(solution)/shard_map/ppermute | solution.py:665
  13.3 9.8 %collective-permute-start.1 = (f32[3,72,128]{2,1,0:T(8,128)S(1)}, f32[3,72,128]{2,1,0:T(8,128)S(1)}, u32[]{:S(2)}, u32[]{:S(2)}) collective-permute-start(f32[3,72,128]{2,1,0:T(8,128)S(1)} %get-tuple-element.202), channel_id=1, source_target_pairs={{0,2},{1,3},{2,0},{3,1},{4,6},{5,7},{6,4},{7,5},{8,10},{9,11},{10,... | collective-permute-start | bytes 331784 | tf_op jit(solution)/shard_map/ppermute | solution.py:665
  14.8 8.2 %collective-permute-start.2 = (f32[3,72,128]{2,1,0:T(8,128)S(1)}, f32[3,72,128]{2,1,0:T(8,128)S(1)}, u32[]{:S(2)}, u32[]{:S(2)}) collective-permute-start(f32[3,72,128]{2,1,0:T(8,128)S(1)} %get-tuple-element.203), channel_id=1, source_target_pairs={{0,3},{1,2},{2,1},{3,0},{4,7},{5,6},{6,5},{7,4},{8,11},{9,10},{10,... | collective-permute-start | bytes 331784 | tf_op jit(solution)/shard_map/ppermute | solution.py:665
  14.8 14.3 %slice-start.1 = ((s8[4718592]{0:T(1024)(128)(4,1)}), s8[524288]{0:T(1024)(128)(4,1)S(1)}, s32[]{:S(2)}) async-start(s8[4718592]{0:T(1024)(128)(4,1)} %bitcast.13), calls=%async_computation.1 | async-start | bytes 1048576
  23.0 58.4 %copy-start.13 = (bf16[512,1536]{1,0:T(8,128)(2,1)}, bf16[512,1536]{1,0:T(8,128)(2,1)S(1)}, u32[]{:S(2)}) copy-start(bf16[512,1536]{1,0:T(8,128)(2,1)S(1)} %get-tuple-element.199.refs_2_.refs_4_.refs_1_) | copy-start | bytes 4718596
  23.9 8.5 %collective-permute-start.5 = (f32[3,72,128]{2,1,0:T(8,128)S(1)}, f32[3,72,128]{2,1,0:T(8,128)S(1)}, u32[]{:S(2)}, u32[]{:S(2)}) collective-permute-start(f32[3,72,128]{2,1,0:T(8,128)S(1)} %get-tuple-element.205), channel_id=1, source_target_pairs={{0,12},{1,13},{2,14},{3,15},{4,0},{5,1},{6,2},{7,3},{8,4},{9,5},{1... | collective-permute-start | bytes 331784 | tf_op jit(solution)/shard_map/ppermute | solution.py:668
  27.9 9.3 %collective-permute-start.4 = (f32[3,72,128]{2,1,0:T(8,128)S(1)}, f32[3,72,128]{2,1,0:T(8,128)S(1)}, u32[]{:S(2)}, u32[]{:S(2)}) collective-permute-start(f32[3,72,128]{2,1,0:T(8,128)S(1)} %get-tuple-element.205), channel_id=1, source_target_pairs={{0,8},{1,9},{2,10},{3,11},{4,12},{5,13},{6,14},{7,15},{8,0},{9,1},... | collective-permute-start | bytes 331784 | tf_op jit(solution)/shard_map/ppermute | solution.py:668
  27.9 9.3 %collective-permute-start.3 = (f32[3,72,128]{2,1,0:T(8,128)S(1)}, f32[3,72,128]{2,1,0:T(8,128)S(1)}, u32[]{:S(2)}, u32[]{:S(2)}) collective-permute-start(f32[3,72,128]{2,1,0:T(8,128)S(1)} %get-tuple-element.205), channel_id=1, source_target_pairs={{0,4},{1,5},{2,6},{3,7},{4,8},{5,9},{6,10},{7,11},{8,12},{9,13},{1... | collective-permute-start | bytes 331784 | tf_op jit(solution)/shard_map/ppermute | solution.py:668
  37.3 6.7 %collective-permute-start.6 = (f32[3,72,128]{2,1,0:T(8,128)S(1)}, f32[3,72,128]{2,1,0:T(8,128)S(1)}, u32[]{:S(2)}, u32[]{:S(2)}) collective-permute-start(f32[3,72,128]{2,1,0:T(8,128)S(1)} %get-tuple-element.209), channel_id=1, source_target_pairs={{0,1},{1,0},{2,3},{3,2},{4,5},{5,4},{6,7},{7,6},{8,9},{9,8},{10,11... | collective-permute-start | bytes 331784 | tf_op jit(solution)/shard_map/ppermute | solution.py:665
  38.9 5.9 %collective-permute-start.7 = (f32[3,72,128]{2,1,0:T(8,128)S(1)}, f32[3,72,128]{2,1,0:T(8,128)S(1)}, u32[]{:S(2)}, u32[]{:S(2)}) collective-permute-start(f32[3,72,128]{2,1,0:T(8,128)S(1)} %get-tuple-element.210), channel_id=1, source_target_pairs={{0,2},{1,3},{2,0},{3,1},{4,6},{5,7},{6,4},{7,5},{8,10},{9,11},{10,... | collective-permute-start | bytes 331784 | tf_op jit(solution)/shard_map/ppermute | solution.py:665
  40.4 5.6 %collective-permute-start.8 = (f32[3,72,128]{2,1,0:T(8,128)S(1)}, f32[3,72,128]{2,1,0:T(8,128)S(1)}, u32[]{:S(2)}, u32[]{:S(2)}) collective-permute-start(f32[3,72,128]{2,1,0:T(8,128)S(1)} %get-tuple-element.211), channel_id=1, source_target_pairs={{0,3},{1,2},{2,1},{3,0},{4,7},{5,6},{6,5},{7,4},{8,11},{9,10},{10,... | collective-permute-start | bytes 331784 | tf_op jit(solution)/shard_map/ppermute | solution.py:665
  63.3 14.9 %collective-permute-start.9 = (f32[2,4,384,768]{3,2,1,0:T(8,128)}, f32[2,4,384,768]{3,2,1,0:T(8,128)S(1)}, u32[]{:S(2)}, u32[]{:S(2)}) collective-permute-start(f32[2,4,384,768]{3,2,1,0:T(8,128)} %get-tuple-element.231), channel_id=1, source_target_pairs={{0,16},{16,0},{1,17},{17,1},{2,18},{18,2},{3,19},{19,3},{4,20},{20... | collective-permute-start | bytes 28311560 | tf_op jit(solution)/shard_map/ppermute | solution.py:641
  79.9 16.2 %collective-permute-start.13 = (f32[192,768]{1,0:T(8,128)S(1)}, f32[192,768]{1,0:T(8,128)S(1)}, u32[]{:S(2)}, u32[]{:S(2)}) collective-permute-start(f32[192,768]{1,0:T(8,128)S(1)} %get-tuple-element.243), channel_id=1, source_target_pairs={{0,1},{1,0},{2,3},{3,2},{4,5},{5,4},{6,7},{7,6},{8,9},{9,8},{10,11... | collective-permute-start | bytes 1769480 | tf_op jit(solution)/shard_map/ppermute | solution.py:662
  80.5 16.4 %collective-permute-start.14 = (f32[192,768]{1,0:T(8,128)S(1)}, f32[192,768]{1,0:T(8,128)S(1)}, u32[]{:S(2)}, u32[]{:S(2)}) collective-permute-start(f32[192,768]{1,0:T(8,128)S(1)} %get-tuple-element.245), channel_id=1, source_target_pairs={{0,2},{1,3},{2,0},{3,1},{4,6},{5,7},{6,4},{7,5},{8,10},{9,11},{10,... | collective-permute-start | bytes 1769480 | tf_op jit(solution)/shard_map/ppermute | solution.py:662
  81.4 15.6 %collective-permute-start.15 = (f32[192,768]{1,0:T(8,128)S(1)}, f32[192,768]{1,0:T(8,128)S(1)}, u32[]{:S(2)}, u32[]{:S(2)}) collective-permute-start(f32[192,768]{1,0:T(8,128)S(1)} %get-tuple-element.247), channel_id=1, source_target_pairs={{0,4},{1,5},{2,6},{3,7},{4,0},{5,1},{6,2},{7,3},{8,12},{9,13},{10,... | collective-permute-start | bytes 1769480 | tf_op jit(solution)/shard_map/ppermute | solution.py:662
  85.5 14.6 %collective-permute-start.10 = (f32[3,72,128]{2,1,0:T(8,128)S(1)}, f32[3,72,128]{2,1,0:T(8,128)S(1)}, u32[]{:S(2)}, u32[]{:S(2)}) collective-permute-start(f32[3,72,128]{2,1,0:T(8,128)S(1)} %get-tuple-element.239), channel_id=1, source_target_pairs={{0,1},{1,0},{2,3},{3,2},{4,5},{5,4},{6,7},{7,6},{8,9},{9,8},{10,11... | collective-permute-start | bytes 331784 | tf_op jit(solution)/shard_map/ppermute | solution.py:665
  87.2 12.9 %collective-permute-start.11 = (f32[3,72,128]{2,1,0:T(8,128)S(1)}, f32[3,72,128]{2,1,0:T(8,128)S(1)}, u32[]{:S(2)}, u32[]{:S(2)}) collective-permute-start(f32[3,72,128]{2,1,0:T(8,128)S(1)} %get-tuple-element.240), channel_id=1, source_target_pairs={{0,2},{1,3},{2,0},{3,1},{4,6},{5,7},{6,4},{7,5},{8,10},{9,11},{10,... | collective-permute-start | bytes 331784 | tf_op jit(solution)/shard_map/ppermute | solution.py:665
  96.1 5.6 %collective-permute-start.12 = (f32[3,72,128]{2,1,0:T(8,128)S(1)}, f32[3,72,128]{2,1,0:T(8,128)S(1)}, u32[]{:S(2)}, u32[]{:S(2)}) collective-permute-start(f32[3,72,128]{2,1,0:T(8,128)S(1)} %get-tuple-element.241), channel_id=1, source_target_pairs={{0,3},{1,2},{2,1},{3,0},{4,7},{5,6},{6,5},{7,4},{8,11},{9,10},{10,... | collective-permute-start | bytes 331784 | tf_op jit(solution)/shard_map/ppermute | solution.py:665
  97.0 11.6 %copy-start.18 = (f32[512,512]{1,0:T(8,128)S(1)}, f32[512,512]{1,0:T(8,128)}, u32[]{:S(2)}) copy-start(f32[512,512]{1,0:T(8,128)} %copy-done.17) | copy-start | bytes 3145732
  97.0 11.6 %copy-start.20 = (bf16[512,768]{1,0:T(8,128)(2,1)S(1)}, bf16[512,768]{1,0:T(8,128)(2,1)}, u32[]{:S(2)}) copy-start(bf16[512,768]{1,0:T(8,128)(2,1)} %copy-done.19) | copy-start | bytes 2359300
  97.0 11.5 %copy-start.23 = (bf16[512,768]{1,0:T(8,128)(2,1)S(1)}, bf16[512,768]{1,0:T(8,128)(2,1)}, u32[]{:S(2)}) copy-start(bf16[512,768]{1,0:T(8,128)(2,1)} %copy-done.22) | copy-start | bytes 2359300
  101.8 18.5 %collective-permute-start.18 = (f32[3,72,128]{2,1,0:T(8,128)S(1)}, f32[3,72,128]{2,1,0:T(8,128)S(1)}, u32[]{:S(2)}, u32[]{:S(2)}) collective-permute-start(f32[3,72,128]{2,1,0:T(8,128)S(1)} %get-tuple-element.265), channel_id=1, source_target_pairs={{0,4},{1,5},{2,6},{3,7},{4,8},{5,9},{6,10},{7,11},{8,12},{9,13},{1... | collective-permute-start | bytes 331784 | tf_op jit(solution)/shard_map/ppermute | solution.py:668
  101.9 18.4 %collective-permute-start.17 = (f32[3,72,128]{2,1,0:T(8,128)S(1)}, f32[3,72,128]{2,1,0:T(8,128)S(1)}, u32[]{:S(2)}, u32[]{:S(2)}) collective-permute-start(f32[3,72,128]{2,1,0:T(8,128)S(1)} %get-tuple-element.265), channel_id=1, source_target_pairs={{0,8},{1,9},{2,10},{3,11},{4,12},{5,13},{6,14},{7,15},{8,0},{9,1},... | collective-permute-start | bytes 331784 | tf_op jit(solution)/shard_map/ppermute | solution.py:668
  103.9 16.4 %collective-permute-start.16 = (f32[3,72,128]{2,1,0:T(8,128)S(1)}, f32[3,72,128]{2,1,0:T(8,128)S(1)}, u32[]{:S(2)}, u32[]{:S(2)}) collective-permute-start(f32[3,72,128]{2,1,0:T(8,128)S(1)} %get-tuple-element.265), channel_id=1, source_target_pairs={{0,12},{1,13},{2,14},{3,15},{4,0},{5,1},{6,2},{7,3},{8,4},{9,5},{1... | collective-permute-start | bytes 331784 | tf_op jit(solution)/shard_map/ppermute | solution.py:668
  107.2 38.7 %collective-permute-start.22 = (f32[480,768]{1,0:T(8,128)S(1)}, f32[480,768]{1,0:T(8,128)S(1)}, u32[]{:S(2)}, u32[]{:S(2)}) collective-permute-start(f32[480,768]{1,0:T(8,128)S(1)} %get-tuple-element.272), channel_id=1, source_target_pairs={{0,2},{1,3},{2,0},{3,1},{4,6},{5,7},{6,4},{7,5},{8,10},{9,11},{10,... | collective-permute-start | bytes 4423688 | tf_op jit(solution)/shard_map/ppermute | solution.py:662
  108.2 37.6 %collective-permute-start.24 = (f32[480,768]{1,0:T(8,128)S(1)}, f32[480,768]{1,0:T(8,128)S(1)}, u32[]{:S(2)}, u32[]{:S(2)}) collective-permute-start(f32[480,768]{1,0:T(8,128)S(1)} %get-tuple-element.276), channel_id=1, source_target_pairs={{0,1},{1,0},{2,3},{3,2},{4,5},{5,4},{6,7},{7,6},{8,9},{9,8},{10,11... | collective-permute-start | bytes 4423688 | tf_op jit(solution)/shard_map/ppermute | solution.py:662
  122.3 23.5 %collective-permute-start.25 = (f32[1,384,768]{2,1,0:T(8,128)S(1)}, f32[1,384,768]{2,1,0:T(8,128)S(1)}, u32[]{:S(2)}, u32[]{:S(2)}) collective-permute-start(f32[1,384,768]{2,1,0:T(8,128)S(1)} %get-tuple-element.284), channel_id=1, source_target_pairs={{0,16},{16,0},{1,17},{17,1},{2,18},{18,2},{3,19},{19,3},{4,20},{20... | collective-permute-start | bytes 3538952 | tf_op jit(solution)/shard_map/ppermute | solution.py:641
  122.6 22.1 %collective-permute-start.23 = (f32[288,768]{1,0:T(8,128)S(1)}, f32[288,768]{1,0:T(8,128)S(1)}, u32[]{:S(2)}, u32[]{:S(2)}) collective-permute-start(f32[288,768]{1,0:T(8,128)S(1)} %get-tuple-element.274), channel_id=1, source_target_pairs={{0,4},{1,5},{2,6},{3,7},{4,0},{5,1},{6,2},{7,3},{8,12},{9,13},{10,... | collective-permute-start | bytes 2654216 | tf_op jit(solution)/shard_map/ppermute | solution.py:662
  122.6 20.7 %collective-permute-start.19 = (f32[6,72,128]{2,1,0:T(8,128)S(1)}, f32[6,72,128]{2,1,0:T(8,128)S(1)}, u32[]{:S(2)}, u32[]{:S(2)}) collective-permute-start(f32[6,72,128]{2,1,0:T(8,128)S(1)} %get-tuple-element.268), channel_id=1, source_target_pairs={{0,1},{1,0},{2,3},{3,2},{4,5},{5,4},{6,7},{7,6},{8,9},{9,8},{10,11... | collective-permute-start | bytes 663560 | tf_op jit(solution)/shard_map/ppermute | solution.py:665
  143.4 7.4 %collective-permute-start.20 = (f32[3,72,128]{2,1,0:T(8,128)S(1)}, f32[3,72,128]{2,1,0:T(8,128)S(1)}, u32[]{:S(2)}, u32[]{:S(2)}) collective-permute-start(f32[3,72,128]{2,1,0:T(8,128)S(1)} %get-tuple-element.269), channel_id=1, source_target_pairs={{0,2},{1,3},{2,0},{3,1},{4,6},{5,7},{6,4},{7,5},{8,10},{9,11},{10,... | collective-permute-start | bytes 331784 | tf_op jit(solution)/shard_map/ppermute | solution.py:665
  144.6 6.2 %collective-permute-start.21 = (f32[3,72,128]{2,1,0:T(8,128)S(1)}, f32[3,72,128]{2,1,0:T(8,128)S(1)}, u32[]{:S(2)}, u32[]{:S(2)}) collective-permute-start(f32[3,72,128]{2,1,0:T(8,128)S(1)} %slice.12), channel_id=1, source_target_pairs={{0,2},{1,3},{2,0},{3,1},{4,6},{5,7},{6,4},{7,5},{8,10},{9,11},{10,... | collective-permute-start | bytes 331784 | tf_op jit(solution)/shard_map/ppermute | solution.py:665
  148.0 21.3 %collective-permute-start.26 = (f32[240,768]{1,0:T(8,128)}, f32[240,768]{1,0:T(8,128)}, u32[]{:S(2)}, u32[]{:S(2)}) collective-permute-start(f32[240,768]{1,0:T(8,128)} %get-tuple-element.298), channel_id=1, source_target_pairs={{0,4},{1,5},{2,6},{3,7},{4,0},{5,1},{6,2},{7,3},{8,12},{9,13},{10,... | collective-permute-start | bytes 2211848 | tf_op jit(solution)/shard_map/ppermute | solution.py:662
  148.3 22.1 %collective-permute-start.28 = (f32[240,768]{1,0:T(8,128)}, f32[240,768]{1,0:T(8,128)}, u32[]{:S(2)}, u32[]{:S(2)}) collective-permute-start(f32[240,768]{1,0:T(8,128)} %get-tuple-element.302), channel_id=1, source_target_pairs={{0,2},{1,3},{2,0},{3,1},{4,6},{5,7},{6,4},{7,5},{8,10},{9,11},{10,... | collective-permute-start | bytes 2211848 | tf_op jit(solution)/shard_map/ppermute | solution.py:662
  149.1 25.7 %collective-permute-start.27 = (f32[336,768]{1,0:T(8,128)}, f32[336,768]{1,0:T(8,128)}, u32[]{:S(2)}, u32[]{:S(2)}) collective-permute-start(f32[336,768]{1,0:T(8,128)} %get-tuple-element.300), channel_id=1, source_target_pairs={{0,1},{1,0},{2,3},{3,2},{4,5},{5,4},{6,7},{7,6},{8,9},{9,8},{10,11... | collective-permute-start | bytes 3096584 | tf_op jit(solution)/shard_map/ppermute | solution.py:662
  158.1 8.3 %collective-permute-start.29 = (f32[3,384,768]{2,1,0:T(8,128)S(1)}, f32[3,384,768]{2,1,0:T(8,128)S(1)}, u32[]{:S(2)}, u32[]{:S(2)}) collective-permute-start(f32[3,384,768]{2,1,0:T(8,128)S(1)} %get-tuple-element.307), channel_id=1, source_target_pairs={{0,16},{16,0},{1,17},{17,1},{2,18},{18,2},{3,19},{19,3},{4,20},{20... | collective-permute-start | bytes 10616840 | tf_op jit(solution)/shard_map/ppermute | solution.py:641
  164.9 1.5 collective-permute-start.30
  167.8 14.1 %collective-permute-start.38 = (f32[72,768]{1,0:T(8,128)S(1)}, f32[72,768]{1,0:T(8,128)S(1)}, u32[]{:S(2)}, u32[]{:S(2)}) collective-permute-start(f32[72,768]{1,0:T(8,128)S(1)} %get-tuple-element.330), channel_id=1, source_target_pairs={{0,8},{1,9},{2,10},{3,11},{4,12},{5,13},{6,14},{7,15},{8,0},{9,1},... | collective-permute-start | bytes 663560 | tf_op jit(solution)/shard_map/ppermute | solution.py:662
  168.8 16.9 %collective-permute-start.35 = (f32[192,768]{1,0:T(8,128)S(1)}, f32[192,768]{1,0:T(8,128)S(1)}, u32[]{:S(2)}, u32[]{:S(2)}) collective-permute-start(f32[192,768]{1,0:T(8,128)S(1)} %get-tuple-element.324), channel_id=1, source_target_pairs={{0,1},{1,0},{2,3},{3,2},{4,5},{5,4},{6,7},{7,6},{8,9},{9,8},{10,11... | collective-permute-start | bytes 1769480 | tf_op jit(solution)/shard_map/ppermute | solution.py:662
  169.3 18.0 %collective-permute-start.36 = (f32[192,768]{1,0:T(8,128)S(1)}, f32[192,768]{1,0:T(8,128)S(1)}, u32[]{:S(2)}, u32[]{:S(2)}) collective-permute-start(f32[192,768]{1,0:T(8,128)S(1)} %get-tuple-element.326), channel_id=1, source_target_pairs={{0,2},{1,3},{2,0},{3,1},{4,6},{5,7},{6,4},{7,5},{8,10},{9,11},{10,... | collective-permute-start | bytes 1769480 | tf_op jit(solution)/shard_map/ppermute | solution.py:662
  170.4 24.4 %collective-permute-start.37 = (f32[192,768]{1,0:T(8,128)S(1)}, f32[192,768]{1,0:T(8,128)S(1)}, u32[]{:S(2)}, u32[]{:S(2)}) collective-permute-start(f32[192,768]{1,0:T(8,128)S(1)} %get-tuple-element.328), channel_id=1, source_target_pairs={{0,4},{1,5},{2,6},{3,7},{4,0},{5,1},{6,2},{7,3},{8,12},{9,13},{10,... | collective-permute-start | bytes 1769480 | tf_op jit(solution)/shard_map/ppermute | solution.py:662
  176.8 19.3 %collective-permute-start.31 = (f32[72,768]{1,0:T(8,128)S(1)}, f32[72,768]{1,0:T(8,128)S(1)}, u32[]{:S(2)}, u32[]{:S(2)}) collective-permute-start(f32[72,768]{1,0:T(8,128)S(1)} %get-tuple-element.313), channel_id=1, source_target_pairs={{0,8},{1,9},{2,10},{3,11},{4,12},{5,13},{6,14},{7,15},{8,0},{9,1},... | collective-permute-start | bytes 663560 | tf_op jit(solution)/shard_map/ppermute | solution.py:662
  181.9 19.3 %collective-permute-start.32 = (f32[96,768]{1,0:T(8,128)S(1)}, f32[96,768]{1,0:T(8,128)S(1)}, u32[]{:S(2)}, u32[]{:S(2)}) collective-permute-start(f32[96,768]{1,0:T(8,128)S(1)} %get-tuple-element.317), channel_id=1, source_target_pairs={{0,4},{1,5},{2,6},{3,7},{4,0},{5,1},{6,2},{7,3},{8,12},{9,13},{10,... | collective-permute-start | bytes 884744 | tf_op jit(solution)/shard_map/ppermute | solution.py:662
  185.7 17.1 %collective-permute-start.33 = (f32[96,768]{1,0:T(8,128)S(1)}, f32[96,768]{1,0:T(8,128)S(1)}, u32[]{:S(2)}, u32[]{:S(2)}) collective-permute-start(f32[96,768]{1,0:T(8,128)S(1)} %get-tuple-element.319), channel_id=1, source_target_pairs={{0,1},{1,0},{2,3},{3,2},{4,5},{5,4},{6,7},{7,6},{8,9},{9,8},{10,11... | collective-permute-start | bytes 884744 | tf_op jit(solution)/shard_map/ppermute | solution.py:662
  187.4 15.4 %collective-permute-start.34 = (f32[144,768]{1,0:T(8,128)S(1)}, f32[144,768]{1,0:T(8,128)S(1)}, u32[]{:S(2)}, u32[]{:S(2)}) collective-permute-start(f32[144,768]{1,0:T(8,128)S(1)} %get-tuple-element.321), channel_id=1, source_target_pairs={{0,2},{1,3},{2,0},{3,1},{4,6},{5,7},{6,4},{7,5},{8,10},{9,11},{10,... | collective-permute-start | bytes 1327112 | tf_op jit(solution)/shard_map/ppermute | solution.py:662
  195.1 12.4 %collective-permute-start.41 = (f32[96,768]{1,0:T(8,128)S(1)}, f32[96,768]{1,0:T(8,128)S(1)}, u32[]{:S(2)}, u32[]{:S(2)}) collective-permute-start(f32[96,768]{1,0:T(8,128)S(1)} %get-tuple-element.341), channel_id=1, source_target_pairs={{0,2},{1,3},{2,0},{3,1},{4,6},{5,7},{6,4},{7,5},{8,10},{9,11},{10,... | collective-permute-start | bytes 884744 | tf_op jit(solution)/shard_map/ppermute | solution.py:662
  196.1 17.1 %collective-permute-start.42 = (f32[96,768]{1,0:T(8,128)S(1)}, f32[96,768]{1,0:T(8,128)S(1)}, u32[]{:S(2)}, u32[]{:S(2)}) collective-permute-start(f32[96,768]{1,0:T(8,128)S(1)} %get-tuple-element.343), channel_id=1, source_target_pairs={{0,4},{1,5},{2,6},{3,7},{4,0},{5,1},{6,2},{7,3},{8,12},{9,13},{10,... | collective-permute-start | bytes 884744 | tf_op jit(solution)/shard_map/ppermute | solution.py:662
  201.2 12.0 %collective-permute-start.43 = (f32[168,768]{1,0:T(8,128)S(1)}, f32[168,768]{1,0:T(8,128)S(1)}, u32[]{:S(2)}, u32[]{:S(2)}) collective-permute-start(f32[168,768]{1,0:T(8,128)S(1)} %get-tuple-element.345), channel_id=1, source_target_pairs={{0,1},{1,0},{2,3},{3,2},{4,5},{5,4},{6,7},{7,6},{8,9},{9,8},{10,11... | collective-permute-start | bytes 1548296 | tf_op jit(solution)/shard_map/ppermute | solution.py:662
  202.9 13.4 %collective-permute-start.40 = (f32[48,768]{1,0:T(8,128)S(1)}, f32[48,768]{1,0:T(8,128)S(1)}, u32[]{:S(2)}, u32[]{:S(2)}) collective-permute-start(f32[48,768]{1,0:T(8,128)S(1)} %get-tuple-element.339), channel_id=1, source_target_pairs={{0,4},{1,5},{2,6},{3,7},{4,0},{5,1},{6,2},{7,3},{8,12},{9,13},{10,... | collective-permute-start | bytes 442376 | tf_op jit(solution)/shard_map/ppermute | solution.py:662
  203.0 18.0 %collective-permute-start.39 = (f32[120,768]{1,0:T(8,128)S(1)}, f32[120,768]{1,0:T(8,128)S(1)}, u32[]{:S(2)}, u32[]{:S(2)}) collective-permute-start(f32[120,768]{1,0:T(8,128)S(1)} %get-tuple-element.335), channel_id=1, source_target_pairs={{0,8},{1,9},{2,10},{3,11},{4,12},{5,13},{6,14},{7,15},{8,0},{9,1},... | collective-permute-start | bytes 1105928 | tf_op jit(solution)/shard_map/ppermute | solution.py:662
  213.3 8.5 %collective-permute-start.45 = (f32[48,768]{1,0:T(8,128)S(1)}, f32[48,768]{1,0:T(8,128)S(1)}, u32[]{:S(2)}, u32[]{:S(2)}) collective-permute-start(f32[48,768]{1,0:T(8,128)S(1)} %get-tuple-element.352), channel_id=1, source_target_pairs={{0,4},{1,5},{2,6},{3,7},{4,0},{5,1},{6,2},{7,3},{8,12},{9,13},{10,... | collective-permute-start | bytes 442376 | tf_op jit(solution)/shard_map/ppermute | solution.py:662
  213.4 8.5 %collective-permute-start.46 = (f32[48,768]{1,0:T(8,128)S(1)}, f32[48,768]{1,0:T(8,128)S(1)}, u32[]{:S(2)}, u32[]{:S(2)}) collective-permute-start(f32[48,768]{1,0:T(8,128)S(1)} %get-tuple-element.354), channel_id=1, source_target_pairs={{0,1},{1,0},{2,3},{3,2},{4,5},{5,4},{6,7},{7,6},{8,9},{9,8},{10,11... | collective-permute-start | bytes 442376 | tf_op jit(solution)/shard_map/ppermute | solution.py:662
  214.9 7.5 %collective-permute-start.47 = (f32[120,768]{1,0:T(8,128)S(1)}, f32[120,768]{1,0:T(8,128)S(1)}, u32[]{:S(2)}, u32[]{:S(2)}) collective-permute-start(f32[120,768]{1,0:T(8,128)S(1)} %get-tuple-element.356), channel_id=1, source_target_pairs={{0,2},{1,3},{2,0},{3,1},{4,6},{5,7},{6,4},{7,5},{8,10},{9,11},{10,... | collective-permute-start | bytes 1105928 | tf_op jit(solution)/shard_map/ppermute | solution.py:662
  222.5 6.3 %collective-permute-start.49 = (f32[72,768]{1,0:T(8,128)S(1)}, f32[72,768]{1,0:T(8,128)S(1)}, u32[]{:S(2)}, u32[]{:S(2)}) collective-permute-start(f32[72,768]{1,0:T(8,128)S(1)} %get-tuple-element.364), channel_id=1, source_target_pairs={{0,4},{1,5},{2,6},{3,7},{4,0},{5,1},{6,2},{7,3},{8,12},{9,13},{10,... | collective-permute-start | bytes 663560 | tf_op jit(solution)/shard_map/ppermute | solution.py:662
  224.5 11.0 %collective-permute-start.48 = (f32[72,768]{1,0:T(8,128)S(1)}, f32[72,768]{1,0:T(8,128)S(1)}, u32[]{:S(2)}, u32[]{:S(2)}) collective-permute-start(f32[72,768]{1,0:T(8,128)S(1)} %get-tuple-element.360), channel_id=1, source_target_pairs={{0,8},{1,9},{2,10},{3,11},{4,12},{5,13},{6,14},{7,15},{8,0},{9,1},... | collective-permute-start | bytes 663560 | tf_op jit(solution)/shard_map/ppermute | solution.py:662
  226.5 9.0 %collective-permute-start.44 = (f32[24,768]{1,0:T(8,128)S(1)}, f32[24,768]{1,0:T(8,128)S(1)}, u32[]{:S(2)}, u32[]{:S(2)}) collective-permute-start(f32[24,768]{1,0:T(8,128)S(1)} %get-tuple-element.350), channel_id=1, source_target_pairs={{0,8},{1,9},{2,10},{3,11},{4,12},{5,13},{6,14},{7,15},{8,0},{9,1},... | collective-permute-start | bytes 221192 | tf_op jit(solution)/shard_map/ppermute | solution.py:662
  228.9 7.4 %collective-permute-start.50 = (f32[72,768]{1,0:T(8,128)S(1)}, f32[72,768]{1,0:T(8,128)S(1)}, u32[]{:S(2)}, u32[]{:S(2)}) collective-permute-start(f32[72,768]{1,0:T(8,128)S(1)} %get-tuple-element.371.refs_0_), channel_id=1, source_target_pairs={{0,16},{16,0},{1,17},{17,1},{2,18},{18,2},{3,19},{19,3},{4,20},{20... | collective-permute-start | bytes 663560 | tf_op jit(solution)/shard_map/ppermute | solution.py:641
  (19 other events, 69.4 us)
